TPU v7x, 32 devices: a whole 2x2x4 slice. The times are simulated.
32 devices in a mesh: ctx: 2 (over y), row: 8 (over z, x), col: 2 (over core).
Axes of the slice: x: 2, y: 2, z: 4, core: 2. Of those that a mesh axis runs over, the one named last changes fastest.
Arguments:
- context_map: bfloat16 [128, 512, 256], P(('ctx', 'row'), 'col'), parts along dimension 0, may hold values from -6 to 6
- norm_gains: float32 [3, 256], replicated, may hold values from 0.25 to 1.75
- conv_biases: float32 [3, 256], replicated, may hold values from -3 to 3
- conv_weights: bfloat16 [3, 3, 3, 256, 256], replicated, may hold values from -0.125 to 0.125
Outputs:
- refined: bfloat16 [128, 512, 256], P(('ctx', 'row'), 'col'), parts along dimension 0
There are 2 independent parts, one for each index of `ctx`. A program takes and returns all parts, laid end to end along the dimension named above; an argument that names none is the same for every part. Nothing has to cross between parts.
All inputs are finite; a program needn't handle non-finite values.
Results may differ from a plain program's by a relative error of at most 0.0052.
Values may be sent and summed in bfloat16 or wider, within the bound.
No kernel may reach another device: no remote copies, remote signals or barrier semaphores. Data moves between devices by JAX's collectives and lax.ppermute only.
A program may use at most 64 MiB of HBM per device.

v0:
```python
import jax
import jax.numpy as jnp
from jax import lax
from jax.sharding import PartitionSpec as P

epsilon = 1e-05


def extended(x, sides, width):
    for axis, dim in sides:
        size, length = (lax.axis_size(axis), x.shape[dim])
        up = [(i, (i + 1) % size) for i in range(size - 1)]
        down = [(j, i) for i, j in up]
        last = lax.slice_in_dim(x, length - width, length, axis=dim)
        first = lax.slice_in_dim(x, 0, width, axis=dim)
        before = lax.ppermute(last, axis, up)
        after = lax.ppermute(first, axis, down)
        x = jnp.concatenate([before, x, after], axis=dim)
    return x


def normalize(current, gain_row):
    values = current.astype(jnp.float32)
    centred = values - jnp.mean(values, axis=-1, keepdims=True)
    variance = jnp.mean(centred * centred, axis=-1, keepdims=True)
    return (centred * lax.rsqrt(variance + epsilon) * gain_row).astype(jnp.bfloat16)


def convolve(padded, kernel, row_step, col_step, out_rows, out_cols):
    channels = padded.shape[2]
    tap_list = []
    for tap_row in range(3):
        for tap_col in range(3):
            tap_list.append(
                lax.slice(
                    padded,
                    (tap_row * row_step, tap_col * col_step, 0),
                    (tap_row * row_step + out_rows, tap_col * col_step + out_cols, channels),
                )
            )
    stacked = jnp.concatenate(tap_list, axis=2).reshape(out_rows * out_cols, 9 * channels)
    product = jnp.dot(
        stacked, kernel.reshape(9 * channels, kernel.shape[3]), preferred_element_type=jnp.float32
    )
    return product.reshape(out_rows, out_cols, kernel.shape[3])


def update(current, response, bias_row):
    return (current.astype(jnp.float32) + jnp.maximum(response + bias_row, 0.0)).astype(
        jnp.bfloat16
    )


def class_rims(normed, width):
    return extended(normed, (("col", 1),), width)


def shards(context_map, norm_gains, conv_biases, conv_weights):
    tile_rows, tile_cols, channels = context_map.shape
    normed = normalize(context_map, norm_gains[0])
    padded = extended(normed, (("row", 0), ("col", 1)), 4)
    current = update(
        context_map, convolve(padded, conv_weights[0], 4, 4, tile_rows, tile_cols), conv_biases[0]
    )
    class_count = lax.axis_size("row") // tile_rows
    sub_cols = tile_cols // class_count
    outgoing = (
        current.reshape(tile_rows, sub_cols, class_count, channels)
        .transpose(0, 2, 1, 3)
        .reshape(tile_rows * class_count, sub_cols, channels)
    )
    grouped = lax.all_to_all(outgoing, "row", split_axis=0, concat_axis=0, tiled=True)
    sub_rows = grouped.shape[0]
    for position, dilation in ((1, 32), (2, 64)):
        normed = normalize(grouped, norm_gains[position])
        row_gap = dilation // tile_rows
        col_gap = dilation // class_count
        with_sides = class_rims(normed, col_gap)
        padded = jnp.pad(with_sides, ((row_gap, row_gap), (0, 0), (0, 0)))
        response = convolve(padded, conv_weights[position], row_gap, col_gap, sub_rows, sub_cols)
        grouped = update(grouped, response, conv_biases[position])
    returned = lax.all_to_all(grouped, "row", split_axis=0, concat_axis=0, tiled=True)
    return (
        returned.reshape(tile_rows, class_count, sub_cols, channels)
        .transpose(0, 2, 1, 3)
        .reshape(tile_rows, tile_cols, channels)
    )


def solution(mesh):
    return jax.shard_map(
        shards,
        mesh=mesh,
        in_specs=(P(("ctx", "row"), "col", None), P(), P(), P()),
        out_specs=P(("ctx", "row"), "col", None),
        check_vma=False,
    )
```

profile of v0, /device:TPU:1, one launch (start us, length us, event | category | flops | bytes accessed | tf_op | source)
XLA Modules:
  0.0 125.4 jit_solution(14104926304411926361)
XLA Ops:
  0.0 1.7 %convert_reduce_fusion.2 = f32[8,256]{1,0:T(8,128)S(1)} fusion(bf16[8,256,256]{2,1,0:T(8,128)(2,1)} %param.4), kind=kLoop, calls=%fused_computation.11 | loop fusion | flops 1046528 | bytes 1056768 | tf_op jit(solution)/shard_map/reduce_sum | solution.py:24
  1.7 1.9 %fusion.18 = f32[8,256]{1,0:T(8,128)S(1)} fusion(bf16[8,256,256]{2,1,0:T(8,128)(2,1)} %param.4, f32[8,256]{1,0:T(8,128)S(1)} %broadcast_multiply_fusion.2), kind=kLoop, calls=%fused_computation.31 | loop fusion | flops 2095104 | bytes 1064960 | tf_op jit(solution)/shard_map/reduce_sum | solution.py:25
  3.6 0.0 copy-start.1
  3.6 0.9 fusion.35
  4.5 0.7 fusion.20
  5.2 0.1 fusion.33
  5.3 4.0 %collective-permute-start = (bf16[4,256,256]{2,1,0:T(8,128)(2,1)S(1)}, bf16[4,256,256]{2,1,0:T(8,128)(2,1)S(1)}, u32[]{:S(2)}, u32[]{:S(2)}) collective-permute-start(bf16[4,256,256]{2,1,0:T(8,128)(2,1)S(1)} %get-tuple-element.16), channel_id=1, source_target_pairs={{0,2},{2,4},{4,6},{6,8},{8,10},{10,12},{12,14},{1,3},{3,5},{5,7},{... | collective-permute-start | bytes 1572872 | tf_op jit(solution)/shard_map/ppermute | solution.py:16
  9.2 1.3 %collective-permute-start.1 = (bf16[4,256,256]{2,1,0:T(8,128)(2,1)S(1)}, bf16[4,256,256]{2,1,0:T(8,128)(2,1)S(1)}, u32[]{:S(2)}, u32[]{:S(2)}) collective-permute-start(bf16[4,256,256]{2,1,0:T(8,128)(2,1)S(1)} %get-tuple-element.17), channel_id=1, source_target_pairs={{2,0},{4,2},{6,4},{8,6},{10,8},{12,10},{14,12},{3,1},{5,3},{7,5},{... | collective-permute-start | bytes 1572872 | tf_op jit(solution)/shard_map/ppermute | solution.py:17
  10.5 0.4 fusion.30
  10.9 0.0 copy-start.2
  10.9 20.1 %collective-permute-done = bf16[4,256,256]{2,1,0:T(8,128)(2,1)S(1)} collective-permute-done((bf16[4,256,256]{2,1,0:T(8,128)(2,1)S(1)}, bf16[4,256,256]{2,1,0:T(8,128)(2,1)S(1)}, u32[]{:S(2)}, u32[]{:S(2)}) %collective-permute-start) | collective-permute-done | bytes 524320 | tf_op jit(solution)/shard_map/ppermute | solution.py:16
  31.0 0.0 collective-permute-done.1
  31.1 1.3 %collective-permute-start.2 = (bf16[16,4,256]{2,1,0:T(4,128)(2,1)S(1)}, bf16[16,4,256]{2,1,0:T(4,128)(2,1)S(1)}, u32[]{:S(2)}, u32[]{:S(2)}) collective-permute-start(bf16[16,4,256]{2,1,0:T(4,128)(2,1)S(1)} %get-tuple-element.11), channel_id=1, source_target_pairs={{0,1},{2,3},{4,5},{6,7},{8,9},{10,11},{12,13},{14,15},{16,17},{18,... | collective-permute-start | bytes 98312 | tf_op jit(solution)/shard_map/ppermute | solution.py:16
  32.4 3.5 %collective-permute-start.3 = (bf16[16,4,256]{2,1,0:T(4,128)(2,1)S(1)}, bf16[16,4,256]{2,1,0:T(4,128)(2,1)S(1)}, u32[]{:S(2)}, u32[]{:S(2)}) collective-permute-start(bf16[16,4,256]{2,1,0:T(4,128)(2,1)S(1)} %get-tuple-element.10), channel_id=1, source_target_pairs={{1,0},{3,2},{5,4},{7,6},{9,8},{11,10},{13,12},{15,14},{17,16},{19,... | collective-permute-start | bytes 98312 | tf_op jit(solution)/shard_map/ppermute | solution.py:17
  35.8 0.0 collective-permute-done.2
  35.8 0.8 collective-permute-done.3
  36.7 1.0 pad_maximum_fusion
  37.6 0.1 slice_dynamic-update-slice_fusion.11
  37.7 0.1 fusion.29
  37.8 0.2 slice_dynamic-update-slice_fusion.10
  38.1 0.1 slice_dynamic-update-slice_fusion.9
  38.1 0.7 constant_dynamic-update-slice_fusion
  38.9 0.2 slice_dynamic-update-slice_fusion.8
  39.1 0.1 slice_dynamic-update-slice_fusion.7
  39.2 0.1 fusion.28
  39.3 0.2 slice_dynamic-update-slice_fusion.6
  39.5 2.6 %fusion.21 = bf16[8,256,256]{2,1,0:T(8,128)(2,1)S(1)} fusion(bf16[8,256,256]{2,1,0:T(8,128)(2,1)S(1)} %copy-done, bf16[8,256,2304]{2,1,0:T(8,128)(2,1)S(1)} %slice_dynamic-update-slice_fusion.6, bf16[2304,256,1]{1,0,2:T(8,128)(2,1)S(1)} %bitcast.23, f32[256]{0:T(256)S(1)} %bitcast.32), kind=kOutput, calls=%fused_computation.34 | convolution fusion | flops 2418540544 | bytes 12715008 | tf_op jit(solution)/shard_map/dot_general | solution.py:42
  42.2 31.8 %all_to_all.10 = bf16[8,256,256]{2,1,0:T(8,128)(2,1)S(1)} all-to-all(bf16[8,256,256]{2,1,0:T(8,128)(2,1)S(1)} %fusion.21), channel_id=1, replica_groups=mesh['ctx'=2,'row'=8,'col'=2] {'row'}, dimensions={0} | all-to-all | bytes 2097152 | tf_op jit(solution)/shard_map/all_to_all | solution.py:72
  74.0 0.3 convert_reduce_fusion.1
  74.3 0.6 fusion.15
  75.0 0.7 fusion.17
  75.8 1.3 %collective-permute-start.4 = (bf16[8,32,256]{2,1,0:T(8,128)(2,1)S(1)}, bf16[8,32,256]{2,1,0:T(8,128)(2,1)S(1)}, u32[]{:S(2)}, u32[]{:S(2)}) collective-permute-start(bf16[8,32,256]{2,1,0:T(8,128)(2,1)S(1)} %get-tuple-element.14), channel_id=1, source_target_pairs={{0,1},{2,3},{4,5},{6,7},{8,9},{10,11},{12,13},{14,15},{16,17},{18,... | collective-permute-start | bytes 393224 | tf_op jit(solution)/shard_map/ppermute | solution.py:16
  77.1 3.9 %collective-permute-start.5 = (bf16[8,32,256]{2,1,0:T(8,128)(2,1)S(1)}, bf16[8,32,256]{2,1,0:T(8,128)(2,1)S(1)}, u32[]{:S(2)}, u32[]{:S(2)}) collective-permute-start(bf16[8,32,256]{2,1,0:T(8,128)(2,1)S(1)} %get-tuple-element.15), channel_id=1, source_target_pairs={{1,0},{3,2},{5,4},{7,6},{9,8},{11,10},{13,12},{15,14},{17,16},{19,... | collective-permute-start | bytes 393224 | tf_op jit(solution)/shard_map/ppermute | solution.py:17
  81.0 0.1 broadcast_dynamic-update-slice_fusion.4
  81.0 0.0 collective-permute-done.4
  81.1 0.7 collective-permute-done.5
  81.7 0.4 fusion.5
  82.2 0.1 slice_dynamic-update-slice_fusion.5
  82.2 0.1 slice_dynamic-update-slice_fusion.4
  82.3 0.1 slice_dynamic-update-slice_fusion.3
  82.4 0.1 fusion.27
  82.5 0.7 constant_dynamic-update-slice_fusion.1
  83.2 0.1 fusion.26
  83.3 0.1 slice_dynamic-update-slice_fusion.2
  83.4 0.1 slice_dynamic-update-slice_fusion.1
  83.4 0.1 slice_dynamic-update-slice_fusion
  83.5 2.8 %convert_reduce_fusion = (f32[8,256]{1,0:T(8,128)S(1)}, bf16[8,256,256]{2,1,0:T(8,128)(2,1)S(1)}) fusion(f32[256]{0:T(256)S(1)} %bitcast.31, bf16[8,256,2304]{2,1,0:T(8,128)(2,1)S(1)} %slice_dynamic-update-slice_fusion, bf16[2304,256,1]{1,0,2:T(8,128)(2,1)S(1)} %bitcast.22, bf16[8,256,256]{2,1,0:T(8,128)(2,1)S(1)} %all_to_all.10), kind=kOutput, calls=%fused_computation.5 | convolution fusion | flops 2419587072 | bytes 12723200 | tf_op jit(solution)/shard_map/dot_general | solution.py:42
  86.3 0.6 fusion.12
  86.9 0.7 fusion.14
  87.7 1.3 %collective-permute-start.6 = (bf16[8,64,256]{2,1,0:T(8,128)(2,1)S(1)}, bf16[8,64,256]{2,1,0:T(8,128)(2,1)S(1)}, u32[]{:S(2)}, u32[]{:S(2)}) collective-permute-start(bf16[8,64,256]{2,1,0:T(8,128)(2,1)S(1)} %get-tuple-element.13), channel_id=1, source_target_pairs={{0,1},{2,3},{4,5},{6,7},{8,9},{10,11},{12,13},{14,15},{16,17},{18,... | collective-permute-start | bytes 786440 | tf_op jit(solution)/shard_map/ppermute | solution.py:16
  89.0 0.1 broadcast_dynamic-update-slice_fusion.3
  89.1 0.1 broadcast_dynamic-update-slice_fusion.2
  89.2 3.1 %collective-permute-start.7 = (bf16[8,64,256]{2,1,0:T(8,128)(2,1)S(1)}, bf16[8,64,256]{2,1,0:T(8,128)(2,1)S(1)}, u32[]{:S(2)}, u32[]{:S(2)}) collective-permute-start(bf16[8,64,256]{2,1,0:T(8,128)(2,1)S(1)} %get-tuple-element.12), channel_id=1, source_target_pairs={{1,0},{3,2},{5,4},{7,6},{9,8},{11,10},{13,12},{15,14},{17,16},{19,... | collective-permute-start | bytes 786440 | tf_op jit(solution)/shard_map/ppermute | solution.py:17
  92.2 0.0 collective-permute-done.6
  92.3 0.1 fusion.25
  92.3 0.7 constant_dynamic-update-slice_fusion.2
  93.1 0.3 collective-permute-done.7
  93.4 0.1 fusion.24
  93.4 0.1 broadcast_dynamic-update-slice_fusion.1
  93.5 0.1 broadcast_dynamic-update-slice_fusion
  93.6 0.1 broadcast_dynamic-update-slice_fusion.5
  93.7 2.6 %fusion.23 = bf16[8,256,256]{2,1,0:T(8,128)(2,1)S(1)} fusion(bf16[8,256,256]{2,1,0:T(8,128)(2,1)S(1)} %get-tuple-element.25, bf16[8,256,2304]{2,1,0:T(8,128)(2,1)S(1)} %broadcast_dynamic-update-slice_fusion.5, bf16[2304,256,1]{1,0,2:T(8,128)(2,1)S(1)} %bitcast.21, f32[256]{0:T(256)S(1)} %bitcast.30), kind=kOutput, calls=%fused_computation.36 | convolution fusion | flops 2418540544 | bytes 12715008 | tf_op jit(solution)/shard_map/dot_general | solution.py:42
  96.3 28.1 %all_to_all.11 = bf16[8,256,256]{2,1,0:T(8,128)(2,1)S(1)} all-to-all(bf16[8,256,256]{2,1,0:T(8,128)(2,1)S(1)} %fusion.23), channel_id=1, replica_groups=mesh['ctx'=2,'row'=8,'col'=2] {'row'}, dimensions={0} | all-to-all | bytes 2097152 | tf_op jit(solution)/shard_map/all_to_all | solution.py:82
  124.4 1.0 copy.30
  (14 shorter events, 0.1 us)
Async XLA Ops:
  0.0 4.5 %copy-start = (bf16[8,256,256]{2,1,0:T(8,128)(2,1)S(1)}, bf16[8,256,256]{2,1,0:T(8,128)(2,1)}, u32[]{:S(2)}) copy-start(bf16[8,256,256]{2,1,0:T(8,128)(2,1)} %param.4) | copy-start | bytes 3145732
  3.6 7.0 %copy-start.1 = (bf16[3,3,3,256,256]{4,3,2,1,0:T(8,128)(2,1)S(1)}, bf16[3,3,3,256,256]{4,3,2,1,0:T(8,128)(2,1)}, u32[]{:S(2)}) copy-start(bf16[3,3,3,256,256]{4,3,2,1,0:T(8,128)(2,1)} %param.7) | copy-start | bytes 10616836
  5.3 25.8 %collective-permute-start = (bf16[4,256,256]{2,1,0:T(8,128)(2,1)S(1)}, bf16[4,256,256]{2,1,0:T(8,128)(2,1)S(1)}, u32[]{:S(2)}, u32[]{:S(2)}) collective-permute-start(bf16[4,256,256]{2,1,0:T(8,128)(2,1)S(1)} %get-tuple-element.16), channel_id=1, source_target_pairs={{0,2},{2,4},{4,6},{6,8},{8,10},{10,12},{12,14},{1,3},{3,5},{5,7},{... | collective-permute-start | bytes 1572872 | tf_op jit(solution)/shard_map/ppermute | solution.py:16
  9.2 21.8 %collective-permute-start.1 = (bf16[4,256,256]{2,1,0:T(8,128)(2,1)S(1)}, bf16[4,256,256]{2,1,0:T(8,128)(2,1)S(1)}, u32[]{:S(2)}, u32[]{:S(2)}) collective-permute-start(bf16[4,256,256]{2,1,0:T(8,128)(2,1)S(1)} %get-tuple-element.17), channel_id=1, source_target_pairs={{2,0},{4,2},{6,4},{8,6},{10,8},{12,10},{14,12},{3,1},{5,3},{7,5},{... | collective-permute-start | bytes 1572872 | tf_op jit(solution)/shard_map/ppermute | solution.py:17
  10.9 24.9 %copy-start.2 = (f32[3,256]{1,0:T(4,128)S(1)}, f32[3,256]{1,0:T(4,128)}, u32[]{:S(2)}) copy-start(f32[3,256]{1,0:T(4,128)} %param.6) | copy-start | bytes 9220
  31.1 4.8 %collective-permute-start.2 = (bf16[16,4,256]{2,1,0:T(4,128)(2,1)S(1)}, bf16[16,4,256]{2,1,0:T(4,128)(2,1)S(1)}, u32[]{:S(2)}, u32[]{:S(2)}) collective-permute-start(bf16[16,4,256]{2,1,0:T(4,128)(2,1)S(1)} %get-tuple-element.11), channel_id=1, source_target_pairs={{0,1},{2,3},{4,5},{6,7},{8,9},{10,11},{12,13},{14,15},{16,17},{18,... | collective-permute-start | bytes 98312 | tf_op jit(solution)/shard_map/ppermute | solution.py:16
  32.4 4.3 %collective-permute-start.3 = (bf16[16,4,256]{2,1,0:T(4,128)(2,1)S(1)}, bf16[16,4,256]{2,1,0:T(4,128)(2,1)S(1)}, u32[]{:S(2)}, u32[]{:S(2)}) collective-permute-start(bf16[16,4,256]{2,1,0:T(4,128)(2,1)S(1)} %get-tuple-element.10), channel_id=1, source_target_pairs={{1,0},{3,2},{5,4},{7,6},{9,8},{11,10},{13,12},{15,14},{17,16},{19,... | collective-permute-start | bytes 98312 | tf_op jit(solution)/shard_map/ppermute | solution.py:17
  75.8 5.3 %collective-permute-start.4 = (bf16[8,32,256]{2,1,0:T(8,128)(2,1)S(1)}, bf16[8,32,256]{2,1,0:T(8,128)(2,1)S(1)}, u32[]{:S(2)}, u32[]{:S(2)}) collective-permute-start(bf16[8,32,256]{2,1,0:T(8,128)(2,1)S(1)} %get-tuple-element.14), channel_id=1, source_target_pairs={{0,1},{2,3},{4,5},{6,7},{8,9},{10,11},{12,13},{14,15},{16,17},{18,... | collective-permute-start | bytes 393224 | tf_op jit(solution)/shard_map/ppermute | solution.py:16
  77.1 4.7 %collective-permute-start.5 = (bf16[8,32,256]{2,1,0:T(8,128)(2,1)S(1)}, bf16[8,32,256]{2,1,0:T(8,128)(2,1)S(1)}, u32[]{:S(2)}, u32[]{:S(2)}) collective-permute-start(bf16[8,32,256]{2,1,0:T(8,128)(2,1)S(1)} %get-tuple-element.15), channel_id=1, source_target_pairs={{1,0},{3,2},{5,4},{7,6},{9,8},{11,10},{13,12},{15,14},{17,16},{19,... | collective-permute-start | bytes 393224 | tf_op jit(solution)/shard_map/ppermute | solution.py:17
  87.7 4.5 %collective-permute-start.6 = (bf16[8,64,256]{2,1,0:T(8,128)(2,1)S(1)}, bf16[8,64,256]{2,1,0:T(8,128)(2,1)S(1)}, u32[]{:S(2)}, u32[]{:S(2)}) collective-permute-start(bf16[8,64,256]{2,1,0:T(8,128)(2,1)S(1)} %get-tuple-element.13), channel_id=1, source_target_pairs={{0,1},{2,3},{4,5},{6,7},{8,9},{10,11},{12,13},{14,15},{16,17},{18,... | collective-permute-start | bytes 786440 | tf_op jit(solution)/shard_map/ppermute | solution.py:16
  89.2 4.2 %collective-permute-start.7 = (bf16[8,64,256]{2,1,0:T(8,128)(2,1)S(1)}, bf16[8,64,256]{2,1,0:T(8,128)(2,1)S(1)}, u32[]{:S(2)}, u32[]{:S(2)}) collective-permute-start(bf16[8,64,256]{2,1,0:T(8,128)(2,1)S(1)} %get-tuple-element.12), channel_id=1, source_target_pairs={{1,0},{3,2},{5,4},{7,6},{9,8},{11,10},{13,12},{15,14},{17,16},{19,... | collective-permute-start | bytes 786440 | tf_op jit(solution)/shard_map/ppermute | solution.py:17
where the time goes:
time: 128 us; the launch traced here: 125 us
  blocking collectives  59.9 us (47%)
  waiting for transfers between devices  21.9 us (17%)
  starting transfers between devices  19.5 us (15%)
  other arithmetic  11.4 us (9%)
  matrix products  8.03 us (6%)
  local copies, waits for them, and re-layouts  4.17 us (3%)
    all_to_all x1, blocking collectives, shards(): lax.all_to_all(outgoing, 'row', split_axis=0, concat_axis=0, tiled=True)  31.8 us
    all_to_all x1, blocking collectives, shards(): lax.all_to_all(grouped, 'row', split_axis=0, concat_axis=0, tiled=True)  28.1 us
    ppermute x4, waiting for transfers between devices, extended(): before = lax.ppermute(last, axis, up)  20.1 us
    ppermute x4, starting transfers between devices, extended(): after = lax.ppermute(first, axis, down)  11.7 us
    dot_general x3, matrix products, convolve(): jnp.dot(stacked, kernel.reshape(9 * channels, kernel.shape[3]), preferred...  8.03 us
    ppermute x4, starting transfers between devices, extended(): before = lax.ppermute(last, axis, up)  7.85 us
    reduce_sum x3, other arithmetic, normalize(): variance = jnp.mean(centred * centred, axis=-1, keepdims=True)  3.16 us
    unnamed x9, other arithmetic  2.59 us
  transfers between devices with their start and end apart: 8, of which 4 were waited for; matrix products, arithmetic and copies ran while one was open for 1% of the time, Pallas kernels for 0%

commit v1 on v0

--- a/solution.py
+++ b/solution.py
@@ -1,9 +1,16 @@
+import functools
+
 import jax
 import jax.numpy as jnp
 from jax import lax
+from jax.experimental import pallas as pl
+from jax.experimental.pallas import tpu as pltpu
 from jax.sharding import PartitionSpec as P
 
 epsilon = 1e-05
+dilations = (4, 32, 64)
+lane_pad = 16
+vmem_limit = 40 * 1024 * 1024
 
 
 def extended(x, sides, width):
@@ -51,11 +58,7 @@
     )
 
 
-def class_rims(normed, width):
-    return extended(normed, (("col", 1),), width)
-
-
-def shards(context_map, norm_gains, conv_biases, conv_weights):
+def by_classes(context_map, norm_gains, conv_biases, conv_weights):
     tile_rows, tile_cols, channels = context_map.shape
     normed = normalize(context_map, norm_gains[0])
     padded = extended(normed, (("row", 0), ("col", 1)), 4)
@@ -75,7 +78,7 @@
         normed = normalize(grouped, norm_gains[position])
         row_gap = dilation // tile_rows
         col_gap = dilation // class_count
-        with_sides = class_rims(normed, col_gap)
+        with_sides = extended(normed, (("col", 1),), col_gap)
         padded = jnp.pad(with_sides, ((row_gap, row_gap), (0, 0), (0, 0)))
         response = convolve(padded, conv_weights[position], row_gap, col_gap, sub_rows, sub_cols)
         grouped = update(grouped, response, conv_biases[position])
@@ -87,6 +90,389 @@
     )
 
 
+def vmem_spec():
+    return pl.BlockSpec(memory_space=pltpu.VMEM)
+
+
+def smem_spec():
+    return pl.BlockSpec(memory_space=pltpu.SMEM)
+
+
+def kernel_call(body, out_shape, in_specs, scratch, flops, bytes_accessed):
+    return pl.pallas_call(
+        body,
+        out_shape=out_shape,
+        in_specs=in_specs,
+        out_specs=jax.tree.map(lambda _: vmem_spec(), out_shape),
+        scratch_shapes=scratch,
+        compiler_params=pltpu.CompilerParams(vmem_limit_bytes=vmem_limit),
+        cost_estimate=pl.CostEstimate(
+            flops=flops, bytes_accessed=bytes_accessed, transcendentals=0
+        ),
+    )
+
+
+def place(core, at_zero, at_one):
+    return pl.multiple_of(jnp.where(core == 0, at_zero, at_one), lane_pad)
+
+
+def first_layer_kernel(
+    segments, zero_at, out_at, rows, width, core_ref, x_ref, gain_ref, bias_ref, w_ref, *rest
+):
+    parts, (next_ref, normed_ref, window, taps) = rest[:-4], rest[-4:]
+    refs = (x_ref,) + tuple(parts)
+    core = core_ref[0]
+    half = rows // 2
+    channels = x_ref.shape[2]
+    gain = gain_ref[0:1, :]
+    for which, source_row, window_row, count, source, target, columns in segments:
+        src, dst = place(core, *source), place(core, *target)
+        for r in range(count):
+            window[window_row + r, pl.ds(dst, columns), :] = normalize(
+                refs[which][source_row + r, pl.ds(src, columns), :], gain
+            )
+    if zero_at is not None:
+        dst = place(core, *zero_at)
+        for r in range(2 * rows):
+            window[r, pl.ds(dst, lane_pad), :] = jnp.zeros((lane_pad, channels), jnp.bfloat16)
+    step = dilations[0]
+    for b in range(3):
+        first = lane_pad + (b - 1) * step
+        for r in range(2 * rows):
+            taps[b, r] = window[r, first : first + width, :]
+    stacked = jnp.concatenate(
+        [
+            taps[b, a * half : a * half + rows].reshape(rows * width, channels)
+            for a in range(3)
+            for b in range(3)
+        ],
+        axis=1,
+    )
+    response = jnp.dot(
+        stacked, w_ref[...].reshape(9 * channels, channels), preferred_element_type=jnp.float32
+    )
+    out_col = place(core, *out_at)
+    current = x_ref[:, pl.ds(out_col, width), :].reshape(rows * width, channels)
+    result = update(current, response, bias_ref[0:1, :])
+    next_ref[...] = result.reshape(rows, width, channels)
+    normed_ref[...] = normalize(result, gain_ref[1:2, :]).reshape(rows, width, channels)
+
+
+def first_layer(core, x, gains, biases, weights, parts, segments, zero_at, out_at, width):
+    rows, _, channels = x.shape
+    out = jax.ShapeDtypeStruct((rows, width, channels), x.dtype)
+    cells = rows * width
+    body = functools.partial(first_layer_kernel, segments, zero_at, out_at, rows, width)
+    return kernel_call(
+        body,
+        (out, out),
+        [smem_spec()] + [vmem_spec()] * (4 + len(parts)),
+        [
+            pltpu.VMEM((2 * rows, width + 2 * lane_pad, channels), x.dtype),
+            pltpu.VMEM((3, 2 * rows, width, channels), x.dtype),
+        ],
+        18 * cells * channels * channels,
+        9 * channels * channels * 2,
+    )(core, x, gains, biases, weights, *parts)
+
+
+def second_layer_kernel(
+    strip,
+    core_ref,
+    gain_ref,
+    bias_ref,
+    w_ref,
+    wx_ref,
+    near_ref,
+    mid_ref,
+    far_ref,
+    cnear_ref,
+    cfar_ref,
+    side_ref,
+    near1_ref,
+    mid1_ref,
+    far1_ref,
+    lows_ref,
+    highs_ref,
+    nlows_ref,
+    nhighs_ref,
+    acc_ref,
+    mids_ref,
+    own,
+    other,
+    x1,
+):
+    core = core_ref[0]
+    step = dilations[1]
+    rows, mid, channels = mid_ref.shape
+    cols = 2 * strip + mid
+    near_at, far_at = (cols - strip, 0), (0, cols - strip)
+    dst = place(core, step + near_at[0], step + near_at[1])
+    own[:, pl.ds(dst, strip), :] = near_ref[...]
+    other[:, pl.ds(dst, strip), :] = cnear_ref[...]
+    dst = place(core, *near_at)
+    x1[:, pl.ds(dst, strip), :] = near1_ref[...]
+    dst = place(core, step + far_at[0], step + far_at[1])
+    own[:, pl.ds(dst, strip), :] = far_ref[...]
+    other[:, pl.ds(dst, strip), :] = cfar_ref[...]
+    dst = place(core, *far_at)
+    x1[:, pl.ds(dst, strip), :] = far1_ref[...]
+    own[:, step + strip : step + strip + mid, :] = mid_ref[...]
+    other[:, step + strip : step + strip + mid, :] = jnp.zeros((rows, mid, channels), own.dtype)
+    x1[:, strip : strip + mid, :] = mid1_ref[...]
+    dst = place(core, step + cols, 0)
+    own[:, pl.ds(dst, step), :] = side_ref[0:rows]
+    other[:, pl.ds(dst, step), :] = side_ref[rows : 2 * rows]
+    dst = place(core, 0, step + cols)
+    own[:, pl.ds(dst, step), :] = jnp.zeros((rows, step, channels), own.dtype)
+    other[:, pl.ds(dst, step), :] = jnp.zeros((rows, step, channels), own.dtype)
+    edge = strip - step
+    w_own = w_ref[...].reshape(3 * channels, channels)
+    w_other = wx_ref[...].reshape(3 * channels, channels)
+    weights = jnp.concatenate([w_own, w_other], axis=0)
+    for first, width in ((0, edge), (edge, mid + 2 * step), (cols - edge, edge)):
+        stacked = jnp.concatenate(
+            [
+                ref[:, first + b * step : first + b * step + width, :].reshape(
+                    rows * width, channels
+                )
+                for ref in (own, other)
+                for b in range(3)
+            ],
+            axis=1,
+        )
+        response = jnp.dot(stacked, weights, preferred_element_type=jnp.float32)
+        current = x1[:, first : first + width, :]
+        if first == edge:
+            acc_ref[...] = response.reshape(rows, width, channels)
+            mids_ref[...] = current
+        else:
+            result = update(
+                current.reshape(rows * width, channels), response, bias_ref[1:2, :]
+            )
+            normed = normalize(result, gain_ref[2:3, :])
+            result_ref, out_ref = (lows_ref, nlows_ref) if first == 0 else (highs_ref, nhighs_ref)
+            result_ref[...] = result.reshape(rows, width, channels)
+            out_ref[...] = normed.reshape(rows, width, channels)
+
+
+def last_kernel(
+    core_ref,
+    gain_ref,
+    bias_ref,
+    wx_ref,
+    w_ref,
+    cmid_ref,
+    acc_ref,
+    mids_ref,
+    lows_ref,
+    highs_ref,
+    nlows_ref,
+    nhighs_ref,
+    side_ref,
+    out_ref,
+    other,
+    normed,
+    x2,
+):
+    core = core_ref[0]
+    rows, mid, channels = cmid_ref.shape
+    edge = nlows_ref.shape[1]
+    step, reach = dilations[1], dilations[2]
+    width = mid + 2 * step
+    cols = 2 * edge + width
+    blank = jnp.zeros((rows, 2 * step, channels), other.dtype)
+    other[:, 0 : 2 * step, :] = blank
+    other[:, 2 * step + mid : 4 * step + mid, :] = blank
+    other[:, 2 * step : 2 * step + mid, :] = cmid_ref[...]
+    stacked = jnp.concatenate(
+        [
+            other[:, b * step : b * step + width, :].reshape(rows * width, channels)
+            for b in range(3)
+        ],
+        axis=1,
+    )
+    response = acc_ref[...].reshape(rows * width, channels) + jnp.dot(
+        stacked, wx_ref[...].reshape(3 * channels, channels), preferred_element_type=jnp.float32
+    )
+    result = update(
+        mids_ref[...].reshape(rows * width, channels), response, bias_ref[1:2, :]
+    )
+    x2[:, 0:edge, :] = lows_ref[...]
+    x2[:, edge : edge + width, :] = result.reshape(rows, width, channels)
+    x2[:, edge + width : cols, :] = highs_ref[...]
+    normed[:, reach : reach + edge, :] = nlows_ref[...]
+    normed[:, reach + edge : reach + edge + width, :] = normalize(
+        result, gain_ref[2:3, :]
+    ).reshape(rows, width, channels)
+    normed[:, reach + edge + width : reach + cols, :] = nhighs_ref[...]
+    dst = place(core, reach + cols, 0)
+    normed[:, pl.ds(dst, reach), :] = side_ref[...]
+    dst = place(core, 0, reach + cols)
+    normed[:, pl.ds(dst, reach), :] = jnp.zeros((rows, reach, channels), normed.dtype)
+    stacked = jnp.concatenate(
+        [
+            normed[:, b * reach : b * reach + cols, :].reshape(rows * cols, channels)
+            for b in range(3)
+        ],
+        axis=1,
+    )
+    response = jnp.dot(
+        stacked, w_ref[...].reshape(3 * channels, channels), preferred_element_type=jnp.float32
+    )
+    out_ref[...] = update(
+        x2[...].reshape(rows * cols, channels), response, bias_ref[2:3, :]
+    ).reshape(rows, cols, channels)
+
+
+def by_halves(context_map, norm_gains, conv_biases, conv_weights):
+    rows, cols, channels = context_map.shape
+    size = lax.axis_size("row")
+    half = rows // 2
+    strip = dilations[1] + dilations[2]
+    mid = cols - 2 * strip
+    pad = lane_pad
+    core = lax.axis_index("col")
+    upper_half = lax.axis_index("row") < size // 2
+    core_array = jnp.full((1,), core, jnp.int32)
+    swap = [(0, 1), (1, 0)]
+    partner = [(i, (i + size // 2) % size) for i in range(size)]
+    down = [(i, i + 1) for i in range(size - 1)]
+    up = [(j, i) for i, j in down]
+
+    def columns(x, at_zero, at_one, width):
+        return lax.dynamic_slice_in_dim(x, jnp.where(core == 0, at_zero, at_one), width, axis=1)
+
+    def halos(at_zero, at_one, width):
+        part = columns(context_map, at_zero, at_one, width)
+        return (
+            lax.ppermute(part[rows - half :], "row", down),
+            lax.ppermute(part[:half], "row", up),
+        )
+
+    wide = strip + pad
+    near_at, far_at = (cols - strip, 0), (0, cols - strip)
+    above_near, below_near = halos(cols - wide, 0, wide)
+    above_far, below_far = halos(0, cols - wide, wide)
+    above_mid, below_mid = halos(wide, wide, cols - 2 * wide)
+
+    rim = jnp.concatenate(
+        [
+            columns(above_near, wide - pad, 0, pad),
+            columns(context_map, cols - pad, 0, pad),
+            columns(below_near, wide - pad, 0, pad),
+        ],
+        axis=0,
+    )
+    rim = lax.ppermute(rim, "col", swap)
+
+    params = (norm_gains, conv_biases, conv_weights[0])
+    near_segments = (
+        (0, 0, half, rows, (cols - wide, 0), (0, pad), wide),
+        (1, 0, 0, half, (0, 0), (0, pad), wide),
+        (2, 0, half + rows, half, (0, 0), (0, pad), wide),
+        (3, 0, 0, 2 * rows, (0, 0), (wide, 0), pad),
+    )
+    near1, near_n = first_layer(
+        core_array, context_map, *params, (above_near, below_near, rim), near_segments, None,
+        near_at, strip,
+    )
+    cross_near = lax.ppermute(near_n, "row", partner)
+    far_segments = (
+        (0, 0, half, rows, (0, cols - wide), (pad, 0), wide),
+        (1, 0, 0, half, (0, 0), (pad, 0), wide),
+        (2, 0, half + rows, half, (0, 0), (pad, 0), wide),
+    )
+    far1, far_n = first_layer(
+        core_array, context_map, *params, (above_far, below_far), far_segments,
+        (0, wide), far_at, strip,
+    )
+    cross_far = lax.ppermute(far_n, "row", partner)
+    mid_segments = (
+        (0, 0, half, rows, (strip - pad, strip - pad), (0, 0), mid + 2 * pad),
+        (1, 0, 0, half, (0, 0), (2 * pad, 2 * pad), mid - 2 * pad),
+        (2, 0, half + rows, half, (0, 0), (2 * pad, 2 * pad), mid - 2 * pad),
+        (3, 0, 0, half, (wide - 2 * pad, 0), (0, mid), 2 * pad),
+        (4, 0, half + rows, half, (wide - 2 * pad, 0), (0, mid), 2 * pad),
+        (5, 0, 0, half, (0, wide - 2 * pad), (mid, 0), 2 * pad),
+        (6, 0, half + rows, half, (0, wide - 2 * pad), (mid, 0), 2 * pad),
+    )
+    mid1, mid_n = first_layer(
+        core_array, context_map, *params,
+        (above_mid, below_mid, above_far, below_far, above_near, below_near), mid_segments,
+        None, (strip, strip), mid,
+    )
+    cross_mid = lax.ppermute(mid_n, "row", partner)
+
+    step, reach = dilations[1], dilations[2]
+    side = jnp.concatenate(
+        [columns(near_n, strip - step, 0, step), columns(cross_near, strip - step, 0, step)], axis=0
+    )
+    side = lax.ppermute(side, "col", swap)
+    toward = lax.dynamic_index_in_dim(
+        conv_weights[1], jnp.where(upper_half, 2, 0), axis=0, keepdims=False
+    )
+    edge = strip - step
+    wider = mid + 2 * step
+    kind = context_map.dtype
+    edge_shape = jax.ShapeDtypeStruct((rows, edge, channels), kind)
+    lows, highs, n_lows, n_highs, acc, mids = kernel_call(
+        functools.partial(second_layer_kernel, strip),
+        (
+            edge_shape,
+            edge_shape,
+            edge_shape,
+            edge_shape,
+            jax.ShapeDtypeStruct((rows, wider, channels), jnp.float32),
+            jax.ShapeDtypeStruct((rows, wider, channels), kind),
+        ),
+        [smem_spec()] + [vmem_spec()] * 13,
+        [
+            pltpu.VMEM((rows, cols + 2 * step, channels), kind),
+            pltpu.VMEM((rows, cols + 2 * step, channels), kind),
+            pltpu.VMEM((rows, cols, channels), kind),
+        ],
+        12 * rows * cols * channels * channels,
+        6 * channels * channels * 2,
+    )(
+        core_array, norm_gains, conv_biases, conv_weights[1, 1], toward, near_n, mid_n, far_n,
+        cross_near, cross_far, side, near1, mid1, far1,
+    )
+    last_side = lax.ppermute(jnp.where(core == 0, n_highs, n_lows), "col", swap)
+    return kernel_call(
+        last_kernel,
+        jax.ShapeDtypeStruct(context_map.shape, kind),
+        [smem_spec()] + [vmem_spec()] * 12,
+        [
+            pltpu.VMEM((rows, mid + 4 * step, channels), kind),
+            pltpu.VMEM((rows, cols + 2 * reach, channels), kind),
+            pltpu.VMEM((rows, cols, channels), kind),
+        ],
+        8 * rows * cols * channels * channels,
+        3 * channels * channels * 2,
+    )(
+        core_array, norm_gains, conv_biases, toward, conv_weights[2, 1], cross_mid, acc, mids, lows,
+        highs, n_lows, n_highs, last_side,
+    )
+
+
+def shards(context_map, *params):
+    rows, cols, _ = context_map.shape
+    map_rows = lax.axis_size("row") * rows
+    strip = dilations[1] + dilations[2]
+    if (
+        map_rows == 2 * dilations[1]
+        and map_rows <= dilations[2]
+        and rows == 2 * dilations[0]
+        and dilations[1] % rows == 0
+        and lax.axis_size("col") == 2
+        and cols >= 2 * strip + 3 * lane_pad
+        and cols % lane_pad == 0
+    ):
+        return by_halves(context_map, *params)
+    return by_classes(context_map, *params)
+
+
 def solution(mesh):
     return jax.shard_map(
         shards,

time: 128 us -> 84.8 us (0.66); the launches traced: 125 us -> 83.9 us
  blocking collectives: 59.9 us -> 0 us
  waiting for transfers between devices: 21.9 us -> 37 us
  Pallas kernels: 0 us -> 13.7 us
  other arithmetic: 11.4 us -> 0.08 us
  matrix products: 8.03 us -> 0 us
  local copies, waits for them, and re-layouts: 4.17 us -> 9.57 us
  starting transfers between devices: 19.5 us -> 23.3 us
    all_to_all x2 -> x0, blocking collectives: 59.9 us -> none  [the longest x1 31.8 us: shards(): lax.all_to_all(outgoing, 'row', split_axis=0, concat_axis=0, tiled=True)]
    ppermute x8 -> x12, waiting for transfers between devices: 21.9 us -> 37 us  [the longest x1 16.8 us: by_halves(): cross_near = lax.ppermute(near_n, 'row', partner)]
    pallas_call x0 -> x5, Pallas kernels: none -> 13.7 us  [the longest x3 6.6 us: first_layer(): kernel_call(body, (out, out), [smem_spec()] + [vmem_spec()] * (4 + len(pa...]
    dot_general x3 -> x0, matrix products: 8.03 us -> none  [convolve(): jnp.dot(stacked, kernel.reshape(9 * channels, kernel.shape[3]), preferred...]
    reduce_sum x5 -> x0, other arithmetic: 5.16 us -> none  [the longest x3 3.16 us: normalize(): variance = jnp.mean(centred * centred, axis=-1, keepdims=True)]
    squeeze x0 -> x2, local copies, waits for them, and re-layouts: none -> 4.15 us  [the longest x1 2.84 us: by_halves(): params = (norm_gains, conv_biases, conv_weights[0])]
    ppermute x8 -> x12, starting transfers between devices: 19.5 us -> 23.3 us  [the longest x3 12.1 us: halos(): lax.ppermute(part[rows - half:], 'row', down)]
    unnamed x9 -> x0, other arithmetic: 2.59 us -> none
  transfers between devices with their start and end apart: 8 -> 12, of which waited for: 4 -> 4; matrix products, arithmetic and copies ran while one was open for 1% -> 8% of each run, Pallas kernels for 0% -> 12%
where the time goes in v1:
time: 84.8 us; the launch traced here: 83.9 us
  waiting for transfers between devices  37 us (44%)
  starting transfers between devices  23.3 us (27%)
  Pallas kernels  13.7 us (16%)
  local copies, waits for them, and re-layouts  9.57 us (11%)
    ppermute x1, waiting for transfers between devices, by_halves(): cross_near = lax.ppermute(near_n, 'row', partner)  16.8 us
    ppermute x3, starting transfers between devices, halos(): lax.ppermute(part[rows - half:], 'row', down)  12.1 us
    ppermute x1, waiting for transfers between devices, by_halves(): cross_far = lax.ppermute(far_n, 'row', partner)  10.3 us
    ppermute x3, waiting for transfers between devices, halos(): lax.ppermute(part[rows - half:], 'row', down)  8.46 us
    pallas_call x3, Pallas kernels, first_layer(): kernel_call(body, (out, out), [smem_spec()] + [vmem_spec()] * (4 + len(pa...  6.6 us
    ppermute x3, starting transfers between devices, halos(): lax.ppermute(part[:half], 'row', up)  3.86 us
    pallas_call x1, Pallas kernels, by_halves(): kernel_call(last_kernel, jax.ShapeDtypeStruct(context_map.shape, kind), [...  3.77 us
    pallas_call x1, Pallas kernels, by_halves(): kernel_call(functools.partial(second_layer_kernel, strip), (edge_shape, e...  3.34 us
  transfers between devices with their start and end apart: 12, of which 4 were waited for; matrix products, arithmetic and copies ran while one was open for 8% of the time, Pallas kernels for 12%

profile of v1, /device:TPU:1, one launch (start us, length us, event | category | flops | bytes accessed | tf_op | source)
XLA Modules:
  0.0 83.9 jit_solution(8672158027439710988)
XLA Ops:
  0.0 0.0 copy-start
  0.0 2.1 %constant_dynamic-slice_fusion.7 = (bf16[4,112,256]{2,1,0:T(8,128)(2,1)S(1)}, bf16[4,112,256]{2,1,0:T(8,128)(2,1)S(1)}, bf16[4,112,256]{2,1,0:T(8,128)(2,1)}, bf16[4,112,256]{2,1,0:T(8,128)(2,1)S(1)}) fusion(bf16[8,256,256]{2,1,0:T(8,128)(2,1)} %x_ref.5, s32[]{:T(128)S(6)} %select_n.42, s32[]{:T(128)S(6)} %add.1, s32[]{:T(128)S(6)} %select_n.41), kind=kLoop, calls=%fused_computation.14 | loop fusion | bytes 1835020 | tf_op jit(solution)/shard_map/slice | solution.py:350
  2.1 1.3 %collective-permute-start.5 = (bf16[4,112,256]{2,1,0:T(8,128)(2,1)S(1)}, bf16[4,112,256]{2,1,0:T(8,128)(2,1)S(1)}, u32[]{:S(2)}, u32[]{:S(2)}) collective-permute-start(bf16[4,112,256]{2,1,0:T(8,128)(2,1)S(1)} %get-tuple-element.33), channel_id=1, source_target_pairs={{2,0},{4,2},{6,4},{8,6},{10,8},{12,10},{14,12},{3,1},{5,3},{7,5},{... | collective-permute-start | bytes 688136 | tf_op jit(solution)/shard_map/ppermute | solution.py:350
  3.4 4.6 %collective-permute-start.4 = (bf16[4,112,256]{2,1,0:T(8,128)(2,1)S(1)}, bf16[4,112,256]{2,1,0:T(8,128)(2,1)S(1)}, u32[]{:S(2)}, u32[]{:S(2)}) collective-permute-start(bf16[4,112,256]{2,1,0:T(8,128)(2,1)S(1)} %get-tuple-element.34), channel_id=1, source_target_pairs={{0,2},{2,4},{4,6},{6,8},{8,10},{10,12},{12,14},{1,3},{3,5},{5,7},{... | collective-permute-start | bytes 688136 | tf_op jit(solution)/shard_map/ppermute | solution.py:349
  8.0 4.3 %collective-permute-start.2 = (bf16[4,112,256]{2,1,0:T(8,128)(2,1)}, bf16[4,112,256]{2,1,0:T(8,128)(2,1)S(1)}, u32[]{:S(2)}, u32[]{:S(2)}) collective-permute-start(bf16[4,112,256]{2,1,0:T(8,128)(2,1)} %get-tuple-element.35), channel_id=1, source_target_pairs={{0,2},{2,4},{4,6},{6,8},{8,10},{10,12},{12,14},{1,3},{3,5},{5,7},{... | collective-permute-start | bytes 688136 | tf_op jit(solution)/shard_map/ppermute | solution.py:349
  12.3 1.3 %collective-permute-start.3 = (bf16[4,112,256]{2,1,0:T(8,128)(2,1)S(1)}, bf16[4,112,256]{2,1,0:T(8,128)(2,1)S(1)}, u32[]{:S(2)}, u32[]{:S(2)}) collective-permute-start(bf16[4,112,256]{2,1,0:T(8,128)(2,1)S(1)} %get-tuple-element.36), channel_id=1, source_target_pairs={{2,0},{4,2},{6,4},{8,6},{10,8},{12,10},{14,12},{3,1},{5,3},{7,5},{... | collective-permute-start | bytes 688136 | tf_op jit(solution)/shard_map/ppermute | solution.py:350
  13.6 0.0 copy-done
  13.6 0.0 collective-permute-done.5.rest_5_.rest_1_
  13.6 8.5 %collective-permute-done.4.rest_4_.rest_0_ = bf16[4,112,256]{2,1,0:T(8,128)(2,1)S(1)} collective-permute-done((bf16[4,112,256]{2,1,0:T(8,128)(2,1)S(1)}, bf16[4,112,256]{2,1,0:T(8,128)(2,1)S(1)}, u32[]{:S(2)}, u32[]{:S(2)}) %collective-permute-start.4) | collective-permute-done | bytes 229408 | tf_op jit(solution)/shard_map/ppermute | solution.py:349
  22.1 0.0 copy-start.1
  22.1 0.0 copy-start.2
  22.1 0.7 collective-permute-start.7
  22.8 2.8 %slice_bitcast_fusion = (bf16[3,3,256,256]{3,2,1,0:T(8,128)(2,1)S(1)}, bf16[1,3,3,256,256]{4,3,2,1,0:T(8,128)(2,1)}) fusion(bf16[3,3,3,256,256]{4,3,2,1,0:T(8,128)(2,1)} %param.7), kind=kLoop, calls=%fused_computation | loop fusion | bytes 4718592 | tf_op jit(solution)/shard_map/squeeze | solution.py:369
  25.6 0.0 collective-permute-done.7.rest_2_
  25.6 0.0 copy-done.1
  25.6 0.0 copy-done.2
  25.6 2.9 %shard_map.47 = (bf16[8,96,256]{2,1,0:T(8,128)(2,1)S(1)}, bf16[8,96,256]{2,1,0:T(8,128)(2,1)}) custom-call(s32[1]{0:T(128)} %bitcast.core_ref, bf16[8,256,256]{2,1,0:T(8,128)(2,1)S(1)} %copy-done, f32[3,256]{1,0:T(4,128)S(1)} %copy-done.1, f32[3,256]{1,0:T(4,128)S(1)} %copy-done.2, bf16[3,3,256,256]{3,2,1,0:T(8,128)(2,1)S(1)} %get-tuple-element.31.w_ref, ...), custom_call_target="tpu_custom_call" | custom-call | flops 905969664 | bytes 1179648 | tf_op jit(solution)/shard_map/pallas_call | solution.py:166
  28.5 0.0 copy-start.3
  28.5 0.8 copy-done.3
  29.3 3.2 %collective-permute-start.8 = (bf16[8,96,256]{2,1,0:T(8,128)(2,1)}, bf16[8,96,256]{2,1,0:T(8,128)(2,1)}, u32[]{:S(2)}, u32[]{:S(2)}) collective-permute-start(bf16[8,96,256]{2,1,0:T(8,128)(2,1)} %get-tuple-element.18.near_ref), channel_id=1, source_target_pairs={{0,8},{2,10},{4,12},{6,14},{8,0},{10,2},{12,4},{14,6},{1,9},{3,11}... | collective-permute-start | bytes 1179656 | tf_op jit(solution)/shard_map/ppermute | solution.py:380
  32.5 0.7 fusion
  33.1 3.2 %collective-permute-start = (bf16[4,32,256]{2,1,0:T(8,128)(2,1)}, bf16[4,32,256]{2,1,0:T(8,128)(2,1)S(1)}, u32[]{:S(2)}, u32[]{:S(2)}) collective-permute-start(bf16[4,32,256]{2,1,0:T(8,128)(2,1)} %get-tuple-element.38), channel_id=1, source_target_pairs={{0,2},{2,4},{4,6},{6,8},{8,10},{10,12},{12,14},{1,3},{3,5},{5,7},{... | collective-permute-start | bytes 196616 | tf_op jit(solution)/shard_map/ppermute | solution.py:349
  36.4 1.3 %collective-permute-start.1 = (bf16[4,32,256]{2,1,0:T(8,128)(2,1)}, bf16[4,32,256]{2,1,0:T(8,128)(2,1)S(1)}, u32[]{:S(2)}, u32[]{:S(2)}) collective-permute-start(bf16[4,32,256]{2,1,0:T(8,128)(2,1)} %get-tuple-element.37), channel_id=1, source_target_pairs={{2,0},{4,2},{6,4},{8,6},{10,8},{12,10},{14,12},{3,1},{5,3},{7,5},{... | collective-permute-start | bytes 196616 | tf_op jit(solution)/shard_map/ppermute | solution.py:350
  37.7 0.0 collective-permute-done.2.rest_2_.rest_0_
  37.7 0.0 collective-permute-done.3.rest_3_.rest_1_
  37.7 2.0 %shard_map.48 = (bf16[8,96,256]{2,1,0:T(8,128)(2,1)S(1)}, bf16[8,96,256]{2,1,0:T(8,128)(2,1)S(1)}) custom-call(s32[1]{0:T(128)} %bitcast.core_ref, bf16[8,256,256]{2,1,0:T(8,128)(2,1)S(1)} %copy-done, f32[3,256]{1,0:T(4,128)S(1)} %copy-done.1, f32[3,256]{1,0:T(4,128)S(1)} %copy-done.2, bf16[3,3,256,256]{3,2,1,0:T(8,128)(2,1)S(1)} %get-tuple-element.31.w_ref, ...), custom_call_target="tpu_custom_call" | custom-call | flops 905969664 | bytes 1179648 | tf_op jit(solution)/shard_map/pallas_call | solution.py:166
  39.7 1.7 %collective-permute-start.9 = (bf16[8,96,256]{2,1,0:T(8,128)(2,1)S(1)}, bf16[8,96,256]{2,1,0:T(8,128)(2,1)S(1)}, u32[]{:S(2)}, u32[]{:S(2)}) collective-permute-start(bf16[8,96,256]{2,1,0:T(8,128)(2,1)S(1)} %get-tuple-element.19.far_ref), channel_id=1, source_target_pairs={{0,8},{2,10},{4,12},{6,14},{8,0},{10,2},{12,4},{14,6},{1,9},{3,11}... | collective-permute-start | bytes 1179656 | tf_op jit(solution)/shard_map/ppermute | solution.py:390
  41.4 0.9 %constant_dynamic-slice_fusion.3 = bf16[8,32,256]{2,1,0:T(8,128)(2,1)S(1)} fusion(bf16[8,96,256]{2,1,0:T(8,128)(2,1)} %get-tuple-element.18.near_ref, s32[]{:T(128)S(6)} %select_n.45), kind=kLoop, calls=%fused_computation.10 | loop fusion | bytes 262148 | tf_op jit(solution)/shard_map/dynamic_slice | solution.py:344
  42.3 16.8 %collective-permute-done.8.cnear_ref = bf16[8,96,256]{2,1,0:T(8,128)(2,1)} collective-permute-done((bf16[8,96,256]{2,1,0:T(8,128)(2,1)}, bf16[8,96,256]{2,1,0:T(8,128)(2,1)}, u32[]{:S(2)}, u32[]{:S(2)}) %collective-permute-start.8) | collective-permute-done | bytes 393248 | tf_op jit(solution)/shard_map/ppermute | solution.py:380
  59.1 0.9 %constant_dynamic-slice_fusion.2 = bf16[8,32,256]{2,1,0:T(8,128)(2,1)S(1)} fusion(bf16[8,96,256]{2,1,0:T(8,128)(2,1)} %collective-permute-done.8.cnear_ref, s32[]{:T(128)S(6)} %select_n.45), kind=kLoop, calls=%fused_computation.9 | loop fusion | bytes 262148 | tf_op jit(solution)/shard_map/dynamic_slice | solution.py:344
  60.1 0.9 %collective-permute-start.10 = (bf16[16,32,256]{2,1,0:T(8,128)(2,1)S(1)}, bf16[16,32,256]{2,1,0:T(8,128)(2,1)S(1)}, u32[]{:S(2)}, u32[]{:S(2)}) collective-permute-start(bf16[16,32,256]{2,1,0:T(8,128)(2,1)S(1)} %pad_maximum_fusion), channel_id=1, source_target_pairs={{0,1},{1,0},{2,3},{3,2},{4,5},{5,4},{6,7},{7,6},{8,9},{9,8},{10,11... | collective-permute-start | bytes 786440 | tf_op jit(solution)/shard_map/ppermute | solution.py:411
  61.0 1.3 %slice_bitcast_fusion.1 = (bf16[3,256,256]{2,1,0:T(8,128)(2,1)S(1)}, bf16[3,256,256]{2,1,0:T(8,128)(2,1)S(1)}, bf16[3,256,256]{2,1,0:T(8,128)(2,1)S(1)}) fusion(bf16[3,3,3,256,256]{4,3,2,1,0:T(8,128)(2,1)} %param.7, bf16[1,3,3,256,256]{4,3,2,1,0:T(8,128)(2,1)} %get-tuple-element.32, s32[]{:T(128)S(6)} %select_n.40), kind=kLoop, calls=%fused_computation.1 | loop fusion | bytes 2359300 | tf_op jit(solution)/shard_map/squeeze | solution.py:438
  62.3 0.0 copy-start.4
  62.3 0.0 collective-permute-done.rest_0_
  62.3 0.0 collective-permute-done.1.rest_1_
  62.3 1.8 %shard_map.46 = (bf16[8,64,256]{2,1,0:T(8,128)(2,1)S(1)}, bf16[8,64,256]{2,1,0:T(8,128)(2,1)S(1)}) custom-call(s32[1]{0:T(128)} %bitcast.core_ref, bf16[8,256,256]{2,1,0:T(8,128)(2,1)S(1)} %copy-done, f32[3,256]{1,0:T(4,128)S(1)} %copy-done.1, f32[3,256]{1,0:T(4,128)S(1)} %copy-done.2, bf16[3,3,256,256]{3,2,1,0:T(8,128)(2,1)S(1)} %get-tuple-element.31.w_ref, ...), custom_call_target="tpu_custom_call" | custom-call | flops 603979776 | bytes 1179648 | tf_op jit(solution)/shard_map/pallas_call | solution.py:166
  64.1 0.1 collective-permute-start.6
  64.2 10.3 %collective-permute-done.9.cfar_ref = bf16[8,96,256]{2,1,0:T(8,128)(2,1)S(1)} collective-permute-done((bf16[8,96,256]{2,1,0:T(8,128)(2,1)S(1)}, bf16[8,96,256]{2,1,0:T(8,128)(2,1)S(1)}, u32[]{:S(2)}, u32[]{:S(2)}) %collective-permute-start.9) | collective-permute-done | bytes 393248 | tf_op jit(solution)/shard_map/ppermute | solution.py:390
  74.5 0.0 collective-permute-done.10.side_ref
  74.5 0.0 copy-done.4
  74.5 3.3 %shard_map.49 = (bf16[8,64,256]{2,1,0:T(8,128)(2,1)S(1)}, bf16[8,64,256]{2,1,0:T(8,128)(2,1)S(1)}, bf16[8,64,256]{2,1,0:T(8,128)(2,1)S(1)}, bf16[8,64,256]{2,1,0...) custom-call(s32[1]{0:T(128)} %bitcast.core_ref, f32[3,256]{1,0:T(4,128)S(1)} %copy-done.1, ...), custom_call_target="tpu_custom_call" | custom-call | flops 1610612736 | bytes 786432 | tf_op jit(solution)/shard_map/pallas_call | solution.py:419
  77.9 0.9 %collective-permute-start.11 = (bf16[8,64,256]{2,1,0:T(8,128)(2,1)S(1)}, bf16[8,64,256]{2,1,0:T(8,128)(2,1)S(1)}, u32[]{:S(2)}, u32[]{:S(2)}) collective-permute-start(bf16[8,64,256]{2,1,0:T(8,128)(2,1)S(1)} %broadcast_select_fusion), channel_id=1, source_target_pairs={{0,1},{1,0},{2,3},{3,2},{4,5},{5,4},{6,7},{7,6},{8,9},{9,8},{10,11... | collective-permute-start | bytes 786440 | tf_op jit(solution)/shard_map/ppermute | solution.py:441
  78.8 1.3 %collective-permute-done.6.cmid_ref = bf16[8,64,256]{2,1,0:T(8,128)(2,1)S(1)} collective-permute-done((bf16[8,64,256]{2,1,0:T(8,128)(2,1)S(1)}, bf16[8,64,256]{2,1,0:T(8,128)(2,1)S(1)}, u32[]{:S(2)}, u32[]{:S(2)}) %collective-permute-start.6) | collective-permute-done | bytes 262176 | tf_op jit(solution)/shard_map/ppermute | solution.py:405
  80.1 0.0 collective-permute-done.11.side_ref
  80.1 3.8 %shard_map.50 = bf16[8,256,256]{2,1,0:T(8,128)(2,1)} custom-call(s32[1]{0:T(128)} %bitcast.core_ref, f32[3,256]{1,0:T(4,128)S(1)} %copy-done.1, f32[3,256]{1,0:T(4,128)S(1)} %copy-done.2, bf16[3,256,256]{2,1,0:T(8,128)(2,1)S(1)} %get-tuple-element.39.wx_ref, bf16[3,256,256]{2,1,0:T(8,128)(2,1)S(1)} %get-tuple-element.30.w_ref, ...), custom_call_target="tpu_custom_call" | custom-call | flops 1073741824 | bytes 393216 | tf_op jit(solution)/shard_map/pallas_call | solution.py:442
  (6 shorter events, 0.1 us)
Async XLA Ops:
  0.0 13.6 %copy-start = (bf16[8,256,256]{2,1,0:T(8,128)(2,1)S(1)}, bf16[8,256,256]{2,1,0:T(8,128)(2,1)}, u32[]{:S(2)}) copy-start(bf16[8,256,256]{2,1,0:T(8,128)(2,1)} %x_ref.5) | copy-start | bytes 3145732
  2.1 11.5 %collective-permute-start.5 = (bf16[4,112,256]{2,1,0:T(8,128)(2,1)S(1)}, bf16[4,112,256]{2,1,0:T(8,128)(2,1)S(1)}, u32[]{:S(2)}, u32[]{:S(2)}) collective-permute-start(bf16[4,112,256]{2,1,0:T(8,128)(2,1)S(1)} %get-tuple-element.33), channel_id=1, source_target_pairs={{2,0},{4,2},{6,4},{8,6},{10,8},{12,10},{14,12},{3,1},{5,3},{7,5},{... | collective-permute-start | bytes 688136 | tf_op jit(solution)/shard_map/ppermute | solution.py:350
  3.4 18.7 %collective-permute-start.4 = (bf16[4,112,256]{2,1,0:T(8,128)(2,1)S(1)}, bf16[4,112,256]{2,1,0:T(8,128)(2,1)S(1)}, u32[]{:S(2)}, u32[]{:S(2)}) collective-permute-start(bf16[4,112,256]{2,1,0:T(8,128)(2,1)S(1)} %get-tuple-element.34), channel_id=1, source_target_pairs={{0,2},{2,4},{4,6},{6,8},{8,10},{10,12},{12,14},{1,3},{3,5},{5,7},{... | collective-permute-start | bytes 688136 | tf_op jit(solution)/shard_map/ppermute | solution.py:349
  8.0 29.7 %collective-permute-start.2 = (bf16[4,112,256]{2,1,0:T(8,128)(2,1)}, bf16[4,112,256]{2,1,0:T(8,128)(2,1)S(1)}, u32[]{:S(2)}, u32[]{:S(2)}) collective-permute-start(bf16[4,112,256]{2,1,0:T(8,128)(2,1)} %get-tuple-element.35), channel_id=1, source_target_pairs={{0,2},{2,4},{4,6},{6,8},{8,10},{10,12},{12,14},{1,3},{3,5},{5,7},{... | collective-permute-start | bytes 688136 | tf_op jit(solution)/shard_map/ppermute | solution.py:349
  12.3 25.4 %collective-permute-start.3 = (bf16[4,112,256]{2,1,0:T(8,128)(2,1)S(1)}, bf16[4,112,256]{2,1,0:T(8,128)(2,1)S(1)}, u32[]{:S(2)}, u32[]{:S(2)}) collective-permute-start(bf16[4,112,256]{2,1,0:T(8,128)(2,1)S(1)} %get-tuple-element.36), channel_id=1, source_target_pairs={{2,0},{4,2},{6,4},{8,6},{10,8},{12,10},{14,12},{3,1},{5,3},{7,5},{... | collective-permute-start | bytes 688136 | tf_op jit(solution)/shard_map/ppermute | solution.py:350
  22.1 3.5 %copy-start.1 = (f32[3,256]{1,0:T(4,128)S(1)}, f32[3,256]{1,0:T(4,128)}, u32[]{:S(2)}) copy-start(f32[3,256]{1,0:T(4,128)} %gain_ref.9) | copy-start | bytes 9220
  22.1 3.5 %copy-start.2 = (f32[3,256]{1,0:T(4,128)S(1)}, f32[3,256]{1,0:T(4,128)}, u32[]{:S(2)}) copy-start(f32[3,256]{1,0:T(4,128)} %bias_ref.9) | copy-start | bytes 9220
  22.1 3.5 %collective-permute-start.7 = (bf16[16,16,256]{2,1,0:T(8,128)(2,1)S(1)}, bf16[16,16,256]{2,1,0:T(8,128)(2,1)S(1)}, u32[]{:S(2)}, u32[]{:S(2)}) collective-permute-start(bf16[16,16,256]{2,1,0:T(8,128)(2,1)S(1)} %pad_maximum_fusion.1), channel_id=1, source_target_pairs={{0,1},{1,0},{2,3},{3,2},{4,5},{5,4},{6,7},{7,6},{8,9},{9,8},{10,11... | collective-permute-start | bytes 393224 | tf_op jit(solution)/shard_map/ppermute | solution.py:367
  28.5 0.8 copy-start.3
  29.3 29.8 %collective-permute-start.8 = (bf16[8,96,256]{2,1,0:T(8,128)(2,1)}, bf16[8,96,256]{2,1,0:T(8,128)(2,1)}, u32[]{:S(2)}, u32[]{:S(2)}) collective-permute-start(bf16[8,96,256]{2,1,0:T(8,128)(2,1)} %get-tuple-element.18.near_ref), channel_id=1, source_target_pairs={{0,8},{2,10},{4,12},{6,14},{8,0},{10,2},{12,4},{14,6},{1,9},{3,11}... | collective-permute-start | bytes 1179656 | tf_op jit(solution)/shard_map/ppermute | solution.py:380
  33.1 29.2 %collective-permute-start = (bf16[4,32,256]{2,1,0:T(8,128)(2,1)}, bf16[4,32,256]{2,1,0:T(8,128)(2,1)S(1)}, u32[]{:S(2)}, u32[]{:S(2)}) collective-permute-start(bf16[4,32,256]{2,1,0:T(8,128)(2,1)} %get-tuple-element.38), channel_id=1, source_target_pairs={{0,2},{2,4},{4,6},{6,8},{8,10},{10,12},{12,14},{1,3},{3,5},{5,7},{... | collective-permute-start | bytes 196616 | tf_op jit(solution)/shard_map/ppermute | solution.py:349
  36.4 25.9 %collective-permute-start.1 = (bf16[4,32,256]{2,1,0:T(8,128)(2,1)}, bf16[4,32,256]{2,1,0:T(8,128)(2,1)S(1)}, u32[]{:S(2)}, u32[]{:S(2)}) collective-permute-start(bf16[4,32,256]{2,1,0:T(8,128)(2,1)} %get-tuple-element.37), channel_id=1, source_target_pairs={{2,0},{4,2},{6,4},{8,6},{10,8},{12,10},{14,12},{3,1},{5,3},{7,5},{... | collective-permute-start | bytes 196616 | tf_op jit(solution)/shard_map/ppermute | solution.py:350
  39.7 34.8 %collective-permute-start.9 = (bf16[8,96,256]{2,1,0:T(8,128)(2,1)S(1)}, bf16[8,96,256]{2,1,0:T(8,128)(2,1)S(1)}, u32[]{:S(2)}, u32[]{:S(2)}) collective-permute-start(bf16[8,96,256]{2,1,0:T(8,128)(2,1)S(1)} %get-tuple-element.19.far_ref), channel_id=1, source_target_pairs={{0,8},{2,10},{4,12},{6,14},{8,0},{10,2},{12,4},{14,6},{1,9},{3,11}... | collective-permute-start | bytes 1179656 | tf_op jit(solution)/shard_map/ppermute | solution.py:390
  60.1 14.4 %collective-permute-start.10 = (bf16[16,32,256]{2,1,0:T(8,128)(2,1)S(1)}, bf16[16,32,256]{2,1,0:T(8,128)(2,1)S(1)}, u32[]{:S(2)}, u32[]{:S(2)}) collective-permute-start(bf16[16,32,256]{2,1,0:T(8,128)(2,1)S(1)} %pad_maximum_fusion), channel_id=1, source_target_pairs={{0,1},{1,0},{2,3},{3,2},{4,5},{5,4},{6,7},{7,6},{8,9},{9,8},{10,11... | collective-permute-start | bytes 786440 | tf_op jit(solution)/shard_map/ppermute | solution.py:411
  62.3 12.2 %copy-start.4 = (bf16[8,96,256]{2,1,0:T(8,128)(2,1)S(1)}, bf16[8,96,256]{2,1,0:T(8,128)(2,1)}, u32[]{:S(2)}) copy-start(bf16[8,96,256]{2,1,0:T(8,128)(2,1)} %copy-done.3) | copy-start | bytes 1179652
  64.1 16.0 %collective-permute-start.6 = (bf16[8,64,256]{2,1,0:T(8,128)(2,1)S(1)}, bf16[8,64,256]{2,1,0:T(8,128)(2,1)S(1)}, u32[]{:S(2)}, u32[]{:S(2)}) collective-permute-start(bf16[8,64,256]{2,1,0:T(8,128)(2,1)S(1)} %get-tuple-element.17.mid_ref), channel_id=1, source_target_pairs={{0,8},{2,10},{4,12},{6,14},{8,0},{10,2},{12,4},{14,6},{1,9},{3,11}... | collective-permute-start | bytes 786440 | tf_op jit(solution)/shard_map/ppermute | solution.py:405
  77.9 2.2 %collective-permute-start.11 = (bf16[8,64,256]{2,1,0:T(8,128)(2,1)S(1)}, bf16[8,64,256]{2,1,0:T(8,128)(2,1)S(1)}, u32[]{:S(2)}, u32[]{:S(2)}) collective-permute-start(bf16[8,64,256]{2,1,0:T(8,128)(2,1)S(1)} %broadcast_select_fusion), channel_id=1, source_target_pairs={{0,1},{1,0},{2,3},{3,2},{4,5},{5,4},{6,7},{7,6},{8,9},{9,8},{10,11... | collective-permute-start | bytes 786440 | tf_op jit(solution)/shard_map/ppermute | solution.py:441

commit v2 on v1

--- a/solution.py
+++ b/solution.py
@@ -116,25 +116,71 @@
     return pl.multiple_of(jnp.where(core == 0, at_zero, at_one), lane_pad)
 
 
-def first_layer_kernel(
-    segments, zero_at, out_at, rows, width, core_ref, x_ref, gain_ref, bias_ref, w_ref, *rest
-):
+def guarded(flag_ref, condition, action):
+    if condition is None:
+        action()
+    else:
+        number, value = condition
+        pl.when(flag_ref[number] == value)(action)
+
+
+def copy_kernel(moves, inputs, flag_ref, *refs):
+    sources, targets, sems = refs[:inputs], refs[inputs:-1], refs[-1]
+
+    def descriptor(at):
+        _, which, row, count, column, width, target, target_row = moves[at]
+        return pltpu.make_async_copy(
+            sources[which].at[pl.ds(row, count), pl.ds(place(flag_ref[0], *column), width)],
+            targets[target].at[pl.ds(target_row, count)],
+            sems.at[at],
+        )
+
+    for at, move in enumerate(moves):
+        guarded(flag_ref, move[0], lambda at=at: descriptor(at).start())
+    for at, move in enumerate(moves):
+        guarded(flag_ref, move[0], lambda at=at: descriptor(at).wait())
+
+
+def copies(flags, arrays, moves):
+    channels, kind = arrays[0].shape[2], arrays[0].dtype
+    shapes = {}
+    for _, _, _, count, _, width, target, target_row in moves:
+        height = max(target_row + count, shapes.get(target, (0, 0))[0])
+        shapes[target] = (height, width)
+    out = tuple(
+        jax.ShapeDtypeStruct(shapes[target] + (channels,), kind) for target in range(len(shapes))
+    )
+    volume = sum(2 * height * width * channels * 2 for height, width in shapes.values())
+    return pl.pallas_call(
+        functools.partial(copy_kernel, moves, len(arrays)),
+        out_shape=out,
+        in_specs=[smem_spec()] + [pl.BlockSpec(memory_space=pl.ANY)] * len(arrays),
+        out_specs=tuple(pl.BlockSpec(memory_space=pl.ANY) for _ in out),
+        scratch_shapes=[pltpu.SemaphoreType.DMA((len(moves),))],
+        cost_estimate=pl.CostEstimate(flops=0, bytes_accessed=volume, transcendentals=0),
+    )(flags, *arrays)
+
+
+def first_layer_kernel(segments, out_at, rows, width, flag_ref, gain_ref, bias_ref, w_ref, *rest):
     parts, (next_ref, normed_ref, window, taps) = rest[:-4], rest[-4:]
-    refs = (x_ref,) + tuple(parts)
-    core = core_ref[0]
+    core = flag_ref[0]
     half = rows // 2
-    channels = x_ref.shape[2]
+    channels = window.shape[2]
     gain = gain_ref[0:1, :]
-    for which, source_row, window_row, count, source, target, columns in segments:
+
+    def fill(which, source_row, window_row, count, source, target, columns):
         src, dst = place(core, *source), place(core, *target)
         for r in range(count):
-            window[window_row + r, pl.ds(dst, columns), :] = normalize(
-                refs[which][source_row + r, pl.ds(src, columns), :], gain
-            )
-    if zero_at is not None:
-        dst = place(core, *zero_at)
-        for r in range(2 * rows):
-            window[r, pl.ds(dst, lane_pad), :] = jnp.zeros((lane_pad, channels), jnp.bfloat16)
+            if which is None:
+                values = jnp.zeros((columns, channels), window.dtype)
+            else:
+                values = normalize(
+                    parts[which][source_row + r, pl.ds(src, columns), :], gain
+                )
+            window[window_row + r, pl.ds(dst, columns), :] = values
+
+    for segment in segments:
+        guarded(flag_ref, segment[0], functools.partial(fill, *segment[1:]))
     step = dilations[0]
     for b in range(3):
         first = lane_pad + (b - 1) * step
@@ -152,33 +198,33 @@
         stacked, w_ref[...].reshape(9 * channels, channels), preferred_element_type=jnp.float32
     )
     out_col = place(core, *out_at)
-    current = x_ref[:, pl.ds(out_col, width), :].reshape(rows * width, channels)
+    current = parts[0][:, pl.ds(out_col, width), :].reshape(rows * width, channels)
     result = update(current, response, bias_ref[0:1, :])
     next_ref[...] = result.reshape(rows, width, channels)
     normed_ref[...] = normalize(result, gain_ref[1:2, :]).reshape(rows, width, channels)
 
 
-def first_layer(core, x, gains, biases, weights, parts, segments, zero_at, out_at, width):
-    rows, _, channels = x.shape
-    out = jax.ShapeDtypeStruct((rows, width, channels), x.dtype)
+def first_layer(flags, params, parts, segments, out_at, width):
+    rows, _, channels = parts[0].shape
+    kind = parts[0].dtype
+    out = jax.ShapeDtypeStruct((rows, width, channels), kind)
     cells = rows * width
-    body = functools.partial(first_layer_kernel, segments, zero_at, out_at, rows, width)
     return kernel_call(
-        body,
+        functools.partial(first_layer_kernel, segments, out_at, rows, width),
         (out, out),
-        [smem_spec()] + [vmem_spec()] * (4 + len(parts)),
+        [smem_spec()] + [vmem_spec()] * (3 + len(parts)),
         [
-            pltpu.VMEM((2 * rows, width + 2 * lane_pad, channels), x.dtype),
-            pltpu.VMEM((3, 2 * rows, width, channels), x.dtype),
+            pltpu.VMEM((2 * rows, width + 2 * lane_pad, channels), kind),
+            pltpu.VMEM((3, 2 * rows, width, channels), kind),
         ],
         18 * cells * channels * channels,
         9 * channels * channels * 2,
-    )(core, x, gains, biases, weights, *parts)
+    )(flags, *params, *parts)
 
 
 def second_layer_kernel(
     strip,
-    core_ref,
+    flag_ref,
     gain_ref,
     bias_ref,
     w_ref,
@@ -196,13 +242,14 @@
     highs_ref,
     nlows_ref,
     nhighs_ref,
+    nside_ref,
     acc_ref,
     mids_ref,
     own,
     other,
     x1,
 ):
-    core = core_ref[0]
+    core = flag_ref[0]
     step = dilations[1]
     rows, mid, channels = mid_ref.shape
     cols = 2 * strip + mid
@@ -254,10 +301,16 @@
             result_ref, out_ref = (lows_ref, nlows_ref) if first == 0 else (highs_ref, nhighs_ref)
             result_ref[...] = result.reshape(rows, width, channels)
             out_ref[...] = normed.reshape(rows, width, channels)
+            near_core = 1 if first == 0 else 0
+
+            def give(normed=normed, width=width):
+                nside_ref[...] = normed.reshape(rows, width, channels)
+
+            pl.when(core == near_core)(give)
 
 
 def last_kernel(
-    core_ref,
+    flag_ref,
     gain_ref,
     bias_ref,
     wx_ref,
@@ -275,7 +328,7 @@
     normed,
     x2,
 ):
-    core = core_ref[0]
+    core = flag_ref[0]
     rows, mid, channels = cmid_ref.shape
     edge = nlows_ref.shape[1]
     step, reach = dilations[1], dilations[2]
@@ -327,86 +380,136 @@
 
 def by_halves(context_map, norm_gains, conv_biases, conv_weights):
     rows, cols, channels = context_map.shape
+    kind = context_map.dtype
     size = lax.axis_size("row")
+    group = size // 2
     half = rows // 2
-    strip = dilations[1] + dilations[2]
+    step, reach = dilations[1], dilations[2]
+    strip = step + reach
     mid = cols - 2 * strip
     pad = lane_pad
-    core = lax.axis_index("col")
-    upper_half = lax.axis_index("row") < size // 2
-    core_array = jnp.full((1,), core, jnp.int32)
+    wide = strip + pad
+    core, row = lax.axis_index("col"), lax.axis_index("row")
+    upper_half = row < group
+    flags = jnp.stack([core, row == group - 1, row == group]).astype(jnp.int32)
+    last_above, first_below = (1, 1), (2, 1)
     swap = [(0, 1), (1, 0)]
-    partner = [(i, (i + size // 2) % size) for i in range(size)]
+    partner = [(i, (i + group) % size) for i in range(size)]
     down = [(i, i + 1) for i in range(size - 1)]
     up = [(j, i) for i, j in down]
-
-    def columns(x, at_zero, at_one, width):
-        return lax.dynamic_slice_in_dim(x, jnp.where(core == 0, at_zero, at_one), width, axis=1)
-
-    def halos(at_zero, at_one, width):
-        part = columns(context_map, at_zero, at_one, width)
-        return (
-            lax.ppermute(part[rows - half :], "row", down),
-            lax.ppermute(part[:half], "row", up),
-        )
-
-    wide = strip + pad
+    within_down = [(i, j) for i, j in down if j != group]
+    within_up = [(j, i) for i, j in within_down]
+    ring_down = [(i, i // group * group + (i + 1) % group) for i in range(size)]
+    ring_up = [(j, i) for i, j in ring_down]
+
     near_at, far_at = (cols - strip, 0), (0, cols - strip)
-    above_near, below_near = halos(cols - wide, 0, wide)
-    above_far, below_far = halos(0, cols - wide, wide)
-    above_mid, below_mid = halos(wide, wide, cols - 2 * wide)
-
-    rim = jnp.concatenate(
-        [
-            columns(above_near, wide - pad, 0, pad),
-            columns(context_map, cols - pad, 0, pad),
-            columns(below_near, wide - pad, 0, pad),
-        ],
-        axis=0,
+    near_wide_at, far_wide_at = (cols - wide, 0), (0, cols - wide)
+    mid_halo_at, far_halo_at = (strip - pad, wide), (0, cols - strip + pad)
+    far_halo = strip - pad
+    raw, near_low, near_high, mid_low, mid_high, far_low, far_high = copies(
+        flags,
+        (context_map,),
+        (
+            (None, 0, 0, rows, far_wide_at, wide, 0, 0),
+            (None, 0, half, half, near_wide_at, wide, 1, 0),
+            (None, 0, 0, half, near_wide_at, wide, 2, 0),
+            (None, 0, half, half, mid_halo_at, mid, 3, 0),
+            (None, 0, 0, half, mid_halo_at, mid, 4, 0),
+            (None, 0, half, half, far_halo_at, far_halo, 5, 0),
+            (None, 0, 0, half, far_halo_at, far_halo, 6, 0),
+        ),
+    )
+    raw = lax.ppermute(raw, "row", partner)
+    above_near = lax.ppermute(near_low, "row", down)
+    below_near = lax.ppermute(near_high, "row", up)
+    above_mid = lax.ppermute(mid_low, "row", down)
+    below_mid = lax.ppermute(mid_high, "row", up)
+    above_far = lax.ppermute(far_low, "row", within_down)
+    below_far = lax.ppermute(far_high, "row", within_up)
+
+    params = (norm_gains, conv_biases, conv_weights[0])
+    (rim,) = copies(
+        flags,
+        (context_map, above_near, below_near),
+        (
+            (None, 1, 0, half, (wide - pad, 0), pad, 0, 0),
+            (None, 0, 0, rows, (cols - pad, 0), pad, 0, half),
+            (None, 2, 0, half, (wide - pad, 0), pad, 0, half + rows),
+        ),
     )
     rim = lax.ppermute(rim, "col", swap)
-
-    params = (norm_gains, conv_biases, conv_weights[0])
     near_segments = (
-        (0, 0, half, rows, (cols - wide, 0), (0, pad), wide),
-        (1, 0, 0, half, (0, 0), (0, pad), wide),
-        (2, 0, half + rows, half, (0, 0), (0, pad), wide),
-        (3, 0, 0, 2 * rows, (0, 0), (wide, 0), pad),
+        (None, 0, 0, half, rows, near_wide_at, (0, pad), wide),
+        (None, 1, 0, 0, half, (0, 0), (0, pad), wide),
+        (None, 2, 0, half + rows, half, (0, 0), (0, pad), wide),
+        (None, 3, 0, 0, 2 * rows, (0, 0), (wide, 0), pad),
     )
     near1, near_n = first_layer(
-        core_array, context_map, *params, (above_near, below_near, rim), near_segments, None,
-        near_at, strip,
+        flags, params, (context_map, above_near, below_near, rim), near_segments, near_at, strip
     )
     cross_near = lax.ppermute(near_n, "row", partner)
+    mid_segments = (
+        (None, 0, 0, half, rows, (strip - pad, strip - pad), (0, 0), mid + 2 * pad),
+        (None, 1, 0, 0, half, (0, 0), (0, 2 * pad), mid),
+        (None, 2, 0, half + rows, half, (0, 0), (0, 2 * pad), mid),
+        (None, 3, 0, 0, half, (0, wide - 2 * pad), (mid, 0), 2 * pad),
+        (None, 4, 0, half + rows, half, (0, wide - 2 * pad), (mid, 0), 2 * pad),
+    )
+    mid1, mid_n = first_layer(
+        flags, params, (context_map, above_mid, below_mid, above_near, below_near), mid_segments,
+        (strip, strip), mid,
+    )
+    cross_mid = lax.ppermute(mid_n, "row", partner)
+
+    ring_low, ring_high = copies(
+        flags,
+        (context_map, raw),
+        (
+            ((1, 1), 0, half, half, far_wide_at, wide, 0, 0),
+            ((1, 0), 1, half, half, (0, 0), wide, 0, 0),
+            ((2, 1), 0, 0, half, far_wide_at, wide, 1, 0),
+            ((2, 0), 1, 0, half, (0, 0), wide, 1, 0),
+        ),
+    )
+    ring_above = lax.ppermute(ring_low, "row", ring_down)
+    ring_below = lax.ppermute(ring_high, "row", ring_up)
+    spare = (0, mid - 2 * pad)
+    body_at, edge_at = (pad, 0), (0, wide)
+    halo_at, inner_at = (pad, 2 * pad), (pad + far_halo, 0)
     far_segments = (
-        (0, 0, half, rows, (0, cols - wide), (pad, 0), wide),
-        (1, 0, 0, half, (0, 0), (pad, 0), wide),
-        (2, 0, half + rows, half, (0, 0), (pad, 0), wide),
+        (None, 0, 0, half, rows, far_wide_at, body_at, wide),
+        (None, 1, 0, 0, half, (0, 0), halo_at, far_halo),
+        (None, 2, 0, half + rows, half, (0, 0), halo_at, far_halo),
+        (None, 3, 0, 0, half, spare, inner_at, 2 * pad),
+        (None, 4, 0, half + rows, half, spare, inner_at, 2 * pad),
+        (first_below, 5, 0, 0, half, (0, 0), body_at, wide),
+        (last_above, 6, 0, half + rows, half, (0, 0), body_at, wide),
+        (None, None, 0, 0, 2 * rows, (0, 0), edge_at, pad),
     )
     far1, far_n = first_layer(
-        core_array, context_map, *params, (above_far, below_far), far_segments,
-        (0, wide), far_at, strip,
-    )
-    cross_far = lax.ppermute(far_n, "row", partner)
-    mid_segments = (
-        (0, 0, half, rows, (strip - pad, strip - pad), (0, 0), mid + 2 * pad),
-        (1, 0, 0, half, (0, 0), (2 * pad, 2 * pad), mid - 2 * pad),
-        (2, 0, half + rows, half, (0, 0), (2 * pad, 2 * pad), mid - 2 * pad),
-        (3, 0, 0, half, (wide - 2 * pad, 0), (0, mid), 2 * pad),
-        (4, 0, half + rows, half, (wide - 2 * pad, 0), (0, mid), 2 * pad),
-        (5, 0, 0, half, (0, wide - 2 * pad), (mid, 0), 2 * pad),
-        (6, 0, half + rows, half, (0, wide - 2 * pad), (mid, 0), 2 * pad),
-    )
-    mid1, mid_n = first_layer(
-        core_array, context_map, *params,
-        (above_mid, below_mid, above_far, below_far, above_near, below_near), mid_segments,
-        None, (strip, strip), mid,
-    )
-    cross_mid = lax.ppermute(mid_n, "row", partner)
-
-    step, reach = dilations[1], dilations[2]
-    side = jnp.concatenate(
-        [columns(near_n, strip - step, 0, step), columns(cross_near, strip - step, 0, step)], axis=0
+        flags, params,
+        (context_map, above_far, below_far, above_mid, below_mid, ring_above, ring_below),
+        far_segments, far_at, strip,
+    )
+    partner_segments = (
+        (None, 0, 0, half, rows, (0, 0), body_at, wide),
+        (None, 1, 0, 0, half, (0, 0), body_at, wide),
+        (None, 2, 0, half + rows, half, (0, 0), body_at, wide),
+        (first_below, None, 0, 0, half, (0, 0), body_at, wide),
+        (last_above, None, 0, half + rows, half, (0, 0), body_at, wide),
+        (None, None, 0, 0, 2 * rows, (0, 0), edge_at, pad),
+    )
+    _, cross_far = first_layer(
+        flags, params, (raw, ring_above, ring_below), partner_segments, (0, pad), strip
+    )
+
+    (side,) = copies(
+        flags,
+        (near_n, cross_near),
+        (
+            (None, 0, 0, rows, (strip - step, 0), step, 0, 0),
+            (None, 1, 0, rows, (strip - step, 0), step, 0, rows),
+        ),
     )
     side = lax.ppermute(side, "col", swap)
     toward = lax.dynamic_index_in_dim(
@@ -414,11 +517,11 @@
     )
     edge = strip - step
     wider = mid + 2 * step
-    kind = context_map.dtype
     edge_shape = jax.ShapeDtypeStruct((rows, edge, channels), kind)
-    lows, highs, n_lows, n_highs, acc, mids = kernel_call(
+    lows, highs, n_lows, n_highs, n_side, acc, mids = kernel_call(
         functools.partial(second_layer_kernel, strip),
         (
+            edge_shape,
             edge_shape,
             edge_shape,
             edge_shape,
@@ -435,10 +538,10 @@
         12 * rows * cols * channels * channels,
         6 * channels * channels * 2,
     )(
-        core_array, norm_gains, conv_biases, conv_weights[1, 1], toward, near_n, mid_n, far_n,
+        flags, norm_gains, conv_biases, conv_weights[1, 1], toward, near_n, mid_n, far_n,
         cross_near, cross_far, side, near1, mid1, far1,
     )
-    last_side = lax.ppermute(jnp.where(core == 0, n_highs, n_lows), "col", swap)
+    last_side = lax.ppermute(n_side, "col", swap)
     return kernel_call(
         last_kernel,
         jax.ShapeDtypeStruct(context_map.shape, kind),
@@ -451,7 +554,7 @@
         8 * rows * cols * channels * channels,
         3 * channels * channels * 2,
     )(
-        core_array, norm_gains, conv_biases, toward, conv_weights[2, 1], cross_mid, acc, mids, lows,
+        flags, norm_gains, conv_biases, toward, conv_weights[2, 1], cross_mid, acc, mids, lows,
         highs, n_lows, n_highs, last_side,
     )
 

time: 84.8 us -> 156 us (1.84)
  Pallas kernels: 13.7 us -> 102 us
  waiting for transfers between devices: 37 us -> 4.1 us
  starting transfers between devices: 23.3 us -> 39.3 us
  local copies, waits for them, and re-layouts: 9.57 us -> 7.3 us
    pallas_call x3 -> x8, Pallas kernels: 6.6 us -> 93.4 us  [the longest x4 78.7 us: copies(): pl.pallas_call(functools.partial(copy_kernel, moves, len(arrays)), out_sh...]
    ppermute x1, waiting for transfers between devices: 16.8 us -> 0.01 us  [by_halves(): cross_near = lax.ppermute(near_n, 'row', partner)]
    ppermute x8 -> x10, waiting for transfers between devices: 18.8 us -> 4.09 us  [the longest x1 2.82 us: by_halves(): below_near = lax.ppermute(near_high, 'row', up)]
    ppermute x1, starting transfers between devices: 3.15 us -> 9.41 us  [by_halves(): cross_near = lax.ppermute(near_n, 'row', partner)]
    ppermute x8 -> x10, starting transfers between devices: 18.5 us -> 22.6 us  [the longest x1 5.57 us: by_halves(): ring_below = lax.ppermute(ring_high, 'row', ring_up)]
    ppermute x1, starting transfers between devices: 0.65 us -> 3.55 us  [by_halves(): rim = lax.ppermute(rim, 'col', swap)]
    slice x2 -> x0, local copies, waits for them, and re-layouts: 2.76 us -> none  [halos(): part[:half]]
    ppermute x1, starting transfers between devices: 0.07 us -> 2.7 us  [by_halves(): cross_mid = lax.ppermute(mid_n, 'row', partner)]
  transfers between devices with their start and end apart: 12 -> 14, of which waited for: 4 -> 2; matrix products, arithmetic and copies ran while one was open for 8% -> 3% of each run, Pallas kernels for 12% -> 33%
where the time goes in v2:
time: 156 us; the launch traced here: 154 us
  Pallas kernels  102 us (65%)
  starting transfers between devices  39.3 us (25%)
  local copies, waits for them, and re-layouts  7.3 us (5%)
  waiting for transfers between devices  4.1 us (3%)
    pallas_call x4, Pallas kernels, copies(): pl.pallas_call(functools.partial(copy_kernel, moves, len(arrays)), out_sh...  78.7 us
    pallas_call x4, Pallas kernels, first_layer(): kernel_call(functools.partial(first_layer_kernel, segments, out_at, rows,...  14.7 us
    ppermute x1, starting transfers between devices, by_halves(): cross_near = lax.ppermute(near_n, 'row', partner)  9.41 us
    ppermute x1, starting transfers between devices, by_halves(): ring_below = lax.ppermute(ring_high, 'row', ring_up)  5.57 us
    pallas_call x1, Pallas kernels, by_halves(): kernel_call(last_kernel, jax.ShapeDtypeStruct(context_map.shape, kind), [...  4.3 us
    pallas_call x1, Pallas kernels, by_halves(): kernel_call(functools.partial(second_layer_kernel, strip), (edge_shape, e...  4.23 us
    ppermute x1, starting transfers between devices, by_halves(): raw = lax.ppermute(raw, 'row', partner)  4.13 us
    ppermute x1, starting transfers between devices, by_halves(): above_near = lax.ppermute(near_low, 'row', down)  3.96 us
  transfers between devices with their start and end apart: 14, of which 2 were waited for; matrix products, arithmetic and copies ran while one was open for 3% of the time, Pallas kernels for 33%

profile of v2, /device:TPU:1, one launch (start us, length us, event | category | flops | bytes accessed | tf_op | source)
XLA Modules:
  0.0 153.6 jit_solution(11908957738446518997)
XLA Ops:
  0.0 0.6 pad_add_fusion.flag_ref
  0.6 47.5 %shard_map.46 = (bf16[8,112,256]{2,1,0:T(8,128)(2,1)}, bf16[4,112,256]{2,1,0:T(8,128)(2,1)}, bf16[4,112,256]{2,1,0:T(8,128)(2,1)}, bf16[4,64,256]{2,1,0:T(8,128)...) custom-call(s32[3]{0:T(128)} %pad_add_fusion.flag_ref, ...), custom_call_target="tpu_custom_call" | custom-call | bytes 3014656 | tf_op jit(solution)/shard_map/pallas_call | solution.py:154
  48.1 4.0 %collective-permute-start.2 = (bf16[4,112,256]{2,1,0:T(8,128)(2,1)}, bf16[4,112,256]{2,1,0:T(8,128)(2,1)S(1)}, u32[]{:S(2)}, u32[]{:S(2)}) collective-permute-start(bf16[4,112,256]{2,1,0:T(8,128)(2,1)} %get-tuple-element.30), channel_id=1, source_target_pairs={{0,2},{2,4},{4,6},{6,8},{8,10},{10,12},{12,14},{1,3},{3,5},{5,7},{... | collective-permute-start | bytes 688136 | tf_op jit(solution)/shard_map/ppermute | solution.py:423
  52.1 1.3 collective-permute-start.3
  53.4 4.1 %collective-permute-start.8 = (bf16[8,112,256]{2,1,0:T(8,128)(2,1)}, bf16[8,112,256]{2,1,0:T(8,128)(2,1)S(1)}, u32[]{:S(2)}, u32[]{:S(2)}) collective-permute-start(bf16[8,112,256]{2,1,0:T(8,128)(2,1)} %get-tuple-element.36), channel_id=1, source_target_pairs={{0,8},{2,10},{4,12},{6,14},{8,0},{10,2},{12,4},{14,6},{1,9},{3,11}... | collective-permute-start | bytes 1376264 | tf_op jit(solution)/shard_map/ppermute | solution.py:422
  57.5 0.0 collective-permute-done.2.rest_3_.refs_1_.rest_1_
  57.5 2.8 %collective-permute-done.3.rest_4_.refs_2_.rest_2_ = bf16[4,112,256]{2,1,0:T(8,128)(2,1)S(1)} collective-permute-done((bf16[4,112,256]{2,1,0:T(8,128)(2,1)}, bf16[4,112,256]{2,1,0:T(8,128)(2,1)S(1)}, u32[]{:S(2)}, u32[]{:S(2)}) %collective-permute-start.3) | collective-permute-done | bytes 229408 | tf_op jit(solution)/shard_map/ppermute | solution.py:424
  60.3 0.0 copy-done.2
  60.3 0.7 copy-done.4
  61.0 5.8 %shard_map.48 = bf16[16,16,256]{2,1,0:T(8,128)(2,1)} custom-call(s32[3]{0:T(128)} %pad_add_fusion.flag_ref, bf16[8,256,256]{2,1,0:T(8,128)(2,1)} %rest_0_.5, bf16[4,112,256]{2,1,0:T(8,128)(2,1)} %copy-done.2, bf16[4,112,256]{2,1,0:T(8,128)(2,1)} %copy-done.4), custom_call_target="tpu_custom_call" | custom-call | bytes 262144 | tf_op jit(solution)/shard_map/pallas_call | solution.py:154
  66.8 0.0 copy-start
  66.8 0.0 copy-start.3
  66.8 0.0 copy-start.5
  66.9 0.0 copy-start.8
  66.9 0.0 copy-start.10
  66.9 0.0 copy-start.11
  66.9 3.6 %collective-permute-start.5 = (bf16[16,16,256]{2,1,0:T(8,128)(2,1)}, bf16[16,16,256]{2,1,0:T(8,128)(2,1)S(1)}, u32[]{:S(2)}, u32[]{:S(2)}) collective-permute-start(bf16[16,16,256]{2,1,0:T(8,128)(2,1)} %shard_map.48), channel_id=1, source_target_pairs={{0,1},{1,0},{2,3},{3,2},{4,5},{5,4},{6,7},{7,6},{8,9},{9,8},{10,11... | collective-permute-start | bytes 393224 | tf_op jit(solution)/shard_map/ppermute | solution.py:440
  70.4 2.9 %slice_bitcast_fusion = (bf16[3,3,256,256]{3,2,1,0:T(8,128)(2,1)S(1)}, bf16[1,3,3,256,256]{4,3,2,1,0:T(8,128)(2,1)}) fusion(bf16[3,3,3,256,256]{4,3,2,1,0:T(8,128)(2,1)} %param.7), kind=kLoop, calls=%fused_computation | loop fusion | bytes 4718592 | tf_op jit(solution)/shard_map/squeeze | solution.py:430
  73.3 0.0 collective-permute-done.5.rest_3_
  73.3 0.0 copy-done
  73.3 0.0 copy-done.3
  73.3 0.0 copy-done.5
  73.3 0.0 copy-done.8
  73.3 0.0 copy-done.10
  73.3 0.0 copy-done.11
  73.3 3.4 %shard_map.49 = (bf16[8,96,256]{2,1,0:T(8,128)(2,1)S(1)}, bf16[8,96,256]{2,1,0:T(8,128)(2,1)}) custom-call(s32[3]{0:T(128)S(1)} %copy-done.8, f32[3,256]{1,0:T(4,128)S(1)} %copy-done.10, f32[3,256]{1,0:T(4,128)S(1)} %copy-done.11, bf16[3,3,256,256]{3,2,1,0:T(8,128)(2,1)S(1)} %get-tuple-element.53.w_ref, bf16[8,256,256]{2,1,0:T(8,128)(2,1)S(1)} %copy-done, ...), custom_call_target="tpu_custom_call" | custom-call | flops 905969664 | bytes 1179648 | tf_op jit(solution)/shard_map/pallas_call | solution.py:212
  76.7 0.7 copy-done.12
  77.5 9.4 %collective-permute-start.11 = (bf16[8,96,256]{2,1,0:T(8,128)(2,1)}, bf16[8,96,256]{2,1,0:T(8,128)(2,1)}, u32[]{:S(2)}, u32[]{:S(2)}) collective-permute-start(bf16[8,96,256]{2,1,0:T(8,128)(2,1)} %get-tuple-element.33.refs_0_.near_ref), channel_id=1, source_target_pairs={{0,8},{2,10},{4,12},{6,14},{8,0},{10,2},{12,4},{14,6},{1,9},{3,11}... | collective-permute-start | bytes 1179656 | tf_op jit(solution)/shard_map/ppermute | solution.py:450
  86.9 1.9 %collective-permute-start = (bf16[4,64,256]{2,1,0:T(8,128)(2,1)}, bf16[4,64,256]{2,1,0:T(8,128)(2,1)}, u32[]{:S(2)}, u32[]{:S(2)}) collective-permute-start(bf16[4,64,256]{2,1,0:T(8,128)(2,1)} %get-tuple-element.28), channel_id=1, source_target_pairs={{0,2},{2,4},{4,6},{6,8},{8,10},{10,12},{12,14},{1,3},{3,5},{5,7},{... | collective-permute-start | bytes 393224 | tf_op jit(solution)/shard_map/ppermute | solution.py:425
  88.8 1.3 collective-permute-start.1
  90.1 0.0 collective-permute-done.8.refs_1_.rest_0_
  90.1 0.0 copy-start.6
  90.1 0.8 copy-done.6
  90.9 15.7 %shard_map.50 = (bf16[4,112,256]{2,1,0:T(8,128)(2,1)}, bf16[4,112,256]{2,1,0:T(8,128)(2,1)}) custom-call(s32[3]{0:T(128)} %pad_add_fusion.flag_ref, bf16[8,256,256]{2,1,0:T(8,128)(2,1)} %rest_0_.5, bf16[8,112,256]{2,1,0:T(8,128)(2,1)} %copy-done.6), custom_call_target="tpu_custom_call" | custom-call | bytes 917504 | tf_op jit(solution)/shard_map/pallas_call | solution.py:154
  106.6 5.6 %collective-permute-start.10 = (bf16[4,112,256]{2,1,0:T(8,128)(2,1)}, bf16[4,112,256]{2,1,0:T(8,128)(2,1)}, u32[]{:S(2)}, u32[]{:S(2)}) collective-permute-start(bf16[4,112,256]{2,1,0:T(8,128)(2,1)} %get-tuple-element.38), channel_id=1, source_target_pairs={{2,0},{4,2},{6,4},{0,6},{10,8},{12,10},{14,12},{8,14},{3,1},{5,3},... | collective-permute-start | bytes 688136 | tf_op jit(solution)/shard_map/ppermute | solution.py:475
  112.2 0.0 collective-permute-start.9
  112.2 1.2 slice_bitcast_fusion.1
  113.4 0.0 copy-start.1
  113.4 0.0 copy-start.9
  113.4 0.0 collective-permute-done.11.refs_1_.cnear_ref
  113.4 2.8 %collective-permute-start.6 = (bf16[4,80,256]{2,1,0:T(8,128)(2,1)}, bf16[4,80,256]{2,1,0:T(8,128)(2,1)}, u32[]{:S(2)}, u32[]{:S(2)}) collective-permute-start(bf16[4,80,256]{2,1,0:T(8,128)(2,1)} %get-tuple-element.34), channel_id=1, source_target_pairs={{0,2},{2,4},{4,6},{8,10},{10,12},{12,14},{1,3},{3,5},{5,7},{9,11},... | collective-permute-start | bytes 491528 | tf_op jit(solution)/shard_map/ppermute | solution.py:427
  116.2 9.7 %shard_map.53 = bf16[16,32,256]{2,1,0:T(8,128)(2,1)} custom-call(s32[3]{0:T(128)} %pad_add_fusion.flag_ref, bf16[8,96,256]{2,1,0:T(8,128)(2,1)} %get-tuple-element.33.refs_0_.near_ref, bf16[8,96,256]{2,1,0:T(8,128)(2,1)} %collective-permute-done.11.refs_1_.cnear_ref), custom_call_target="tpu_custom_call" | custom-call | bytes 524288 | tf_op jit(solution)/shard_map/pallas_call | solution.py:154
  125.9 0.0 collective-permute-done.rest_1_.rest_3_
  125.9 1.3 collective-permute-start.7
  127.2 0.0 collective-permute-done.1.rest_2_.rest_4_
  127.2 1.1 collective-permute-start.12
  128.3 1.0 dynamic-slice_bitcast_fusion.wx_ref
  129.3 0.0 copy-done.1
  129.3 0.0 copy-done.9
  129.3 0.0 copy-start.7
  129.4 2.8 %shard_map.47 = (bf16[8,64,256]{2,1,0:T(8,128)(2,1)S(1)}, bf16[8,64,256]{2,1,0:T(8,128)(2,1)S(1)}) custom-call(s32[3]{0:T(128)S(1)} %copy-done.9, f32[3,256]{1,0:T(4,128)S(1)} %copy-done.10, f32[3,256]{1,0:T(4,128)S(1)} %copy-done.11, bf16[3,3,256,256]{3,2,1,0:T(8,128)(2,1)S(1)} %get-tuple-element.53.w_ref, bf16[8,256,256]{2,1,0:T(8,128)(2,1)S(1)} %copy-done.1, ...), custom_call_target="tpu_custom_call" | custom-call | flops 603979776 | bytes 1179648 | tf_op jit(solution)/shard_map/pallas_call | solution.py:212
  132.2 0.0 collective-permute-done.10.rest_6_.rest_2_
  132.2 2.7 %collective-permute-start.4 = (bf16[8,64,256]{2,1,0:T(8,128)(2,1)S(1)}, bf16[8,64,256]{2,1,0:T(8,128)(2,1)S(1)}, u32[]{:S(2)}, u32[]{:S(2)}) collective-permute-start(bf16[8,64,256]{2,1,0:T(8,128)(2,1)S(1)} %get-tuple-element.32.mid_ref), channel_id=1, source_target_pairs={{0,8},{2,10},{4,12},{6,14},{8,0},{10,2},{12,4},{14,6},{1,9},{3,11}... | collective-permute-start | bytes 786440 | tf_op jit(solution)/shard_map/ppermute | solution.py:462
  134.9 0.0 collective-permute-done.9.rest_5_.rest_1_
  134.9 4.3 %shard_map.52 = (bf16[8,96,256]{2,1,0:T(8,128)(2,1)}, bf16[8,96,256]{2,1,0:T(8,128)(2,1)S(1)}) custom-call(s32[3]{0:T(128)S(1)} %copy-done.9, f32[3,256]{1,0:T(4,128)S(1)} %copy-done.10, f32[3,256]{1,0:T(4,128)S(1)} %copy-done.11, bf16[3,3,256,256]{3,2,1,0:T(8,128)(2,1)S(1)} %get-tuple-element.53.w_ref, bf16[8,112,256]{2,1,0:T(8,128)(2,1)S(1)} %copy-done.7, ...), custom_call_target="tpu_custom_call" | custom-call | flops 905969664 | bytes 1179648 | tf_op jit(solution)/shard_map/pallas_call | solution.py:212
  139.2 0.0 collective-permute-done.6.rest_1_
  139.2 0.0 collective-permute-done.7.rest_2_
  139.2 4.2 %shard_map.51 = (bf16[8,96,256]{2,1,0:T(8,128)(2,1)S(1)}, bf16[8,96,256]{2,1,0:T(8,128)(2,1)S(1)}) custom-call(s32[3]{0:T(128)S(1)} %copy-done.9, f32[3,256]{1,0:T(4,128)S(1)} %copy-done.10, f32[3,256]{1,0:T(4,128)S(1)} %copy-done.11, bf16[3,3,256,256]{3,2,1,0:T(8,128)(2,1)S(1)} %get-tuple-element.53.w_ref, bf16[8,256,256]{2,1,0:T(8,128)(2,1)S(1)} %copy-done.1, ...), custom_call_target="tpu_custom_call" | custom-call | flops 905969664 | bytes 1179648 | tf_op jit(solution)/shard_map/pallas_call | solution.py:212
  143.4 0.0 collective-permute-done.12.side_ref
  143.4 4.2 %shard_map.54 = (bf16[8,64,256]{2,1,0:T(8,128)(2,1)S(1)}, bf16[8,64,256]{2,1,0:T(8,128)(2,1)S(1)}, bf16[8,64,256]{2,1,0:T(8,128)(2,1)S(1)}, bf16[8,64,256]{2,1,0...) custom-call(s32[3]{0:T(128)S(1)} %copy-done.9, ...), custom_call_target="tpu_custom_call" | custom-call | flops 1610612736 | bytes 786432 | tf_op jit(solution)/shard_map/pallas_call | solution.py:521
  147.7 0.3 collective-permute-start.13
  148.0 0.0 collective-permute-done.4.cmid_ref
  148.0 1.3 collective-permute-done.13.side_ref
  149.3 4.3 %shard_map.55 = bf16[8,256,256]{2,1,0:T(8,128)(2,1)} custom-call(s32[3]{0:T(128)S(1)} %copy-done.9, f32[3,256]{1,0:T(4,128)S(1)} %copy-done.10, f32[3,256]{1,0:T(4,128)S(1)} %copy-done.11, bf16[3,256,256]{2,1,0:T(8,128)(2,1)S(1)} %dynamic-slice_bitcast_fusion.wx_ref, bf16[3,256,256]{2,1,0:T(8,128)(2,1)S(1)} %get-tuple-element.52.w_ref, ...), custom_call_target="tpu_custom_call" | custom-call | flops 1073741824 | bytes 393216 | tf_op jit(solution)/shard_map/pallas_call | solution.py:545
  (6 shorter events, 0.0 us)
Async XLA Ops:
  48.1 9.4 %collective-permute-start.2 = (bf16[4,112,256]{2,1,0:T(8,128)(2,1)}, bf16[4,112,256]{2,1,0:T(8,128)(2,1)S(1)}, u32[]{:S(2)}, u32[]{:S(2)}) collective-permute-start(bf16[4,112,256]{2,1,0:T(8,128)(2,1)} %get-tuple-element.30), channel_id=1, source_target_pairs={{0,2},{2,4},{4,6},{6,8},{8,10},{10,12},{12,14},{1,3},{3,5},{5,7},{... | collective-permute-start | bytes 688136 | tf_op jit(solution)/shard_map/ppermute | solution.py:423
  52.1 8.3 %collective-permute-start.3 = (bf16[4,112,256]{2,1,0:T(8,128)(2,1)}, bf16[4,112,256]{2,1,0:T(8,128)(2,1)S(1)}, u32[]{:S(2)}, u32[]{:S(2)}) collective-permute-start(bf16[4,112,256]{2,1,0:T(8,128)(2,1)} %get-tuple-element.31), channel_id=1, source_target_pairs={{2,0},{4,2},{6,4},{8,6},{10,8},{12,10},{14,12},{3,1},{5,3},{7,5},{... | collective-permute-start | bytes 688136 | tf_op jit(solution)/shard_map/ppermute | solution.py:424
  53.4 36.7 %collective-permute-start.8 = (bf16[8,112,256]{2,1,0:T(8,128)(2,1)}, bf16[8,112,256]{2,1,0:T(8,128)(2,1)S(1)}, u32[]{:S(2)}, u32[]{:S(2)}) collective-permute-start(bf16[8,112,256]{2,1,0:T(8,128)(2,1)} %get-tuple-element.36), channel_id=1, source_target_pairs={{0,8},{2,10},{4,12},{6,14},{8,0},{10,2},{12,4},{14,6},{1,9},{3,11}... | collective-permute-start | bytes 1376264 | tf_op jit(solution)/shard_map/ppermute | solution.py:422
  57.5 2.8 %copy-start.2 = (bf16[4,112,256]{2,1,0:T(8,128)(2,1)}, bf16[4,112,256]{2,1,0:T(8,128)(2,1)S(1)}, u32[]{:S(2)}) copy-start(bf16[4,112,256]{2,1,0:T(8,128)(2,1)S(1)} %collective-permute-done.2.rest_3_.refs_1_.rest_1_) | copy-start | bytes 688132
  60.3 0.7 copy-start.4
  66.8 6.5 %copy-start = (bf16[8,256,256]{2,1,0:T(8,128)(2,1)S(1)}, bf16[8,256,256]{2,1,0:T(8,128)(2,1)}, u32[]{:S(2)}) copy-start(bf16[8,256,256]{2,1,0:T(8,128)(2,1)} %rest_0_.5) | copy-start | bytes 3145732
  66.8 6.5 %copy-start.3 = (bf16[4,112,256]{2,1,0:T(8,128)(2,1)S(1)}, bf16[4,112,256]{2,1,0:T(8,128)(2,1)}, u32[]{:S(2)}) copy-start(bf16[4,112,256]{2,1,0:T(8,128)(2,1)} %copy-done.2) | copy-start | bytes 688132
  66.8 6.5 %copy-start.5 = (bf16[4,112,256]{2,1,0:T(8,128)(2,1)S(1)}, bf16[4,112,256]{2,1,0:T(8,128)(2,1)}, u32[]{:S(2)}) copy-start(bf16[4,112,256]{2,1,0:T(8,128)(2,1)} %copy-done.4) | copy-start | bytes 688132
  66.9 6.5 %copy-start.8 = (s32[3]{0:T(128)S(1)}, s32[3]{0:T(128)}, u32[]{:S(2)}) copy-start(s32[3]{0:T(128)} %pad_add_fusion.flag_ref) | copy-start | bytes 40
  66.9 6.5 %copy-start.10 = (f32[3,256]{1,0:T(4,128)S(1)}, f32[3,256]{1,0:T(4,128)}, u32[]{:S(2)}) copy-start(f32[3,256]{1,0:T(4,128)} %gain_ref.11) | copy-start | bytes 9220
  66.9 6.5 %copy-start.11 = (f32[3,256]{1,0:T(4,128)S(1)}, f32[3,256]{1,0:T(4,128)}, u32[]{:S(2)}) copy-start(f32[3,256]{1,0:T(4,128)} %bias_ref.11) | copy-start | bytes 9220
  66.9 6.4 %collective-permute-start.5 = (bf16[16,16,256]{2,1,0:T(8,128)(2,1)}, bf16[16,16,256]{2,1,0:T(8,128)(2,1)S(1)}, u32[]{:S(2)}, u32[]{:S(2)}) collective-permute-start(bf16[16,16,256]{2,1,0:T(8,128)(2,1)} %shard_map.48), channel_id=1, source_target_pairs={{0,1},{1,0},{2,3},{3,2},{4,5},{5,4},{6,7},{7,6},{8,9},{9,8},{10,11... | collective-permute-start | bytes 393224 | tf_op jit(solution)/shard_map/ppermute | solution.py:440
  76.7 0.7 copy-start.12
  77.5 35.9 %collective-permute-start.11 = (bf16[8,96,256]{2,1,0:T(8,128)(2,1)}, bf16[8,96,256]{2,1,0:T(8,128)(2,1)}, u32[]{:S(2)}, u32[]{:S(2)}) collective-permute-start(bf16[8,96,256]{2,1,0:T(8,128)(2,1)} %get-tuple-element.33.refs_0_.near_ref), channel_id=1, source_target_pairs={{0,8},{2,10},{4,12},{6,14},{8,0},{10,2},{12,4},{14,6},{1,9},{3,11}... | collective-permute-start | bytes 1179656 | tf_op jit(solution)/shard_map/ppermute | solution.py:450
  86.9 39.0 %collective-permute-start = (bf16[4,64,256]{2,1,0:T(8,128)(2,1)}, bf16[4,64,256]{2,1,0:T(8,128)(2,1)}, u32[]{:S(2)}, u32[]{:S(2)}) collective-permute-start(bf16[4,64,256]{2,1,0:T(8,128)(2,1)} %get-tuple-element.28), channel_id=1, source_target_pairs={{0,2},{2,4},{4,6},{6,8},{8,10},{10,12},{12,14},{1,3},{3,5},{5,7},{... | collective-permute-start | bytes 393224 | tf_op jit(solution)/shard_map/ppermute | solution.py:425
  88.8 38.4 %collective-permute-start.1 = (bf16[4,64,256]{2,1,0:T(8,128)(2,1)}, bf16[4,64,256]{2,1,0:T(8,128)(2,1)}, u32[]{:S(2)}, u32[]{:S(2)}) collective-permute-start(bf16[4,64,256]{2,1,0:T(8,128)(2,1)} %get-tuple-element.29), channel_id=1, source_target_pairs={{2,0},{4,2},{6,4},{8,6},{10,8},{12,10},{14,12},{3,1},{5,3},{7,5},{... | collective-permute-start | bytes 393224 | tf_op jit(solution)/shard_map/ppermute | solution.py:426
  90.1 0.8 copy-start.6
  106.6 25.6 %collective-permute-start.10 = (bf16[4,112,256]{2,1,0:T(8,128)(2,1)}, bf16[4,112,256]{2,1,0:T(8,128)(2,1)}, u32[]{:S(2)}, u32[]{:S(2)}) collective-permute-start(bf16[4,112,256]{2,1,0:T(8,128)(2,1)} %get-tuple-element.38), channel_id=1, source_target_pairs={{2,0},{4,2},{6,4},{0,6},{10,8},{12,10},{14,12},{8,14},{3,1},{5,3},... | collective-permute-start | bytes 688136 | tf_op jit(solution)/shard_map/ppermute | solution.py:475
  112.2 22.7 %collective-permute-start.9 = (bf16[4,112,256]{2,1,0:T(8,128)(2,1)}, bf16[4,112,256]{2,1,0:T(8,128)(2,1)}, u32[]{:S(2)}, u32[]{:S(2)}) collective-permute-start(bf16[4,112,256]{2,1,0:T(8,128)(2,1)} %get-tuple-element.37), channel_id=1, source_target_pairs={{0,2},{2,4},{4,6},{6,0},{8,10},{10,12},{12,14},{14,8},{1,3},{3,5},... | collective-permute-start | bytes 688136 | tf_op jit(solution)/shard_map/ppermute | solution.py:474
  113.4 16.0 %copy-start.1 = (bf16[8,256,256]{2,1,0:T(8,128)(2,1)S(1)}, bf16[8,256,256]{2,1,0:T(8,128)(2,1)}, u32[]{:S(2)}) copy-start(bf16[8,256,256]{2,1,0:T(8,128)(2,1)} %rest_0_.5) | copy-start | bytes 3145732
  113.4 16.0 %copy-start.9 = (s32[3]{0:T(128)S(1)}, s32[3]{0:T(128)}, u32[]{:S(2)}) copy-start(s32[3]{0:T(128)} %pad_add_fusion.flag_ref) | copy-start | bytes 40
  113.4 25.8 %collective-permute-start.6 = (bf16[4,80,256]{2,1,0:T(8,128)(2,1)}, bf16[4,80,256]{2,1,0:T(8,128)(2,1)}, u32[]{:S(2)}, u32[]{:S(2)}) collective-permute-start(bf16[4,80,256]{2,1,0:T(8,128)(2,1)} %get-tuple-element.34), channel_id=1, source_target_pairs={{0,2},{2,4},{4,6},{8,10},{10,12},{12,14},{1,3},{3,5},{5,7},{9,11},... | collective-permute-start | bytes 491528 | tf_op jit(solution)/shard_map/ppermute | solution.py:427
  125.9 13.3 %collective-permute-start.7 = (bf16[4,80,256]{2,1,0:T(8,128)(2,1)}, bf16[4,80,256]{2,1,0:T(8,128)(2,1)S(1)}, u32[]{:S(2)}, u32[]{:S(2)}) collective-permute-start(bf16[4,80,256]{2,1,0:T(8,128)(2,1)} %get-tuple-element.35), channel_id=1, source_target_pairs={{2,0},{4,2},{6,4},{10,8},{12,10},{14,12},{3,1},{5,3},{7,5},{11,9},... | collective-permute-start | bytes 491528 | tf_op jit(solution)/shard_map/ppermute | solution.py:428
  127.2 16.2 %collective-permute-start.12 = (bf16[16,32,256]{2,1,0:T(8,128)(2,1)}, bf16[16,32,256]{2,1,0:T(8,128)(2,1)S(1)}, u32[]{:S(2)}, u32[]{:S(2)}) collective-permute-start(bf16[16,32,256]{2,1,0:T(8,128)(2,1)} %shard_map.53), channel_id=1, source_target_pairs={{0,1},{1,0},{2,3},{3,2},{4,5},{5,4},{6,7},{7,6},{8,9},{9,8},{10,11... | collective-permute-start | bytes 786440 | tf_op jit(solution)/shard_map/ppermute | solution.py:514
  129.3 5.5 %copy-start.7 = (bf16[8,112,256]{2,1,0:T(8,128)(2,1)S(1)}, bf16[8,112,256]{2,1,0:T(8,128)(2,1)}, u32[]{:S(2)}) copy-start(bf16[8,112,256]{2,1,0:T(8,128)(2,1)} %copy-done.6) | copy-start | bytes 1376260
  132.2 15.8 %collective-permute-start.4 = (bf16[8,64,256]{2,1,0:T(8,128)(2,1)S(1)}, bf16[8,64,256]{2,1,0:T(8,128)(2,1)S(1)}, u32[]{:S(2)}, u32[]{:S(2)}) collective-permute-start(bf16[8,64,256]{2,1,0:T(8,128)(2,1)S(1)} %get-tuple-element.32.mid_ref), channel_id=1, source_target_pairs={{0,8},{2,10},{4,12},{6,14},{8,0},{10,2},{12,4},{14,6},{1,9},{3,11}... | collective-permute-start | bytes 786440 | tf_op jit(solution)/shard_map/ppermute | solution.py:462
  139.2 4.2 %copy-start.13 = (bf16[8,96,256]{2,1,0:T(8,128)(2,1)S(1)}, bf16[8,96,256]{2,1,0:T(8,128)(2,1)}, u32[]{:S(2)}) copy-start(bf16[8,96,256]{2,1,0:T(8,128)(2,1)} %copy-done.12) | copy-start | bytes 1179652
  147.7 1.6 %collective-permute-start.13 = (bf16[8,64,256]{2,1,0:T(8,128)(2,1)S(1)}, bf16[8,64,256]{2,1,0:T(8,128)(2,1)S(1)}, u32[]{:S(2)}, u32[]{:S(2)}) collective-permute-start(bf16[8,64,256]{2,1,0:T(8,128)(2,1)S(1)} %get-tuple-element.50), channel_id=1, source_target_pairs={{0,1},{1,0},{2,3},{3,2},{4,5},{5,4},{6,7},{7,6},{8,9},{9,8},{10,11... | collective-permute-start | bytes 786440 | tf_op jit(solution)/shard_map/ppermute | solution.py:544

commit v3 on v2

--- a/solution.py
+++ b/solution.py
@@ -98,6 +98,10 @@
     return pl.BlockSpec(memory_space=pltpu.SMEM)
 
 
+def any_spec():
+    return pl.BlockSpec(memory_space=pl.ANY)
+
+
 def kernel_call(body, out_shape, in_specs, scratch, flops, bytes_accessed):
     return pl.pallas_call(
         body,
@@ -125,20 +129,15 @@
 
 
 def copy_kernel(moves, inputs, flag_ref, *refs):
-    sources, targets, sems = refs[:inputs], refs[inputs:-1], refs[-1]
-
-    def descriptor(at):
-        _, which, row, count, column, width, target, target_row = moves[at]
-        return pltpu.make_async_copy(
-            sources[which].at[pl.ds(row, count), pl.ds(place(flag_ref[0], *column), width)],
-            targets[target].at[pl.ds(target_row, count)],
-            sems.at[at],
-        )
-
-    for at, move in enumerate(moves):
-        guarded(flag_ref, move[0], lambda at=at: descriptor(at).start())
-    for at, move in enumerate(moves):
-        guarded(flag_ref, move[0], lambda at=at: descriptor(at).wait())
+    sources, targets = refs[:inputs], refs[inputs:]
+
+    def move(which, row, count, column, width, target, target_row):
+        src = place(flag_ref[0], *column)
+        for r in range(count):
+            targets[target][target_row + r] = sources[which][row + r, pl.ds(src, width), :]
+
+    for parts in moves:
+        guarded(flag_ref, parts[0], functools.partial(move, *parts[1:]))
 
 
 def copies(flags, arrays, moves):
@@ -151,18 +150,20 @@
         jax.ShapeDtypeStruct(shapes[target] + (channels,), kind) for target in range(len(shapes))
     )
     volume = sum(2 * height * width * channels * 2 for height, width in shapes.values())
-    return pl.pallas_call(
+    return kernel_call(
         functools.partial(copy_kernel, moves, len(arrays)),
-        out_shape=out,
-        in_specs=[smem_spec()] + [pl.BlockSpec(memory_space=pl.ANY)] * len(arrays),
-        out_specs=tuple(pl.BlockSpec(memory_space=pl.ANY) for _ in out),
-        scratch_shapes=[pltpu.SemaphoreType.DMA((len(moves),))],
-        cost_estimate=pl.CostEstimate(flops=0, bytes_accessed=volume, transcendentals=0),
+        out,
+        [smem_spec()] + [vmem_spec()] * len(arrays),
+        [],
+        0,
+        volume,
     )(flags, *arrays)
 
 
 def first_layer_kernel(segments, out_at, rows, width, flag_ref, gain_ref, bias_ref, w_ref, *rest):
-    parts, (next_ref, normed_ref, window, taps) = rest[:-4], rest[-4:]
+    parts, (next_ref, normed_ref, window, taps, weights, sem) = rest[:-6], rest[-6:]
+    load = pltpu.make_async_copy(w_ref.at[0], weights, sem)
+    load.start()
     core = flag_ref[0]
     half = rows // 2
     channels = window.shape[2]
@@ -194,8 +195,9 @@
         ],
         axis=1,
     )
+    load.wait()
     response = jnp.dot(
-        stacked, w_ref[...].reshape(9 * channels, channels), preferred_element_type=jnp.float32
+        stacked, weights[...].reshape(9 * channels, channels), preferred_element_type=jnp.float32
     )
     out_col = place(core, *out_at)
     current = parts[0][:, pl.ds(out_col, width), :].reshape(rows * width, channels)
@@ -212,10 +214,12 @@
     return kernel_call(
         functools.partial(first_layer_kernel, segments, out_at, rows, width),
         (out, out),
-        [smem_spec()] + [vmem_spec()] * (3 + len(parts)),
+        [smem_spec(), vmem_spec(), vmem_spec(), any_spec()] + [vmem_spec()] * len(parts),
         [
             pltpu.VMEM((2 * rows, width + 2 * lane_pad, channels), kind),
             pltpu.VMEM((3, 2 * rows, width, channels), kind),
+            pltpu.VMEM(params[2].shape[1:], kind),
+            pltpu.SemaphoreType.DMA,
         ],
         18 * cells * channels * channels,
         9 * channels * channels * 2,
@@ -228,7 +232,6 @@
     gain_ref,
     bias_ref,
     w_ref,
-    wx_ref,
     near_ref,
     mid_ref,
     far_ref,
@@ -248,8 +251,16 @@
     own,
     other,
     x1,
+    weights,
+    sems,
 ):
     core = flag_ref[0]
+    loads = (
+        pltpu.make_async_copy(w_ref.at[1, 1], weights.at[0], sems.at[0]),
+        pltpu.make_async_copy(w_ref.at[1, flag_ref[3]], weights.at[1], sems.at[1]),
+    )
+    for load in loads:
+        load.start()
     step = dilations[1]
     rows, mid, channels = mid_ref.shape
     cols = 2 * strip + mid
@@ -274,9 +285,8 @@
     own[:, pl.ds(dst, step), :] = jnp.zeros((rows, step, channels), own.dtype)
     other[:, pl.ds(dst, step), :] = jnp.zeros((rows, step, channels), own.dtype)
     edge = strip - step
-    w_own = w_ref[...].reshape(3 * channels, channels)
-    w_other = wx_ref[...].reshape(3 * channels, channels)
-    weights = jnp.concatenate([w_own, w_other], axis=0)
+    for load in loads:
+        load.wait()
     for first, width in ((0, edge), (edge, mid + 2 * step), (cols - edge, edge)):
         stacked = jnp.concatenate(
             [
@@ -288,7 +298,11 @@
             ],
             axis=1,
         )
-        response = jnp.dot(stacked, weights, preferred_element_type=jnp.float32)
+        response = jnp.dot(
+            stacked,
+            weights[...].reshape(6 * channels, channels),
+            preferred_element_type=jnp.float32,
+        )
         current = x1[:, first : first + width, :]
         if first == edge:
             acc_ref[...] = response.reshape(rows, width, channels)
@@ -313,7 +327,6 @@
     flag_ref,
     gain_ref,
     bias_ref,
-    wx_ref,
     w_ref,
     cmid_ref,
     acc_ref,
@@ -327,8 +340,16 @@
     other,
     normed,
     x2,
+    weights,
+    sems,
 ):
     core = flag_ref[0]
+    loads = (
+        pltpu.make_async_copy(w_ref.at[1, flag_ref[3]], weights.at[0], sems.at[0]),
+        pltpu.make_async_copy(w_ref.at[2, 1], weights.at[1], sems.at[1]),
+    )
+    for load in loads:
+        load.start()
     rows, mid, channels = cmid_ref.shape
     edge = nlows_ref.shape[1]
     step, reach = dilations[1], dilations[2]
@@ -345,8 +366,9 @@
         ],
         axis=1,
     )
+    loads[0].wait()
     response = acc_ref[...].reshape(rows * width, channels) + jnp.dot(
-        stacked, wx_ref[...].reshape(3 * channels, channels), preferred_element_type=jnp.float32
+        stacked, weights[0].reshape(3 * channels, channels), preferred_element_type=jnp.float32
     )
     result = update(
         mids_ref[...].reshape(rows * width, channels), response, bias_ref[1:2, :]
@@ -370,8 +392,9 @@
         ],
         axis=1,
     )
+    loads[1].wait()
     response = jnp.dot(
-        stacked, w_ref[...].reshape(3 * channels, channels), preferred_element_type=jnp.float32
+        stacked, weights[1].reshape(3 * channels, channels), preferred_element_type=jnp.float32
     )
     out_ref[...] = update(
         x2[...].reshape(rows * cols, channels), response, bias_ref[2:3, :]
@@ -391,7 +414,9 @@
     wide = strip + pad
     core, row = lax.axis_index("col"), lax.axis_index("row")
     upper_half = row < group
-    flags = jnp.stack([core, row == group - 1, row == group]).astype(jnp.int32)
+    flags = jnp.stack(
+        [core, row == group - 1, row == group, jnp.where(upper_half, 2, 0)]
+    ).astype(jnp.int32)
     last_above, first_below = (1, 1), (2, 1)
     swap = [(0, 1), (1, 0)]
     partner = [(i, (i + group) % size) for i in range(size)]
@@ -427,7 +452,7 @@
     above_far = lax.ppermute(far_low, "row", within_down)
     below_far = lax.ppermute(far_high, "row", within_up)
 
-    params = (norm_gains, conv_biases, conv_weights[0])
+    params = (norm_gains, conv_biases, conv_weights)
     (rim,) = copies(
         flags,
         (context_map, above_near, below_near),
@@ -512,9 +537,6 @@
         ),
     )
     side = lax.ppermute(side, "col", swap)
-    toward = lax.dynamic_index_in_dim(
-        conv_weights[1], jnp.where(upper_half, 2, 0), axis=0, keepdims=False
-    )
     edge = strip - step
     wider = mid + 2 * step
     edge_shape = jax.ShapeDtypeStruct((rows, edge, channels), kind)
@@ -529,32 +551,36 @@
             jax.ShapeDtypeStruct((rows, wider, channels), jnp.float32),
             jax.ShapeDtypeStruct((rows, wider, channels), kind),
         ),
-        [smem_spec()] + [vmem_spec()] * 13,
+        [smem_spec(), vmem_spec(), vmem_spec(), any_spec()] + [vmem_spec()] * 9,
         [
             pltpu.VMEM((rows, cols + 2 * step, channels), kind),
             pltpu.VMEM((rows, cols + 2 * step, channels), kind),
             pltpu.VMEM((rows, cols, channels), kind),
+            pltpu.VMEM((2, 3, channels, channels), kind),
+            pltpu.SemaphoreType.DMA((2,)),
         ],
         12 * rows * cols * channels * channels,
         6 * channels * channels * 2,
     )(
-        flags, norm_gains, conv_biases, conv_weights[1, 1], toward, near_n, mid_n, far_n,
+        flags, norm_gains, conv_biases, conv_weights, near_n, mid_n, far_n,
         cross_near, cross_far, side, near1, mid1, far1,
     )
     last_side = lax.ppermute(n_side, "col", swap)
     return kernel_call(
         last_kernel,
         jax.ShapeDtypeStruct(context_map.shape, kind),
-        [smem_spec()] + [vmem_spec()] * 12,
+        [smem_spec(), vmem_spec(), vmem_spec(), any_spec()] + [vmem_spec()] * 8,
         [
             pltpu.VMEM((rows, mid + 4 * step, channels), kind),
             pltpu.VMEM((rows, cols + 2 * reach, channels), kind),
             pltpu.VMEM((rows, cols, channels), kind),
+            pltpu.VMEM((2, 3, channels, channels), kind),
+            pltpu.SemaphoreType.DMA((2,)),
         ],
         8 * rows * cols * channels * channels,
         3 * channels * channels * 2,
     )(
-        flags, norm_gains, conv_biases, toward, conv_weights[2, 1], cross_mid, acc, mids, lows,
+        flags, norm_gains, conv_biases, conv_weights, cross_mid, acc, mids, lows,
         highs, n_lows, n_highs, last_side,
     )
 

time: 156 us -> 99.1 us (0.64); the launches traced: 154 us -> 98.4 us
  Pallas kernels: 102 us -> 27.3 us
  waiting for transfers between devices: 4.1 us -> 37.1 us
  starting transfers between devices: 39.3 us -> 29 us
  local copies, waits for them, and re-layouts: 7.3 us -> 4.62 us
    pallas_call x4, Pallas kernels: 78.7 us -> 2.36 us  [copies(): kernel_call(functools.partial(copy_kernel, moves, len(arrays)), out, [sme...]
    ppermute x1, waiting for transfers between devices: 0.01 us -> 20.5 us  [by_halves(): raw = lax.ppermute(raw, 'row', partner)]
    ppermute x1, starting transfers between devices: 9.41 us -> 1.03 us  [by_halves(): cross_near = lax.ppermute(near_n, 'row', partner)]
    ppermute x1, waiting for transfers between devices: 0.01 us -> 6.57 us  [by_halves(): above_mid = lax.ppermute(mid_low, 'row', down)]
    ppermute x1, starting transfers between devices: 5.57 us -> 0.06 us  [by_halves(): ring_below = lax.ppermute(ring_high, 'row', ring_up)]
    squeeze x3 -> x0, local copies, waits for them, and re-layouts: 5.04 us -> none  [the longest x1 2.85 us: by_halves(): params = (norm_gains, conv_biases, conv_weights[0])]
    ppermute x1, waiting for transfers between devices: 0.01 us -> 2.94 us  [by_halves(): above_near = lax.ppermute(near_low, 'row', down)]
    unnamed x28 -> x16, local copies, waits for them, and re-layouts: 2.26 us -> 4.62 us
  transfers between devices with their start and end apart: 14 -> 14, of which waited for: 2 -> 6; matrix products, arithmetic and copies ran while one was open for 3% -> 0% of each run, Pallas kernels for 33% -> 22%
where the time goes in v3:
time: 99.1 us; the launch traced here: 98.4 us
  waiting for transfers between devices  37.1 us (37%)
  starting transfers between devices  29 us (29%)
  Pallas kernels  27.3 us (28%)
  local copies, waits for them, and re-layouts  4.62 us (5%)
    ppermute x1, waiting for transfers between devices, by_halves(): raw = lax.ppermute(raw, 'row', partner)  20.5 us
    pallas_call x4, Pallas kernels, first_layer(): kernel_call(functools.partial(first_layer_kernel, segments, out_at, rows,...  15.8 us
    ppermute x1, waiting for transfers between devices, by_halves(): above_mid = lax.ppermute(mid_low, 'row', down)  6.57 us
    pallas_call x1, Pallas kernels, by_halves(): kernel_call(last_kernel, jax.ShapeDtypeStruct(context_map.shape, kind), [...  4.75 us
    unnamed x16, local copies, waits for them, and re-layouts  4.62 us
    pallas_call x1, Pallas kernels, by_halves(): kernel_call(functools.partial(second_layer_kernel, strip), (edge_shape, e...  4.38 us
    ppermute x1, starting transfers between devices, by_halves(): raw = lax.ppermute(raw, 'row', partner)  4.21 us
    ppermute x1, starting transfers between devices, by_halves(): above_far = lax.ppermute(far_low, 'row', within_down)  4.1 us
  transfers between devices with their start and end apart: 14, of which 6 were waited for; matrix products, arithmetic and copies ran while one was open for 0% of the time, Pallas kernels for 22%

profile of v3, /device:TPU:1, one launch (start us, length us, event | category | flops | bytes accessed | tf_op | source)
XLA Modules:
  0.0 98.4 jit_solution(88204083047338274)
XLA Ops:
  0.0 0.1 pad_add_fusion.flag_ref
  0.1 0.0 copy-start.2
  0.1 1.2 %copy-done.2 = bf16[8,256,256]{2,1,0:T(8,128)(2,1)S(1)} copy-done((bf16[8,256,256]{2,1,0:T(8,128)(2,1)S(1)}, bf16[8,256,256]{2,1,0:T(8,128)(2,1)}, u32[]{:S(2)}) %copy-start.2) | copy-done | bytes 1048600
  1.3 0.6 shard_map.46
  2.0 4.0 %collective-permute-start.2 = (bf16[4,112,256]{2,1,0:T(8,128)(2,1)S(1)}, bf16[4,112,256]{2,1,0:T(8,128)(2,1)S(1)}, u32[]{:S(2)}, u32[]{:S(2)}) collective-permute-start(bf16[4,112,256]{2,1,0:T(8,128)(2,1)S(1)} %get-tuple-element.30), channel_id=1, source_target_pairs={{0,2},{2,4},{4,6},{6,8},{8,10},{10,12},{12,14},{1,3},{3,5},{5,7},{... | collective-permute-start | bytes 688136 | tf_op jit(solution)/shard_map/ppermute | solution.py:448
  5.9 1.3 %collective-permute-start.3 = (bf16[4,112,256]{2,1,0:T(8,128)(2,1)S(1)}, bf16[4,112,256]{2,1,0:T(8,128)(2,1)S(1)}, u32[]{:S(2)}, u32[]{:S(2)}) collective-permute-start(bf16[4,112,256]{2,1,0:T(8,128)(2,1)S(1)} %get-tuple-element.31), channel_id=1, source_target_pairs={{2,0},{4,2},{6,4},{8,6},{10,8},{12,10},{14,12},{3,1},{5,3},{7,5},{... | collective-permute-start | bytes 688136 | tf_op jit(solution)/shard_map/ppermute | solution.py:449
  7.2 2.9 %collective-permute-done.2.rest_3_.refs_1_.rest_1_ = bf16[4,112,256]{2,1,0:T(8,128)(2,1)S(1)} collective-permute-done((bf16[4,112,256]{2,1,0:T(8,128)(2,1)S(1)}, bf16[4,112,256]{2,1,0:T(8,128)(2,1)S(1)}, u32[]{:S(2)}, u32[]{:S(2)}) %collective-permute-start.2) | collective-permute-done | bytes 229408 | tf_op jit(solution)/shard_map/ppermute | solution.py:448
  10.2 3.8 %collective-permute-done.3.rest_4_.refs_2_.rest_2_ = bf16[4,112,256]{2,1,0:T(8,128)(2,1)S(1)} collective-permute-done((bf16[4,112,256]{2,1,0:T(8,128)(2,1)S(1)}, bf16[4,112,256]{2,1,0:T(8,128)(2,1)S(1)}, u32[]{:S(2)}, u32[]{:S(2)}) %collective-permute-start.3) | collective-permute-done | bytes 229408 | tf_op jit(solution)/shard_map/ppermute | solution.py:449
  14.0 0.6 shard_map.48
  14.5 2.7 %collective-permute-start.5 = (bf16[16,16,256]{2,1,0:T(8,128)(2,1)S(1)}, bf16[16,16,256]{2,1,0:T(8,128)(2,1)S(1)}, u32[]{:S(2)}, u32[]{:S(2)}) collective-permute-start(bf16[16,16,256]{2,1,0:T(8,128)(2,1)S(1)} %shard_map.48), channel_id=1, source_target_pairs={{0,1},{1,0},{2,3},{3,2},{4,5},{5,4},{6,7},{7,6},{8,9},{9,8},{10,11... | collective-permute-start | bytes 393224 | tf_op jit(solution)/shard_map/ppermute | solution.py:465
  17.3 4.2 %collective-permute-start.8 = (bf16[8,112,256]{2,1,0:T(8,128)(2,1)S(1)}, bf16[8,112,256]{2,1,0:T(8,128)(2,1)S(1)}, u32[]{:S(2)}, u32[]{:S(2)}) collective-permute-start(bf16[8,112,256]{2,1,0:T(8,128)(2,1)S(1)} %get-tuple-element.36), channel_id=1, source_target_pairs={{0,8},{2,10},{4,12},{6,14},{8,0},{10,2},{12,4},{14,6},{1,9},{3,11}... | collective-permute-start | bytes 1376264 | tf_op jit(solution)/shard_map/ppermute | solution.py:447
  21.5 0.0 collective-permute-done.5.rest_3_
  21.5 0.0 copy-start
  21.5 2.0 %copy-done = bf16[3,3,3,256,256]{4,3,2,1,0:T(8,128)(2,1)S(1)} copy-done((bf16[3,3,3,256,256]{4,3,2,1,0:T(8,128)(2,1)S(1)}, bf16[3,3,3,256,256]{4,3,2,1,0:T(8,128)(2,1)}, u32[]{:S(2)}) %copy-start) | copy-done | bytes 3538968
  23.5 0.0 copy-start.4
  23.5 0.7 copy-done.4
  24.2 0.0 copy-start.6
  24.2 0.7 copy-done.6
  24.8 0.0 copy-start.1
  24.8 0.0 copy-start.3
  24.9 4.1 %shard_map.49 = (bf16[8,96,256]{2,1,0:T(8,128)(2,1)S(1)}, bf16[8,96,256]{2,1,0:T(8,128)(2,1)S(1)}) custom-call(s32[4]{0:T(128)S(1)} %pad_add_fusion.flag_ref, f32[3,256]{1,0:T(4,128)S(1)} %copy-done.4, f32[3,256]{1,0:T(4,128)S(1)} %copy-done.6, bf16[3,3,3,256,256]{4,3,2,1,0:T(8,128)(2,1)S(1)} %copy-done, bf16[8,256,256]{2,1,0:T(8,128)(2,1)S(1)} %copy-done.2, ...), custom_call_target="tpu_custom_call" | custom-call | flops 905969664 | bytes 1179648 | tf_op jit(solution)/shard_map/pallas_call | solution.py:214
  29.0 1.0 %collective-permute-start.11 = (bf16[8,96,256]{2,1,0:T(8,128)(2,1)S(1)}, bf16[8,96,256]{2,1,0:T(8,128)(2,1)S(1)}, u32[]{:S(2)}, u32[]{:S(2)}) collective-permute-start(bf16[8,96,256]{2,1,0:T(8,128)(2,1)S(1)} %get-tuple-element.33.refs_0_.near_ref), channel_id=1, source_target_pairs={{0,8},{2,10},{4,12},{6,14},{8,0},{10,2},{12,4},{14,6},{1,9},{3,11}... | collective-permute-start | bytes 1179656 | tf_op jit(solution)/shard_map/ppermute | solution.py:475
  30.0 20.5 %collective-permute-done.8.refs_1_.rest_0_ = bf16[8,112,256]{2,1,0:T(8,128)(2,1)S(1)} collective-permute-done((bf16[8,112,256]{2,1,0:T(8,128)(2,1)S(1)}, bf16[8,112,256]{2,1,0:T(8,128)(2,1)S(1)}, u32[]{:S(2)}, u32[]{:S(2)}) %collective-permute-start.8) | collective-permute-done | bytes 458784 | tf_op jit(solution)/shard_map/ppermute | solution.py:447
  50.5 0.6 shard_map.50
  51.1 0.1 collective-permute-start.10
  51.2 1.5 %collective-permute-start.9 = (bf16[4,112,256]{2,1,0:T(8,128)(2,1)S(1)}, bf16[4,112,256]{2,1,0:T(8,128)(2,1)S(1)}, u32[]{:S(2)}, u32[]{:S(2)}) collective-permute-start(bf16[4,112,256]{2,1,0:T(8,128)(2,1)S(1)} %get-tuple-element.37), channel_id=1, source_target_pairs={{0,2},{2,4},{4,6},{6,0},{8,10},{10,12},{12,14},{14,8},{1,3},{3,5},... | collective-permute-start | bytes 688136 | tf_op jit(solution)/shard_map/ppermute | solution.py:499
  52.6 3.0 %collective-permute-start = (bf16[4,64,256]{2,1,0:T(8,128)(2,1)S(1)}, bf16[4,64,256]{2,1,0:T(8,128)(2,1)S(1)}, u32[]{:S(2)}, u32[]{:S(2)}) collective-permute-start(bf16[4,64,256]{2,1,0:T(8,128)(2,1)S(1)} %get-tuple-element.28), channel_id=1, source_target_pairs={{0,2},{2,4},{4,6},{6,8},{8,10},{10,12},{12,14},{1,3},{3,5},{5,7},{... | collective-permute-start | bytes 393224 | tf_op jit(solution)/shard_map/ppermute | solution.py:450
  55.6 1.3 %collective-permute-start.1 = (bf16[4,64,256]{2,1,0:T(8,128)(2,1)S(1)}, bf16[4,64,256]{2,1,0:T(8,128)(2,1)S(1)}, u32[]{:S(2)}, u32[]{:S(2)}) collective-permute-start(bf16[4,64,256]{2,1,0:T(8,128)(2,1)S(1)} %get-tuple-element.29), channel_id=1, source_target_pairs={{2,0},{4,2},{6,4},{8,6},{10,8},{12,10},{14,12},{3,1},{5,3},{7,5},{... | collective-permute-start | bytes 393224 | tf_op jit(solution)/shard_map/ppermute | solution.py:451
  56.9 2.1 %collective-permute-done.11.refs_1_.cnear_ref = bf16[8,96,256]{2,1,0:T(8,128)(2,1)S(1)} collective-permute-done((bf16[8,96,256]{2,1,0:T(8,128)(2,1)S(1)}, bf16[8,96,256]{2,1,0:T(8,128)(2,1)S(1)}, u32[]{:S(2)}, u32[]{:S(2)}) %collective-permute-start.11) | collective-permute-done | bytes 393248 | tf_op jit(solution)/shard_map/ppermute | solution.py:475
  59.0 0.6 shard_map.53
  59.6 0.8 collective-permute-start.12
  60.3 6.6 %collective-permute-done.rest_1_.rest_3_ = bf16[4,64,256]{2,1,0:T(8,128)(2,1)S(1)} collective-permute-done((bf16[4,64,256]{2,1,0:T(8,128)(2,1)S(1)}, bf16[4,64,256]{2,1,0:T(8,128)(2,1)S(1)}, u32[]{:S(2)}, u32[]{:S(2)}) %collective-permute-start) | collective-permute-done | bytes 131104 | tf_op jit(solution)/shard_map/ppermute | solution.py:450
  66.9 4.1 %collective-permute-start.6 = (bf16[4,80,256]{2,1,0:T(8,128)(2,1)S(1)}, bf16[4,80,256]{2,1,0:T(8,128)(2,1)S(1)}, u32[]{:S(2)}, u32[]{:S(2)}) collective-permute-start(bf16[4,80,256]{2,1,0:T(8,128)(2,1)S(1)} %get-tuple-element.34), channel_id=1, source_target_pairs={{0,2},{2,4},{4,6},{8,10},{10,12},{12,14},{1,3},{3,5},{5,7},{9,11},... | collective-permute-start | bytes 491528 | tf_op jit(solution)/shard_map/ppermute | solution.py:452
  71.0 0.0 collective-permute-done.1.rest_2_.rest_4_
  71.0 1.3 %collective-permute-start.7 = (bf16[4,80,256]{2,1,0:T(8,128)(2,1)S(1)}, bf16[4,80,256]{2,1,0:T(8,128)(2,1)S(1)}, u32[]{:S(2)}, u32[]{:S(2)}) collective-permute-start(bf16[4,80,256]{2,1,0:T(8,128)(2,1)S(1)} %get-tuple-element.35), channel_id=1, source_target_pairs={{2,0},{4,2},{6,4},{10,8},{12,10},{14,12},{3,1},{5,3},{7,5},{11,9},... | collective-permute-start | bytes 491528 | tf_op jit(solution)/shard_map/ppermute | solution.py:453
  72.3 0.0 copy-done.1
  72.3 0.0 copy-done.3
  72.4 3.3 %shard_map.47 = (bf16[8,64,256]{2,1,0:T(8,128)(2,1)S(1)}, bf16[8,64,256]{2,1,0:T(8,128)(2,1)S(1)}) custom-call(s32[4]{0:T(128)S(1)} %pad_add_fusion.flag_ref, f32[3,256]{1,0:T(4,128)S(1)} %copy-done.4, f32[3,256]{1,0:T(4,128)S(1)} %copy-done.6, bf16[3,3,3,256,256]{4,3,2,1,0:T(8,128)(2,1)S(1)} %copy-done.1, bf16[8,256,256]{2,1,0:T(8,128)(2,1)S(1)} %copy-done.3, ...), custom_call_target="tpu_custom_call" | custom-call | flops 603979776 | bytes 1179648 | tf_op jit(solution)/shard_map/pallas_call | solution.py:214
  75.7 0.0 collective-permute-done.10.rest_6_.rest_2_
  75.7 1.6 %collective-permute-start.4 = (bf16[8,64,256]{2,1,0:T(8,128)(2,1)S(1)}, bf16[8,64,256]{2,1,0:T(8,128)(2,1)S(1)}, u32[]{:S(2)}, u32[]{:S(2)}) collective-permute-start(bf16[8,64,256]{2,1,0:T(8,128)(2,1)S(1)} %get-tuple-element.32.mid_ref), channel_id=1, source_target_pairs={{0,8},{2,10},{4,12},{6,14},{8,0},{10,2},{12,4},{14,6},{1,9},{3,11}... | collective-permute-start | bytes 786440 | tf_op jit(solution)/shard_map/ppermute | solution.py:487
  77.3 0.0 collective-permute-done.9.rest_5_.rest_1_
  77.3 4.4 %shard_map.52 = (bf16[8,96,256]{2,1,0:T(8,128)(2,1)}, bf16[8,96,256]{2,1,0:T(8,128)(2,1)S(1)}) custom-call(s32[4]{0:T(128)S(1)} %pad_add_fusion.flag_ref, f32[3,256]{1,0:T(4,128)S(1)} %copy-done.4, f32[3,256]{1,0:T(4,128)S(1)} %copy-done.6, bf16[3,3,3,256,256]{4,3,2,1,0:T(8,128)(2,1)S(1)} %copy-done.1, ...), custom_call_target="tpu_custom_call" | custom-call | flops 905969664 | bytes 1179648 | tf_op jit(solution)/shard_map/pallas_call | solution.py:214
  81.6 0.0 copy-start.5
  81.6 0.0 copy-start.7
  81.7 0.0 collective-permute-done.6.rest_1_
  81.7 0.0 collective-permute-done.7.rest_2_
  81.7 4.0 %shard_map.51 = (bf16[8,96,256]{2,1,0:T(8,128)(2,1)S(1)}, bf16[8,96,256]{2,1,0:T(8,128)(2,1)S(1)}) custom-call(s32[4]{0:T(128)S(1)} %pad_add_fusion.flag_ref, f32[3,256]{1,0:T(4,128)S(1)} %copy-done.4, f32[3,256]{1,0:T(4,128)S(1)} %copy-done.6, bf16[3,3,3,256,256]{4,3,2,1,0:T(8,128)(2,1)S(1)} %copy-done.1, bf16[8,256,256]{2,1,0:T(8,128)(2,1)S(1)} %copy-done.3, ...), custom_call_target="tpu_custom_call" | custom-call | flops 905969664 | bytes 1179648 | tf_op jit(solution)/shard_map/pallas_call | solution.py:214
  85.7 0.0 collective-permute-done.12.side_ref
  85.7 0.0 copy-done.5
  85.7 0.0 copy-done.7
  85.7 4.4 %shard_map.54 = (bf16[8,64,256]{2,1,0:T(8,128)(2,1)S(1)}, bf16[8,64,256]{2,1,0:T(8,128)(2,1)S(1)}, bf16[8,64,256]{2,1,0:T(8,128)(2,1)S(1)}, bf16[8,64,256]{2,1,0...) custom-call(s32[4]{0:T(128)S(1)} %pad_add_fusion.flag_ref, ...), custom_call_target="tpu_custom_call" | custom-call | flops 1610612736 | bytes 786432 | tf_op jit(solution)/shard_map/pallas_call | solution.py:543
  90.1 2.2 %collective-permute-start.13 = (bf16[8,64,256]{2,1,0:T(8,128)(2,1)S(1)}, bf16[8,64,256]{2,1,0:T(8,128)(2,1)S(1)}, u32[]{:S(2)}, u32[]{:S(2)}) collective-permute-start(bf16[8,64,256]{2,1,0:T(8,128)(2,1)S(1)} %get-tuple-element.50), channel_id=1, source_target_pairs={{0,1},{1,0},{2,3},{3,2},{4,5},{5,4},{6,7},{7,6},{8,9},{9,8},{10,11... | collective-permute-start | bytes 786440 | tf_op jit(solution)/shard_map/ppermute | solution.py:568
  92.3 0.0 collective-permute-done.4.cmid_ref
  92.3 1.2 %collective-permute-done.13.side_ref = bf16[8,64,256]{2,1,0:T(8,128)(2,1)S(1)} collective-permute-done((bf16[8,64,256]{2,1,0:T(8,128)(2,1)S(1)}, bf16[8,64,256]{2,1,0:T(8,128)(2,1)S(1)}, u32[]{:S(2)}, u32[]{:S(2)}) %collective-permute-start.13) | collective-permute-done | bytes 262176 | tf_op jit(solution)/shard_map/ppermute | solution.py:568
  93.5 4.8 %shard_map.55 = bf16[8,256,256]{2,1,0:T(8,128)(2,1)} custom-call(s32[4]{0:T(128)S(1)} %pad_add_fusion.flag_ref, f32[3,256]{1,0:T(4,128)S(1)} %copy-done.5, f32[3,256]{1,0:T(4,128)S(1)} %copy-done.7, bf16[3,3,3,256,256]{4,3,2,1,0:T(8,128)(2,1)S(1)} %copy-done.1, bf16[8,64,256]{2,1,0:T(8,128)(2,1)S(1)} %collective-permute-done.4.cmid_ref, ...), custom_call_target="tpu_custom_call" | custom-call | flops 1073741824 | bytes 393216 | tf_op jit(solution)/shard_map/pallas_call | solution.py:569
Async XLA Ops:
  0.1 1.2 %copy-start.2 = (bf16[8,256,256]{2,1,0:T(8,128)(2,1)S(1)}, bf16[8,256,256]{2,1,0:T(8,128)(2,1)}, u32[]{:S(2)}) copy-start(bf16[8,256,256]{2,1,0:T(8,128)(2,1)} %rest_0_.5) | copy-start | bytes 3145732
  2.0 8.2 %collective-permute-start.2 = (bf16[4,112,256]{2,1,0:T(8,128)(2,1)S(1)}, bf16[4,112,256]{2,1,0:T(8,128)(2,1)S(1)}, u32[]{:S(2)}, u32[]{:S(2)}) collective-permute-start(bf16[4,112,256]{2,1,0:T(8,128)(2,1)S(1)} %get-tuple-element.30), channel_id=1, source_target_pairs={{0,2},{2,4},{4,6},{6,8},{8,10},{10,12},{12,14},{1,3},{3,5},{5,7},{... | collective-permute-start | bytes 688136 | tf_op jit(solution)/shard_map/ppermute | solution.py:448
  5.9 8.0 %collective-permute-start.3 = (bf16[4,112,256]{2,1,0:T(8,128)(2,1)S(1)}, bf16[4,112,256]{2,1,0:T(8,128)(2,1)S(1)}, u32[]{:S(2)}, u32[]{:S(2)}) collective-permute-start(bf16[4,112,256]{2,1,0:T(8,128)(2,1)S(1)} %get-tuple-element.31), channel_id=1, source_target_pairs={{2,0},{4,2},{6,4},{8,6},{10,8},{12,10},{14,12},{3,1},{5,3},{7,5},{... | collective-permute-start | bytes 688136 | tf_op jit(solution)/shard_map/ppermute | solution.py:449
  14.5 6.9 %collective-permute-start.5 = (bf16[16,16,256]{2,1,0:T(8,128)(2,1)S(1)}, bf16[16,16,256]{2,1,0:T(8,128)(2,1)S(1)}, u32[]{:S(2)}, u32[]{:S(2)}) collective-permute-start(bf16[16,16,256]{2,1,0:T(8,128)(2,1)S(1)} %shard_map.48), channel_id=1, source_target_pairs={{0,1},{1,0},{2,3},{3,2},{4,5},{5,4},{6,7},{7,6},{8,9},{9,8},{10,11... | collective-permute-start | bytes 393224 | tf_op jit(solution)/shard_map/ppermute | solution.py:465
  17.3 33.3 %collective-permute-start.8 = (bf16[8,112,256]{2,1,0:T(8,128)(2,1)S(1)}, bf16[8,112,256]{2,1,0:T(8,128)(2,1)S(1)}, u32[]{:S(2)}, u32[]{:S(2)}) collective-permute-start(bf16[8,112,256]{2,1,0:T(8,128)(2,1)S(1)} %get-tuple-element.36), channel_id=1, source_target_pairs={{0,8},{2,10},{4,12},{6,14},{8,0},{10,2},{12,4},{14,6},{1,9},{3,11}... | collective-permute-start | bytes 1376264 | tf_op jit(solution)/shard_map/ppermute | solution.py:447
  21.5 2.0 %copy-start = (bf16[3,3,3,256,256]{4,3,2,1,0:T(8,128)(2,1)S(1)}, bf16[3,3,3,256,256]{4,3,2,1,0:T(8,128)(2,1)}, u32[]{:S(2)}) copy-start(bf16[3,3,3,256,256]{4,3,2,1,0:T(8,128)(2,1)} %w_ref.11) | copy-start | bytes 10616836
  23.5 0.7 copy-start.4
  24.2 0.7 copy-start.6
  24.8 47.5 %copy-start.1 = (bf16[3,3,3,256,256]{4,3,2,1,0:T(8,128)(2,1)S(1)}, bf16[3,3,3,256,256]{4,3,2,1,0:T(8,128)(2,1)}, u32[]{:S(2)}) copy-start(bf16[3,3,3,256,256]{4,3,2,1,0:T(8,128)(2,1)} %w_ref.11) | copy-start | bytes 10616836
  24.8 47.5 %copy-start.3 = (bf16[8,256,256]{2,1,0:T(8,128)(2,1)S(1)}, bf16[8,256,256]{2,1,0:T(8,128)(2,1)}, u32[]{:S(2)}) copy-start(bf16[8,256,256]{2,1,0:T(8,128)(2,1)} %rest_0_.5) | copy-start | bytes 3145732
  29.0 30.0 %collective-permute-start.11 = (bf16[8,96,256]{2,1,0:T(8,128)(2,1)S(1)}, bf16[8,96,256]{2,1,0:T(8,128)(2,1)S(1)}, u32[]{:S(2)}, u32[]{:S(2)}) collective-permute-start(bf16[8,96,256]{2,1,0:T(8,128)(2,1)S(1)} %get-tuple-element.33.refs_0_.near_ref), channel_id=1, source_target_pairs={{0,8},{2,10},{4,12},{6,14},{8,0},{10,2},{12,4},{14,6},{1,9},{3,11}... | collective-permute-start | bytes 1179656 | tf_op jit(solution)/shard_map/ppermute | solution.py:475
  51.1 24.6 %collective-permute-start.10 = (bf16[4,112,256]{2,1,0:T(8,128)(2,1)S(1)}, bf16[4,112,256]{2,1,0:T(8,128)(2,1)S(1)}, u32[]{:S(2)}, u32[]{:S(2)}) collective-permute-start(bf16[4,112,256]{2,1,0:T(8,128)(2,1)S(1)} %get-tuple-element.38), channel_id=1, source_target_pairs={{2,0},{4,2},{6,4},{0,6},{10,8},{12,10},{14,12},{8,14},{3,1},{5,3},... | collective-permute-start | bytes 688136 | tf_op jit(solution)/shard_map/ppermute | solution.py:500
  51.2 26.1 %collective-permute-start.9 = (bf16[4,112,256]{2,1,0:T(8,128)(2,1)S(1)}, bf16[4,112,256]{2,1,0:T(8,128)(2,1)S(1)}, u32[]{:S(2)}, u32[]{:S(2)}) collective-permute-start(bf16[4,112,256]{2,1,0:T(8,128)(2,1)S(1)} %get-tuple-element.37), channel_id=1, source_target_pairs={{0,2},{2,4},{4,6},{6,0},{8,10},{10,12},{12,14},{14,8},{1,3},{3,5},... | collective-permute-start | bytes 688136 | tf_op jit(solution)/shard_map/ppermute | solution.py:499
  52.6 14.3 %collective-permute-start = (bf16[4,64,256]{2,1,0:T(8,128)(2,1)S(1)}, bf16[4,64,256]{2,1,0:T(8,128)(2,1)S(1)}, u32[]{:S(2)}, u32[]{:S(2)}) collective-permute-start(bf16[4,64,256]{2,1,0:T(8,128)(2,1)S(1)} %get-tuple-element.28), channel_id=1, source_target_pairs={{0,2},{2,4},{4,6},{6,8},{8,10},{10,12},{12,14},{1,3},{3,5},{5,7},{... | collective-permute-start | bytes 393224 | tf_op jit(solution)/shard_map/ppermute | solution.py:450
  55.6 15.4 %collective-permute-start.1 = (bf16[4,64,256]{2,1,0:T(8,128)(2,1)S(1)}, bf16[4,64,256]{2,1,0:T(8,128)(2,1)S(1)}, u32[]{:S(2)}, u32[]{:S(2)}) collective-permute-start(bf16[4,64,256]{2,1,0:T(8,128)(2,1)S(1)} %get-tuple-element.29), channel_id=1, source_target_pairs={{2,0},{4,2},{6,4},{8,6},{10,8},{12,10},{14,12},{3,1},{5,3},{7,5},{... | collective-permute-start | bytes 393224 | tf_op jit(solution)/shard_map/ppermute | solution.py:451
  59.6 26.1 %collective-permute-start.12 = (bf16[16,32,256]{2,1,0:T(8,128)(2,1)S(1)}, bf16[16,32,256]{2,1,0:T(8,128)(2,1)S(1)}, u32[]{:S(2)}, u32[]{:S(2)}) collective-permute-start(bf16[16,32,256]{2,1,0:T(8,128)(2,1)S(1)} %shard_map.53), channel_id=1, source_target_pairs={{0,1},{1,0},{2,3},{3,2},{4,5},{5,4},{6,7},{7,6},{8,9},{9,8},{10,11... | collective-permute-start | bytes 786440 | tf_op jit(solution)/shard_map/ppermute | solution.py:539
  66.9 14.7 %collective-permute-start.6 = (bf16[4,80,256]{2,1,0:T(8,128)(2,1)S(1)}, bf16[4,80,256]{2,1,0:T(8,128)(2,1)S(1)}, u32[]{:S(2)}, u32[]{:S(2)}) collective-permute-start(bf16[4,80,256]{2,1,0:T(8,128)(2,1)S(1)} %get-tuple-element.34), channel_id=1, source_target_pairs={{0,2},{2,4},{4,6},{8,10},{10,12},{12,14},{1,3},{3,5},{5,7},{9,11},... | collective-permute-start | bytes 491528 | tf_op jit(solution)/shard_map/ppermute | solution.py:452
  71.0 10.6 %collective-permute-start.7 = (bf16[4,80,256]{2,1,0:T(8,128)(2,1)S(1)}, bf16[4,80,256]{2,1,0:T(8,128)(2,1)S(1)}, u32[]{:S(2)}, u32[]{:S(2)}) collective-permute-start(bf16[4,80,256]{2,1,0:T(8,128)(2,1)S(1)} %get-tuple-element.35), channel_id=1, source_target_pairs={{2,0},{4,2},{6,4},{10,8},{12,10},{14,12},{3,1},{5,3},{7,5},{11,9},... | collective-permute-start | bytes 491528 | tf_op jit(solution)/shard_map/ppermute | solution.py:453
  75.7 16.6 %collective-permute-start.4 = (bf16[8,64,256]{2,1,0:T(8,128)(2,1)S(1)}, bf16[8,64,256]{2,1,0:T(8,128)(2,1)S(1)}, u32[]{:S(2)}, u32[]{:S(2)}) collective-permute-start(bf16[8,64,256]{2,1,0:T(8,128)(2,1)S(1)} %get-tuple-element.32.mid_ref), channel_id=1, source_target_pairs={{0,8},{2,10},{4,12},{6,14},{8,0},{10,2},{12,4},{14,6},{1,9},{3,11}... | collective-permute-start | bytes 786440 | tf_op jit(solution)/shard_map/ppermute | solution.py:487
  81.6 4.0 %copy-start.5 = (f32[3,256]{1,0:T(4,128)S(1)}, f32[3,256]{1,0:T(4,128)}, u32[]{:S(2)}) copy-start(f32[3,256]{1,0:T(4,128)} %gain_ref.11) | copy-start | bytes 9220
  81.6 4.0 %copy-start.7 = (f32[3,256]{1,0:T(4,128)S(1)}, f32[3,256]{1,0:T(4,128)}, u32[]{:S(2)}) copy-start(f32[3,256]{1,0:T(4,128)} %bias_ref.11) | copy-start | bytes 9220
  90.1 3.4 %collective-permute-start.13 = (bf16[8,64,256]{2,1,0:T(8,128)(2,1)S(1)}, bf16[8,64,256]{2,1,0:T(8,128)(2,1)S(1)}, u32[]{:S(2)}, u32[]{:S(2)}) collective-permute-start(bf16[8,64,256]{2,1,0:T(8,128)(2,1)S(1)} %get-tuple-element.50), channel_id=1, source_target_pairs={{0,1},{1,0},{2,3},{3,2},{4,5},{5,4},{6,7},{7,6},{8,9},{9,8},{10,11... | collective-permute-start | bytes 786440 | tf_op jit(solution)/shard_map/ppermute | solution.py:568

commit v4 on v0

--- a/solution.py
+++ b/solution.py
@@ -1,9 +1,16 @@
+import functools
+
 import jax
 import jax.numpy as jnp
 from jax import lax
+from jax.experimental import pallas as pl
+from jax.experimental.pallas import tpu as pltpu
 from jax.sharding import PartitionSpec as P
 
 epsilon = 1e-05
+dilations = (4, 32, 64)
+lane_pad = 16
+vmem_limit = 40 * 1024 * 1024
 
 
 def extended(x, sides, width):
@@ -51,11 +58,7 @@
     )
 
 
-def class_rims(normed, width):
-    return extended(normed, (("col", 1),), width)
-
-
-def shards(context_map, norm_gains, conv_biases, conv_weights):
+def by_classes(context_map, norm_gains, conv_biases, conv_weights):
     tile_rows, tile_cols, channels = context_map.shape
     normed = normalize(context_map, norm_gains[0])
     padded = extended(normed, (("row", 0), ("col", 1)), 4)
@@ -75,7 +78,7 @@
         normed = normalize(grouped, norm_gains[position])
         row_gap = dilation // tile_rows
         col_gap = dilation // class_count
-        with_sides = class_rims(normed, col_gap)
+        with_sides = extended(normed, (("col", 1),), col_gap)
         padded = jnp.pad(with_sides, ((row_gap, row_gap), (0, 0), (0, 0)))
         response = convolve(padded, conv_weights[position], row_gap, col_gap, sub_rows, sub_cols)
         grouped = update(grouped, response, conv_biases[position])
@@ -87,6 +90,455 @@
     )
 
 
+def vmem_spec():
+    return pl.BlockSpec(memory_space=pltpu.VMEM)
+
+
+def smem_spec():
+    return pl.BlockSpec(memory_space=pltpu.SMEM)
+
+
+def any_spec():
+    return pl.BlockSpec(memory_space=pl.ANY)
+
+
+def kernel_call(body, out_shape, in_specs, scratch):
+    return pl.pallas_call(
+        body,
+        out_shape=out_shape,
+        in_specs=in_specs,
+        out_specs=jax.tree.map(lambda _: vmem_spec(), out_shape),
+        scratch_shapes=scratch,
+        compiler_params=pltpu.CompilerParams(vmem_limit_bytes=vmem_limit),
+        cost_estimate=pl.CostEstimate(flops=1, bytes_accessed=1, transcendentals=0),
+    )
+
+
+def place(core, at_zero, at_one):
+    return pl.multiple_of(jnp.where(core == 0, at_zero, at_one), lane_pad)
+
+
+def guarded(flag_ref, condition, action):
+    if condition is None:
+        action()
+    else:
+        number, value = condition
+        pl.when(flag_ref[number] == value)(action)
+
+
+def copy_kernel(moves, inputs, flag_ref, *refs):
+    sources, targets = refs[:inputs], refs[inputs:]
+
+    def move(which, row, count, column, width, target, target_row):
+        src = place(flag_ref[0], *column)
+        for r in range(count):
+            targets[target][target_row + r] = sources[which][row + r, pl.ds(src, width), :]
+
+    for parts in moves:
+        guarded(flag_ref, parts[0], functools.partial(move, *parts[1:]))
+
+
+def copies(flags, arrays, moves):
+    channels, kind = arrays[0].shape[2], arrays[0].dtype
+    shapes = {}
+    for _, _, _, count, _, width, target, target_row in moves:
+        height = max(target_row + count, shapes.get(target, (0, 0))[0])
+        shapes[target] = (height, width)
+    out = tuple(
+        jax.ShapeDtypeStruct(shapes[target] + (channels,), kind) for target in range(len(shapes))
+    )
+    return kernel_call(
+        functools.partial(copy_kernel, moves, len(arrays)),
+        out,
+        [smem_spec()] + [vmem_spec()] * len(arrays),
+        [],
+    )(flags, *arrays)
+
+
+def hold_kernel(flag_ref, gain_ref, bias_ref, w_ref, scale_ref, first_ref, second_ref, last_ref):
+    scale_ref[0:3, :] = gain_ref[...]
+    scale_ref[3:6, :] = bias_ref[...]
+    first_ref[...] = w_ref[0]
+    second_ref[0] = w_ref[1, 1]
+    second_ref[1] = w_ref[1, flag_ref[3]]
+    last_ref[...] = w_ref[2, 1]
+
+
+def first_layer_kernel(segments, out_at, rows, width, flag_ref, scale_ref, w_ref, *rest):
+    parts, (next_ref, normed_ref, window, taps) = rest[:-4], rest[-4:]
+    core = flag_ref[0]
+    half = rows // 2
+    channels = window.shape[2]
+    gain = scale_ref[0:1, :]
+
+    def fill(which, source_row, window_row, count, source, target, columns):
+        src, dst = place(core, *source), place(core, *target)
+        for r in range(count):
+            if which is None:
+                values = jnp.zeros((columns, channels), window.dtype)
+            else:
+                values = normalize(
+                    parts[which][source_row + r, pl.ds(src, columns), :], gain
+                )
+            window[window_row + r, pl.ds(dst, columns), :] = values
+
+    for segment in segments:
+        guarded(flag_ref, segment[0], functools.partial(fill, *segment[1:]))
+    step = dilations[0]
+    for b in range(3):
+        first = lane_pad + (b - 1) * step
+        for r in range(2 * rows):
+            taps[b, r] = window[r, first : first + width, :]
+    stacked = jnp.concatenate(
+        [
+            taps[b, a * half : a * half + rows].reshape(rows * width, channels)
+            for a in range(3)
+            for b in range(3)
+        ],
+        axis=1,
+    )
+    response = jnp.dot(
+        stacked, w_ref[...].reshape(9 * channels, channels), preferred_element_type=jnp.float32
+    )
+    out_col = place(core, *out_at)
+    current = parts[0][:, pl.ds(out_col, width), :].reshape(rows * width, channels)
+    result = update(current, response, scale_ref[3:4, :])
+    next_ref[...] = result.reshape(rows, width, channels)
+    normed_ref[...] = normalize(result, scale_ref[1:2, :]).reshape(rows, width, channels)
+
+
+def first_layer(flags, params, parts, segments, out_at, width):
+    rows, _, channels = parts[0].shape
+    kind = parts[0].dtype
+    out = jax.ShapeDtypeStruct((rows, width, channels), kind)
+    return kernel_call(
+        functools.partial(first_layer_kernel, segments, out_at, rows, width),
+        (out, out),
+        [smem_spec()] + [vmem_spec()] * (2 + len(parts)),
+        [
+            pltpu.VMEM((2 * rows, width + 2 * lane_pad, channels), kind),
+            pltpu.VMEM((3, 2 * rows, width, channels), kind),
+        ],
+    )(flags, *params, *parts)
+
+
+def partial_kernel(
+    flag_ref, scale_ref, w_ref, near_ref, mid_ref, far_ref, cfar_ref, side_ref, near1_ref, mid1_ref,
+    far1_ref, acc_ref, next_ref, own, other,
+):
+    core = flag_ref[0]
+    step = dilations[1]
+    rows, near, channels = near_ref.shape
+    mid, far = mid_ref.shape[1], far_ref.shape[1]
+    cols = near + mid + far
+    other[...] = jnp.zeros(other.shape, other.dtype)
+    pieces = (
+        (near_ref, near1_ref, (cols - near, 0)),
+        (mid_ref, mid1_ref, (far, near)),
+        (far_ref, far1_ref, (0, cols - far)),
+    )
+    for normed, current, at in pieces:
+        width = normed.shape[1]
+        next_ref[:, pl.ds(place(core, *at), width), :] = current[...]
+        inside = pl.ds(place(core, at[0] + step, at[1] + step), width)
+        own[:, inside, :] = normed[...]
+        if normed is far_ref:
+            other[:, inside, :] = cfar_ref[...]
+    spare = side_ref.shape[1] - step
+    own[:, pl.ds(place(core, step + cols, 0), step), :] = side_ref[
+        :, pl.ds(place(core, 0, spare), step), :
+    ]
+    own[:, pl.ds(place(core, 0, step + cols), step), :] = jnp.zeros(
+        (rows, step, channels), own.dtype
+    )
+    stacked = jnp.concatenate(
+        [
+            ref[:, b * step : b * step + cols, :].reshape(rows * cols, channels)
+            for ref in (own, other)
+            for b in range(3)
+        ],
+        axis=1,
+    )
+    acc_ref[...] = jnp.dot(
+        stacked, w_ref[...].reshape(6 * channels, channels), preferred_element_type=jnp.float32
+    ).reshape(rows, cols, channels)
+
+
+def second_layer(flag_ref, scale_ref, w_ref, window, acc, current):
+    step = dilations[1]
+    rows, width, channels = current.shape
+    cells = rows * width
+    stacked = jnp.concatenate(
+        [window[:, b * step : b * step + width, :].reshape(cells, channels) for b in range(3)],
+        axis=1,
+    )
+    response = acc.reshape(cells, channels) + jnp.dot(
+        stacked,
+        w_ref[1].reshape(3 * channels, channels),
+        preferred_element_type=jnp.float32,
+    )
+    result = update(current.reshape(cells, channels), response, scale_ref[4:5, :])
+    normed = normalize(result, scale_ref[2:3, :])
+    return result.reshape(current.shape), normed.reshape(current.shape)
+
+
+def near_kernel(
+    flag_ref, scale_ref, w_ref, cnear_ref, side_ref, acc_ref, x1_ref, next_ref, normed_ref, window
+):
+    core = flag_ref[0]
+    step, reach = dilations[1], dilations[2]
+    near, cols = cnear_ref.shape[1], x1_ref.shape[1]
+    window[:, pl.ds(place(core, 0, step), near), :] = cnear_ref[...]
+    window[:, pl.ds(place(core, near, 0), step), :] = side_ref[...]
+    at = pl.ds(place(core, cols - reach, 0), reach)
+    next_ref[...], normed_ref[...] = second_layer(
+        flag_ref, scale_ref, w_ref, window[...], acc_ref[:, at, :], x1_ref[:, at, :]
+    )
+
+
+def rest_kernel(
+    flag_ref, scale_ref, w_ref, cmid_ref, cnear_ref, acc_ref, x1_ref, next_ref, normed_ref, window
+):
+    core = flag_ref[0]
+    step, reach = dilations[1], dilations[2]
+    rows, mid, channels = cmid_ref.shape
+    near, cols = cnear_ref.shape[1], x1_ref.shape[1]
+    width, far = cols - reach, cols - near - mid
+    count = width + step - far - mid
+    window[:, pl.ds(place(core, step + far + mid, 0), count), :] = cnear_ref[
+        :, pl.ds(place(core, 0, near - count), count), :
+    ]
+    window[:, pl.ds(place(core, step + far, count), mid), :] = cmid_ref[...]
+    window[:, pl.ds(place(core, 0, count + mid), step + far), :] = jnp.zeros(
+        (rows, step + far, channels), window.dtype
+    )
+    at = pl.ds(place(core, 0, reach), width)
+    next_ref[...], normed_ref[...] = second_layer(
+        flag_ref, scale_ref, w_ref, window[...], acc_ref[:, at, :], x1_ref[:, at, :]
+    )
+
+
+def last_kernel(
+    flag_ref, scale_ref, w_ref, near2_ref, rest2_ref, near_ref, rest_ref, side_ref, out_ref, window,
+    current,
+):
+    core = flag_ref[0]
+    reach = dilations[2]
+    rows, cols, channels = out_ref.shape
+    rest = cols - reach
+    dst = place(core, rest, 0)
+    current[:, pl.ds(dst, reach), :] = near2_ref[...]
+    window[:, pl.ds(pl.multiple_of(dst + reach, lane_pad), reach), :] = near_ref[...]
+    dst = place(core, 0, reach)
+    current[:, pl.ds(dst, rest), :] = rest2_ref[...]
+    window[:, pl.ds(pl.multiple_of(dst + reach, lane_pad), rest), :] = rest_ref[...]
+    window[:, pl.ds(place(core, reach + cols, 0), reach), :] = side_ref[...]
+    window[:, pl.ds(place(core, 0, reach + cols), reach), :] = jnp.zeros(
+        (rows, reach, channels), window.dtype
+    )
+    stacked = jnp.concatenate(
+        [
+            window[:, b * reach : b * reach + cols, :].reshape(rows * cols, channels)
+            for b in range(3)
+        ],
+        axis=1,
+    )
+    response = jnp.dot(
+        stacked, w_ref[...].reshape(3 * channels, channels), preferred_element_type=jnp.float32
+    )
+    out_ref[...] = update(
+        current[...].reshape(rows * cols, channels), response, scale_ref[5:6, :]
+    ).reshape(rows, cols, channels)
+
+
+def by_halves(context_map, norm_gains, conv_biases, conv_weights):
+    rows, cols, channels = context_map.shape
+    kind = context_map.dtype
+    size = lax.axis_size("row")
+    group = size // 2
+    half = rows // 2
+    step, reach = dilations[1], dilations[2]
+    strip = step + reach
+    mid = cols - 2 * strip
+    pad = lane_pad
+    wide = strip + pad
+    core, row = lax.axis_index("col"), lax.axis_index("row")
+    upper_half = row < group
+    flags = jnp.stack(
+        [core, row == group - 1, row == group, jnp.where(upper_half, 2, 0)]
+    ).astype(jnp.int32)
+    swap = [(0, 1), (1, 0)]
+    partner = [(i, (i + group) % size) for i in range(size)]
+    down = [(i, i + 1) for i in range(size - 1)]
+    up = [(j, i) for i, j in down]
+    within_down = [(i, j) for i, j in down if j != group]
+    within_up = [(j, i) for i, j in within_down]
+
+    far_wide_at, near_wide_at = (0, cols - wide), (cols - wide, 0)
+    span, span_at = cols - wide, (wide, 0)
+    parts = (
+        (None, 0, 0, rows, far_wide_at, wide, 0, 0),
+        (None, 0, 0, rows, near_wide_at, wide, 1, 0),
+        (None, 0, 0, rows, (strip - pad, strip - pad), mid + 2 * pad, 2, 0),
+        (None, 0, half, half, far_wide_at, wide, 3, 0),
+        (None, 0, 0, half, far_wide_at, wide, 4, 0),
+        (None, 0, half, half, span_at, span, 5, 0),
+        (None, 0, 0, half, span_at, span, 6, 0),
+        ((1, 1), 0, half, half, span_at, span, 7, 0),
+        ((1, 0), 0, 0, half, span_at, span, 7, 0),
+    )
+    (
+        far_x, near_x, mid_x, far_low, far_high, low, high, middle
+    ) = copies(flags, (context_map,), parts)
+    above_far = lax.ppermute(far_low, "row", down)
+    below_far = lax.ppermute(far_high, "row", up)
+    above = lax.ppermute(low, "row", within_down)
+    below = lax.ppermute(high, "row", within_up)
+    middle = lax.ppermute(middle, "row", [(group - 1, group), (group, group - 1)])
+
+    tail = conv_weights.shape[2:]
+    scales, first_w, second_w, last_w = kernel_call(
+        hold_kernel,
+        (
+            jax.ShapeDtypeStruct((2 * norm_gains.shape[0], channels), jnp.float32),
+            jax.ShapeDtypeStruct((3,) + tail, kind),
+            jax.ShapeDtypeStruct((2,) + tail, kind),
+            jax.ShapeDtypeStruct(tail, kind),
+        ),
+        [smem_spec()] + [vmem_spec()] * 3,
+        [],
+    )(flags, norm_gains, conv_biases, conv_weights)
+    params = (scales, first_w)
+    far_body, far_edge = (pad, 0), (0, wide)
+    far_segments = (
+        (None, 0, 0, half, rows, (0, 0), far_body, wide),
+        (None, 1, 0, 0, half, (0, 0), far_body, wide),
+        (None, 2, 0, half + rows, half, (0, 0), far_body, wide),
+        (None, None, 0, 0, 2 * rows, (0, 0), far_edge, pad),
+    )
+    far1, far_n = first_layer(
+        flags, params, (far_x, above_far, below_far), far_segments, (0, pad), strip
+    )
+    cross_far = lax.ppermute(far_n, "row", partner)
+
+    near_end, span_end = (wide - pad, 0), (span - pad, 0)
+    (rim,) = copies(
+        flags,
+        (near_x, above, below, middle),
+        (
+            ((2, 0), 1, 0, half, span_end, pad, 0, 0),
+            ((2, 1), 3, 0, half, span_end, pad, 0, 0),
+            (None, 0, 0, rows, near_end, pad, 0, half),
+            ((1, 0), 2, 0, half, span_end, pad, 0, half + rows),
+            ((1, 1), 3, 0, half, span_end, pad, 0, half + rows),
+        ),
+    )
+    rim = lax.ppermute(rim, "col", swap)
+    near_body, near_span = (0, pad), (span - wide, 0)
+    near_segments = (
+        (None, 0, 0, half, rows, (0, 0), near_body, wide),
+        ((2, 0), 1, 0, 0, half, near_span, near_body, wide),
+        ((2, 1), 4, 0, 0, half, near_span, near_body, wide),
+        ((1, 0), 2, 0, half + rows, half, near_span, near_body, wide),
+        ((1, 1), 4, 0, half + rows, half, near_span, near_body, wide),
+        (None, 3, 0, 0, 2 * rows, (0, 0), (wide, 0), pad),
+    )
+    near1, near_n = first_layer(
+        flags, params, (near_x, above, below, rim, middle), near_segments, (pad, 0), strip
+    )
+    cross_near = lax.ppermute(near_n, "row", partner)
+    two = 2 * pad
+    far_side, rest_side = ((wide - two, 0), (0, mid)), ((0, span - mid), (two, 0))
+    mid_segments = (
+        (None, 0, 0, half, rows, (0, 0), (0, 0), mid + two),
+        (None, 1, 0, 0, half, *far_side, two),
+        (None, 2, 0, half + rows, half, *far_side, two),
+        ((2, 0), 3, 0, 0, half, *rest_side, mid),
+        ((2, 1), 5, 0, 0, half, *rest_side, mid),
+        ((1, 0), 4, 0, half + rows, half, *rest_side, mid),
+        ((1, 1), 5, 0, half + rows, half, *rest_side, mid),
+    )
+    mid1, mid_n = first_layer(
+        flags,
+        params,
+        (
+            mid_x, above_far, below_far, above, below, middle
+        ),
+        mid_segments,
+        (pad, pad),
+        mid,
+    )
+    cross_mid = lax.ppermute(mid_n, "row", partner)
+
+    (near_side,) = copies(
+        flags, (near_n, cross_far), ((None, 0, 0, rows, (strip - reach, 0), reach, 0, 0),)
+    )
+    near_side = lax.ppermute(near_side, "col", swap)
+    def plain(body, weights, out, operands, scratch):
+        return kernel_call(
+            body,
+            out,
+            [smem_spec()] + [vmem_spec()] * (len(operands) + 2),
+            [pltpu.VMEM((rows, width, channels), kind) for width in scratch],
+        )(flags, scales, weights, *operands)
+
+    def strip_shape(width, kind=kind):
+        return jax.ShapeDtypeStruct((rows, width, channels), kind)
+
+    acc, x1 = plain(
+        partial_kernel,
+        second_w,
+        (strip_shape(cols, jnp.float32), strip_shape(cols)),
+        (near_n, mid_n, far_n, cross_far, near_side, near1, mid1, far1),
+        (cols + 2 * step, cols + 2 * step),
+    )
+    cross_near, acc = lax.optimization_barrier((cross_near, acc))
+    (cross_side,) = copies(
+        flags, (cross_near,), ((None, 0, 0, rows, (strip - step, 0), step, 0, 0),)
+    )
+    cross_side = lax.ppermute(cross_side, "col", swap)
+    near2, near_n = plain(
+        near_kernel,
+        second_w,
+        (strip_shape(reach), strip_shape(reach)),
+        (cross_near, cross_side, acc, x1),
+        (reach + 2 * step,),
+    )
+    near_n, cross_mid = lax.optimization_barrier((near_n, cross_mid))
+    last_side = lax.ppermute(near_n, "col", swap)
+    rest2, rest_n = plain(
+        rest_kernel,
+        second_w,
+        (strip_shape(cols - reach), strip_shape(cols - reach)),
+        (cross_mid, cross_near, acc, x1),
+        (cols - reach + 2 * step,),
+    )
+    return plain(
+        last_kernel,
+        last_w,
+        strip_shape(cols),
+        (near2, rest2, near_n, rest_n, last_side),
+        (cols + 2 * reach, cols),
+    )
+
+
+def shards(context_map, *params):
+    rows, cols, _ = context_map.shape
+    map_rows = lax.axis_size("row") * rows
+    strip = dilations[1] + dilations[2]
+    if (
+        map_rows == 2 * dilations[1]
+        and map_rows <= dilations[2]
+        and rows == 2 * dilations[0]
+        and dilations[1] % rows == 0
+        and lax.axis_size("col") == 2
+        and cols >= 2 * strip + 3 * lane_pad
+        and cols % lane_pad == 0
+    ):
+        return by_halves(context_map, *params)
+    return by_classes(context_map, *params)
+
+
 def solution(mesh):
     return jax.shard_map(
         shards,

time: 128 us -> 77.8 us (0.61); the launches traced: 125 us -> 77.5 us
  blocking collectives: 59.9 us -> 0 us
  starting transfers between devices: 19.5 us -> 40.9 us
  Pallas kernels: 0 us -> 19.9 us
  other arithmetic: 11.4 us -> 0.08 us
  waiting for transfers between devices: 21.9 us -> 11.8 us
  matrix products: 8.03 us -> 0 us
    all_to_all x2 -> x0, blocking collectives: 59.9 us -> none  [the longest x1 31.8 us: shards(): lax.all_to_all(outgoing, 'row', split_axis=0, concat_axis=0, tiled=True)]
    ppermute x8 -> x12, starting transfers between devices: 19.5 us -> 40.9 us  [the longest x1 18.1 us: by_halves(): near_side = lax.ppermute(near_side, 'col', swap)]
    pallas_call x0 -> x12, Pallas kernels: none -> 19.9 us  [the longest x3 8.56 us: first_layer(): kernel_call(functools.partial(first_layer_kernel, segments, out_at, rows,...]
    ppermute x8 -> x12, waiting for transfers between devices: 21.9 us -> 11.8 us  [the longest x1 6.69 us: by_halves(): cross_mid = lax.ppermute(mid_n, 'row', partner)]
    dot_general x3 -> x0, matrix products: 8.03 us -> none  [convolve(): jnp.dot(stacked, kernel.reshape(9 * channels, kernel.shape[3]), preferred...]
    reduce_sum x5 -> x0, other arithmetic: 5.16 us -> none  [the longest x3 3.16 us: normalize(): variance = jnp.mean(centred * centred, axis=-1, keepdims=True)]
    unnamed x9 -> x0, other arithmetic: 2.59 us -> none
    unnamed x22 -> x8, local copies, waits for them, and re-layouts: 2.39 us -> 4.59 us
  transfers between devices with their start and end apart: 8 -> 12, of which waited for: 4 -> 4; matrix products, arithmetic and copies ran while one was open for 1% -> 0% of each run, Pallas kernels for 0% -> 21%
where the time goes in v4:
time: 77.8 us; the launch traced here: 77.5 us
  starting transfers between devices  40.9 us (53%)
  Pallas kernels  19.9 us (26%)
  waiting for transfers between devices  11.8 us (15%)
  local copies, waits for them, and re-layouts  4.59 us (6%)
    ppermute x1, starting transfers between devices, by_halves(): near_side = lax.ppermute(near_side, 'col', swap)  18.1 us
    pallas_call x3, Pallas kernels, first_layer(): kernel_call(functools.partial(first_layer_kernel, segments, out_at, rows,...  8.56 us
    pallas_call x4, Pallas kernels, plain(): kernel_call(body, out, [smem_spec()] + [vmem_spec()] * (len(operands) + 2...  8.21 us
    ppermute x1, waiting for transfers between devices, by_halves(): cross_mid = lax.ppermute(mid_n, 'row', partner)  6.69 us
    ppermute x1, starting transfers between devices, by_halves(): cross_far = lax.ppermute(far_n, 'row', partner)  5.56 us
    unnamed x8, local copies, waits for them, and re-layouts  4.59 us
    ppermute x1, starting transfers between devices, by_halves(): above = lax.ppermute(low, 'row', within_down)  4 us
    ppermute x1, starting transfers between devices, by_halves(): above_far = lax.ppermute(far_low, 'row', down)  3.96 us
  transfers between devices with their start and end apart: 12, of which 4 were waited for; matrix products, arithmetic and copies ran while one was open for 0% of the time, Pallas kernels for 21%

profile of v4, /device:TPU:1, one launch (start us, length us, event | category | flops | bytes accessed | tf_op | source)
XLA Modules:
  0.0 77.5 jit_solution(12829119534168641138)
XLA Ops:
  0.0 0.1 pad_add_fusion.flag_ref
  0.1 0.0 copy-start.1
  0.1 1.2 %copy-done.1 = bf16[8,256,256]{2,1,0:T(8,128)(2,1)S(1)} copy-done((bf16[8,256,256]{2,1,0:T(8,128)(2,1)S(1)}, bf16[8,256,256]{2,1,0:T(8,128)(2,1)}, u32[]{:S(2)}) %copy-start.1) | copy-done | bytes 1048600
  1.3 0.7 shard_map.47
  2.0 4.0 %collective-permute-start.5 = (bf16[4,112,256]{2,1,0:T(8,128)(2,1)S(1)}, bf16[4,112,256]{2,1,0:T(8,128)(2,1)S(1)}, u32[]{:S(2)}, u32[]{:S(2)}) collective-permute-start(bf16[4,112,256]{2,1,0:T(8,128)(2,1)S(1)} %get-tuple-element.43), channel_id=1, source_target_pairs={{0,2},{2,4},{4,6},{6,8},{8,10},{10,12},{12,14},{1,3},{3,5},{5,7},{... | collective-permute-start | bytes 688136 | tf_op jit(solution)/shard_map/ppermute | solution.py:393
  6.0 1.3 %collective-permute-start.6 = (bf16[4,112,256]{2,1,0:T(8,128)(2,1)S(1)}, bf16[4,112,256]{2,1,0:T(8,128)(2,1)S(1)}, u32[]{:S(2)}, u32[]{:S(2)}) collective-permute-start(bf16[4,112,256]{2,1,0:T(8,128)(2,1)S(1)} %get-tuple-element.44), channel_id=1, source_target_pairs={{2,0},{4,2},{6,4},{8,6},{10,8},{12,10},{14,12},{3,1},{5,3},{7,5},{... | collective-permute-start | bytes 688136 | tf_op jit(solution)/shard_map/ppermute | solution.py:394
  7.3 4.0 %collective-permute-start = (bf16[4,144,256]{2,1,0:T(8,128)(2,1)S(1)}, bf16[4,144,256]{2,1,0:T(8,128)(2,1)S(1)}, u32[]{:S(2)}, u32[]{:S(2)}) collective-permute-start(bf16[4,144,256]{2,1,0:T(8,128)(2,1)S(1)} %get-tuple-element.38), channel_id=1, source_target_pairs={{0,2},{2,4},{4,6},{8,10},{10,12},{12,14},{1,3},{3,5},{5,7},{9,11},... | collective-permute-start | bytes 884744 | tf_op jit(solution)/shard_map/ppermute | solution.py:395
  11.3 1.3 %collective-permute-start.1 = (bf16[4,144,256]{2,1,0:T(8,128)(2,1)S(1)}, bf16[4,144,256]{2,1,0:T(8,128)(2,1)S(1)}, u32[]{:S(2)}, u32[]{:S(2)}) collective-permute-start(bf16[4,144,256]{2,1,0:T(8,128)(2,1)S(1)} %get-tuple-element.39), channel_id=1, source_target_pairs={{2,0},{4,2},{6,4},{10,8},{12,10},{14,12},{3,1},{5,3},{7,5},{11,9},... | collective-permute-start | bytes 884744 | tf_op jit(solution)/shard_map/ppermute | solution.py:396
  12.6 0.7 collective-permute-start.2
  13.3 0.0 copy-start
  13.3 2.0 %copy-done = bf16[3,3,3,256,256]{4,3,2,1,0:T(8,128)(2,1)S(1)} copy-done((bf16[3,3,3,256,256]{4,3,2,1,0:T(8,128)(2,1)S(1)}, bf16[3,3,3,256,256]{4,3,2,1,0:T(8,128)(2,1)}, u32[]{:S(2)}) %copy-start) | copy-done | bytes 3538968
  15.3 0.0 copy-start.2
  15.3 0.7 copy-done.2
  16.0 0.0 copy-start.3
  16.0 0.7 copy-done.3
  16.7 0.7 shard_map.46
  17.4 0.0 collective-permute-done.5.rest_1_
  17.4 0.0 collective-permute-done.6.rest_2_
  17.4 2.5 %shard_map.51 = (bf16[8,96,256]{2,1,0:T(8,128)(2,1)S(1)}, bf16[8,96,256]{2,1,0:T(8,128)(2,1)S(1)}) custom-call(s32[4]{0:T(128)S(1)} %pad_add_fusion.flag_ref, f32[6,256]{1,0:T(8,128)S(1)} %get-tuple-element.33.scale_ref, bf16[3,3,256,256]{3,2,1,0:T(8,128)(2,1)S(1)} %get-tuple-element.36.w_ref, bf16[8,112,256]{2,1,0:T(8,128)(2,1)S(1)} %get-tuple-element.46.rest_0_, ...), custom_call_target="tpu_custom_call" | custom-call | flops 1 | bytes 1 | tf_op jit(solution)/shard_map/pallas_call | solution.py:214
  19.9 5.6 %collective-permute-start.7 = (bf16[8,96,256]{2,1,0:T(8,128)(2,1)S(1)}, bf16[8,96,256]{2,1,0:T(8,128)(2,1)S(1)}, u32[]{:S(2)}, u32[]{:S(2)}) collective-permute-start(bf16[8,96,256]{2,1,0:T(8,128)(2,1)S(1)} %get-tuple-element.47.far_ref), channel_id=1, source_target_pairs={{0,8},{2,10},{4,12},{6,14},{8,0},{10,2},{12,4},{14,6},{1,9},{3,11}... | collective-permute-start | bytes 1179656 | tf_op jit(solution)/shard_map/ppermute | solution.py:422
  25.5 2.8 %collective-permute-done.refs_1_.rest_1_.rest_3_ = bf16[4,144,256]{2,1,0:T(8,128)(2,1)S(1)} collective-permute-done((bf16[4,144,256]{2,1,0:T(8,128)(2,1)S(1)}, bf16[4,144,256]{2,1,0:T(8,128)(2,1)S(1)}, u32[]{:S(2)}, u32[]{:S(2)}) %collective-permute-start) | collective-permute-done | bytes 294944 | tf_op jit(solution)/shard_map/ppermute | solution.py:395
  28.3 0.0 collective-permute-done.1.refs_2_.rest_2_.rest_4_
  28.3 0.0 collective-permute-done.2.refs_3_.rest_4_.rest_5_
  28.3 0.6 shard_map.48
  28.9 2.0 %collective-permute-start.3 = (bf16[16,16,256]{2,1,0:T(8,128)(2,1)S(1)}, bf16[16,16,256]{2,1,0:T(8,128)(2,1)S(1)}, u32[]{:S(2)}, u32[]{:S(2)}) collective-permute-start(bf16[16,16,256]{2,1,0:T(8,128)(2,1)S(1)} %shard_map.48), channel_id=1, source_target_pairs={{0,1},{1,0},{2,3},{3,2},{4,5},{5,4},{6,7},{7,6},{8,9},{9,8},{10,11... | collective-permute-start | bytes 393224 | tf_op jit(solution)/shard_map/ppermute | solution.py:436
  30.8 1.0 %collective-permute-done.3.rest_3_ = bf16[16,16,256]{2,1,0:T(8,128)(2,1)S(1)} collective-permute-done((bf16[16,16,256]{2,1,0:T(8,128)(2,1)S(1)}, bf16[16,16,256]{2,1,0:T(8,128)(2,1)S(1)}, u32[]{:S(2)}, u32[]{:S(2)}) %collective-permute-start.3) | collective-permute-done | bytes 131104 | tf_op jit(solution)/shard_map/ppermute | solution.py:436
  31.8 3.2 %shard_map.49 = (bf16[8,96,256]{2,1,0:T(8,128)(2,1)S(1)}, bf16[8,96,256]{2,1,0:T(8,128)(2,1)S(1)}) custom-call(s32[4]{0:T(128)S(1)} %pad_add_fusion.flag_ref, f32[6,256]{1,0:T(8,128)S(1)} %get-tuple-element.33.scale_ref, bf16[3,3,256,256]{3,2,1,0:T(8,128)(2,1)S(1)} %get-tuple-element.36.w_ref, bf16[8,112,256]{2,1,0:T(8,128)(2,1)S(1)} %get-tuple-element.37.refs_0_.rest_0_, ...), custom_call_target="tpu_custom_call" | custom-call | flops 1 | bytes 1 | tf_op jit(solution)/shard_map/pallas_call | solution.py:214
  35.1 3.4 %collective-permute-start.4 = (bf16[8,96,256]{2,1,0:T(8,128)(2,1)S(1)}, bf16[8,96,256]{2,1,0:T(8,128)(2,1)S(1)}, u32[]{:S(2)}, u32[]{:S(2)}) collective-permute-start(bf16[8,96,256]{2,1,0:T(8,128)(2,1)S(1)} %get-tuple-element.41.refs_0_.near_ref), channel_id=1, source_target_pairs={{0,8},{2,10},{4,12},{6,14},{8,0},{10,2},{12,4},{14,6},{1,9},{3,11}... | collective-permute-start | bytes 1179656 | tf_op jit(solution)/shard_map/ppermute | solution.py:449
  38.5 0.0 collective-permute-done.7.refs_1_.cfar_ref
  38.5 0.6 shard_map.52
  39.0 18.1 %collective-permute-start.8 = (bf16[8,64,256]{2,1,0:T(8,128)(2,1)S(1)}, bf16[8,64,256]{2,1,0:T(8,128)(2,1)S(1)}, u32[]{:S(2)}, u32[]{:S(2)}) collective-permute-start(bf16[8,64,256]{2,1,0:T(8,128)(2,1)S(1)} %shard_map.52), channel_id=1, source_target_pairs={{0,1},{1,0},{2,3},{3,2},{4,5},{5,4},{6,7},{7,6},{8,9},{9,8},{10,11... | collective-permute-start | bytes 786440 | tf_op jit(solution)/shard_map/ppermute | solution.py:476
  57.2 2.8 %shard_map.50 = (bf16[8,64,256]{2,1,0:T(8,128)(2,1)S(1)}, bf16[8,64,256]{2,1,0:T(8,128)(2,1)S(1)}) custom-call(s32[4]{0:T(128)S(1)} %pad_add_fusion.flag_ref, f32[6,256]{1,0:T(8,128)S(1)} %get-tuple-element.33.scale_ref, bf16[3,3,256,256]{3,2,1,0:T(8,128)(2,1)S(1)} %get-tuple-element.36.w_ref, bf16[8,96,256]{2,1,0:T(8,128)(2,1)S(1)} %get-tuple-element.42.rest_0_, ...), custom_call_target="tpu_custom_call" | custom-call | flops 1 | bytes 1 | tf_op jit(solution)/shard_map/pallas_call | solution.py:214
  60.0 0.1 collective-permute-start.10
  60.1 0.0 collective-permute-done.8.side_ref
  60.1 2.5 %shard_map.53 = (f32[8,256,256]{2,1,0:T(8,128)S(1)}, bf16[8,256,256]{2,1,0:T(8,128)(2,1)S(1)}) custom-call(s32[4]{0:T(128)S(1)} %pad_add_fusion.flag_ref, f32[6,256]{1,0:T(8,128)S(1)} %get-tuple-element.33.scale_ref, bf16[2,3,256,256]{3,2,1,0:T(8,128)(2,1)S(1)} %get-tuple-element.35.w_ref, bf16[8,96,256]{2,1,0:T(8,128)(2,1)S(1)} %get-tuple-element.41.refs_0_.near_ref, ...), custom_call_target="tpu_custom_call" | custom-call | flops 1 | bytes 1 | tf_op jit(solution)/shard_map/pallas_call | solution.py:478
  62.6 0.0 collective-permute-done.4.refs_0_.cnear_ref
  62.6 0.6 shard_map.54
  63.2 0.1 collective-permute-start.9
  63.2 1.3 %collective-permute-done.9.side_ref = bf16[8,32,256]{2,1,0:T(8,128)(2,1)S(1)} collective-permute-done((bf16[8,32,256]{2,1,0:T(8,128)(2,1)S(1)}, bf16[8,32,256]{2,1,0:T(8,128)(2,1)S(1)}, u32[]{:S(2)}, u32[]{:S(2)}) %collective-permute-start.9) | collective-permute-done | bytes 131104 | tf_op jit(solution)/shard_map/ppermute | solution.py:499
  64.6 1.1 %shard_map.55 = (bf16[8,64,256]{2,1,0:T(8,128)(2,1)S(1)}, bf16[8,64,256]{2,1,0:T(8,128)(2,1)S(1)}) custom-call(s32[4]{0:T(128)S(1)} %pad_add_fusion.flag_ref, f32[6,256]{1,0:T(8,128)S(1)} %get-tuple-element.33.scale_ref, bf16[2,3,256,256]{3,2,1,0:T(8,128)(2,1)S(1)} %get-tuple-element.35.w_ref, ...), custom_call_target="tpu_custom_call" | custom-call | flops 1 | bytes 1 | tf_op jit(solution)/shard_map/pallas_call | solution.py:478
  65.7 6.7 %collective-permute-done.10.cmid_ref = bf16[8,64,256]{2,1,0:T(8,128)(2,1)S(1)} collective-permute-done((bf16[8,64,256]{2,1,0:T(8,128)(2,1)S(1)}, bf16[8,64,256]{2,1,0:T(8,128)(2,1)S(1)}, u32[]{:S(2)}, u32[]{:S(2)}) %collective-permute-start.10) | collective-permute-done | bytes 262176 | tf_op jit(solution)/shard_map/ppermute | solution.py:471
  72.4 0.4 collective-permute-start.11
  72.8 1.9 %shard_map.56 = (bf16[8,192,256]{2,1,0:T(8,128)(2,1)S(1)}, bf16[8,192,256]{2,1,0:T(8,128)(2,1)S(1)}) custom-call(s32[4]{0:T(128)S(1)} %pad_add_fusion.flag_ref, f32[6,256]{1,0:T(8,128)S(1)} %get-tuple-element.33.scale_ref, bf16[2,3,256,256]{3,2,1,0:T(8,128)(2,1)S(1)} %get-tuple-element.35.w_ref, bf16[8,64,256]{2,1,0:T(8,128)(2,1)S(1)} %collective-permute-done.10.cmid_ref, ...), custom_call_target="tpu_custom_call" | custom-call | flops 1 | bytes 1 | tf_op jit(solution)/shard_map/pallas_call | solution.py:478
  74.8 0.0 collective-permute-done.11.side_ref
  74.8 2.7 %shard_map.57 = bf16[8,256,256]{2,1,0:T(8,128)(2,1)} custom-call(s32[4]{0:T(128)S(1)} %pad_add_fusion.flag_ref, f32[6,256]{1,0:T(8,128)S(1)} %get-tuple-element.33.scale_ref, bf16[3,256,256]{2,1,0:T(8,128)(2,1)S(1)} %get-tuple-element.34.w_ref, bf16[8,64,256]{2,1,0:T(8,128)(2,1)S(1)} %get-tuple-element.55.near2_ref, ...), custom_call_target="tpu_custom_call" | custom-call | flops 1 | bytes 1 | tf_op jit(solution)/shard_map/pallas_call | solution.py:478
Async XLA Ops:
  0.1 1.2 %copy-start.1 = (bf16[8,256,256]{2,1,0:T(8,128)(2,1)S(1)}, bf16[8,256,256]{2,1,0:T(8,128)(2,1)}, u32[]{:S(2)}) copy-start(bf16[8,256,256]{2,1,0:T(8,128)(2,1)} %refs_0_.1) | copy-start | bytes 3145732
  2.0 15.3 %collective-permute-start.5 = (bf16[4,112,256]{2,1,0:T(8,128)(2,1)S(1)}, bf16[4,112,256]{2,1,0:T(8,128)(2,1)S(1)}, u32[]{:S(2)}, u32[]{:S(2)}) collective-permute-start(bf16[4,112,256]{2,1,0:T(8,128)(2,1)S(1)} %get-tuple-element.43), channel_id=1, source_target_pairs={{0,2},{2,4},{4,6},{6,8},{8,10},{10,12},{12,14},{1,3},{3,5},{5,7},{... | collective-permute-start | bytes 688136 | tf_op jit(solution)/shard_map/ppermute | solution.py:393
  6.0 11.4 %collective-permute-start.6 = (bf16[4,112,256]{2,1,0:T(8,128)(2,1)S(1)}, bf16[4,112,256]{2,1,0:T(8,128)(2,1)S(1)}, u32[]{:S(2)}, u32[]{:S(2)}) collective-permute-start(bf16[4,112,256]{2,1,0:T(8,128)(2,1)S(1)} %get-tuple-element.44), channel_id=1, source_target_pairs={{2,0},{4,2},{6,4},{8,6},{10,8},{12,10},{14,12},{3,1},{5,3},{7,5},{... | collective-permute-start | bytes 688136 | tf_op jit(solution)/shard_map/ppermute | solution.py:394
  7.3 21.0 %collective-permute-start = (bf16[4,144,256]{2,1,0:T(8,128)(2,1)S(1)}, bf16[4,144,256]{2,1,0:T(8,128)(2,1)S(1)}, u32[]{:S(2)}, u32[]{:S(2)}) collective-permute-start(bf16[4,144,256]{2,1,0:T(8,128)(2,1)S(1)} %get-tuple-element.38), channel_id=1, source_target_pairs={{0,2},{2,4},{4,6},{8,10},{10,12},{12,14},{1,3},{3,5},{5,7},{9,11},... | collective-permute-start | bytes 884744 | tf_op jit(solution)/shard_map/ppermute | solution.py:395
  11.3 17.0 %collective-permute-start.1 = (bf16[4,144,256]{2,1,0:T(8,128)(2,1)S(1)}, bf16[4,144,256]{2,1,0:T(8,128)(2,1)S(1)}, u32[]{:S(2)}, u32[]{:S(2)}) collective-permute-start(bf16[4,144,256]{2,1,0:T(8,128)(2,1)S(1)} %get-tuple-element.39), channel_id=1, source_target_pairs={{2,0},{4,2},{6,4},{10,8},{12,10},{14,12},{3,1},{5,3},{7,5},{11,9},... | collective-permute-start | bytes 884744 | tf_op jit(solution)/shard_map/ppermute | solution.py:396
  12.6 15.7 %collective-permute-start.2 = (bf16[4,144,256]{2,1,0:T(8,128)(2,1)S(1)}, bf16[4,144,256]{2,1,0:T(8,128)(2,1)S(1)}, u32[]{:S(2)}, u32[]{:S(2)}) collective-permute-start(bf16[4,144,256]{2,1,0:T(8,128)(2,1)S(1)} %get-tuple-element.40), channel_id=1, source_target_pairs={{6,8},{8,6},{7,9},{9,7},{22,24},{24,22},{23,25},{25,23}} | collective-permute-start | bytes 884744 | tf_op jit(solution)/shard_map/ppermute | solution.py:397
  13.3 2.0 %copy-start = (bf16[3,3,3,256,256]{4,3,2,1,0:T(8,128)(2,1)S(1)}, bf16[3,3,3,256,256]{4,3,2,1,0:T(8,128)(2,1)}, u32[]{:S(2)}) copy-start(bf16[3,3,3,256,256]{4,3,2,1,0:T(8,128)(2,1)} %w_ref.1) | copy-start | bytes 10616836
  15.3 0.7 copy-start.2
  16.0 0.7 copy-start.3
  19.9 18.5 %collective-permute-start.7 = (bf16[8,96,256]{2,1,0:T(8,128)(2,1)S(1)}, bf16[8,96,256]{2,1,0:T(8,128)(2,1)S(1)}, u32[]{:S(2)}, u32[]{:S(2)}) collective-permute-start(bf16[8,96,256]{2,1,0:T(8,128)(2,1)S(1)} %get-tuple-element.47.far_ref), channel_id=1, source_target_pairs={{0,8},{2,10},{4,12},{6,14},{8,0},{10,2},{12,4},{14,6},{1,9},{3,11}... | collective-permute-start | bytes 1179656 | tf_op jit(solution)/shard_map/ppermute | solution.py:422
  28.9 3.0 %collective-permute-start.3 = (bf16[16,16,256]{2,1,0:T(8,128)(2,1)S(1)}, bf16[16,16,256]{2,1,0:T(8,128)(2,1)S(1)}, u32[]{:S(2)}, u32[]{:S(2)}) collective-permute-start(bf16[16,16,256]{2,1,0:T(8,128)(2,1)S(1)} %shard_map.48), channel_id=1, source_target_pairs={{0,1},{1,0},{2,3},{3,2},{4,5},{5,4},{6,7},{7,6},{8,9},{9,8},{10,11... | collective-permute-start | bytes 393224 | tf_op jit(solution)/shard_map/ppermute | solution.py:436
  35.1 27.5 %collective-permute-start.4 = (bf16[8,96,256]{2,1,0:T(8,128)(2,1)S(1)}, bf16[8,96,256]{2,1,0:T(8,128)(2,1)S(1)}, u32[]{:S(2)}, u32[]{:S(2)}) collective-permute-start(bf16[8,96,256]{2,1,0:T(8,128)(2,1)S(1)} %get-tuple-element.41.refs_0_.near_ref), channel_id=1, source_target_pairs={{0,8},{2,10},{4,12},{6,14},{8,0},{10,2},{12,4},{14,6},{1,9},{3,11}... | collective-permute-start | bytes 1179656 | tf_op jit(solution)/shard_map/ppermute | solution.py:449
  39.0 21.1 %collective-permute-start.8 = (bf16[8,64,256]{2,1,0:T(8,128)(2,1)S(1)}, bf16[8,64,256]{2,1,0:T(8,128)(2,1)S(1)}, u32[]{:S(2)}, u32[]{:S(2)}) collective-permute-start(bf16[8,64,256]{2,1,0:T(8,128)(2,1)S(1)} %shard_map.52), channel_id=1, source_target_pairs={{0,1},{1,0},{2,3},{3,2},{4,5},{5,4},{6,7},{7,6},{8,9},{9,8},{10,11... | collective-permute-start | bytes 786440 | tf_op jit(solution)/shard_map/ppermute | solution.py:476
  60.0 12.4 %collective-permute-start.10 = (bf16[8,64,256]{2,1,0:T(8,128)(2,1)S(1)}, bf16[8,64,256]{2,1,0:T(8,128)(2,1)S(1)}, u32[]{:S(2)}, u32[]{:S(2)}) collective-permute-start(bf16[8,64,256]{2,1,0:T(8,128)(2,1)S(1)} %get-tuple-element.45.mid_ref), channel_id=1, source_target_pairs={{0,8},{2,10},{4,12},{6,14},{8,0},{10,2},{12,4},{14,6},{1,9},{3,11}... | collective-permute-start | bytes 786440 | tf_op jit(solution)/shard_map/ppermute | solution.py:471
  63.2 1.4 %collective-permute-start.9 = (bf16[8,32,256]{2,1,0:T(8,128)(2,1)S(1)}, bf16[8,32,256]{2,1,0:T(8,128)(2,1)S(1)}, u32[]{:S(2)}, u32[]{:S(2)}) collective-permute-start(bf16[8,32,256]{2,1,0:T(8,128)(2,1)S(1)} %shard_map.54), channel_id=1, source_target_pairs={{0,1},{1,0},{2,3},{3,2},{4,5},{5,4},{6,7},{7,6},{8,9},{9,8},{10,11... | collective-permute-start | bytes 393224 | tf_op jit(solution)/shard_map/ppermute | solution.py:499
  72.4 2.4 %collective-permute-start.11 = (bf16[8,64,256]{2,1,0:T(8,128)(2,1)S(1)}, bf16[8,64,256]{2,1,0:T(8,128)(2,1)S(1)}, u32[]{:S(2)}, u32[]{:S(2)}) collective-permute-start(bf16[8,64,256]{2,1,0:T(8,128)(2,1)S(1)} %get-tuple-element.59.near_ref), channel_id=1, source_target_pairs={{0,1},{1,0},{2,3},{3,2},{4,5},{5,4},{6,7},{7,6},{8,9},{9,8},{10,11... | collective-permute-start | bytes 786440 | tf_op jit(solution)/shard_map/ppermute | solution.py:508

commit v5 on v4

--- a/solution.py
+++ b/solution.py
@@ -244,10 +244,7 @@
         own[:, inside, :] = normed[...]
         if normed is far_ref:
             other[:, inside, :] = cfar_ref[...]
-    spare = side_ref.shape[1] - step
-    own[:, pl.ds(place(core, step + cols, 0), step), :] = side_ref[
-        :, pl.ds(place(core, 0, spare), step), :
-    ]
+    own[:, pl.ds(place(core, step + cols, 0), step), :] = side_ref[...]
     own[:, pl.ds(place(core, 0, step + cols), step), :] = jnp.zeros(
         (rows, step, channels), own.dtype
     )
@@ -283,13 +280,15 @@
 
 
 def near_kernel(
-    flag_ref, scale_ref, w_ref, cnear_ref, side_ref, acc_ref, x1_ref, next_ref, normed_ref, window
+    flag_ref, scale_ref, w_ref, cnear_ref, rim_ref, side_ref, acc_ref, x1_ref, next_ref, normed_ref,
+    window,
 ):
     core = flag_ref[0]
     step, reach = dilations[1], dilations[2]
     near, cols = cnear_ref.shape[1], x1_ref.shape[1]
-    window[:, pl.ds(place(core, 0, step), near), :] = cnear_ref[...]
-    window[:, pl.ds(place(core, near, 0), step), :] = side_ref[...]
+    window[:, pl.ds(place(core, 0, 2 * step), near), :] = cnear_ref[...]
+    window[:, pl.ds(place(core, near, step), step), :] = rim_ref[...]
+    window[:, pl.ds(place(core, near + step, 0), step), :] = side_ref[...]
     at = pl.ds(place(core, cols - reach, 0), reach)
     next_ref[...], normed_ref[...] = second_layer(
         flag_ref, scale_ref, w_ref, window[...], acc_ref[:, at, :], x1_ref[:, at, :]
@@ -303,7 +302,7 @@
     step, reach = dilations[1], dilations[2]
     rows, mid, channels = cmid_ref.shape
     near, cols = cnear_ref.shape[1], x1_ref.shape[1]
-    width, far = cols - reach, cols - near - mid
+    width, far = cols - reach, cols - near - step - mid
     count = width + step - far - mid
     window[:, pl.ds(place(core, step + far + mid, 0), count), :] = cnear_ref[
         :, pl.ds(place(core, 0, near - count), count), :
@@ -446,7 +445,16 @@
     near1, near_n = first_layer(
         flags, params, (near_x, above, below, rim, middle), near_segments, (pad, 0), strip
     )
-    cross_near = lax.ppermute(near_n, "row", partner)
+    near_rim, near_rest = copies(
+        flags,
+        (near_n,),
+        (
+            (None, 0, 0, rows, (strip - step, 0), step, 0, 0),
+            (None, 0, 0, rows, (0, step), strip - step, 1, 0),
+        ),
+    )
+    cross_rim = lax.ppermute(near_rim, "row", partner)
+    cross_near = lax.ppermute(near_rest, "row", partner)
     two = 2 * pad
     far_side, rest_side = ((wide - two, 0), (0, mid)), ((0, span - mid), (two, 0))
     mid_segments = (
@@ -470,10 +478,8 @@
     )
     cross_mid = lax.ppermute(mid_n, "row", partner)
 
-    (near_side,) = copies(
-        flags, (near_n, cross_far), ((None, 0, 0, rows, (strip - reach, 0), reach, 0, 0),)
-    )
-    near_side = lax.ppermute(near_side, "col", swap)
+    near_rim, cross_far = lax.optimization_barrier((near_rim, cross_far))
+    near_side = lax.ppermute(near_rim, "col", swap)
     def plain(body, weights, out, operands, scratch):
         return kernel_call(
             body,
@@ -492,16 +498,12 @@
         (near_n, mid_n, far_n, cross_far, near_side, near1, mid1, far1),
         (cols + 2 * step, cols + 2 * step),
     )
-    cross_near, acc = lax.optimization_barrier((cross_near, acc))
-    (cross_side,) = copies(
-        flags, (cross_near,), ((None, 0, 0, rows, (strip - step, 0), step, 0, 0),)
-    )
-    cross_side = lax.ppermute(cross_side, "col", swap)
+    cross_side = lax.ppermute(cross_rim, "col", swap)
     near2, near_n = plain(
         near_kernel,
         second_w,
         (strip_shape(reach), strip_shape(reach)),
-        (cross_near, cross_side, acc, x1),
+        (cross_near, cross_rim, cross_side, acc, x1),
         (reach + 2 * step,),
     )
     near_n, cross_mid = lax.optimization_barrier((near_n, cross_mid))

time: 77.8 us -> 77.4 us (level)
  starting transfers between devices: 40.9 us -> 49 us
  waiting for transfers between devices: 11.8 us -> 3.8 us
    ppermute x1, waiting for transfers between devices: 6.69 us -> 0.01 us  [by_halves(): cross_mid = lax.ppermute(mid_n, 'row', partner)]
    ppermute x1, starting transfers between devices: 0.44 us -> 3.96 us  [by_halves(): last_side = lax.ppermute(near_n, 'col', swap)]
    ppermute x3 -> x4, starting transfers between devices: 21.6 us -> 24 us  [the longest x1 17.7 us: by_halves(): near_side = lax.ppermute(near_rim, 'col', swap)]
    ppermute x1, starting transfers between devices: 0.07 us -> 2.35 us  [by_halves(): cross_mid = lax.ppermute(mid_n, 'row', partner)]
    ppermute x3 -> x4, waiting for transfers between devices: 1.34 us -> 0.01 us  [the longest x1 0.01 us: by_halves(): near_side = lax.ppermute(near_rim, 'col', swap)]
    pallas_call x4 -> x3, Pallas kernels: 2.43 us -> 1.88 us  [copies(): kernel_call(functools.partial(copy_kernel, moves, len(arrays)), out, [sme...]
  transfers between devices with their start and end apart: 12 -> 13, of which waited for: 4 -> 2; matrix products, arithmetic and copies ran while one was open for 0% -> 0% of each run, Pallas kernels for 21% -> 21%
where the time goes in v5:
time: 77.4 us; the launch traced here: 77.1 us
  starting transfers between devices  49 us (63%)
  Pallas kernels  19.4 us (25%)
  local copies, waits for them, and re-layouts  4.59 us (6%)
  waiting for transfers between devices  3.8 us (5%)
    ppermute x1, starting transfers between devices, by_halves(): near_side = lax.ppermute(near_rim, 'col', swap)  17.7 us
    pallas_call x3, Pallas kernels, first_layer(): kernel_call(functools.partial(first_layer_kernel, segments, out_at, rows,...  8.56 us
    pallas_call x4, Pallas kernels, plain(): kernel_call(body, out, [smem_spec()] + [vmem_spec()] * (len(operands) + 2...  8.23 us
    ppermute x1, starting transfers between devices, by_halves(): cross_far = lax.ppermute(far_n, 'row', partner)  5.56 us
    unnamed x8, local copies, waits for them, and re-layouts  4.59 us
    ppermute x1, starting transfers between devices, by_halves(): above = lax.ppermute(low, 'row', within_down)  4 us
    ppermute x1, starting transfers between devices, by_halves(): above_far = lax.ppermute(far_low, 'row', down)  3.96 us
    ppermute x1, starting transfers between devices, by_halves(): last_side = lax.ppermute(near_n, 'col', swap)  3.96 us
  transfers between devices with their start and end apart: 13, of which 2 were waited for; matrix products, arithmetic and copies ran while one was open for 0% of the time, Pallas kernels for 21%

profile of v5, /device:TPU:1, one launch (start us, length us, event | category | flops | bytes accessed | tf_op | source)
XLA Modules:
  0.0 77.1 jit_solution(588225880493885493)
XLA Ops:
  0.0 0.1 pad_add_fusion.flag_ref
  0.1 0.0 copy-start.1
  0.1 1.2 %copy-done.1 = bf16[8,256,256]{2,1,0:T(8,128)(2,1)S(1)} copy-done((bf16[8,256,256]{2,1,0:T(8,128)(2,1)S(1)}, bf16[8,256,256]{2,1,0:T(8,128)(2,1)}, u32[]{:S(2)}) %copy-start.1) | copy-done | bytes 1048600
  1.3 0.7 shard_map.47
  2.0 4.0 %collective-permute-start.7 = (bf16[4,112,256]{2,1,0:T(8,128)(2,1)S(1)}, bf16[4,112,256]{2,1,0:T(8,128)(2,1)S(1)}, u32[]{:S(2)}, u32[]{:S(2)}) collective-permute-start(bf16[4,112,256]{2,1,0:T(8,128)(2,1)S(1)} %get-tuple-element.47), channel_id=1, source_target_pairs={{0,2},{2,4},{4,6},{6,8},{8,10},{10,12},{12,14},{1,3},{3,5},{5,7},{... | collective-permute-start | bytes 688136 | tf_op jit(solution)/shard_map/ppermute | solution.py:392
  6.0 1.3 %collective-permute-start.8 = (bf16[4,112,256]{2,1,0:T(8,128)(2,1)S(1)}, bf16[4,112,256]{2,1,0:T(8,128)(2,1)S(1)}, u32[]{:S(2)}, u32[]{:S(2)}) collective-permute-start(bf16[4,112,256]{2,1,0:T(8,128)(2,1)S(1)} %get-tuple-element.48), channel_id=1, source_target_pairs={{2,0},{4,2},{6,4},{8,6},{10,8},{12,10},{14,12},{3,1},{5,3},{7,5},{... | collective-permute-start | bytes 688136 | tf_op jit(solution)/shard_map/ppermute | solution.py:393
  7.3 4.0 %collective-permute-start = (bf16[4,144,256]{2,1,0:T(8,128)(2,1)S(1)}, bf16[4,144,256]{2,1,0:T(8,128)(2,1)S(1)}, u32[]{:S(2)}, u32[]{:S(2)}) collective-permute-start(bf16[4,144,256]{2,1,0:T(8,128)(2,1)S(1)} %get-tuple-element.40), channel_id=1, source_target_pairs={{0,2},{2,4},{4,6},{8,10},{10,12},{12,14},{1,3},{3,5},{5,7},{9,11},... | collective-permute-start | bytes 884744 | tf_op jit(solution)/shard_map/ppermute | solution.py:394
  11.3 1.3 %collective-permute-start.1 = (bf16[4,144,256]{2,1,0:T(8,128)(2,1)S(1)}, bf16[4,144,256]{2,1,0:T(8,128)(2,1)S(1)}, u32[]{:S(2)}, u32[]{:S(2)}) collective-permute-start(bf16[4,144,256]{2,1,0:T(8,128)(2,1)S(1)} %get-tuple-element.41), channel_id=1, source_target_pairs={{2,0},{4,2},{6,4},{10,8},{12,10},{14,12},{3,1},{5,3},{7,5},{11,9},... | collective-permute-start | bytes 884744 | tf_op jit(solution)/shard_map/ppermute | solution.py:395
  12.6 0.7 collective-permute-start.2
  13.3 0.0 copy-start
  13.3 2.0 %copy-done = bf16[3,3,3,256,256]{4,3,2,1,0:T(8,128)(2,1)S(1)} copy-done((bf16[3,3,3,256,256]{4,3,2,1,0:T(8,128)(2,1)S(1)}, bf16[3,3,3,256,256]{4,3,2,1,0:T(8,128)(2,1)}, u32[]{:S(2)}) %copy-start) | copy-done | bytes 3538968
  15.3 0.0 copy-start.2
  15.3 0.7 copy-done.2
  16.0 0.0 copy-start.3
  16.0 0.7 copy-done.3
  16.7 0.7 shard_map.46
  17.4 0.0 collective-permute-done.7.rest_1_
  17.4 0.0 collective-permute-done.8.rest_2_
  17.4 2.5 %shard_map.52 = (bf16[8,96,256]{2,1,0:T(8,128)(2,1)S(1)}, bf16[8,96,256]{2,1,0:T(8,128)(2,1)S(1)}) custom-call(s32[4]{0:T(128)S(1)} %pad_add_fusion.flag_ref, f32[6,256]{1,0:T(8,128)S(1)} %get-tuple-element.35.scale_ref, bf16[3,3,256,256]{3,2,1,0:T(8,128)(2,1)S(1)} %get-tuple-element.38.w_ref, bf16[8,112,256]{2,1,0:T(8,128)(2,1)S(1)} %get-tuple-element.50.rest_0_, ...), custom_call_target="tpu_custom_call" | custom-call | flops 1 | bytes 1 | tf_op jit(solution)/shard_map/pallas_call | solution.py:214
  19.9 5.6 %collective-permute-start.9 = (bf16[8,96,256]{2,1,0:T(8,128)(2,1)S(1)}, bf16[8,96,256]{2,1,0:T(8,128)(2,1)S(1)}, u32[]{:S(2)}, u32[]{:S(2)}) collective-permute-start(bf16[8,96,256]{2,1,0:T(8,128)(2,1)S(1)} %get-tuple-element.51.far_ref), channel_id=1, source_target_pairs={{0,8},{2,10},{4,12},{6,14},{8,0},{10,2},{12,4},{14,6},{1,9},{3,11}... | collective-permute-start | bytes 1179656 | tf_op jit(solution)/shard_map/ppermute | solution.py:421
  25.5 2.8 %collective-permute-done.refs_1_.rest_1_.rest_3_ = bf16[4,144,256]{2,1,0:T(8,128)(2,1)S(1)} collective-permute-done((bf16[4,144,256]{2,1,0:T(8,128)(2,1)S(1)}, bf16[4,144,256]{2,1,0:T(8,128)(2,1)S(1)}, u32[]{:S(2)}, u32[]{:S(2)}) %collective-permute-start) | collective-permute-done | bytes 294944 | tf_op jit(solution)/shard_map/ppermute | solution.py:394
  28.3 0.0 collective-permute-done.1.refs_2_.rest_2_.rest_4_
  28.3 0.0 collective-permute-done.2.refs_3_.rest_4_.rest_5_
  28.3 0.6 shard_map.48
  28.9 2.0 %collective-permute-start.3 = (bf16[16,16,256]{2,1,0:T(8,128)(2,1)S(1)}, bf16[16,16,256]{2,1,0:T(8,128)(2,1)S(1)}, u32[]{:S(2)}, u32[]{:S(2)}) collective-permute-start(bf16[16,16,256]{2,1,0:T(8,128)(2,1)S(1)} %shard_map.48), channel_id=1, source_target_pairs={{0,1},{1,0},{2,3},{3,2},{4,5},{5,4},{6,7},{7,6},{8,9},{9,8},{10,11... | collective-permute-start | bytes 393224 | tf_op jit(solution)/shard_map/ppermute | solution.py:435
  30.8 1.0 %collective-permute-done.3.rest_3_ = bf16[16,16,256]{2,1,0:T(8,128)(2,1)S(1)} collective-permute-done((bf16[16,16,256]{2,1,0:T(8,128)(2,1)S(1)}, bf16[16,16,256]{2,1,0:T(8,128)(2,1)S(1)}, u32[]{:S(2)}, u32[]{:S(2)}) %collective-permute-start.3) | collective-permute-done | bytes 131104 | tf_op jit(solution)/shard_map/ppermute | solution.py:435
  31.8 3.2 %shard_map.49 = (bf16[8,96,256]{2,1,0:T(8,128)(2,1)S(1)}, bf16[8,96,256]{2,1,0:T(8,128)(2,1)S(1)}) custom-call(s32[4]{0:T(128)S(1)} %pad_add_fusion.flag_ref, f32[6,256]{1,0:T(8,128)S(1)} %get-tuple-element.35.scale_ref, bf16[3,3,256,256]{3,2,1,0:T(8,128)(2,1)S(1)} %get-tuple-element.38.w_ref, bf16[8,112,256]{2,1,0:T(8,128)(2,1)S(1)} %get-tuple-element.39.refs_0_.rest_0_, ...), custom_call_target="tpu_custom_call" | custom-call | flops 1 | bytes 1 | tf_op jit(solution)/shard_map/pallas_call | solution.py:214
  35.0 0.6 shard_map.50
  35.6 3.4 %collective-permute-start.5 = (bf16[8,32,256]{2,1,0:T(8,128)(2,1)S(1)}, bf16[8,32,256]{2,1,0:T(8,128)(2,1)S(1)}, u32[]{:S(2)}, u32[]{:S(2)}) collective-permute-start(bf16[8,32,256]{2,1,0:T(8,128)(2,1)S(1)} %get-tuple-element.53), channel_id=1, source_target_pairs={{0,8},{2,10},{4,12},{6,14},{8,0},{10,2},{12,4},{14,6},{1,9},{3,11}... | collective-permute-start | bytes 393224 | tf_op jit(solution)/shard_map/ppermute | solution.py:456
  39.0 0.1 collective-permute-start.4
  39.1 2.8 %shard_map.51 = (bf16[8,64,256]{2,1,0:T(8,128)(2,1)S(1)}, bf16[8,64,256]{2,1,0:T(8,128)(2,1)S(1)}) custom-call(s32[4]{0:T(128)S(1)} %pad_add_fusion.flag_ref, f32[6,256]{1,0:T(8,128)S(1)} %get-tuple-element.35.scale_ref, bf16[3,3,256,256]{3,2,1,0:T(8,128)(2,1)S(1)} %get-tuple-element.38.w_ref, bf16[8,96,256]{2,1,0:T(8,128)(2,1)S(1)} %get-tuple-element.46.rest_0_, ...), custom_call_target="tpu_custom_call" | custom-call | flops 1 | bytes 1 | tf_op jit(solution)/shard_map/pallas_call | solution.py:214
  42.0 2.3 %collective-permute-start.11 = (bf16[8,64,256]{2,1,0:T(8,128)(2,1)S(1)}, bf16[8,64,256]{2,1,0:T(8,128)(2,1)S(1)}, u32[]{:S(2)}, u32[]{:S(2)}) collective-permute-start(bf16[8,64,256]{2,1,0:T(8,128)(2,1)S(1)} %get-tuple-element.49.mid_ref), channel_id=1, source_target_pairs={{0,8},{2,10},{4,12},{6,14},{8,0},{10,2},{12,4},{14,6},{1,9},{3,11}... | collective-permute-start | bytes 786440 | tf_op jit(solution)/shard_map/ppermute | solution.py:479
  44.3 0.0 collective-permute-done.9.cfar_ref
  44.3 17.7 %collective-permute-start.10 = (bf16[8,32,256]{2,1,0:T(8,128)(2,1)S(1)}, bf16[8,32,256]{2,1,0:T(8,128)(2,1)S(1)}, u32[]{:S(2)}, u32[]{:S(2)}) collective-permute-start(bf16[8,32,256]{2,1,0:T(8,128)(2,1)S(1)} %get-tuple-element.53), channel_id=1, source_target_pairs={{0,1},{1,0},{2,3},{3,2},{4,5},{5,4},{6,7},{7,6},{8,9},{9,8},{10,11... | collective-permute-start | bytes 393224 | tf_op jit(solution)/shard_map/ppermute | solution.py:482
  62.0 0.0 collective-permute-done.5.rim_ref
  62.0 2.8 %collective-permute-start.6 = (bf16[8,32,256]{2,1,0:T(8,128)(2,1)S(1)}, bf16[8,32,256]{2,1,0:T(8,128)(2,1)S(1)}, u32[]{:S(2)}, u32[]{:S(2)}) collective-permute-start(bf16[8,32,256]{2,1,0:T(8,128)(2,1)S(1)} %collective-permute-done.5.rim_ref), channel_id=1, source_target_pairs={{0,1},{1,0},{2,3},{3,2},{4,5},{5,4},{6,7},{7,6},{8,9},{9,8},{10,11... | collective-permute-start | bytes 393224 | tf_op jit(solution)/shard_map/ppermute | solution.py:501
  64.8 0.0 collective-permute-done.10.side_ref
  64.8 2.5 %shard_map.53 = (f32[8,256,256]{2,1,0:T(8,128)S(1)}, bf16[8,256,256]{2,1,0:T(8,128)(2,1)S(1)}) custom-call(s32[4]{0:T(128)S(1)} %pad_add_fusion.flag_ref, f32[6,256]{1,0:T(8,128)S(1)} %get-tuple-element.35.scale_ref, bf16[2,3,256,256]{3,2,1,0:T(8,128)(2,1)S(1)} %get-tuple-element.37.w_ref, bf16[8,96,256]{2,1,0:T(8,128)(2,1)S(1)} %get-tuple-element.43.refs_0_.near_ref, ...), custom_call_target="tpu_custom_call" | custom-call | flops 1 | bytes 1 | tf_op jit(solution)/shard_map/pallas_call | solution.py:484
  67.3 0.0 collective-permute-done.6.side_ref
  67.3 0.0 collective-permute-done.4.cnear_ref
  67.3 1.1 %shard_map.54 = (bf16[8,64,256]{2,1,0:T(8,128)(2,1)S(1)}, bf16[8,64,256]{2,1,0:T(8,128)(2,1)S(1)}) custom-call(s32[4]{0:T(128)S(1)} %pad_add_fusion.flag_ref, f32[6,256]{1,0:T(8,128)S(1)} %get-tuple-element.35.scale_ref, bf16[2,3,256,256]{3,2,1,0:T(8,128)(2,1)S(1)} %get-tuple-element.37.w_ref, bf16[8,64,256]{2,1,0:T(8,128)(2,1)S(1)} %collective-permute-done.4.cnear_ref, ...), custom_call_target="tpu_custom_call" | custom-call | flops 1 | bytes 1 | tf_op jit(solution)/shard_map/pallas_call | solution.py:484
  68.5 0.0 collective-permute-done.11.cmid_ref
  68.5 4.0 %collective-permute-start.12 = (bf16[8,64,256]{2,1,0:T(8,128)(2,1)S(1)}, bf16[8,64,256]{2,1,0:T(8,128)(2,1)S(1)}, u32[]{:S(2)}, u32[]{:S(2)}) collective-permute-start(bf16[8,64,256]{2,1,0:T(8,128)(2,1)S(1)} %get-tuple-element.63.near_ref), channel_id=1, source_target_pairs={{0,1},{1,0},{2,3},{3,2},{4,5},{5,4},{6,7},{7,6},{8,9},{9,8},{10,11... | collective-permute-start | bytes 786440 | tf_op jit(solution)/shard_map/ppermute | solution.py:510
  72.4 1.9 %shard_map.55 = (bf16[8,192,256]{2,1,0:T(8,128)(2,1)S(1)}, bf16[8,192,256]{2,1,0:T(8,128)(2,1)S(1)}) custom-call(s32[4]{0:T(128)S(1)} %pad_add_fusion.flag_ref, f32[6,256]{1,0:T(8,128)S(1)} %get-tuple-element.35.scale_ref, bf16[2,3,256,256]{3,2,1,0:T(8,128)(2,1)S(1)} %get-tuple-element.37.w_ref, bf16[8,64,256]{2,1,0:T(8,128)(2,1)S(1)} %collective-permute-done.11.cmid_ref, ...), custom_call_target="tpu_custom_call" | custom-call | flops 1 | bytes 1 | tf_op jit(solution)/shard_map/pallas_call | solution.py:484
  74.4 0.0 collective-permute-done.12.side_ref
  74.4 2.7 %shard_map.56 = bf16[8,256,256]{2,1,0:T(8,128)(2,1)} custom-call(s32[4]{0:T(128)S(1)} %pad_add_fusion.flag_ref, f32[6,256]{1,0:T(8,128)S(1)} %get-tuple-element.35.scale_ref, bf16[3,256,256]{2,1,0:T(8,128)(2,1)S(1)} %get-tuple-element.36.w_ref, bf16[8,64,256]{2,1,0:T(8,128)(2,1)S(1)} %get-tuple-element.59.near2_ref, ...), custom_call_target="tpu_custom_call" | custom-call | flops 1 | bytes 1 | tf_op jit(solution)/shard_map/pallas_call | solution.py:484
Async XLA Ops:
  0.1 1.2 %copy-start.1 = (bf16[8,256,256]{2,1,0:T(8,128)(2,1)S(1)}, bf16[8,256,256]{2,1,0:T(8,128)(2,1)}, u32[]{:S(2)}) copy-start(bf16[8,256,256]{2,1,0:T(8,128)(2,1)} %refs_0_.1) | copy-start | bytes 3145732
  2.0 15.3 %collective-permute-start.7 = (bf16[4,112,256]{2,1,0:T(8,128)(2,1)S(1)}, bf16[4,112,256]{2,1,0:T(8,128)(2,1)S(1)}, u32[]{:S(2)}, u32[]{:S(2)}) collective-permute-start(bf16[4,112,256]{2,1,0:T(8,128)(2,1)S(1)} %get-tuple-element.47), channel_id=1, source_target_pairs={{0,2},{2,4},{4,6},{6,8},{8,10},{10,12},{12,14},{1,3},{3,5},{5,7},{... | collective-permute-start | bytes 688136 | tf_op jit(solution)/shard_map/ppermute | solution.py:392
  6.0 11.4 %collective-permute-start.8 = (bf16[4,112,256]{2,1,0:T(8,128)(2,1)S(1)}, bf16[4,112,256]{2,1,0:T(8,128)(2,1)S(1)}, u32[]{:S(2)}, u32[]{:S(2)}) collective-permute-start(bf16[4,112,256]{2,1,0:T(8,128)(2,1)S(1)} %get-tuple-element.48), channel_id=1, source_target_pairs={{2,0},{4,2},{6,4},{8,6},{10,8},{12,10},{14,12},{3,1},{5,3},{7,5},{... | collective-permute-start | bytes 688136 | tf_op jit(solution)/shard_map/ppermute | solution.py:393
  7.3 21.0 %collective-permute-start = (bf16[4,144,256]{2,1,0:T(8,128)(2,1)S(1)}, bf16[4,144,256]{2,1,0:T(8,128)(2,1)S(1)}, u32[]{:S(2)}, u32[]{:S(2)}) collective-permute-start(bf16[4,144,256]{2,1,0:T(8,128)(2,1)S(1)} %get-tuple-element.40), channel_id=1, source_target_pairs={{0,2},{2,4},{4,6},{8,10},{10,12},{12,14},{1,3},{3,5},{5,7},{9,11},... | collective-permute-start | bytes 884744 | tf_op jit(solution)/shard_map/ppermute | solution.py:394
  11.3 17.0 %collective-permute-start.1 = (bf16[4,144,256]{2,1,0:T(8,128)(2,1)S(1)}, bf16[4,144,256]{2,1,0:T(8,128)(2,1)S(1)}, u32[]{:S(2)}, u32[]{:S(2)}) collective-permute-start(bf16[4,144,256]{2,1,0:T(8,128)(2,1)S(1)} %get-tuple-element.41), channel_id=1, source_target_pairs={{2,0},{4,2},{6,4},{10,8},{12,10},{14,12},{3,1},{5,3},{7,5},{11,9},... | collective-permute-start | bytes 884744 | tf_op jit(solution)/shard_map/ppermute | solution.py:395
  12.6 15.7 %collective-permute-start.2 = (bf16[4,144,256]{2,1,0:T(8,128)(2,1)S(1)}, bf16[4,144,256]{2,1,0:T(8,128)(2,1)S(1)}, u32[]{:S(2)}, u32[]{:S(2)}) collective-permute-start(bf16[4,144,256]{2,1,0:T(8,128)(2,1)S(1)} %get-tuple-element.42), channel_id=1, source_target_pairs={{6,8},{8,6},{7,9},{9,7},{22,24},{24,22},{23,25},{25,23}} | collective-permute-start | bytes 884744 | tf_op jit(solution)/shard_map/ppermute | solution.py:396
  13.3 2.0 %copy-start = (bf16[3,3,3,256,256]{4,3,2,1,0:T(8,128)(2,1)S(1)}, bf16[3,3,3,256,256]{4,3,2,1,0:T(8,128)(2,1)}, u32[]{:S(2)}) copy-start(bf16[3,3,3,256,256]{4,3,2,1,0:T(8,128)(2,1)} %w_ref.1) | copy-start | bytes 10616836
  15.3 0.7 copy-start.2
  16.0 0.7 copy-start.3
  19.9 24.4 %collective-permute-start.9 = (bf16[8,96,256]{2,1,0:T(8,128)(2,1)S(1)}, bf16[8,96,256]{2,1,0:T(8,128)(2,1)S(1)}, u32[]{:S(2)}, u32[]{:S(2)}) collective-permute-start(bf16[8,96,256]{2,1,0:T(8,128)(2,1)S(1)} %get-tuple-element.51.far_ref), channel_id=1, source_target_pairs={{0,8},{2,10},{4,12},{6,14},{8,0},{10,2},{12,4},{14,6},{1,9},{3,11}... | collective-permute-start | bytes 1179656 | tf_op jit(solution)/shard_map/ppermute | solution.py:421
  28.9 2.9 %collective-permute-start.3 = (bf16[16,16,256]{2,1,0:T(8,128)(2,1)S(1)}, bf16[16,16,256]{2,1,0:T(8,128)(2,1)S(1)}, u32[]{:S(2)}, u32[]{:S(2)}) collective-permute-start(bf16[16,16,256]{2,1,0:T(8,128)(2,1)S(1)} %shard_map.48), channel_id=1, source_target_pairs={{0,1},{1,0},{2,3},{3,2},{4,5},{5,4},{6,7},{7,6},{8,9},{9,8},{10,11... | collective-permute-start | bytes 393224 | tf_op jit(solution)/shard_map/ppermute | solution.py:435
  35.6 26.4 %collective-permute-start.5 = (bf16[8,32,256]{2,1,0:T(8,128)(2,1)S(1)}, bf16[8,32,256]{2,1,0:T(8,128)(2,1)S(1)}, u32[]{:S(2)}, u32[]{:S(2)}) collective-permute-start(bf16[8,32,256]{2,1,0:T(8,128)(2,1)S(1)} %get-tuple-element.53), channel_id=1, source_target_pairs={{0,8},{2,10},{4,12},{6,14},{8,0},{10,2},{12,4},{14,6},{1,9},{3,11}... | collective-permute-start | bytes 393224 | tf_op jit(solution)/shard_map/ppermute | solution.py:456
  39.0 28.3 %collective-permute-start.4 = (bf16[8,64,256]{2,1,0:T(8,128)(2,1)S(1)}, bf16[8,64,256]{2,1,0:T(8,128)(2,1)S(1)}, u32[]{:S(2)}, u32[]{:S(2)}) collective-permute-start(bf16[8,64,256]{2,1,0:T(8,128)(2,1)S(1)} %get-tuple-element.44), channel_id=1, source_target_pairs={{0,8},{2,10},{4,12},{6,14},{8,0},{10,2},{12,4},{14,6},{1,9},{3,11}... | collective-permute-start | bytes 786440 | tf_op jit(solution)/shard_map/ppermute | solution.py:457
  42.0 26.5 %collective-permute-start.11 = (bf16[8,64,256]{2,1,0:T(8,128)(2,1)S(1)}, bf16[8,64,256]{2,1,0:T(8,128)(2,1)S(1)}, u32[]{:S(2)}, u32[]{:S(2)}) collective-permute-start(bf16[8,64,256]{2,1,0:T(8,128)(2,1)S(1)} %get-tuple-element.49.mid_ref), channel_id=1, source_target_pairs={{0,8},{2,10},{4,12},{6,14},{8,0},{10,2},{12,4},{14,6},{1,9},{3,11}... | collective-permute-start | bytes 786440 | tf_op jit(solution)/shard_map/ppermute | solution.py:479
  44.3 20.5 %collective-permute-start.10 = (bf16[8,32,256]{2,1,0:T(8,128)(2,1)S(1)}, bf16[8,32,256]{2,1,0:T(8,128)(2,1)S(1)}, u32[]{:S(2)}, u32[]{:S(2)}) collective-permute-start(bf16[8,32,256]{2,1,0:T(8,128)(2,1)S(1)} %get-tuple-element.53), channel_id=1, source_target_pairs={{0,1},{1,0},{2,3},{3,2},{4,5},{5,4},{6,7},{7,6},{8,9},{9,8},{10,11... | collective-permute-start | bytes 393224 | tf_op jit(solution)/shard_map/ppermute | solution.py:482
  62.0 5.3 %collective-permute-start.6 = (bf16[8,32,256]{2,1,0:T(8,128)(2,1)S(1)}, bf16[8,32,256]{2,1,0:T(8,128)(2,1)S(1)}, u32[]{:S(2)}, u32[]{:S(2)}) collective-permute-start(bf16[8,32,256]{2,1,0:T(8,128)(2,1)S(1)} %collective-permute-done.5.rim_ref), channel_id=1, source_target_pairs={{0,1},{1,0},{2,3},{3,2},{4,5},{5,4},{6,7},{7,6},{8,9},{9,8},{10,11... | collective-permute-start | bytes 393224 | tf_op jit(solution)/shard_map/ppermute | solution.py:501
  68.5 5.9 %collective-permute-start.12 = (bf16[8,64,256]{2,1,0:T(8,128)(2,1)S(1)}, bf16[8,64,256]{2,1,0:T(8,128)(2,1)S(1)}, u32[]{:S(2)}, u32[]{:S(2)}) collective-permute-start(bf16[8,64,256]{2,1,0:T(8,128)(2,1)S(1)} %get-tuple-element.63.near_ref), channel_id=1, source_target_pairs={{0,1},{1,0},{2,3},{3,2},{4,5},{5,4},{6,7},{7,6},{8,9},{9,8},{10,11... | collective-permute-start | bytes 786440 | tf_op jit(solution)/shard_map/ppermute | solution.py:510

commit v6 on v5

--- a/solution.py
+++ b/solution.py
@@ -375,6 +375,7 @@
 
     far_wide_at, near_wide_at = (0, cols - wide), (cols - wide, 0)
     span, span_at = cols - wide, (wide, 0)
+    middle_at = (wide - pad, 0)
     parts = (
         (None, 0, 0, rows, far_wide_at, wide, 0, 0),
         (None, 0, 0, rows, near_wide_at, wide, 1, 0),
@@ -383,18 +384,14 @@
         (None, 0, 0, half, far_wide_at, wide, 4, 0),
         (None, 0, half, half, span_at, span, 5, 0),
         (None, 0, 0, half, span_at, span, 6, 0),
-        ((1, 1), 0, half, half, span_at, span, 7, 0),
-        ((1, 0), 0, 0, half, span_at, span, 7, 0),
+        ((1, 1), 0, half, half, middle_at, span + pad, 7, 0),
+        ((1, 0), 0, 0, half, middle_at, span + pad, 7, 0),
     )
     (
         far_x, near_x, mid_x, far_low, far_high, low, high, middle
     ) = copies(flags, (context_map,), parts)
     above_far = lax.ppermute(far_low, "row", down)
     below_far = lax.ppermute(far_high, "row", up)
-    above = lax.ppermute(low, "row", within_down)
-    below = lax.ppermute(high, "row", within_up)
-    middle = lax.ppermute(middle, "row", [(group - 1, group), (group, group - 1)])
-
     tail = conv_weights.shape[2:]
     scales, first_w, second_w, last_w = kernel_call(
         hold_kernel,
@@ -407,6 +404,11 @@
         [smem_spec()] + [vmem_spec()] * 3,
         [],
     )(flags, norm_gains, conv_biases, conv_weights)
+    low, high, middle, scales = lax.optimization_barrier((low, high, middle, scales))
+    above = lax.ppermute(low, "row", within_down)
+    below = lax.ppermute(high, "row", within_up)
+    middle = lax.ppermute(middle, "row", [(group - 1, group), (group, group - 1)])
+
     params = (scales, first_w)
     far_body, far_edge = (pad, 0), (0, wide)
     far_segments = (
@@ -420,26 +422,26 @@
     )
     cross_far = lax.ppermute(far_n, "row", partner)
 
-    near_end, span_end = (wide - pad, 0), (span - pad, 0)
+    near_end, span_end, middle_end = (wide - pad, 0), (span - pad, 0), (span, 0)
     (rim,) = copies(
         flags,
         (near_x, above, below, middle),
         (
             ((2, 0), 1, 0, half, span_end, pad, 0, 0),
-            ((2, 1), 3, 0, half, span_end, pad, 0, 0),
+            ((2, 1), 3, 0, half, middle_end, pad, 0, 0),
             (None, 0, 0, rows, near_end, pad, 0, half),
             ((1, 0), 2, 0, half, span_end, pad, 0, half + rows),
-            ((1, 1), 3, 0, half, span_end, pad, 0, half + rows),
+            ((1, 1), 3, 0, half, middle_end, pad, 0, half + rows),
         ),
     )
     rim = lax.ppermute(rim, "col", swap)
-    near_body, near_span = (0, pad), (span - wide, 0)
+    near_body, near_span, near_middle = (0, pad), (span - wide, 0), (span + pad - wide, 0)
     near_segments = (
         (None, 0, 0, half, rows, (0, 0), near_body, wide),
         ((2, 0), 1, 0, 0, half, near_span, near_body, wide),
-        ((2, 1), 4, 0, 0, half, near_span, near_body, wide),
+        ((2, 1), 4, 0, 0, half, near_middle, near_body, wide),
         ((1, 0), 2, 0, half + rows, half, near_span, near_body, wide),
-        ((1, 1), 4, 0, half + rows, half, near_span, near_body, wide),
+        ((1, 1), 4, 0, half + rows, half, near_middle, near_body, wide),
         (None, 3, 0, 0, 2 * rows, (0, 0), (wide, 0), pad),
     )
     near1, near_n = first_layer(
@@ -457,14 +459,15 @@
     cross_near = lax.ppermute(near_rest, "row", partner)
     two = 2 * pad
     far_side, rest_side = ((wide - two, 0), (0, mid)), ((0, span - mid), (two, 0))
+    middle_side = ((pad, span - mid), (two, 0))
     mid_segments = (
         (None, 0, 0, half, rows, (0, 0), (0, 0), mid + two),
         (None, 1, 0, 0, half, *far_side, two),
         (None, 2, 0, half + rows, half, *far_side, two),
         ((2, 0), 3, 0, 0, half, *rest_side, mid),
-        ((2, 1), 5, 0, 0, half, *rest_side, mid),
+        ((2, 1), 5, 0, 0, half, *middle_side, mid),
         ((1, 0), 4, 0, half + rows, half, *rest_side, mid),
-        ((1, 1), 5, 0, half + rows, half, *rest_side, mid),
+        ((1, 1), 5, 0, half + rows, half, *middle_side, mid),
     )
     mid1, mid_n = first_layer(
         flags,

time: 77.4 us -> 76.2 us (0.984)
  starting transfers between devices: 49 us -> 43 us
  waiting for transfers between devices: 3.8 us -> 8.64 us
    ppermute x1, starting transfers between devices: 17.7 us -> 13 us  [by_halves(): near_side = lax.ppermute(near_rim, 'col', swap)]
    ppermute x1, waiting for transfers between devices: 0.01 us -> 4.47 us  [by_halves(): cross_mid = lax.ppermute(mid_n, 'row', partner)]
    ppermute x1, starting transfers between devices: 3.41 us -> 6.66 us  [by_halves(): cross_rim = lax.ppermute(near_rim, 'row', partner)]
    ppermute x1, waiting for transfers between devices: 0.01 us -> 2.92 us  [by_halves(): below = lax.ppermute(high, 'row', within_up)]
    ppermute x1, waiting for transfers between devices: 2.79 us -> 0.01 us  [by_halves(): above = lax.ppermute(low, 'row', within_down)]
    ppermute x1, starting transfers between devices: 5.56 us -> 3.07 us  [by_halves(): cross_far = lax.ppermute(far_n, 'row', partner)]
    ppermute x1, starting transfers between devices: 3.96 us -> 1.65 us  [by_halves(): last_side = lax.ppermute(near_n, 'col', swap)]
  transfers between devices with their start and end apart: 13 -> 13, of which waited for: 2 -> 4; matrix products, arithmetic and copies ran while one was open for 0% -> 0% of each run, Pallas kernels for 21% -> 21%
where the time goes in v6:
time: 76.2 us; the launch traced here: 75.8 us
  starting transfers between devices  43 us (56%)
  Pallas kernels  19.3 us (25%)
  waiting for transfers between devices  8.64 us (11%)
  local copies, waits for them, and re-layouts  4.59 us (6%)
    ppermute x1, starting transfers between devices, by_halves(): near_side = lax.ppermute(near_rim, 'col', swap)  13 us
    pallas_call x3, Pallas kernels, first_layer(): kernel_call(functools.partial(first_layer_kernel, segments, out_at, rows,...  8.55 us
    pallas_call x4, Pallas kernels, plain(): kernel_call(body, out, [smem_spec()] + [vmem_spec()] * (len(operands) + 2...  8.19 us
    ppermute x1, starting transfers between devices, by_halves(): cross_rim = lax.ppermute(near_rim, 'row', partner)  6.66 us
    unnamed x8, local copies, waits for them, and re-layouts  4.59 us
    ppermute x1, waiting for transfers between devices, by_halves(): cross_mid = lax.ppermute(mid_n, 'row', partner)  4.47 us
    ppermute x1, starting transfers between devices, by_halves(): above = lax.ppermute(low, 'row', within_down)  4 us
    ppermute x1, starting transfers between devices, by_halves(): above_far = lax.ppermute(far_low, 'row', down)  3.96 us
  transfers between devices with their start and end apart: 13, of which 4 were waited for; matrix products, arithmetic and copies ran while one was open for 0% of the time, Pallas kernels for 21%

profile of v6, /device:TPU:1, one launch (start us, length us, event | category | flops | bytes accessed | tf_op | source)
XLA Modules:
  0.0 75.8 jit_solution(3422072997840277921)
XLA Ops:
  0.0 0.1 pad_add_fusion.flag_ref
  0.1 0.0 copy-start.1
  0.1 1.2 %copy-done.1 = bf16[8,256,256]{2,1,0:T(8,128)(2,1)S(1)} copy-done((bf16[8,256,256]{2,1,0:T(8,128)(2,1)S(1)}, bf16[8,256,256]{2,1,0:T(8,128)(2,1)}, u32[]{:S(2)}) %copy-start.1) | copy-done | bytes 1048600
  1.3 0.7 shard_map.46
  2.0 4.0 %collective-permute-start.7 = (bf16[4,112,256]{2,1,0:T(8,128)(2,1)S(1)}, bf16[4,112,256]{2,1,0:T(8,128)(2,1)S(1)}, u32[]{:S(2)}, u32[]{:S(2)}) collective-permute-start(bf16[4,112,256]{2,1,0:T(8,128)(2,1)S(1)} %get-tuple-element.55), channel_id=1, source_target_pairs={{0,2},{2,4},{4,6},{6,8},{8,10},{10,12},{12,14},{1,3},{3,5},{5,7},{... | collective-permute-start | bytes 688136 | tf_op jit(solution)/shard_map/ppermute | solution.py:393
  6.0 1.3 %collective-permute-start.8 = (bf16[4,112,256]{2,1,0:T(8,128)(2,1)S(1)}, bf16[4,112,256]{2,1,0:T(8,128)(2,1)S(1)}, u32[]{:S(2)}, u32[]{:S(2)}) collective-permute-start(bf16[4,112,256]{2,1,0:T(8,128)(2,1)S(1)} %get-tuple-element.56), channel_id=1, source_target_pairs={{2,0},{4,2},{6,4},{8,6},{10,8},{12,10},{14,12},{3,1},{5,3},{7,5},{... | collective-permute-start | bytes 688136 | tf_op jit(solution)/shard_map/ppermute | solution.py:394
  7.3 0.0 copy-start
  7.3 2.0 %copy-done = bf16[3,3,3,256,256]{4,3,2,1,0:T(8,128)(2,1)S(1)} copy-done((bf16[3,3,3,256,256]{4,3,2,1,0:T(8,128)(2,1)S(1)}, bf16[3,3,3,256,256]{4,3,2,1,0:T(8,128)(2,1)}, u32[]{:S(2)}) %copy-start) | copy-done | bytes 3538968
  9.3 0.0 copy-start.2
  9.3 0.7 copy-done.2
  10.0 0.0 copy-start.3
  10.0 0.7 copy-done.3
  10.7 0.7 shard_map.47
  11.4 0.7 collective-permute-start.2
  12.1 4.0 %collective-permute-start = (bf16[4,144,256]{2,1,0:T(8,128)(2,1)S(1)}, bf16[4,144,256]{2,1,0:T(8,128)(2,1)S(1)}, u32[]{:S(2)}, u32[]{:S(2)}) collective-permute-start(bf16[4,144,256]{2,1,0:T(8,128)(2,1)S(1)} %get-tuple-element.48), channel_id=1, source_target_pairs={{0,2},{2,4},{4,6},{8,10},{10,12},{12,14},{1,3},{3,5},{5,7},{9,11},... | collective-permute-start | bytes 884744 | tf_op jit(solution)/shard_map/ppermute | solution.py:408
  16.1 1.3 %collective-permute-start.1 = (bf16[4,144,256]{2,1,0:T(8,128)(2,1)S(1)}, bf16[4,144,256]{2,1,0:T(8,128)(2,1)S(1)}, u32[]{:S(2)}, u32[]{:S(2)}) collective-permute-start(bf16[4,144,256]{2,1,0:T(8,128)(2,1)S(1)} %get-tuple-element.49), channel_id=1, source_target_pairs={{2,0},{4,2},{6,4},{10,8},{12,10},{14,12},{3,1},{5,3},{7,5},{11,9},... | collective-permute-start | bytes 884744 | tf_op jit(solution)/shard_map/ppermute | solution.py:409
  17.4 0.0 collective-permute-done.7.rest_1_
  17.4 0.0 collective-permute-done.8.rest_2_
  17.4 2.5 %shard_map.52 = (bf16[8,96,256]{2,1,0:T(8,128)(2,1)S(1)}, bf16[8,96,256]{2,1,0:T(8,128)(2,1)S(1)}) custom-call(s32[4]{0:T(128)S(1)} %pad_add_fusion.flag_ref, f32[6,256]{1,0:T(8,128)S(1)} %get-tuple-element.43.scale_ref, bf16[3,3,256,256]{3,2,1,0:T(8,128)(2,1)S(1)} %get-tuple-element.46.w_ref, bf16[8,112,256]{2,1,0:T(8,128)(2,1)S(1)} %get-tuple-element.58.rest_0_, ...), custom_call_target="tpu_custom_call" | custom-call | flops 1 | bytes 1 | tf_op jit(solution)/shard_map/pallas_call | solution.py:214
  19.9 3.1 %collective-permute-start.9 = (bf16[8,96,256]{2,1,0:T(8,128)(2,1)S(1)}, bf16[8,96,256]{2,1,0:T(8,128)(2,1)S(1)}, u32[]{:S(2)}, u32[]{:S(2)}) collective-permute-start(bf16[8,96,256]{2,1,0:T(8,128)(2,1)S(1)} %get-tuple-element.59.far_ref), channel_id=1, source_target_pairs={{0,8},{2,10},{4,12},{6,14},{8,0},{10,2},{12,4},{14,6},{1,9},{3,11}... | collective-permute-start | bytes 1179656 | tf_op jit(solution)/shard_map/ppermute | solution.py:423
  23.0 0.0 collective-permute-done.refs_1_.rest_1_.rest_3_
  23.0 2.9 %collective-permute-done.1.refs_2_.rest_2_.rest_4_ = bf16[4,144,256]{2,1,0:T(8,128)(2,1)S(1)} collective-permute-done((bf16[4,144,256]{2,1,0:T(8,128)(2,1)S(1)}, bf16[4,144,256]{2,1,0:T(8,128)(2,1)S(1)}, u32[]{:S(2)}, u32[]{:S(2)}) %collective-permute-start.1) | collective-permute-done | bytes 294944 | tf_op jit(solution)/shard_map/ppermute | solution.py:409
  25.9 0.0 collective-permute-done.2.refs_3_.rest_4_.rest_5_
  25.9 0.6 shard_map.48
  26.5 2.2 %collective-permute-start.3 = (bf16[16,16,256]{2,1,0:T(8,128)(2,1)S(1)}, bf16[16,16,256]{2,1,0:T(8,128)(2,1)S(1)}, u32[]{:S(2)}, u32[]{:S(2)}) collective-permute-start(bf16[16,16,256]{2,1,0:T(8,128)(2,1)S(1)} %shard_map.48), channel_id=1, source_target_pairs={{0,1},{1,0},{2,3},{3,2},{4,5},{5,4},{6,7},{7,6},{8,9},{9,8},{10,11... | collective-permute-start | bytes 393224 | tf_op jit(solution)/shard_map/ppermute | solution.py:437
  28.8 1.0 %collective-permute-done.3.rest_3_ = bf16[16,16,256]{2,1,0:T(8,128)(2,1)S(1)} collective-permute-done((bf16[16,16,256]{2,1,0:T(8,128)(2,1)S(1)}, bf16[16,16,256]{2,1,0:T(8,128)(2,1)S(1)}, u32[]{:S(2)}, u32[]{:S(2)}) %collective-permute-start.3) | collective-permute-done | bytes 131104 | tf_op jit(solution)/shard_map/ppermute | solution.py:437
  29.7 3.2 %shard_map.49 = (bf16[8,96,256]{2,1,0:T(8,128)(2,1)S(1)}, bf16[8,96,256]{2,1,0:T(8,128)(2,1)S(1)}) custom-call(s32[4]{0:T(128)S(1)} %pad_add_fusion.flag_ref, f32[6,256]{1,0:T(8,128)S(1)} %get-tuple-element.43.scale_ref, bf16[3,3,256,256]{3,2,1,0:T(8,128)(2,1)S(1)} %get-tuple-element.46.w_ref, bf16[8,112,256]{2,1,0:T(8,128)(2,1)S(1)} %get-tuple-element.47.refs_0_.rest_0_, ...), custom_call_target="tpu_custom_call" | custom-call | flops 1 | bytes 1 | tf_op jit(solution)/shard_map/pallas_call | solution.py:214
  32.9 0.6 shard_map.50
  33.5 6.7 %collective-permute-start.5 = (bf16[8,32,256]{2,1,0:T(8,128)(2,1)S(1)}, bf16[8,32,256]{2,1,0:T(8,128)(2,1)S(1)}, u32[]{:S(2)}, u32[]{:S(2)}) collective-permute-start(bf16[8,32,256]{2,1,0:T(8,128)(2,1)S(1)} %get-tuple-element.61), channel_id=1, source_target_pairs={{0,8},{2,10},{4,12},{6,14},{8,0},{10,2},{12,4},{14,6},{1,9},{3,11}... | collective-permute-start | bytes 393224 | tf_op jit(solution)/shard_map/ppermute | solution.py:458
  40.2 0.1 collective-permute-start.4
  40.3 2.8 %shard_map.51 = (bf16[8,64,256]{2,1,0:T(8,128)(2,1)S(1)}, bf16[8,64,256]{2,1,0:T(8,128)(2,1)S(1)}) custom-call(s32[4]{0:T(128)S(1)} %pad_add_fusion.flag_ref, f32[6,256]{1,0:T(8,128)S(1)} %get-tuple-element.43.scale_ref, bf16[3,3,256,256]{3,2,1,0:T(8,128)(2,1)S(1)} %get-tuple-element.46.w_ref, bf16[8,96,256]{2,1,0:T(8,128)(2,1)S(1)} %get-tuple-element.54.rest_0_, ...), custom_call_target="tpu_custom_call" | custom-call | flops 1 | bytes 1 | tf_op jit(solution)/shard_map/pallas_call | solution.py:214
  43.1 2.3 %collective-permute-start.11 = (bf16[8,64,256]{2,1,0:T(8,128)(2,1)S(1)}, bf16[8,64,256]{2,1,0:T(8,128)(2,1)S(1)}, u32[]{:S(2)}, u32[]{:S(2)}) collective-permute-start(bf16[8,64,256]{2,1,0:T(8,128)(2,1)S(1)} %get-tuple-element.57.mid_ref), channel_id=1, source_target_pairs={{0,8},{2,10},{4,12},{6,14},{8,0},{10,2},{12,4},{14,6},{1,9},{3,11}... | collective-permute-start | bytes 786440 | tf_op jit(solution)/shard_map/ppermute | solution.py:482
  45.5 0.0 collective-permute-done.9.cfar_ref
  45.5 13.0 %collective-permute-start.10 = (bf16[8,32,256]{2,1,0:T(8,128)(2,1)S(1)}, bf16[8,32,256]{2,1,0:T(8,128)(2,1)S(1)}, u32[]{:S(2)}, u32[]{:S(2)}) collective-permute-start(bf16[8,32,256]{2,1,0:T(8,128)(2,1)S(1)} %get-tuple-element.61), channel_id=1, source_target_pairs={{0,1},{1,0},{2,3},{3,2},{4,5},{5,4},{6,7},{7,6},{8,9},{9,8},{10,11... | collective-permute-start | bytes 393224 | tf_op jit(solution)/shard_map/ppermute | solution.py:485
  58.4 0.0 collective-permute-done.5.rim_ref
  58.4 2.8 %collective-permute-start.6 = (bf16[8,32,256]{2,1,0:T(8,128)(2,1)S(1)}, bf16[8,32,256]{2,1,0:T(8,128)(2,1)S(1)}, u32[]{:S(2)}, u32[]{:S(2)}) collective-permute-start(bf16[8,32,256]{2,1,0:T(8,128)(2,1)S(1)} %collective-permute-done.5.rim_ref), channel_id=1, source_target_pairs={{0,1},{1,0},{2,3},{3,2},{4,5},{5,4},{6,7},{7,6},{8,9},{9,8},{10,11... | collective-permute-start | bytes 393224 | tf_op jit(solution)/shard_map/ppermute | solution.py:504
  61.2 0.0 collective-permute-done.10.side_ref
  61.2 2.5 %shard_map.53 = (f32[8,256,256]{2,1,0:T(8,128)S(1)}, bf16[8,256,256]{2,1,0:T(8,128)(2,1)S(1)}) custom-call(s32[4]{0:T(128)S(1)} %pad_add_fusion.flag_ref, f32[6,256]{1,0:T(8,128)S(1)} %get-tuple-element.43.scale_ref, bf16[2,3,256,256]{3,2,1,0:T(8,128)(2,1)S(1)} %get-tuple-element.45.w_ref, bf16[8,96,256]{2,1,0:T(8,128)(2,1)S(1)} %get-tuple-element.51.refs_0_.near_ref, ...), custom_call_target="tpu_custom_call" | custom-call | flops 1 | bytes 1 | tf_op jit(solution)/shard_map/pallas_call | solution.py:487
  63.7 0.0 collective-permute-done.6.side_ref
  63.7 0.2 collective-permute-done.4.cnear_ref
  64.0 1.1 %shard_map.54 = (bf16[8,64,256]{2,1,0:T(8,128)(2,1)S(1)}, bf16[8,64,256]{2,1,0:T(8,128)(2,1)S(1)}) custom-call(s32[4]{0:T(128)S(1)} %pad_add_fusion.flag_ref, f32[6,256]{1,0:T(8,128)S(1)} %get-tuple-element.43.scale_ref, bf16[2,3,256,256]{3,2,1,0:T(8,128)(2,1)S(1)} %get-tuple-element.45.w_ref, bf16[8,64,256]{2,1,0:T(8,128)(2,1)S(1)} %collective-permute-done.4.cnear_ref, ...), custom_call_target="tpu_custom_call" | custom-call | flops 1 | bytes 1 | tf_op jit(solution)/shard_map/pallas_call | solution.py:487
  65.1 4.5 %collective-permute-done.11.cmid_ref = bf16[8,64,256]{2,1,0:T(8,128)(2,1)S(1)} collective-permute-done((bf16[8,64,256]{2,1,0:T(8,128)(2,1)S(1)}, bf16[8,64,256]{2,1,0:T(8,128)(2,1)S(1)}, u32[]{:S(2)}, u32[]{:S(2)}) %collective-permute-start.11) | collective-permute-done | bytes 262176 | tf_op jit(solution)/shard_map/ppermute | solution.py:482
  69.6 1.6 %collective-permute-start.12 = (bf16[8,64,256]{2,1,0:T(8,128)(2,1)S(1)}, bf16[8,64,256]{2,1,0:T(8,128)(2,1)S(1)}, u32[]{:S(2)}, u32[]{:S(2)}) collective-permute-start(bf16[8,64,256]{2,1,0:T(8,128)(2,1)S(1)} %get-tuple-element.71.near_ref), channel_id=1, source_target_pairs={{0,1},{1,0},{2,3},{3,2},{4,5},{5,4},{6,7},{7,6},{8,9},{9,8},{10,11... | collective-permute-start | bytes 786440 | tf_op jit(solution)/shard_map/ppermute | solution.py:513
  71.2 1.9 %shard_map.55 = (bf16[8,192,256]{2,1,0:T(8,128)(2,1)S(1)}, bf16[8,192,256]{2,1,0:T(8,128)(2,1)S(1)}) custom-call(s32[4]{0:T(128)S(1)} %pad_add_fusion.flag_ref, f32[6,256]{1,0:T(8,128)S(1)} %get-tuple-element.43.scale_ref, bf16[2,3,256,256]{3,2,1,0:T(8,128)(2,1)S(1)} %get-tuple-element.45.w_ref, bf16[8,64,256]{2,1,0:T(8,128)(2,1)S(1)} %collective-permute-done.11.cmid_ref, ...), custom_call_target="tpu_custom_call" | custom-call | flops 1 | bytes 1 | tf_op jit(solution)/shard_map/pallas_call | solution.py:487
  73.2 0.0 collective-permute-done.12.side_ref
  73.2 2.7 %shard_map.56 = bf16[8,256,256]{2,1,0:T(8,128)(2,1)} custom-call(s32[4]{0:T(128)S(1)} %pad_add_fusion.flag_ref, f32[6,256]{1,0:T(8,128)S(1)} %get-tuple-element.43.scale_ref, bf16[3,256,256]{2,1,0:T(8,128)(2,1)S(1)} %get-tuple-element.44.w_ref, bf16[8,64,256]{2,1,0:T(8,128)(2,1)S(1)} %get-tuple-element.67.near2_ref, ...), custom_call_target="tpu_custom_call" | custom-call | flops 1 | bytes 1 | tf_op jit(solution)/shard_map/pallas_call | solution.py:487
Async XLA Ops:
  0.1 1.2 %copy-start.1 = (bf16[8,256,256]{2,1,0:T(8,128)(2,1)S(1)}, bf16[8,256,256]{2,1,0:T(8,128)(2,1)}, u32[]{:S(2)}) copy-start(bf16[8,256,256]{2,1,0:T(8,128)(2,1)} %refs_0_.1) | copy-start | bytes 3145732
  2.0 15.4 %collective-permute-start.7 = (bf16[4,112,256]{2,1,0:T(8,128)(2,1)S(1)}, bf16[4,112,256]{2,1,0:T(8,128)(2,1)S(1)}, u32[]{:S(2)}, u32[]{:S(2)}) collective-permute-start(bf16[4,112,256]{2,1,0:T(8,128)(2,1)S(1)} %get-tuple-element.55), channel_id=1, source_target_pairs={{0,2},{2,4},{4,6},{6,8},{8,10},{10,12},{12,14},{1,3},{3,5},{5,7},{... | collective-permute-start | bytes 688136 | tf_op jit(solution)/shard_map/ppermute | solution.py:393
  6.0 11.4 %collective-permute-start.8 = (bf16[4,112,256]{2,1,0:T(8,128)(2,1)S(1)}, bf16[4,112,256]{2,1,0:T(8,128)(2,1)S(1)}, u32[]{:S(2)}, u32[]{:S(2)}) collective-permute-start(bf16[4,112,256]{2,1,0:T(8,128)(2,1)S(1)} %get-tuple-element.56), channel_id=1, source_target_pairs={{2,0},{4,2},{6,4},{8,6},{10,8},{12,10},{14,12},{3,1},{5,3},{7,5},{... | collective-permute-start | bytes 688136 | tf_op jit(solution)/shard_map/ppermute | solution.py:394
  7.3 2.0 %copy-start = (bf16[3,3,3,256,256]{4,3,2,1,0:T(8,128)(2,1)S(1)}, bf16[3,3,3,256,256]{4,3,2,1,0:T(8,128)(2,1)}, u32[]{:S(2)}) copy-start(bf16[3,3,3,256,256]{4,3,2,1,0:T(8,128)(2,1)} %w_ref.1) | copy-start | bytes 10616836
  9.3 0.7 copy-start.2
  10.0 0.7 copy-start.3
  11.4 14.6 %collective-permute-start.2 = (bf16[4,160,256]{2,1,0:T(8,128)(2,1)S(1)}, bf16[4,160,256]{2,1,0:T(8,128)(2,1)S(1)}, u32[]{:S(2)}, u32[]{:S(2)}) collective-permute-start(bf16[4,160,256]{2,1,0:T(8,128)(2,1)S(1)} %get-tuple-element.50), channel_id=1, source_target_pairs={{6,8},{8,6},{7,9},{9,7},{22,24},{24,22},{23,25},{25,23}} | collective-permute-start | bytes 983048 | tf_op jit(solution)/shard_map/ppermute | solution.py:410
  12.1 10.9 %collective-permute-start = (bf16[4,144,256]{2,1,0:T(8,128)(2,1)S(1)}, bf16[4,144,256]{2,1,0:T(8,128)(2,1)S(1)}, u32[]{:S(2)}, u32[]{:S(2)}) collective-permute-start(bf16[4,144,256]{2,1,0:T(8,128)(2,1)S(1)} %get-tuple-element.48), channel_id=1, source_target_pairs={{0,2},{2,4},{4,6},{8,10},{10,12},{12,14},{1,3},{3,5},{5,7},{9,11},... | collective-permute-start | bytes 884744 | tf_op jit(solution)/shard_map/ppermute | solution.py:408
  16.1 9.8 %collective-permute-start.1 = (bf16[4,144,256]{2,1,0:T(8,128)(2,1)S(1)}, bf16[4,144,256]{2,1,0:T(8,128)(2,1)S(1)}, u32[]{:S(2)}, u32[]{:S(2)}) collective-permute-start(bf16[4,144,256]{2,1,0:T(8,128)(2,1)S(1)} %get-tuple-element.49), channel_id=1, source_target_pairs={{2,0},{4,2},{6,4},{10,8},{12,10},{14,12},{3,1},{5,3},{7,5},{11,9},... | collective-permute-start | bytes 884744 | tf_op jit(solution)/shard_map/ppermute | solution.py:409
  19.9 25.5 %collective-permute-start.9 = (bf16[8,96,256]{2,1,0:T(8,128)(2,1)S(1)}, bf16[8,96,256]{2,1,0:T(8,128)(2,1)S(1)}, u32[]{:S(2)}, u32[]{:S(2)}) collective-permute-start(bf16[8,96,256]{2,1,0:T(8,128)(2,1)S(1)} %get-tuple-element.59.far_ref), channel_id=1, source_target_pairs={{0,8},{2,10},{4,12},{6,14},{8,0},{10,2},{12,4},{14,6},{1,9},{3,11}... | collective-permute-start | bytes 1179656 | tf_op jit(solution)/shard_map/ppermute | solution.py:423
  26.5 3.2 %collective-permute-start.3 = (bf16[16,16,256]{2,1,0:T(8,128)(2,1)S(1)}, bf16[16,16,256]{2,1,0:T(8,128)(2,1)S(1)}, u32[]{:S(2)}, u32[]{:S(2)}) collective-permute-start(bf16[16,16,256]{2,1,0:T(8,128)(2,1)S(1)} %shard_map.48), channel_id=1, source_target_pairs={{0,1},{1,0},{2,3},{3,2},{4,5},{5,4},{6,7},{7,6},{8,9},{9,8},{10,11... | collective-permute-start | bytes 393224 | tf_op jit(solution)/shard_map/ppermute | solution.py:437
  33.5 24.9 %collective-permute-start.5 = (bf16[8,32,256]{2,1,0:T(8,128)(2,1)S(1)}, bf16[8,32,256]{2,1,0:T(8,128)(2,1)S(1)}, u32[]{:S(2)}, u32[]{:S(2)}) collective-permute-start(bf16[8,32,256]{2,1,0:T(8,128)(2,1)S(1)} %get-tuple-element.61), channel_id=1, source_target_pairs={{0,8},{2,10},{4,12},{6,14},{8,0},{10,2},{12,4},{14,6},{1,9},{3,11}... | collective-permute-start | bytes 393224 | tf_op jit(solution)/shard_map/ppermute | solution.py:458
  40.2 23.8 %collective-permute-start.4 = (bf16[8,64,256]{2,1,0:T(8,128)(2,1)S(1)}, bf16[8,64,256]{2,1,0:T(8,128)(2,1)S(1)}, u32[]{:S(2)}, u32[]{:S(2)}) collective-permute-start(bf16[8,64,256]{2,1,0:T(8,128)(2,1)S(1)} %get-tuple-element.52), channel_id=1, source_target_pairs={{0,8},{2,10},{4,12},{6,14},{8,0},{10,2},{12,4},{14,6},{1,9},{3,11}... | collective-permute-start | bytes 786440 | tf_op jit(solution)/shard_map/ppermute | solution.py:459
  43.1 26.5 %collective-permute-start.11 = (bf16[8,64,256]{2,1,0:T(8,128)(2,1)S(1)}, bf16[8,64,256]{2,1,0:T(8,128)(2,1)S(1)}, u32[]{:S(2)}, u32[]{:S(2)}) collective-permute-start(bf16[8,64,256]{2,1,0:T(8,128)(2,1)S(1)} %get-tuple-element.57.mid_ref), channel_id=1, source_target_pairs={{0,8},{2,10},{4,12},{6,14},{8,0},{10,2},{12,4},{14,6},{1,9},{3,11}... | collective-permute-start | bytes 786440 | tf_op jit(solution)/shard_map/ppermute | solution.py:482
  45.5 15.8 %collective-permute-start.10 = (bf16[8,32,256]{2,1,0:T(8,128)(2,1)S(1)}, bf16[8,32,256]{2,1,0:T(8,128)(2,1)S(1)}, u32[]{:S(2)}, u32[]{:S(2)}) collective-permute-start(bf16[8,32,256]{2,1,0:T(8,128)(2,1)S(1)} %get-tuple-element.61), channel_id=1, source_target_pairs={{0,1},{1,0},{2,3},{3,2},{4,5},{5,4},{6,7},{7,6},{8,9},{9,8},{10,11... | collective-permute-start | bytes 393224 | tf_op jit(solution)/shard_map/ppermute | solution.py:485
  58.4 5.3 %collective-permute-start.6 = (bf16[8,32,256]{2,1,0:T(8,128)(2,1)S(1)}, bf16[8,32,256]{2,1,0:T(8,128)(2,1)S(1)}, u32[]{:S(2)}, u32[]{:S(2)}) collective-permute-start(bf16[8,32,256]{2,1,0:T(8,128)(2,1)S(1)} %collective-permute-done.5.rim_ref), channel_id=1, source_target_pairs={{0,1},{1,0},{2,3},{3,2},{4,5},{5,4},{6,7},{7,6},{8,9},{9,8},{10,11... | collective-permute-start | bytes 393224 | tf_op jit(solution)/shard_map/ppermute | solution.py:504
  69.6 3.6 %collective-permute-start.12 = (bf16[8,64,256]{2,1,0:T(8,128)(2,1)S(1)}, bf16[8,64,256]{2,1,0:T(8,128)(2,1)S(1)}, u32[]{:S(2)}, u32[]{:S(2)}) collective-permute-start(bf16[8,64,256]{2,1,0:T(8,128)(2,1)S(1)} %get-tuple-element.71.near_ref), channel_id=1, source_target_pairs={{0,1},{1,0},{2,3},{3,2},{4,5},{5,4},{6,7},{7,6},{8,9},{9,8},{10,11... | collective-permute-start | bytes 786440 | tf_op jit(solution)/shard_map/ppermute | solution.py:513

commit v7 on v6

--- a/solution.py
+++ b/solution.py
@@ -102,12 +102,12 @@
     return pl.BlockSpec(memory_space=pl.ANY)
 
 
-def kernel_call(body, out_shape, in_specs, scratch):
+def kernel_call(body, out_shape, in_specs, scratch, out_specs=None):
     return pl.pallas_call(
         body,
         out_shape=out_shape,
         in_specs=in_specs,
-        out_specs=jax.tree.map(lambda _: vmem_spec(), out_shape),
+        out_specs=out_specs or jax.tree.map(lambda _: vmem_spec(), out_shape),
         scratch_shapes=scratch,
         compiler_params=pltpu.CompilerParams(vmem_limit_bytes=vmem_limit),
         cost_estimate=pl.CostEstimate(flops=1, bytes_accessed=1, transcendentals=0),
@@ -224,7 +224,7 @@
 
 def partial_kernel(
     flag_ref, scale_ref, w_ref, near_ref, mid_ref, far_ref, cfar_ref, side_ref, near1_ref, mid1_ref,
-    far1_ref, acc_ref, next_ref, own, other,
+    far1_ref, acc_ref, next_ref, far2_ref, farn_ref, own, other,
 ):
     core = flag_ref[0]
     step = dilations[1]
@@ -259,6 +259,10 @@
     acc_ref[...] = jnp.dot(
         stacked, w_ref[...].reshape(6 * channels, channels), preferred_element_type=jnp.float32
     ).reshape(rows, cols, channels)
+    edge = pl.ds(place(core, 0, cols - far2_ref.shape[1]), far2_ref.shape[1])
+    far2_ref[...], farn_ref[...] = after_second(
+        scale_ref, acc_ref[:, edge, :], next_ref[:, edge, :]
+    )
 
 
 def second_layer(flag_ref, scale_ref, w_ref, window, acc, current):
@@ -274,7 +278,14 @@
         w_ref[1].reshape(3 * channels, channels),
         preferred_element_type=jnp.float32,
     )
-    result = update(current.reshape(cells, channels), response, scale_ref[4:5, :])
+    return after_second(scale_ref, response, current)
+
+
+def after_second(scale_ref, response, current):
+    cells, channels = current.shape[0] * current.shape[1], current.shape[2]
+    result = update(
+        current.reshape(cells, channels), response.reshape(cells, channels), scale_ref[4:5, :]
+    )
     normed = normalize(result, scale_ref[2:3, :])
     return result.reshape(current.shape), normed.reshape(current.shape)
 
@@ -295,59 +306,73 @@
     )
 
 
-def rest_kernel(
+def mid_kernel(
     flag_ref, scale_ref, w_ref, cmid_ref, cnear_ref, acc_ref, x1_ref, next_ref, normed_ref, window
 ):
     core = flag_ref[0]
     step, reach = dilations[1], dilations[2]
     rows, mid, channels = cmid_ref.shape
-    near, cols = cnear_ref.shape[1], x1_ref.shape[1]
-    width, far = cols - reach, cols - near - step - mid
-    count = width + step - far - mid
-    window[:, pl.ds(place(core, step + far + mid, 0), count), :] = cnear_ref[
-        :, pl.ds(place(core, 0, near - count), count), :
-    ]
-    window[:, pl.ds(place(core, step + far, count), mid), :] = cmid_ref[...]
-    window[:, pl.ds(place(core, 0, count + mid), step + far), :] = jnp.zeros(
-        (rows, step + far, channels), window.dtype
-    )
-    at = pl.ds(place(core, 0, reach), width)
+    near, width = cnear_ref.shape[1], next_ref.shape[1]
+    blank = width + 2 * step - near - mid
+    window[:, pl.ds(place(core, blank + mid, 0), near), :] = cnear_ref[...]
+    window[:, pl.ds(place(core, blank, near), mid), :] = cmid_ref[...]
+    window[:, pl.ds(place(core, 0, near + mid), blank), :] = jnp.zeros(
+        (rows, blank, channels), window.dtype
+    )
+    at = pl.ds(place(core, x1_ref.shape[1] - reach - width, reach), width)
     next_ref[...], normed_ref[...] = second_layer(
         flag_ref, scale_ref, w_ref, window[...], acc_ref[:, at, :], x1_ref[:, at, :]
     )
 
 
-def last_kernel(
-    flag_ref, scale_ref, w_ref, near2_ref, rest2_ref, near_ref, rest_ref, side_ref, out_ref, window,
-    current,
+def sides_kernel(
+    flag_ref, scale_ref, w_ref, near2_ref, far2_ref, near_ref, far_ref, acc_ref, ends_ref, normed
 ):
     core = flag_ref[0]
-    reach = dilations[2]
-    rows, cols, channels = out_ref.shape
-    rest = cols - reach
-    dst = place(core, rest, 0)
-    current[:, pl.ds(dst, reach), :] = near2_ref[...]
-    window[:, pl.ds(pl.multiple_of(dst + reach, lane_pad), reach), :] = near_ref[...]
-    dst = place(core, 0, reach)
-    current[:, pl.ds(dst, rest), :] = rest2_ref[...]
-    window[:, pl.ds(pl.multiple_of(dst + reach, lane_pad), rest), :] = rest_ref[...]
-    window[:, pl.ds(place(core, reach + cols, 0), reach), :] = side_ref[...]
-    window[:, pl.ds(place(core, 0, reach + cols), reach), :] = jnp.zeros(
-        (rows, reach, channels), window.dtype
-    )
-    stacked = jnp.concatenate(
-        [
-            window[:, b * reach : b * reach + cols, :].reshape(rows * cols, channels)
-            for b in range(3)
-        ],
-        axis=1,
-    )
-    response = jnp.dot(
-        stacked, w_ref[...].reshape(3 * channels, channels), preferred_element_type=jnp.float32
-    )
-    out_ref[...] = update(
-        current[...].reshape(rows * cols, channels), response, scale_ref[5:6, :]
-    ).reshape(rows, cols, channels)
+    rows, reach, channels = near_ref.shape
+    ends_ref[core], ends_ref[1 - core] = far2_ref[...], near2_ref[...]
+    normed[core], normed[1 - core] = far_ref[...], near_ref[...]
+    for block, (end, tap) in enumerate(((0, 1), (0, 0), (1, 2), (1, 1))):
+        acc_ref[:, block * reach : (block + 1) * reach, :] = jnp.dot(
+            normed[end].reshape(rows * reach, channels),
+            w_ref[tap],
+            preferred_element_type=jnp.float32,
+        ).reshape(rows, reach, channels)
+
+
+def last_kernel(
+    flag_ref, scale_ref, w_ref, ends_ref, mid2_ref, mid_ref, side_ref, acc_ref, out_ref, total,
+    result, sems,
+):
+    core = flag_ref[0]
+    rows, reach, channels = side_ref.shape
+    cells = rows * reach
+    side = side_ref[...].reshape(cells, channels)
+    nothing = jnp.zeros_like(side)
+    inner = [
+        mid_ref[:, at * reach : (at + 1) * reach, :].reshape(cells, channels) for at in range(2)
+    ]
+    blocks = (
+        (inner[0], 2, jnp.where(core == 1, side, nothing), 0, ends_ref[0]),
+        (inner[0], 1, inner[1], 2, mid2_ref[:, 0:reach, :]),
+        (inner[0], 0, inner[1], 1, mid2_ref[:, reach : 2 * reach, :]),
+        (inner[1], 0, jnp.where(core == 0, side, nothing), 2, ends_ref[1]),
+    )
+    for block, (one, tap, two, other_tap, _) in enumerate(blocks):
+        at = slice(block * reach, (block + 1) * reach)
+        total[:, at, :] = acc_ref[:, at, :] + jnp.dot(
+            jnp.concatenate([one, two], axis=1),
+            jnp.concatenate([w_ref[tap], w_ref[other_tap]], axis=0),
+            preferred_element_type=jnp.float32,
+        ).reshape(rows, reach, channels)
+    leaving = [pltpu.make_async_copy(result.at[r], out_ref.at[r], sems.at[r]) for r in range(rows)]
+    for r in range(rows):
+        for block, (*_, current) in enumerate(blocks):
+            at = slice(block * reach, (block + 1) * reach)
+            result[r, at, :] = update(current[r], total[r, at, :], scale_ref[5:6, :])
+        leaving[r].start()
+    for copy in leaving:
+        copy.wait()
 
 
 def by_halves(context_map, norm_gains, conv_biases, conv_weights):
@@ -483,21 +508,26 @@
 
     near_rim, cross_far = lax.optimization_barrier((near_rim, cross_far))
     near_side = lax.ppermute(near_rim, "col", swap)
-    def plain(body, weights, out, operands, scratch):
+    def plain(body, weights, out, operands, scratch, more=()):
         return kernel_call(
             body,
             out,
             [smem_spec()] + [vmem_spec()] * (len(operands) + 2),
-            [pltpu.VMEM((rows, width, channels), kind) for width in scratch],
+            [pltpu.VMEM((rows, width, channels), kind) for width in scratch] + list(more),
         )(flags, scales, weights, *operands)
 
     def strip_shape(width, kind=kind):
         return jax.ShapeDtypeStruct((rows, width, channels), kind)
 
-    acc, x1 = plain(
+    acc, x1, far2, far_n = plain(
         partial_kernel,
         second_w,
-        (strip_shape(cols, jnp.float32), strip_shape(cols)),
+        (
+            strip_shape(cols, jnp.float32),
+            strip_shape(cols),
+            strip_shape(strip - step),
+            strip_shape(strip - step),
+        ),
         (near_n, mid_n, far_n, cross_far, near_side, near1, mid1, far1),
         (cols + 2 * step, cols + 2 * step),
     )
@@ -509,22 +539,37 @@
         (cross_near, cross_rim, cross_side, acc, x1),
         (reach + 2 * step,),
     )
-    near_n, cross_mid = lax.optimization_barrier((near_n, cross_mid))
+    sums, ends = plain(
+        sides_kernel,
+        last_w,
+        (
+            strip_shape(cols, jnp.float32),
+            jax.ShapeDtypeStruct((2, rows, reach, channels), kind),
+        ),
+        (near2, far2, near_n, far_n),
+        (),
+        [pltpu.VMEM((2, rows, reach, channels), kind)],
+    )
+    near_n, cross_mid, sums = lax.optimization_barrier((near_n, cross_mid, sums))
     last_side = lax.ppermute(near_n, "col", swap)
-    rest2, rest_n = plain(
-        rest_kernel,
+    mid2, mid_n = plain(
+        mid_kernel,
         second_w,
-        (strip_shape(cols - reach), strip_shape(cols - reach)),
+        (strip_shape(2 * reach), strip_shape(2 * reach)),
         (cross_mid, cross_near, acc, x1),
-        (cols - reach + 2 * step,),
-    )
-    return plain(
+        (2 * reach + 2 * step,),
+    )
+    return kernel_call(
         last_kernel,
-        last_w,
         strip_shape(cols),
-        (near2, rest2, near_n, rest_n, last_side),
-        (cols + 2 * reach, cols),
-    )
+        [smem_spec()] + [vmem_spec()] * 7,
+        [
+            pltpu.VMEM((rows, cols, channels), jnp.float32),
+            pltpu.VMEM((rows, cols, channels), kind),
+            pltpu.SemaphoreType.DMA((rows,)),
+        ],
+        any_spec(),
+    )(flags, scales, last_w, ends, mid2, mid_n, last_side, sums)
 
 
 def shards(context_map, *params):
@@ -537,8 +582,8 @@
         and rows == 2 * dilations[0]
         and dilations[1] % rows == 0
         and lax.axis_size("col") == 2
-        and cols >= 2 * strip + 3 * lane_pad
-        and cols % lane_pad == 0
+        and cols == 4 * dilations[2]
+        and dilations[2] == 2 * dilations[1]
     ):
         return by_halves(context_map, *params)
     return by_classes(context_map, *params)

time: 76.2 us -> 75.4 us (0.990)
  waiting for transfers between devices: 8.64 us -> 7.21 us
    pallas_call x0 -> x1, Pallas kernels: none -> 2.2 us  [by_halves(): kernel_call(last_kernel, strip_shape(cols), [smem_spec()] + [vmem_spec()]...]
    pallas_call x4, Pallas kernels: 8.19 us -> 6.52 us  [plain(): kernel_call(body, out, [smem_spec()] + [vmem_spec()] * (len(operands) + 2...]
    ppermute x1, waiting for transfers between devices: 4.47 us -> 3.28 us  [by_halves(): cross_mid = lax.ppermute(mid_n, 'row', partner)]
  transfers between devices with their start and end apart: 13 -> 13, of which waited for: 4 -> 3; matrix products, arithmetic and copies ran while one was open for 0% -> 0% of each run, Pallas kernels for 21% -> 23%
where the time goes in v7:
time: 75.4 us; the launch traced here: 75.1 us
  starting transfers between devices  43 us (57%)
  Pallas kernels  19.9 us (26%)
  waiting for transfers between devices  7.21 us (10%)
  local copies, waits for them, and re-layouts  4.59 us (6%)
    ppermute x1, starting transfers between devices, by_halves(): near_side = lax.ppermute(near_rim, 'col', swap)  13 us
    pallas_call x3, Pallas kernels, first_layer(): kernel_call(functools.partial(first_layer_kernel, segments, out_at, rows,...  8.55 us
    ppermute x1, starting transfers between devices, by_halves(): cross_rim = lax.ppermute(near_rim, 'row', partner)  6.66 us
    pallas_call x4, Pallas kernels, plain(): kernel_call(body, out, [smem_spec()] + [vmem_spec()] * (len(operands) + 2...  6.52 us
    unnamed x8, local copies, waits for them, and re-layouts  4.59 us
    ppermute x1, starting transfers between devices, by_halves(): above = lax.ppermute(low, 'row', within_down)  4 us
    ppermute x1, starting transfers between devices, by_halves(): above_far = lax.ppermute(far_low, 'row', down)  3.96 us
    ppermute x1, waiting for transfers between devices, by_halves(): cross_mid = lax.ppermute(mid_n, 'row', partner)  3.28 us
  transfers between devices with their start and end apart: 13, of which 3 were waited for; matrix products, arithmetic and copies ran while one was open for 0% of the time, Pallas kernels for 23%

profile of v7, /device:TPU:1, one launch (start us, length us, event | category | flops | bytes accessed | tf_op | source)
XLA Modules:
  0.0 75.1 jit_solution(1936330858140810354)
XLA Ops:
  0.0 0.1 pad_add_fusion.flag_ref
  0.1 0.0 copy-start.1
  0.1 1.2 %copy-done.1 = bf16[8,256,256]{2,1,0:T(8,128)(2,1)S(1)} copy-done((bf16[8,256,256]{2,1,0:T(8,128)(2,1)S(1)}, bf16[8,256,256]{2,1,0:T(8,128)(2,1)}, u32[]{:S(2)}) %copy-start.1) | copy-done | bytes 1048600
  1.3 0.7 shard_map.46
  2.0 4.0 %collective-permute-start.7 = (bf16[4,112,256]{2,1,0:T(8,128)(2,1)S(1)}, bf16[4,112,256]{2,1,0:T(8,128)(2,1)S(1)}, u32[]{:S(2)}, u32[]{:S(2)}) collective-permute-start(bf16[4,112,256]{2,1,0:T(8,128)(2,1)S(1)} %get-tuple-element.60), channel_id=1, source_target_pairs={{0,2},{2,4},{4,6},{6,8},{8,10},{10,12},{12,14},{1,3},{3,5},{5,7},{... | collective-permute-start | bytes 688136 | tf_op jit(solution)/shard_map/ppermute | solution.py:418
  6.0 1.3 %collective-permute-start.8 = (bf16[4,112,256]{2,1,0:T(8,128)(2,1)S(1)}, bf16[4,112,256]{2,1,0:T(8,128)(2,1)S(1)}, u32[]{:S(2)}, u32[]{:S(2)}) collective-permute-start(bf16[4,112,256]{2,1,0:T(8,128)(2,1)S(1)} %get-tuple-element.61), channel_id=1, source_target_pairs={{2,0},{4,2},{6,4},{8,6},{10,8},{12,10},{14,12},{3,1},{5,3},{7,5},{... | collective-permute-start | bytes 688136 | tf_op jit(solution)/shard_map/ppermute | solution.py:419
  7.3 0.0 copy-start
  7.3 2.0 %copy-done = bf16[3,3,3,256,256]{4,3,2,1,0:T(8,128)(2,1)S(1)} copy-done((bf16[3,3,3,256,256]{4,3,2,1,0:T(8,128)(2,1)S(1)}, bf16[3,3,3,256,256]{4,3,2,1,0:T(8,128)(2,1)}, u32[]{:S(2)}) %copy-start) | copy-done | bytes 3538968
  9.3 0.0 copy-start.2
  9.3 0.7 copy-done.2
  10.0 0.0 copy-start.3
  10.0 0.7 copy-done.3
  10.7 0.7 shard_map.47
  11.4 0.7 collective-permute-start.2
  12.1 4.0 %collective-permute-start = (bf16[4,144,256]{2,1,0:T(8,128)(2,1)S(1)}, bf16[4,144,256]{2,1,0:T(8,128)(2,1)S(1)}, u32[]{:S(2)}, u32[]{:S(2)}) collective-permute-start(bf16[4,144,256]{2,1,0:T(8,128)(2,1)S(1)} %get-tuple-element.53), channel_id=1, source_target_pairs={{0,2},{2,4},{4,6},{8,10},{10,12},{12,14},{1,3},{3,5},{5,7},{9,11},... | collective-permute-start | bytes 884744 | tf_op jit(solution)/shard_map/ppermute | solution.py:433
  16.1 1.3 %collective-permute-start.1 = (bf16[4,144,256]{2,1,0:T(8,128)(2,1)S(1)}, bf16[4,144,256]{2,1,0:T(8,128)(2,1)S(1)}, u32[]{:S(2)}, u32[]{:S(2)}) collective-permute-start(bf16[4,144,256]{2,1,0:T(8,128)(2,1)S(1)} %get-tuple-element.54), channel_id=1, source_target_pairs={{2,0},{4,2},{6,4},{10,8},{12,10},{14,12},{3,1},{5,3},{7,5},{11,9},... | collective-permute-start | bytes 884744 | tf_op jit(solution)/shard_map/ppermute | solution.py:434
  17.4 0.0 collective-permute-done.7.rest_1_
  17.4 0.0 collective-permute-done.8.rest_2_
  17.4 2.5 %shard_map.52 = (bf16[8,96,256]{2,1,0:T(8,128)(2,1)S(1)}, bf16[8,96,256]{2,1,0:T(8,128)(2,1)S(1)}) custom-call(s32[4]{0:T(128)S(1)} %pad_add_fusion.flag_ref, f32[6,256]{1,0:T(8,128)S(1)} %get-tuple-element.48.scale_ref, bf16[3,3,256,256]{3,2,1,0:T(8,128)(2,1)S(1)} %get-tuple-element.51.w_ref, bf16[8,112,256]{2,1,0:T(8,128)(2,1)S(1)} %get-tuple-element.63.rest_0_, ...), custom_call_target="tpu_custom_call" | custom-call | flops 1 | bytes 1 | tf_op jit(solution)/shard_map/pallas_call | solution.py:214
  19.9 3.1 %collective-permute-start.9 = (bf16[8,96,256]{2,1,0:T(8,128)(2,1)S(1)}, bf16[8,96,256]{2,1,0:T(8,128)(2,1)S(1)}, u32[]{:S(2)}, u32[]{:S(2)}) collective-permute-start(bf16[8,96,256]{2,1,0:T(8,128)(2,1)S(1)} %get-tuple-element.64.far_ref), channel_id=1, source_target_pairs={{0,8},{2,10},{4,12},{6,14},{8,0},{10,2},{12,4},{14,6},{1,9},{3,11}... | collective-permute-start | bytes 1179656 | tf_op jit(solution)/shard_map/ppermute | solution.py:448
  23.0 0.0 collective-permute-done.refs_1_.rest_1_.rest_3_
  23.0 2.9 %collective-permute-done.1.refs_2_.rest_2_.rest_4_ = bf16[4,144,256]{2,1,0:T(8,128)(2,1)S(1)} collective-permute-done((bf16[4,144,256]{2,1,0:T(8,128)(2,1)S(1)}, bf16[4,144,256]{2,1,0:T(8,128)(2,1)S(1)}, u32[]{:S(2)}, u32[]{:S(2)}) %collective-permute-start.1) | collective-permute-done | bytes 294944 | tf_op jit(solution)/shard_map/ppermute | solution.py:434
  25.9 0.0 collective-permute-done.2.refs_3_.rest_4_.rest_5_
  25.9 0.6 shard_map.48
  26.5 2.2 %collective-permute-start.3 = (bf16[16,16,256]{2,1,0:T(8,128)(2,1)S(1)}, bf16[16,16,256]{2,1,0:T(8,128)(2,1)S(1)}, u32[]{:S(2)}, u32[]{:S(2)}) collective-permute-start(bf16[16,16,256]{2,1,0:T(8,128)(2,1)S(1)} %shard_map.48), channel_id=1, source_target_pairs={{0,1},{1,0},{2,3},{3,2},{4,5},{5,4},{6,7},{7,6},{8,9},{9,8},{10,11... | collective-permute-start | bytes 393224 | tf_op jit(solution)/shard_map/ppermute | solution.py:462
  28.8 1.0 %collective-permute-done.3.rest_3_ = bf16[16,16,256]{2,1,0:T(8,128)(2,1)S(1)} collective-permute-done((bf16[16,16,256]{2,1,0:T(8,128)(2,1)S(1)}, bf16[16,16,256]{2,1,0:T(8,128)(2,1)S(1)}, u32[]{:S(2)}, u32[]{:S(2)}) %collective-permute-start.3) | collective-permute-done | bytes 131104 | tf_op jit(solution)/shard_map/ppermute | solution.py:462
  29.7 3.2 %shard_map.49 = (bf16[8,96,256]{2,1,0:T(8,128)(2,1)S(1)}, bf16[8,96,256]{2,1,0:T(8,128)(2,1)S(1)}) custom-call(s32[4]{0:T(128)S(1)} %pad_add_fusion.flag_ref, f32[6,256]{1,0:T(8,128)S(1)} %get-tuple-element.48.scale_ref, bf16[3,3,256,256]{3,2,1,0:T(8,128)(2,1)S(1)} %get-tuple-element.51.w_ref, bf16[8,112,256]{2,1,0:T(8,128)(2,1)S(1)} %get-tuple-element.52.refs_0_.rest_0_, ...), custom_call_target="tpu_custom_call" | custom-call | flops 1 | bytes 1 | tf_op jit(solution)/shard_map/pallas_call | solution.py:214
  32.9 0.6 shard_map.50
  33.5 6.7 %collective-permute-start.5 = (bf16[8,32,256]{2,1,0:T(8,128)(2,1)S(1)}, bf16[8,32,256]{2,1,0:T(8,128)(2,1)S(1)}, u32[]{:S(2)}, u32[]{:S(2)}) collective-permute-start(bf16[8,32,256]{2,1,0:T(8,128)(2,1)S(1)} %get-tuple-element.66), channel_id=1, source_target_pairs={{0,8},{2,10},{4,12},{6,14},{8,0},{10,2},{12,4},{14,6},{1,9},{3,11}... | collective-permute-start | bytes 393224 | tf_op jit(solution)/shard_map/ppermute | solution.py:483
  40.2 0.1 collective-permute-start.4
  40.3 2.8 %shard_map.51 = (bf16[8,64,256]{2,1,0:T(8,128)(2,1)S(1)}, bf16[8,64,256]{2,1,0:T(8,128)(2,1)S(1)}) custom-call(s32[4]{0:T(128)S(1)} %pad_add_fusion.flag_ref, f32[6,256]{1,0:T(8,128)S(1)} %get-tuple-element.48.scale_ref, bf16[3,3,256,256]{3,2,1,0:T(8,128)(2,1)S(1)} %get-tuple-element.51.w_ref, bf16[8,96,256]{2,1,0:T(8,128)(2,1)S(1)} %get-tuple-element.59.rest_0_, ...), custom_call_target="tpu_custom_call" | custom-call | flops 1 | bytes 1 | tf_op jit(solution)/shard_map/pallas_call | solution.py:214
  43.1 2.3 %collective-permute-start.11 = (bf16[8,64,256]{2,1,0:T(8,128)(2,1)S(1)}, bf16[8,64,256]{2,1,0:T(8,128)(2,1)S(1)}, u32[]{:S(2)}, u32[]{:S(2)}) collective-permute-start(bf16[8,64,256]{2,1,0:T(8,128)(2,1)S(1)} %get-tuple-element.62.mid_ref), channel_id=1, source_target_pairs={{0,8},{2,10},{4,12},{6,14},{8,0},{10,2},{12,4},{14,6},{1,9},{3,11}... | collective-permute-start | bytes 786440 | tf_op jit(solution)/shard_map/ppermute | solution.py:507
  45.5 0.0 collective-permute-done.9.cfar_ref
  45.5 13.0 %collective-permute-start.10 = (bf16[8,32,256]{2,1,0:T(8,128)(2,1)S(1)}, bf16[8,32,256]{2,1,0:T(8,128)(2,1)S(1)}, u32[]{:S(2)}, u32[]{:S(2)}) collective-permute-start(bf16[8,32,256]{2,1,0:T(8,128)(2,1)S(1)} %get-tuple-element.66), channel_id=1, source_target_pairs={{0,1},{1,0},{2,3},{3,2},{4,5},{5,4},{6,7},{7,6},{8,9},{9,8},{10,11... | collective-permute-start | bytes 393224 | tf_op jit(solution)/shard_map/ppermute | solution.py:510
  58.4 0.0 collective-permute-done.5.rim_ref
  58.4 2.8 %collective-permute-start.6 = (bf16[8,32,256]{2,1,0:T(8,128)(2,1)S(1)}, bf16[8,32,256]{2,1,0:T(8,128)(2,1)S(1)}, u32[]{:S(2)}, u32[]{:S(2)}) collective-permute-start(bf16[8,32,256]{2,1,0:T(8,128)(2,1)S(1)} %collective-permute-done.5.rim_ref), channel_id=1, source_target_pairs={{0,1},{1,0},{2,3},{3,2},{4,5},{5,4},{6,7},{7,6},{8,9},{9,8},{10,11... | collective-permute-start | bytes 393224 | tf_op jit(solution)/shard_map/ppermute | solution.py:534
  61.2 0.0 collective-permute-done.10.side_ref
  61.2 2.9 %shard_map.53 = (f32[8,256,256]{2,1,0:T(8,128)S(1)}, bf16[8,256,256]{2,1,0:T(8,128)(2,1)S(1)}, bf16[8,64,256]{2,1,0:T(8,128)(2,1)S(1)}, bf16[8,64,256]{2,1,0:T(8,128)(2,1)S(1)}) custom-call(s32[4]{0:T(128)S(1)} %pad_add_fusion.flag_ref, f32[6,256]{1,0:T(8,128)S(1)} %get-tuple-element.48.scale_ref, bf16[2,3,256,256]{3,2,1,0:T(8,128)(2,1)S(1)} %get-tuple-element.50.w_ref, ...), custom_call_target="tpu_custom_call" | custom-call | flops 1 | bytes 1 | tf_op jit(solution)/shard_map/pallas_call | solution.py:512
  64.1 0.0 collective-permute-done.6.side_ref
  64.1 0.0 collective-permute-done.4.cnear_ref
  64.1 1.1 %shard_map.54 = (bf16[8,64,256]{2,1,0:T(8,128)(2,1)S(1)}, bf16[8,64,256]{2,1,0:T(8,128)(2,1)S(1)}) custom-call(s32[4]{0:T(128)S(1)} %pad_add_fusion.flag_ref, f32[6,256]{1,0:T(8,128)S(1)} %get-tuple-element.48.scale_ref, bf16[2,3,256,256]{3,2,1,0:T(8,128)(2,1)S(1)} %get-tuple-element.50.w_ref, bf16[8,64,256]{2,1,0:T(8,128)(2,1)S(1)} %collective-permute-done.4.cnear_ref, ...), custom_call_target="tpu_custom_call" | custom-call | flops 1 | bytes 1 | tf_op jit(solution)/shard_map/pallas_call | solution.py:512
  65.3 1.0 %shard_map.55 = (f32[8,256,256]{2,1,0:T(8,128)S(1)}, bf16[2,8,64,256]{3,2,1,0:T(8,128)(2,1)S(1)}) custom-call(s32[4]{0:T(128)S(1)} %pad_add_fusion.flag_ref, f32[6,256]{1,0:T(8,128)S(1)} %get-tuple-element.48.scale_ref, bf16[3,256,256]{2,1,0:T(8,128)(2,1)S(1)} %get-tuple-element.49.w_ref, bf16[8,64,256]{2,1,0:T(8,128)(2,1)S(1)} %get-tuple-element.72.near2_ref, ...), custom_call_target="tpu_custom_call" | custom-call | flops 1 | bytes 1 | tf_op jit(solution)/shard_map/pallas_call | solution.py:512
  66.3 3.3 %collective-permute-done.11.cmid_ref = bf16[8,64,256]{2,1,0:T(8,128)(2,1)S(1)} collective-permute-done((bf16[8,64,256]{2,1,0:T(8,128)(2,1)S(1)}, bf16[8,64,256]{2,1,0:T(8,128)(2,1)S(1)}, u32[]{:S(2)}, u32[]{:S(2)}) %collective-permute-start.11) | collective-permute-done | bytes 262176 | tf_op jit(solution)/shard_map/ppermute | solution.py:507
  69.6 1.6 %collective-permute-start.12 = (bf16[8,64,256]{2,1,0:T(8,128)(2,1)S(1)}, bf16[8,64,256]{2,1,0:T(8,128)(2,1)S(1)}, u32[]{:S(2)}, u32[]{:S(2)}) collective-permute-start(bf16[8,64,256]{2,1,0:T(8,128)(2,1)S(1)} %get-tuple-element.81.near_ref), channel_id=1, source_target_pairs={{0,1},{1,0},{2,3},{3,2},{4,5},{5,4},{6,7},{7,6},{8,9},{9,8},{10,11... | collective-permute-start | bytes 786440 | tf_op jit(solution)/shard_map/ppermute | solution.py:554
  71.2 1.5 %shard_map.56 = (bf16[8,128,256]{2,1,0:T(8,128)(2,1)S(1)}, bf16[8,128,256]{2,1,0:T(8,128)(2,1)S(1)}) custom-call(s32[4]{0:T(128)S(1)} %pad_add_fusion.flag_ref, f32[6,256]{1,0:T(8,128)S(1)} %get-tuple-element.48.scale_ref, bf16[2,3,256,256]{3,2,1,0:T(8,128)(2,1)S(1)} %get-tuple-element.50.w_ref, bf16[8,64,256]{2,1,0:T(8,128)(2,1)S(1)} %collective-permute-done.11.cmid_ref, ...), custom_call_target="tpu_custom_call" | custom-call | flops 1 | bytes 1 | tf_op jit(solution)/shard_map/pallas_call | solution.py:512
  72.7 0.0 collective-permute-done.12.side_ref
  72.7 2.2 %shard_map.57 = bf16[8,256,256]{2,1,0:T(8,128)(2,1)} custom-call(s32[4]{0:T(128)S(1)} %pad_add_fusion.flag_ref, f32[6,256]{1,0:T(8,128)S(1)} %get-tuple-element.48.scale_ref, bf16[3,256,256]{2,1,0:T(8,128)(2,1)S(1)} %get-tuple-element.49.w_ref, bf16[2,8,64,256]{3,2,1,0:T(8,128)(2,1)S(1)} %get-tuple-element.76.ends_ref, ...), custom_call_target="tpu_custom_call" | custom-call | flops 1 | bytes 1 | tf_op jit(solution)/shard_map/pallas_call | solution.py:562
Async XLA Ops:
  0.1 1.2 %copy-start.1 = (bf16[8,256,256]{2,1,0:T(8,128)(2,1)S(1)}, bf16[8,256,256]{2,1,0:T(8,128)(2,1)}, u32[]{:S(2)}) copy-start(bf16[8,256,256]{2,1,0:T(8,128)(2,1)} %refs_0_.1) | copy-start | bytes 3145732
  2.0 15.4 %collective-permute-start.7 = (bf16[4,112,256]{2,1,0:T(8,128)(2,1)S(1)}, bf16[4,112,256]{2,1,0:T(8,128)(2,1)S(1)}, u32[]{:S(2)}, u32[]{:S(2)}) collective-permute-start(bf16[4,112,256]{2,1,0:T(8,128)(2,1)S(1)} %get-tuple-element.60), channel_id=1, source_target_pairs={{0,2},{2,4},{4,6},{6,8},{8,10},{10,12},{12,14},{1,3},{3,5},{5,7},{... | collective-permute-start | bytes 688136 | tf_op jit(solution)/shard_map/ppermute | solution.py:418
  6.0 11.4 %collective-permute-start.8 = (bf16[4,112,256]{2,1,0:T(8,128)(2,1)S(1)}, bf16[4,112,256]{2,1,0:T(8,128)(2,1)S(1)}, u32[]{:S(2)}, u32[]{:S(2)}) collective-permute-start(bf16[4,112,256]{2,1,0:T(8,128)(2,1)S(1)} %get-tuple-element.61), channel_id=1, source_target_pairs={{2,0},{4,2},{6,4},{8,6},{10,8},{12,10},{14,12},{3,1},{5,3},{7,5},{... | collective-permute-start | bytes 688136 | tf_op jit(solution)/shard_map/ppermute | solution.py:419
  7.3 2.0 %copy-start = (bf16[3,3,3,256,256]{4,3,2,1,0:T(8,128)(2,1)S(1)}, bf16[3,3,3,256,256]{4,3,2,1,0:T(8,128)(2,1)}, u32[]{:S(2)}) copy-start(bf16[3,3,3,256,256]{4,3,2,1,0:T(8,128)(2,1)} %w_ref.1) | copy-start | bytes 10616836
  9.3 0.7 copy-start.2
  10.0 0.7 copy-start.3
  11.4 14.6 %collective-permute-start.2 = (bf16[4,160,256]{2,1,0:T(8,128)(2,1)S(1)}, bf16[4,160,256]{2,1,0:T(8,128)(2,1)S(1)}, u32[]{:S(2)}, u32[]{:S(2)}) collective-permute-start(bf16[4,160,256]{2,1,0:T(8,128)(2,1)S(1)} %get-tuple-element.55), channel_id=1, source_target_pairs={{6,8},{8,6},{7,9},{9,7},{22,24},{24,22},{23,25},{25,23}} | collective-permute-start | bytes 983048 | tf_op jit(solution)/shard_map/ppermute | solution.py:435
  12.1 10.9 %collective-permute-start = (bf16[4,144,256]{2,1,0:T(8,128)(2,1)S(1)}, bf16[4,144,256]{2,1,0:T(8,128)(2,1)S(1)}, u32[]{:S(2)}, u32[]{:S(2)}) collective-permute-start(bf16[4,144,256]{2,1,0:T(8,128)(2,1)S(1)} %get-tuple-element.53), channel_id=1, source_target_pairs={{0,2},{2,4},{4,6},{8,10},{10,12},{12,14},{1,3},{3,5},{5,7},{9,11},... | collective-permute-start | bytes 884744 | tf_op jit(solution)/shard_map/ppermute | solution.py:433
  16.1 9.8 %collective-permute-start.1 = (bf16[4,144,256]{2,1,0:T(8,128)(2,1)S(1)}, bf16[4,144,256]{2,1,0:T(8,128)(2,1)S(1)}, u32[]{:S(2)}, u32[]{:S(2)}) collective-permute-start(bf16[4,144,256]{2,1,0:T(8,128)(2,1)S(1)} %get-tuple-element.54), channel_id=1, source_target_pairs={{2,0},{4,2},{6,4},{10,8},{12,10},{14,12},{3,1},{5,3},{7,5},{11,9},... | collective-permute-start | bytes 884744 | tf_op jit(solution)/shard_map/ppermute | solution.py:434
  19.9 25.5 %collective-permute-start.9 = (bf16[8,96,256]{2,1,0:T(8,128)(2,1)S(1)}, bf16[8,96,256]{2,1,0:T(8,128)(2,1)S(1)}, u32[]{:S(2)}, u32[]{:S(2)}) collective-permute-start(bf16[8,96,256]{2,1,0:T(8,128)(2,1)S(1)} %get-tuple-element.64.far_ref), channel_id=1, source_target_pairs={{0,8},{2,10},{4,12},{6,14},{8,0},{10,2},{12,4},{14,6},{1,9},{3,11}... | collective-permute-start | bytes 1179656 | tf_op jit(solution)/shard_map/ppermute | solution.py:448
  26.5 3.2 %collective-permute-start.3 = (bf16[16,16,256]{2,1,0:T(8,128)(2,1)S(1)}, bf16[16,16,256]{2,1,0:T(8,128)(2,1)S(1)}, u32[]{:S(2)}, u32[]{:S(2)}) collective-permute-start(bf16[16,16,256]{2,1,0:T(8,128)(2,1)S(1)} %shard_map.48), channel_id=1, source_target_pairs={{0,1},{1,0},{2,3},{3,2},{4,5},{5,4},{6,7},{7,6},{8,9},{9,8},{10,11... | collective-permute-start | bytes 393224 | tf_op jit(solution)/shard_map/ppermute | solution.py:462
  33.5 24.9 %collective-permute-start.5 = (bf16[8,32,256]{2,1,0:T(8,128)(2,1)S(1)}, bf16[8,32,256]{2,1,0:T(8,128)(2,1)S(1)}, u32[]{:S(2)}, u32[]{:S(2)}) collective-permute-start(bf16[8,32,256]{2,1,0:T(8,128)(2,1)S(1)} %get-tuple-element.66), channel_id=1, source_target_pairs={{0,8},{2,10},{4,12},{6,14},{8,0},{10,2},{12,4},{14,6},{1,9},{3,11}... | collective-permute-start | bytes 393224 | tf_op jit(solution)/shard_map/ppermute | solution.py:483
  40.2 23.9 %collective-permute-start.4 = (bf16[8,64,256]{2,1,0:T(8,128)(2,1)S(1)}, bf16[8,64,256]{2,1,0:T(8,128)(2,1)S(1)}, u32[]{:S(2)}, u32[]{:S(2)}) collective-permute-start(bf16[8,64,256]{2,1,0:T(8,128)(2,1)S(1)} %get-tuple-element.57), channel_id=1, source_target_pairs={{0,8},{2,10},{4,12},{6,14},{8,0},{10,2},{12,4},{14,6},{1,9},{3,11}... | collective-permute-start | bytes 786440 | tf_op jit(solution)/shard_map/ppermute | solution.py:484
  43.1 26.5 %collective-permute-start.11 = (bf16[8,64,256]{2,1,0:T(8,128)(2,1)S(1)}, bf16[8,64,256]{2,1,0:T(8,128)(2,1)S(1)}, u32[]{:S(2)}, u32[]{:S(2)}) collective-permute-start(bf16[8,64,256]{2,1,0:T(8,128)(2,1)S(1)} %get-tuple-element.62.mid_ref), channel_id=1, source_target_pairs={{0,8},{2,10},{4,12},{6,14},{8,0},{10,2},{12,4},{14,6},{1,9},{3,11}... | collective-permute-start | bytes 786440 | tf_op jit(solution)/shard_map/ppermute | solution.py:507
  45.5 15.8 %collective-permute-start.10 = (bf16[8,32,256]{2,1,0:T(8,128)(2,1)S(1)}, bf16[8,32,256]{2,1,0:T(8,128)(2,1)S(1)}, u32[]{:S(2)}, u32[]{:S(2)}) collective-permute-start(bf16[8,32,256]{2,1,0:T(8,128)(2,1)S(1)} %get-tuple-element.66), channel_id=1, source_target_pairs={{0,1},{1,0},{2,3},{3,2},{4,5},{5,4},{6,7},{7,6},{8,9},{9,8},{10,11... | collective-permute-start | bytes 393224 | tf_op jit(solution)/shard_map/ppermute | solution.py:510
  58.4 5.7 %collective-permute-start.6 = (bf16[8,32,256]{2,1,0:T(8,128)(2,1)S(1)}, bf16[8,32,256]{2,1,0:T(8,128)(2,1)S(1)}, u32[]{:S(2)}, u32[]{:S(2)}) collective-permute-start(bf16[8,32,256]{2,1,0:T(8,128)(2,1)S(1)} %collective-permute-done.5.rim_ref), channel_id=1, source_target_pairs={{0,1},{1,0},{2,3},{3,2},{4,5},{5,4},{6,7},{7,6},{8,9},{9,8},{10,11... | collective-permute-start | bytes 393224 | tf_op jit(solution)/shard_map/ppermute | solution.py:534
  69.6 3.1 %collective-permute-start.12 = (bf16[8,64,256]{2,1,0:T(8,128)(2,1)S(1)}, bf16[8,64,256]{2,1,0:T(8,128)(2,1)S(1)}, u32[]{:S(2)}, u32[]{:S(2)}) collective-permute-start(bf16[8,64,256]{2,1,0:T(8,128)(2,1)S(1)} %get-tuple-element.81.near_ref), channel_id=1, source_target_pairs={{0,1},{1,0},{2,3},{3,2},{4,5},{5,4},{6,7},{7,6},{8,9},{9,8},{10,11... | collective-permute-start | bytes 786440 | tf_op jit(solution)/shard_map/ppermute | solution.py:554

commit v8 on v7

--- a/solution.py
+++ b/solution.py
@@ -341,36 +341,41 @@
 
 
 def last_kernel(
-    flag_ref, scale_ref, w_ref, ends_ref, mid2_ref, mid_ref, side_ref, acc_ref, out_ref, total,
-    result, sems,
+    flag_ref, scale_ref, w_ref, ends_ref, mid2_ref, mid_ref, side_ref, acc_ref, out_ref, result, sems
 ):
     core = flag_ref[0]
     rows, reach, channels = side_ref.shape
-    cells = rows * reach
-    side = side_ref[...].reshape(cells, channels)
-    nothing = jnp.zeros_like(side)
-    inner = [
-        mid_ref[:, at * reach : (at + 1) * reach, :].reshape(cells, channels) for at in range(2)
-    ]
-    blocks = (
-        (inner[0], 2, jnp.where(core == 1, side, nothing), 0, ends_ref[0]),
-        (inner[0], 1, inner[1], 2, mid2_ref[:, 0:reach, :]),
-        (inner[0], 0, inner[1], 1, mid2_ref[:, reach : 2 * reach, :]),
-        (inner[1], 0, jnp.where(core == 0, side, nothing), 2, ends_ref[1]),
-    )
-    for block, (one, tap, two, other_tap, _) in enumerate(blocks):
-        at = slice(block * reach, (block + 1) * reach)
-        total[:, at, :] = acc_ref[:, at, :] + jnp.dot(
-            jnp.concatenate([one, two], axis=1),
-            jnp.concatenate([w_ref[tap], w_ref[other_tap]], axis=0),
-            preferred_element_type=jnp.float32,
-        ).reshape(rows, reach, channels)
-    leaving = [pltpu.make_async_copy(result.at[r], out_ref.at[r], sems.at[r]) for r in range(rows)]
-    for r in range(rows):
-        for block, (*_, current) in enumerate(blocks):
+    group = 2
+    leaving = []
+    for first in range(0, rows, group):
+        some = slice(first, first + group)
+        cells = group * reach
+        side = side_ref[some].reshape(cells, channels)
+        nothing = jnp.zeros_like(side)
+        inner = [
+            mid_ref[some, at * reach : (at + 1) * reach, :].reshape(cells, channels)
+            for at in range(2)
+        ]
+        blocks = (
+            (inner[0], 2, jnp.where(core == 1, side, nothing), 0, ends_ref[0, some]),
+            (inner[0], 1, inner[1], 2, mid2_ref[some, 0:reach, :]),
+            (inner[0], 0, inner[1], 1, mid2_ref[some, reach : 2 * reach, :]),
+            (inner[1], 0, jnp.where(core == 0, side, nothing), 2, ends_ref[1, some]),
+        )
+        for block, (one, tap, two, other_tap, current) in enumerate(blocks):
             at = slice(block * reach, (block + 1) * reach)
-            result[r, at, :] = update(current[r], total[r, at, :], scale_ref[5:6, :])
-        leaving[r].start()
+            response = acc_ref[some, at, :].reshape(cells, channels) + jnp.dot(
+                jnp.concatenate([one, two], axis=1),
+                jnp.concatenate([w_ref[tap], w_ref[other_tap]], axis=0),
+                preferred_element_type=jnp.float32,
+            )
+            result[some, at, :] = update(
+                current.reshape(cells, channels), response, scale_ref[5:6, :]
+            ).reshape(group, reach, channels)
+        leaving.append(
+            pltpu.make_async_copy(result.at[some], out_ref.at[some], sems.at[first // group])
+        )
+        leaving[-1].start()
     for copy in leaving:
         copy.wait()
 
@@ -388,15 +393,26 @@
     wide = strip + pad
     core, row = lax.axis_index("col"), lax.axis_index("row")
     upper_half = row < group
+    parity = row % 2
     flags = jnp.stack(
-        [core, row == group - 1, row == group, jnp.where(upper_half, 2, 0)]
+        [
+            core,
+            row == group - 1,
+            row == group,
+            jnp.where(upper_half, 2, 0),
+            parity,
+            jnp.where(row == group, 3, 2 - parity),
+            jnp.where(row == group - 1, 3, 1 + parity),
+        ]
     ).astype(jnp.int32)
+    even, odd = (4, 0), (4, 1)
+    above_in, below_in = ([(flag, which) for which in (1, 2, 3)] for flag in (5, 6))
     swap = [(0, 1), (1, 0)]
     partner = [(i, (i + group) % size) for i in range(size)]
-    down = [(i, i + 1) for i in range(size - 1)]
-    up = [(j, i) for i, j in down]
-    within_down = [(i, j) for i, j in down if j != group]
-    within_up = [(j, i) for i, j in within_down]
+    first_pairs = [(i, i ^ 1) for i in range(size)]
+    second_pairs = [(i, ((i + 1) ^ 1) - 1) for i in range(1, size - 1)]
+    across = [(group - 1, group), (group, group - 1)]
+    second_within = [pair for pair in second_pairs if pair not in across]
 
     far_wide_at, near_wide_at = (0, cols - wide), (cols - wide, 0)
     span, span_at = cols - wide, (wide, 0)
@@ -405,18 +421,22 @@
         (None, 0, 0, rows, far_wide_at, wide, 0, 0),
         (None, 0, 0, rows, near_wide_at, wide, 1, 0),
         (None, 0, 0, rows, (strip - pad, strip - pad), mid + 2 * pad, 2, 0),
-        (None, 0, half, half, far_wide_at, wide, 3, 0),
-        (None, 0, 0, half, far_wide_at, wide, 4, 0),
-        (None, 0, half, half, span_at, span, 5, 0),
-        (None, 0, 0, half, span_at, span, 6, 0),
+        (even, 0, half, half, far_wide_at, wide, 3, 0),
+        (odd, 0, 0, half, far_wide_at, wide, 3, 0),
+        (even, 0, 0, half, far_wide_at, wide, 4, 0),
+        (odd, 0, half, half, far_wide_at, wide, 4, 0),
+        (even, 0, half, half, span_at, span, 5, 0),
+        (odd, 0, 0, half, span_at, span, 5, 0),
+        (even, 0, 0, half, span_at, span, 6, 0),
+        (odd, 0, half, half, span_at, span, 6, 0),
         ((1, 1), 0, half, half, middle_at, span + pad, 7, 0),
         ((1, 0), 0, 0, half, middle_at, span + pad, 7, 0),
     )
     (
-        far_x, near_x, mid_x, far_low, far_high, low, high, middle
+        far_x, near_x, mid_x, far_one, far_two, one, two, middle
     ) = copies(flags, (context_map,), parts)
-    above_far = lax.ppermute(far_low, "row", down)
-    below_far = lax.ppermute(far_high, "row", up)
+    far_one = lax.ppermute(far_one, "row", first_pairs)
+    far_two = lax.ppermute(far_two, "row", second_pairs)
     tail = conv_weights.shape[2:]
     scales, first_w, second_w, last_w = kernel_call(
         hold_kernel,
@@ -429,48 +449,54 @@
         [smem_spec()] + [vmem_spec()] * 3,
         [],
     )(flags, norm_gains, conv_biases, conv_weights)
-    low, high, middle, scales = lax.optimization_barrier((low, high, middle, scales))
-    above = lax.ppermute(low, "row", within_down)
-    below = lax.ppermute(high, "row", within_up)
-    middle = lax.ppermute(middle, "row", [(group - 1, group), (group, group - 1)])
+    one, two, middle, scales = lax.optimization_barrier((one, two, middle, scales))
+    one = lax.ppermute(one, "row", first_pairs)
+    two = lax.ppermute(two, "row", second_within)
+    middle = lax.ppermute(middle, "row", across)
 
     params = (scales, first_w)
     far_body, far_edge = (pad, 0), (0, wide)
     far_segments = (
         (None, 0, 0, half, rows, (0, 0), far_body, wide),
-        (None, 1, 0, 0, half, (0, 0), far_body, wide),
-        (None, 2, 0, half + rows, half, (0, 0), far_body, wide),
+        (odd, 1, 0, 0, half, (0, 0), far_body, wide),
+        (even, 2, 0, 0, half, (0, 0), far_body, wide),
+        (even, 1, 0, half + rows, half, (0, 0), far_body, wide),
+        (odd, 2, 0, half + rows, half, (0, 0), far_body, wide),
         (None, None, 0, 0, 2 * rows, (0, 0), far_edge, pad),
     )
     far1, far_n = first_layer(
-        flags, params, (far_x, above_far, below_far), far_segments, (0, pad), strip
+        flags, params, (far_x, far_one, far_two), far_segments, (0, pad), strip
     )
     cross_far = lax.ppermute(far_n, "row", partner)
 
     near_end, span_end, middle_end = (wide - pad, 0), (span - pad, 0), (span, 0)
     (rim,) = copies(
         flags,
-        (near_x, above, below, middle),
+        (near_x, one, two, middle),
         (
-            ((2, 0), 1, 0, half, span_end, pad, 0, 0),
-            ((2, 1), 3, 0, half, middle_end, pad, 0, 0),
+            (above_in[0], 1, 0, half, span_end, pad, 0, 0),
+            (above_in[1], 2, 0, half, span_end, pad, 0, 0),
+            (above_in[2], 3, 0, half, middle_end, pad, 0, 0),
             (None, 0, 0, rows, near_end, pad, 0, half),
-            ((1, 0), 2, 0, half, span_end, pad, 0, half + rows),
-            ((1, 1), 3, 0, half, middle_end, pad, 0, half + rows),
+            (below_in[0], 1, 0, half, span_end, pad, 0, half + rows),
+            (below_in[1], 2, 0, half, span_end, pad, 0, half + rows),
+            (below_in[2], 3, 0, half, middle_end, pad, 0, half + rows),
         ),
     )
     rim = lax.ppermute(rim, "col", swap)
     near_body, near_span, near_middle = (0, pad), (span - wide, 0), (span + pad - wide, 0)
     near_segments = (
         (None, 0, 0, half, rows, (0, 0), near_body, wide),
-        ((2, 0), 1, 0, 0, half, near_span, near_body, wide),
-        ((2, 1), 4, 0, 0, half, near_middle, near_body, wide),
-        ((1, 0), 2, 0, half + rows, half, near_span, near_body, wide),
-        ((1, 1), 4, 0, half + rows, half, near_middle, near_body, wide),
+        (above_in[0], 1, 0, 0, half, near_span, near_body, wide),
+        (above_in[1], 2, 0, 0, half, near_span, near_body, wide),
+        (above_in[2], 4, 0, 0, half, near_middle, near_body, wide),
+        (below_in[0], 1, 0, half + rows, half, near_span, near_body, wide),
+        (below_in[1], 2, 0, half + rows, half, near_span, near_body, wide),
+        (below_in[2], 4, 0, half + rows, half, near_middle, near_body, wide),
         (None, 3, 0, 0, 2 * rows, (0, 0), (wide, 0), pad),
     )
     near1, near_n = first_layer(
-        flags, params, (near_x, above, below, rim, middle), near_segments, (pad, 0), strip
+        flags, params, (near_x, one, two, rim, middle), near_segments, (pad, 0), strip
     )
     near_rim, near_rest = copies(
         flags,
@@ -482,23 +508,27 @@
     )
     cross_rim = lax.ppermute(near_rim, "row", partner)
     cross_near = lax.ppermute(near_rest, "row", partner)
-    two = 2 * pad
-    far_side, rest_side = ((wide - two, 0), (0, mid)), ((0, span - mid), (two, 0))
-    middle_side = ((pad, span - mid), (two, 0))
+    side_pads = 2 * pad
+    far_side, rest_side = ((wide - side_pads, 0), (0, mid)), ((0, span - mid), (side_pads, 0))
+    middle_side = ((pad, span - mid), (side_pads, 0))
     mid_segments = (
-        (None, 0, 0, half, rows, (0, 0), (0, 0), mid + two),
-        (None, 1, 0, 0, half, *far_side, two),
-        (None, 2, 0, half + rows, half, *far_side, two),
-        ((2, 0), 3, 0, 0, half, *rest_side, mid),
-        ((2, 1), 5, 0, 0, half, *middle_side, mid),
-        ((1, 0), 4, 0, half + rows, half, *rest_side, mid),
-        ((1, 1), 5, 0, half + rows, half, *middle_side, mid),
+        (None, 0, 0, half, rows, (0, 0), (0, 0), mid + side_pads),
+        (odd, 1, 0, 0, half, *far_side, side_pads),
+        (even, 2, 0, 0, half, *far_side, side_pads),
+        (even, 1, 0, half + rows, half, *far_side, side_pads),
+        (odd, 2, 0, half + rows, half, *far_side, side_pads),
+        (above_in[0], 3, 0, 0, half, *rest_side, mid),
+        (above_in[1], 4, 0, 0, half, *rest_side, mid),
+        (above_in[2], 5, 0, 0, half, *middle_side, mid),
+        (below_in[0], 3, 0, half + rows, half, *rest_side, mid),
+        (below_in[1], 4, 0, half + rows, half, *rest_side, mid),
+        (below_in[2], 5, 0, half + rows, half, *middle_side, mid),
     )
     mid1, mid_n = first_layer(
         flags,
         params,
         (
-            mid_x, above_far, below_far, above, below, middle
+            mid_x, far_one, far_two, one, two, middle
         ),
         mid_segments,
         (pad, pad),
@@ -564,7 +594,6 @@
         strip_shape(cols),
         [smem_spec()] + [vmem_spec()] * 7,
         [
-            pltpu.VMEM((rows, cols, channels), jnp.float32),
             pltpu.VMEM((rows, cols, channels), kind),
             pltpu.SemaphoreType.DMA((rows,)),
         ],

time: 75.4 us -> 74.5 us (0.988)
  starting transfers between devices: 43 us -> 29.8 us
  waiting for transfers between devices: 7.21 us -> 19 us
    ppermute x1, waiting for transfers between devices: 0.01 us -> 11.4 us  [by_halves(): cross_far = lax.ppermute(far_n, 'row', partner)]
    ppermute x1, starting transfers between devices: 13 us -> 3.82 us  [by_halves(): near_side = lax.ppermute(near_rim, 'col', swap)]
    ppermute x5, starting transfers between devices: 11.2 us -> 7.9 us  [the longest x1 3.78 us: by_halves(): one = lax.ppermute(one, 'row', first_pairs)]
    ppermute x1, starting transfers between devices: 6.66 us -> 4.36 us  [by_halves(): cross_rim = lax.ppermute(near_rim, 'row', partner)]
    ppermute x5, waiting for transfers between devices: 2.93 us -> 4.21 us  [the longest x1 4.2 us: by_halves(): one = lax.ppermute(one, 'row', first_pairs)]
    ppermute x1, waiting for transfers between devices: 3.28 us -> 2.35 us  [by_halves(): cross_mid = lax.ppermute(mid_n, 'row', partner)]
  transfers between devices with their start and end apart: 13 -> 13, of which waited for: 3 -> 4; matrix products, arithmetic and copies ran while one was open for 0% -> 0% of each run, Pallas kernels for 23% -> 24%
where the time goes in v8:
time: 74.5 us; the launch traced here: 74.2 us
  starting transfers between devices  29.8 us (40%)
  Pallas kernels  20.4 us (27%)
  waiting for transfers between devices  19 us (26%)
  local copies, waits for them, and re-layouts  4.68 us (6%)
    ppermute x1, waiting for transfers between devices, by_halves(): cross_far = lax.ppermute(far_n, 'row', partner)  11.4 us
    pallas_call x3, Pallas kernels, first_layer(): kernel_call(functools.partial(first_layer_kernel, segments, out_at, rows,...  9.08 us
    pallas_call x4, Pallas kernels, plain(): kernel_call(body, out, [smem_spec()] + [vmem_spec()] * (len(operands) + 2...  6.51 us
    unnamed x8, local copies, waits for them, and re-layouts  4.59 us
    ppermute x1, starting transfers between devices, by_halves(): cross_rim = lax.ppermute(near_rim, 'row', partner)  4.36 us
    ppermute x1, waiting for transfers between devices, by_halves(): one = lax.ppermute(one, 'row', first_pairs)  4.2 us
    ppermute x1, starting transfers between devices, by_halves(): near_side = lax.ppermute(near_rim, 'col', swap)  3.82 us
    ppermute x1, starting transfers between devices, by_halves(): one = lax.ppermute(one, 'row', first_pairs)  3.78 us
  transfers between devices with their start and end apart: 13, of which 4 were waited for; matrix products, arithmetic and copies ran while one was open for 0% of the time, Pallas kernels for 24%

profile of v8, /device:TPU:1, one launch (start us, length us, event | category | flops | bytes accessed | tf_op | source)
XLA Modules:
  0.0 74.2 jit_solution(10780170546857728859)
XLA Ops:
  0.0 0.1 stack.39.flag_ref
  0.1 0.0 copy-start.1
  0.1 1.2 %copy-done.1 = bf16[8,256,256]{2,1,0:T(8,128)(2,1)S(1)} copy-done((bf16[8,256,256]{2,1,0:T(8,128)(2,1)S(1)}, bf16[8,256,256]{2,1,0:T(8,128)(2,1)}, u32[]{:S(2)}) %copy-start.1) | copy-done | bytes 1048600
  1.3 0.8 %shard_map.46 = (bf16[8,112,256]{2,1,0:T(8,128)(2,1)S(1)}, bf16[8,112,256]{2,1,0:T(8,128)(2,1)S(1)}, bf16[8,96,256]{2,1,0:T(8,128)(2,1)S(1)}, bf16[4,112,256]{2,...) custom-call(s32[7]{0:T(128)S(1)} %stack.39.flag_ref, ...), custom_call_target="tpu_custom_call" | custom-call | flops 1 | bytes 1 | tf_op jit(solution)/shard_map/pallas_call | solution.py:150
  2.1 2.1 %collective-permute-start.7 = (bf16[4,112,256]{2,1,0:T(8,128)(2,1)S(1)}, bf16[4,112,256]{2,1,0:T(8,128)(2,1)S(1)}, u32[]{:S(2)}, u32[]{:S(2)}) collective-permute-start(bf16[4,112,256]{2,1,0:T(8,128)(2,1)S(1)} %get-tuple-element.60), channel_id=1, source_target_pairs={{0,2},{2,0},{4,6},{6,4},{8,10},{10,8},{12,14},{14,12},{1,3},{3,1},... | collective-permute-start | bytes 688136 | tf_op jit(solution)/shard_map/ppermute | solution.py:438
  4.2 0.7 collective-permute-start.8
  4.9 0.0 copy-start
  4.9 2.0 %copy-done = bf16[3,3,3,256,256]{4,3,2,1,0:T(8,128)(2,1)S(1)} copy-done((bf16[3,3,3,256,256]{4,3,2,1,0:T(8,128)(2,1)S(1)}, bf16[3,3,3,256,256]{4,3,2,1,0:T(8,128)(2,1)}, u32[]{:S(2)}) %copy-start) | copy-done | bytes 3538968
  6.9 0.0 copy-start.2
  6.9 0.7 copy-done.2
  7.6 0.0 copy-start.3
  7.6 0.7 copy-done.3
  8.3 0.7 shard_map.47
  9.0 0.7 collective-permute-start.2
  9.7 3.8 %collective-permute-start = (bf16[4,144,256]{2,1,0:T(8,128)(2,1)S(1)}, bf16[4,144,256]{2,1,0:T(8,128)(2,1)S(1)}, u32[]{:S(2)}, u32[]{:S(2)}) collective-permute-start(bf16[4,144,256]{2,1,0:T(8,128)(2,1)S(1)} %get-tuple-element.53), channel_id=1, source_target_pairs={{0,2},{2,0},{4,6},{6,4},{8,10},{10,8},{12,14},{14,12},{1,3},{3,1},... | collective-permute-start | bytes 884744 | tf_op jit(solution)/shard_map/ppermute | solution.py:453
  13.4 0.7 collective-permute-start.1
  14.1 0.0 collective-permute-done.7.rest_1_
  14.1 0.0 collective-permute-done.8.rest_2_
  14.1 2.9 %shard_map.52 = (bf16[8,96,256]{2,1,0:T(8,128)(2,1)S(1)}, bf16[8,96,256]{2,1,0:T(8,128)(2,1)S(1)}) custom-call(s32[7]{0:T(128)S(1)} %stack.39.flag_ref, f32[6,256]{1,0:T(8,128)S(1)} %get-tuple-element.48.scale_ref, bf16[3,3,256,256]{3,2,1,0:T(8,128)(2,1)S(1)} %get-tuple-element.51.w_ref, bf16[8,112,256]{2,1,0:T(8,128)(2,1)S(1)} %get-tuple-element.63.rest_0_, ...), custom_call_target="tpu_custom_call" | custom-call | flops 1 | bytes 1 | tf_op jit(solution)/shard_map/pallas_call | solution.py:214
  17.1 3.5 %collective-permute-start.9 = (bf16[8,96,256]{2,1,0:T(8,128)(2,1)S(1)}, bf16[8,96,256]{2,1,0:T(8,128)(2,1)S(1)}, u32[]{:S(2)}, u32[]{:S(2)}) collective-permute-start(bf16[8,96,256]{2,1,0:T(8,128)(2,1)S(1)} %get-tuple-element.64.far_ref), channel_id=1, source_target_pairs={{0,8},{2,10},{4,12},{6,14},{8,0},{10,2},{12,4},{14,6},{1,9},{3,11}... | collective-permute-start | bytes 1179656 | tf_op jit(solution)/shard_map/ppermute | solution.py:470
  20.6 4.2 %collective-permute-done.refs_1_.rest_1_.rest_3_ = bf16[4,144,256]{2,1,0:T(8,128)(2,1)S(1)} collective-permute-done((bf16[4,144,256]{2,1,0:T(8,128)(2,1)S(1)}, bf16[4,144,256]{2,1,0:T(8,128)(2,1)S(1)}, u32[]{:S(2)}, u32[]{:S(2)}) %collective-permute-start) | collective-permute-done | bytes 294944 | tf_op jit(solution)/shard_map/ppermute | solution.py:453
  24.8 0.0 collective-permute-done.1.refs_2_.rest_2_.rest_4_
  24.8 0.0 collective-permute-done.2.refs_3_.rest_4_.rest_5_
  24.8 0.6 shard_map.48
  25.4 2.9 %collective-permute-start.3 = (bf16[16,16,256]{2,1,0:T(8,128)(2,1)S(1)}, bf16[16,16,256]{2,1,0:T(8,128)(2,1)S(1)}, u32[]{:S(2)}, u32[]{:S(2)}) collective-permute-start(bf16[16,16,256]{2,1,0:T(8,128)(2,1)S(1)} %shard_map.48), channel_id=1, source_target_pairs={{0,1},{1,0},{2,3},{3,2},{4,5},{5,4},{6,7},{7,6},{8,9},{9,8},{10,11... | collective-permute-start | bytes 393224 | tf_op jit(solution)/shard_map/ppermute | solution.py:486
  28.3 1.0 %collective-permute-done.3.rest_3_ = bf16[16,16,256]{2,1,0:T(8,128)(2,1)S(1)} collective-permute-done((bf16[16,16,256]{2,1,0:T(8,128)(2,1)S(1)}, bf16[16,16,256]{2,1,0:T(8,128)(2,1)S(1)}, u32[]{:S(2)}, u32[]{:S(2)}) %collective-permute-start.3) | collective-permute-done | bytes 131104 | tf_op jit(solution)/shard_map/ppermute | solution.py:486
  29.3 3.2 %shard_map.49 = (bf16[8,96,256]{2,1,0:T(8,128)(2,1)S(1)}, bf16[8,96,256]{2,1,0:T(8,128)(2,1)S(1)}) custom-call(s32[7]{0:T(128)S(1)} %stack.39.flag_ref, f32[6,256]{1,0:T(8,128)S(1)} %get-tuple-element.48.scale_ref, bf16[3,3,256,256]{3,2,1,0:T(8,128)(2,1)S(1)} %get-tuple-element.51.w_ref, bf16[8,112,256]{2,1,0:T(8,128)(2,1)S(1)} %get-tuple-element.52.refs_0_.rest_0_, ...), custom_call_target="tpu_custom_call" | custom-call | flops 1 | bytes 1 | tf_op jit(solution)/shard_map/pallas_call | solution.py:214
  32.5 0.6 shard_map.50
  33.1 4.4 %collective-permute-start.5 = (bf16[8,32,256]{2,1,0:T(8,128)(2,1)S(1)}, bf16[8,32,256]{2,1,0:T(8,128)(2,1)S(1)}, u32[]{:S(2)}, u32[]{:S(2)}) collective-permute-start(bf16[8,32,256]{2,1,0:T(8,128)(2,1)S(1)} %get-tuple-element.66), channel_id=1, source_target_pairs={{0,8},{2,10},{4,12},{6,14},{8,0},{10,2},{12,4},{14,6},{1,9},{3,11}... | collective-permute-start | bytes 393224 | tf_op jit(solution)/shard_map/ppermute | solution.py:509
  37.4 0.1 collective-permute-start.4
  37.5 3.0 %shard_map.51 = (bf16[8,64,256]{2,1,0:T(8,128)(2,1)S(1)}, bf16[8,64,256]{2,1,0:T(8,128)(2,1)S(1)}) custom-call(s32[7]{0:T(128)S(1)} %stack.39.flag_ref, f32[6,256]{1,0:T(8,128)S(1)} %get-tuple-element.48.scale_ref, bf16[3,3,256,256]{3,2,1,0:T(8,128)(2,1)S(1)} %get-tuple-element.51.w_ref, bf16[8,96,256]{2,1,0:T(8,128)(2,1)S(1)} %get-tuple-element.59.rest_0_, ...), custom_call_target="tpu_custom_call" | custom-call | flops 1 | bytes 1 | tf_op jit(solution)/shard_map/pallas_call | solution.py:214
  40.5 2.4 %collective-permute-start.11 = (bf16[8,64,256]{2,1,0:T(8,128)(2,1)S(1)}, bf16[8,64,256]{2,1,0:T(8,128)(2,1)S(1)}, u32[]{:S(2)}, u32[]{:S(2)}) collective-permute-start(bf16[8,64,256]{2,1,0:T(8,128)(2,1)S(1)} %get-tuple-element.62.mid_ref), channel_id=1, source_target_pairs={{0,8},{2,10},{4,12},{6,14},{8,0},{10,2},{12,4},{14,6},{1,9},{3,11}... | collective-permute-start | bytes 786440 | tf_op jit(solution)/shard_map/ppermute | solution.py:537
  42.8 11.4 %collective-permute-done.9.cfar_ref = bf16[8,96,256]{2,1,0:T(8,128)(2,1)S(1)} collective-permute-done((bf16[8,96,256]{2,1,0:T(8,128)(2,1)S(1)}, bf16[8,96,256]{2,1,0:T(8,128)(2,1)S(1)}, u32[]{:S(2)}, u32[]{:S(2)}) %collective-permute-start.9) | collective-permute-done | bytes 393248 | tf_op jit(solution)/shard_map/ppermute | solution.py:470
  54.3 3.8 %collective-permute-start.10 = (bf16[8,32,256]{2,1,0:T(8,128)(2,1)S(1)}, bf16[8,32,256]{2,1,0:T(8,128)(2,1)S(1)}, u32[]{:S(2)}, u32[]{:S(2)}) collective-permute-start(bf16[8,32,256]{2,1,0:T(8,128)(2,1)S(1)} %get-tuple-element.66), channel_id=1, source_target_pairs={{0,1},{1,0},{2,3},{3,2},{4,5},{5,4},{6,7},{7,6},{8,9},{9,8},{10,11... | collective-permute-start | bytes 393224 | tf_op jit(solution)/shard_map/ppermute | solution.py:540
  58.1 0.0 collective-permute-done.5.rim_ref
  58.1 2.8 %collective-permute-start.6 = (bf16[8,32,256]{2,1,0:T(8,128)(2,1)S(1)}, bf16[8,32,256]{2,1,0:T(8,128)(2,1)S(1)}, u32[]{:S(2)}, u32[]{:S(2)}) collective-permute-start(bf16[8,32,256]{2,1,0:T(8,128)(2,1)S(1)} %collective-permute-done.5.rim_ref), channel_id=1, source_target_pairs={{0,1},{1,0},{2,3},{3,2},{4,5},{5,4},{6,7},{7,6},{8,9},{9,8},{10,11... | collective-permute-start | bytes 393224 | tf_op jit(solution)/shard_map/ppermute | solution.py:564
  60.9 0.0 collective-permute-done.10.side_ref
  60.9 2.9 %shard_map.53 = (f32[8,256,256]{2,1,0:T(8,128)S(1)}, bf16[8,256,256]{2,1,0:T(8,128)(2,1)S(1)}, bf16[8,64,256]{2,1,0:T(8,128)(2,1)S(1)}, bf16[8,64,256]{2,1,0:T(8,128)(2,1)S(1)}) custom-call(s32[7]{0:T(128)S(1)} %stack.39.flag_ref, f32[6,256]{1,0:T(8,128)S(1)} %get-tuple-element.48.scale_ref, bf16[2,3,256,256]{3,2,1,0:T(8,128)(2,1)S(1)} %get-tuple-element.50.w_ref, ...), custom_call_target="tpu_custom_call" | custom-call | flops 1 | bytes 1 | tf_op jit(solution)/shard_map/pallas_call | solution.py:542
  63.8 0.0 collective-permute-done.6.side_ref
  63.8 0.0 collective-permute-done.4.cnear_ref
  63.8 1.1 %shard_map.54 = (bf16[8,64,256]{2,1,0:T(8,128)(2,1)S(1)}, bf16[8,64,256]{2,1,0:T(8,128)(2,1)S(1)}) custom-call(s32[7]{0:T(128)S(1)} %stack.39.flag_ref, f32[6,256]{1,0:T(8,128)S(1)} %get-tuple-element.48.scale_ref, bf16[2,3,256,256]{3,2,1,0:T(8,128)(2,1)S(1)} %get-tuple-element.50.w_ref, bf16[8,64,256]{2,1,0:T(8,128)(2,1)S(1)} %collective-permute-done.4.cnear_ref, ...), custom_call_target="tpu_custom_call" | custom-call | flops 1 | bytes 1 | tf_op jit(solution)/shard_map/pallas_call | solution.py:542
  64.9 1.0 %shard_map.55 = (f32[8,256,256]{2,1,0:T(8,128)S(1)}, bf16[2,8,64,256]{3,2,1,0:T(8,128)(2,1)S(1)}) custom-call(s32[7]{0:T(128)S(1)} %stack.39.flag_ref, f32[6,256]{1,0:T(8,128)S(1)} %get-tuple-element.48.scale_ref, bf16[3,256,256]{2,1,0:T(8,128)(2,1)S(1)} %get-tuple-element.49.w_ref, bf16[8,64,256]{2,1,0:T(8,128)(2,1)S(1)} %get-tuple-element.72.near2_ref, ...), custom_call_target="tpu_custom_call" | custom-call | flops 1 | bytes 1 | tf_op jit(solution)/shard_map/pallas_call | solution.py:542
  66.0 2.3 %collective-permute-done.11.cmid_ref = bf16[8,64,256]{2,1,0:T(8,128)(2,1)S(1)} collective-permute-done((bf16[8,64,256]{2,1,0:T(8,128)(2,1)S(1)}, bf16[8,64,256]{2,1,0:T(8,128)(2,1)S(1)}, u32[]{:S(2)}, u32[]{:S(2)}) %collective-permute-start.11) | collective-permute-done | bytes 262176 | tf_op jit(solution)/shard_map/ppermute | solution.py:537
  68.3 2.1 %collective-permute-start.12 = (bf16[8,64,256]{2,1,0:T(8,128)(2,1)S(1)}, bf16[8,64,256]{2,1,0:T(8,128)(2,1)S(1)}, u32[]{:S(2)}, u32[]{:S(2)}) collective-permute-start(bf16[8,64,256]{2,1,0:T(8,128)(2,1)S(1)} %get-tuple-element.81.near_ref), channel_id=1, source_target_pairs={{0,1},{1,0},{2,3},{3,2},{4,5},{5,4},{6,7},{7,6},{8,9},{9,8},{10,11... | collective-permute-start | bytes 786440 | tf_op jit(solution)/shard_map/ppermute | solution.py:584
  70.4 1.5 %shard_map.56 = (bf16[8,128,256]{2,1,0:T(8,128)(2,1)S(1)}, bf16[8,128,256]{2,1,0:T(8,128)(2,1)S(1)}) custom-call(s32[7]{0:T(128)S(1)} %stack.39.flag_ref, f32[6,256]{1,0:T(8,128)S(1)} %get-tuple-element.48.scale_ref, bf16[2,3,256,256]{3,2,1,0:T(8,128)(2,1)S(1)} %get-tuple-element.50.w_ref, bf16[8,64,256]{2,1,0:T(8,128)(2,1)S(1)} %collective-permute-done.11.cmid_ref, ...), custom_call_target="tpu_custom_call" | custom-call | flops 1 | bytes 1 | tf_op jit(solution)/shard_map/pallas_call | solution.py:542
  71.9 0.0 collective-permute-done.12.side_ref
  71.9 2.1 %shard_map.57 = bf16[8,256,256]{2,1,0:T(8,128)(2,1)} custom-call(s32[7]{0:T(128)S(1)} %stack.39.flag_ref, f32[6,256]{1,0:T(8,128)S(1)} %get-tuple-element.48.scale_ref, bf16[3,256,256]{2,1,0:T(8,128)(2,1)S(1)} %get-tuple-element.49.w_ref, bf16[2,8,64,256]{3,2,1,0:T(8,128)(2,1)S(1)} %get-tuple-element.76.ends_ref, ...), custom_call_target="tpu_custom_call" | custom-call | flops 1 | bytes 1 | tf_op jit(solution)/shard_map/pallas_call | solution.py:592
Async XLA Ops:
  0.1 1.2 %copy-start.1 = (bf16[8,256,256]{2,1,0:T(8,128)(2,1)S(1)}, bf16[8,256,256]{2,1,0:T(8,128)(2,1)}, u32[]{:S(2)}) copy-start(bf16[8,256,256]{2,1,0:T(8,128)(2,1)} %refs_0_.1) | copy-start | bytes 3145732
  2.1 12.0 %collective-permute-start.7 = (bf16[4,112,256]{2,1,0:T(8,128)(2,1)S(1)}, bf16[4,112,256]{2,1,0:T(8,128)(2,1)S(1)}, u32[]{:S(2)}, u32[]{:S(2)}) collective-permute-start(bf16[4,112,256]{2,1,0:T(8,128)(2,1)S(1)} %get-tuple-element.60), channel_id=1, source_target_pairs={{0,2},{2,0},{4,6},{6,4},{8,10},{10,8},{12,14},{14,12},{1,3},{3,1},... | collective-permute-start | bytes 688136 | tf_op jit(solution)/shard_map/ppermute | solution.py:438
  4.2 9.9 %collective-permute-start.8 = (bf16[4,112,256]{2,1,0:T(8,128)(2,1)S(1)}, bf16[4,112,256]{2,1,0:T(8,128)(2,1)S(1)}, u32[]{:S(2)}, u32[]{:S(2)}) collective-permute-start(bf16[4,112,256]{2,1,0:T(8,128)(2,1)S(1)} %get-tuple-element.61), channel_id=1, source_target_pairs={{2,4},{4,2},{6,8},{8,6},{10,12},{12,10},{3,5},{5,3},{7,9},{9,7},{1... | collective-permute-start | bytes 688136 | tf_op jit(solution)/shard_map/ppermute | solution.py:439
  4.9 2.0 %copy-start = (bf16[3,3,3,256,256]{4,3,2,1,0:T(8,128)(2,1)S(1)}, bf16[3,3,3,256,256]{4,3,2,1,0:T(8,128)(2,1)}, u32[]{:S(2)}) copy-start(bf16[3,3,3,256,256]{4,3,2,1,0:T(8,128)(2,1)} %w_ref.1) | copy-start | bytes 10616836
  6.9 0.7 copy-start.2
  7.6 0.7 copy-start.3
  9.0 15.8 %collective-permute-start.2 = (bf16[4,160,256]{2,1,0:T(8,128)(2,1)S(1)}, bf16[4,160,256]{2,1,0:T(8,128)(2,1)S(1)}, u32[]{:S(2)}, u32[]{:S(2)}) collective-permute-start(bf16[4,160,256]{2,1,0:T(8,128)(2,1)S(1)} %get-tuple-element.55), channel_id=1, source_target_pairs={{6,8},{8,6},{7,9},{9,7},{22,24},{24,22},{23,25},{25,23}} | collective-permute-start | bytes 983048 | tf_op jit(solution)/shard_map/ppermute | solution.py:455
  9.7 15.1 %collective-permute-start = (bf16[4,144,256]{2,1,0:T(8,128)(2,1)S(1)}, bf16[4,144,256]{2,1,0:T(8,128)(2,1)S(1)}, u32[]{:S(2)}, u32[]{:S(2)}) collective-permute-start(bf16[4,144,256]{2,1,0:T(8,128)(2,1)S(1)} %get-tuple-element.53), channel_id=1, source_target_pairs={{0,2},{2,0},{4,6},{6,4},{8,10},{10,8},{12,14},{14,12},{1,3},{3,1},... | collective-permute-start | bytes 884744 | tf_op jit(solution)/shard_map/ppermute | solution.py:453
  13.4 11.3 %collective-permute-start.1 = (bf16[4,144,256]{2,1,0:T(8,128)(2,1)S(1)}, bf16[4,144,256]{2,1,0:T(8,128)(2,1)S(1)}, u32[]{:S(2)}, u32[]{:S(2)}) collective-permute-start(bf16[4,144,256]{2,1,0:T(8,128)(2,1)S(1)} %get-tuple-element.54), channel_id=1, source_target_pairs={{2,4},{4,2},{10,12},{12,10},{3,5},{5,3},{11,13},{13,11},{18,20},{2... | collective-permute-start | bytes 884744 | tf_op jit(solution)/shard_map/ppermute | solution.py:454
  17.1 37.2 %collective-permute-start.9 = (bf16[8,96,256]{2,1,0:T(8,128)(2,1)S(1)}, bf16[8,96,256]{2,1,0:T(8,128)(2,1)S(1)}, u32[]{:S(2)}, u32[]{:S(2)}) collective-permute-start(bf16[8,96,256]{2,1,0:T(8,128)(2,1)S(1)} %get-tuple-element.64.far_ref), channel_id=1, source_target_pairs={{0,8},{2,10},{4,12},{6,14},{8,0},{10,2},{12,4},{14,6},{1,9},{3,11}... | collective-permute-start | bytes 1179656 | tf_op jit(solution)/shard_map/ppermute | solution.py:470
  25.4 3.9 %collective-permute-start.3 = (bf16[16,16,256]{2,1,0:T(8,128)(2,1)S(1)}, bf16[16,16,256]{2,1,0:T(8,128)(2,1)S(1)}, u32[]{:S(2)}, u32[]{:S(2)}) collective-permute-start(bf16[16,16,256]{2,1,0:T(8,128)(2,1)S(1)} %shard_map.48), channel_id=1, source_target_pairs={{0,1},{1,0},{2,3},{3,2},{4,5},{5,4},{6,7},{7,6},{8,9},{9,8},{10,11... | collective-permute-start | bytes 393224 | tf_op jit(solution)/shard_map/ppermute | solution.py:486
  33.1 25.0 %collective-permute-start.5 = (bf16[8,32,256]{2,1,0:T(8,128)(2,1)S(1)}, bf16[8,32,256]{2,1,0:T(8,128)(2,1)S(1)}, u32[]{:S(2)}, u32[]{:S(2)}) collective-permute-start(bf16[8,32,256]{2,1,0:T(8,128)(2,1)S(1)} %get-tuple-element.66), channel_id=1, source_target_pairs={{0,8},{2,10},{4,12},{6,14},{8,0},{10,2},{12,4},{14,6},{1,9},{3,11}... | collective-permute-start | bytes 393224 | tf_op jit(solution)/shard_map/ppermute | solution.py:509
  37.4 26.4 %collective-permute-start.4 = (bf16[8,64,256]{2,1,0:T(8,128)(2,1)S(1)}, bf16[8,64,256]{2,1,0:T(8,128)(2,1)S(1)}, u32[]{:S(2)}, u32[]{:S(2)}) collective-permute-start(bf16[8,64,256]{2,1,0:T(8,128)(2,1)S(1)} %get-tuple-element.57), channel_id=1, source_target_pairs={{0,8},{2,10},{4,12},{6,14},{8,0},{10,2},{12,4},{14,6},{1,9},{3,11}... | collective-permute-start | bytes 786440 | tf_op jit(solution)/shard_map/ppermute | solution.py:510
  40.5 27.8 %collective-permute-start.11 = (bf16[8,64,256]{2,1,0:T(8,128)(2,1)S(1)}, bf16[8,64,256]{2,1,0:T(8,128)(2,1)S(1)}, u32[]{:S(2)}, u32[]{:S(2)}) collective-permute-start(bf16[8,64,256]{2,1,0:T(8,128)(2,1)S(1)} %get-tuple-element.62.mid_ref), channel_id=1, source_target_pairs={{0,8},{2,10},{4,12},{6,14},{8,0},{10,2},{12,4},{14,6},{1,9},{3,11}... | collective-permute-start | bytes 786440 | tf_op jit(solution)/shard_map/ppermute | solution.py:537
  54.3 6.6 %collective-permute-start.10 = (bf16[8,32,256]{2,1,0:T(8,128)(2,1)S(1)}, bf16[8,32,256]{2,1,0:T(8,128)(2,1)S(1)}, u32[]{:S(2)}, u32[]{:S(2)}) collective-permute-start(bf16[8,32,256]{2,1,0:T(8,128)(2,1)S(1)} %get-tuple-element.66), channel_id=1, source_target_pairs={{0,1},{1,0},{2,3},{3,2},{4,5},{5,4},{6,7},{7,6},{8,9},{9,8},{10,11... | collective-permute-start | bytes 393224 | tf_op jit(solution)/shard_map/ppermute | solution.py:540
  58.1 5.7 %collective-permute-start.6 = (bf16[8,32,256]{2,1,0:T(8,128)(2,1)S(1)}, bf16[8,32,256]{2,1,0:T(8,128)(2,1)S(1)}, u32[]{:S(2)}, u32[]{:S(2)}) collective-permute-start(bf16[8,32,256]{2,1,0:T(8,128)(2,1)S(1)} %collective-permute-done.5.rim_ref), channel_id=1, source_target_pairs={{0,1},{1,0},{2,3},{3,2},{4,5},{5,4},{6,7},{7,6},{8,9},{9,8},{10,11... | collective-permute-start | bytes 393224 | tf_op jit(solution)/shard_map/ppermute | solution.py:564
  68.3 3.6 %collective-permute-start.12 = (bf16[8,64,256]{2,1,0:T(8,128)(2,1)S(1)}, bf16[8,64,256]{2,1,0:T(8,128)(2,1)S(1)}, u32[]{:S(2)}, u32[]{:S(2)}) collective-permute-start(bf16[8,64,256]{2,1,0:T(8,128)(2,1)S(1)} %get-tuple-element.81.near_ref), channel_id=1, source_target_pairs={{0,1},{1,0},{2,3},{3,2},{4,5},{5,4},{6,7},{7,6},{8,9},{9,8},{10,11... | collective-permute-start | bytes 786440 | tf_op jit(solution)/shard_map/ppermute | solution.py:584

commit v9 on v8

--- a/solution.py
+++ b/solution.py
@@ -118,6 +118,10 @@
     return pl.multiple_of(jnp.where(core == 0, at_zero, at_one), lane_pad)
 
 
+def row_of(flag_ref, row):
+    return row if isinstance(row, int) else jnp.where(flag_ref[4] == 0, *row)
+
+
 def guarded(flag_ref, condition, action):
     if condition is None:
         action()
@@ -131,8 +135,9 @@
 
     def move(which, row, count, column, width, target, target_row):
         src = place(flag_ref[0], *column)
+        first = row_of(flag_ref, target_row)
         for r in range(count):
-            targets[target][target_row + r] = sources[which][row + r, pl.ds(src, width), :]
+            targets[target][first + r] = sources[which][row + r, pl.ds(src, width), :]
 
     for parts in moves:
         guarded(flag_ref, parts[0], functools.partial(move, *parts[1:]))
@@ -142,7 +147,8 @@
     channels, kind = arrays[0].shape[2], arrays[0].dtype
     shapes = {}
     for _, _, _, count, _, width, target, target_row in moves:
-        height = max(target_row + count, shapes.get(target, (0, 0))[0])
+        end = count + (target_row if isinstance(target_row, int) else max(target_row))
+        height = max(end, shapes.get(target, (0, 0))[0])
         shapes[target] = (height, width)
     out = tuple(
         jax.ShapeDtypeStruct(shapes[target] + (channels,), kind) for target in range(len(shapes))
@@ -155,9 +161,7 @@
     )(flags, *arrays)
 
 
-def hold_kernel(flag_ref, gain_ref, bias_ref, w_ref, scale_ref, first_ref, second_ref, last_ref):
-    scale_ref[0:3, :] = gain_ref[...]
-    scale_ref[3:6, :] = bias_ref[...]
+def hold_kernel(flag_ref, w_ref, first_ref, second_ref, last_ref):
     first_ref[...] = w_ref[0]
     second_ref[0] = w_ref[1, 1]
     second_ref[1] = w_ref[1, flag_ref[3]]
@@ -173,6 +177,7 @@
 
     def fill(which, source_row, window_row, count, source, target, columns):
         src, dst = place(core, *source), place(core, *target)
+        first = row_of(flag_ref, window_row)
         for r in range(count):
             if which is None:
                 values = jnp.zeros((columns, channels), window.dtype)
@@ -180,7 +185,7 @@
                 values = normalize(
                     parts[which][source_row + r, pl.ds(src, columns), :], gain
                 )
-            window[window_row + r, pl.ds(dst, columns), :] = values
+            window[first + r, pl.ds(dst, columns), :] = values
 
     for segment in segments:
         guarded(flag_ref, segment[0], functools.partial(fill, *segment[1:]))
@@ -393,20 +398,12 @@
     wide = strip + pad
     core, row = lax.axis_index("col"), lax.axis_index("row")
     upper_half = row < group
-    parity = row % 2
+    beside = (row == group) | (row == group - 1)
     flags = jnp.stack(
-        [
-            core,
-            row == group - 1,
-            row == group,
-            jnp.where(upper_half, 2, 0),
-            parity,
-            jnp.where(row == group, 3, 2 - parity),
-            jnp.where(row == group - 1, 3, 1 + parity),
-        ]
+        [core, row == group - 1, row == group, jnp.where(upper_half, 2, 0), row % 2, beside]
     ).astype(jnp.int32)
-    even, odd = (4, 0), (4, 1)
-    above_in, below_in = ([(flag, which) for which in (1, 2, 3)] for flag in (5, 6))
+    even, odd, apart, at_middle = (4, 0), (4, 1), (5, 0), (5, 1)
+    one_at, two_at = (half + rows, 0), (0, half + rows)
     swap = [(0, 1), (1, 0)]
     partner = [(i, (i + group) % size) for i in range(size)]
     first_pairs = [(i, i ^ 1) for i in range(size)]
@@ -438,18 +435,18 @@
     far_one = lax.ppermute(far_one, "row", first_pairs)
     far_two = lax.ppermute(far_two, "row", second_pairs)
     tail = conv_weights.shape[2:]
-    scales, first_w, second_w, last_w = kernel_call(
+    scales = jnp.concatenate([norm_gains, conv_biases], axis=0)
+    first_w, second_w, last_w = kernel_call(
         hold_kernel,
         (
-            jax.ShapeDtypeStruct((2 * norm_gains.shape[0], channels), jnp.float32),
             jax.ShapeDtypeStruct((3,) + tail, kind),
             jax.ShapeDtypeStruct((2,) + tail, kind),
             jax.ShapeDtypeStruct(tail, kind),
         ),
-        [smem_spec()] + [vmem_spec()] * 3,
+        [smem_spec(), vmem_spec()],
         [],
-    )(flags, norm_gains, conv_biases, conv_weights)
-    one, two, middle, scales = lax.optimization_barrier((one, two, middle, scales))
+    )(flags, conv_weights)
+    one, two, middle, first_w = lax.optimization_barrier((one, two, middle, first_w))
     one = lax.ppermute(one, "row", first_pairs)
     two = lax.ppermute(two, "row", second_within)
     middle = lax.ppermute(middle, "row", across)
@@ -458,10 +455,8 @@
     far_body, far_edge = (pad, 0), (0, wide)
     far_segments = (
         (None, 0, 0, half, rows, (0, 0), far_body, wide),
-        (odd, 1, 0, 0, half, (0, 0), far_body, wide),
-        (even, 2, 0, 0, half, (0, 0), far_body, wide),
-        (even, 1, 0, half + rows, half, (0, 0), far_body, wide),
-        (odd, 2, 0, half + rows, half, (0, 0), far_body, wide),
+        (None, 1, 0, one_at, half, (0, 0), far_body, wide),
+        (None, 2, 0, two_at, half, (0, 0), far_body, wide),
         (None, None, 0, 0, 2 * rows, (0, 0), far_edge, pad),
     )
     far1, far_n = first_layer(
@@ -474,25 +469,19 @@
         flags,
         (near_x, one, two, middle),
         (
-            (above_in[0], 1, 0, half, span_end, pad, 0, 0),
-            (above_in[1], 2, 0, half, span_end, pad, 0, 0),
-            (above_in[2], 3, 0, half, middle_end, pad, 0, 0),
+            (None, 1, 0, half, span_end, pad, 0, one_at),
+            (apart, 2, 0, half, span_end, pad, 0, two_at),
+            (at_middle, 3, 0, half, middle_end, pad, 0, two_at),
             (None, 0, 0, rows, near_end, pad, 0, half),
-            (below_in[0], 1, 0, half, span_end, pad, 0, half + rows),
-            (below_in[1], 2, 0, half, span_end, pad, 0, half + rows),
-            (below_in[2], 3, 0, half, middle_end, pad, 0, half + rows),
         ),
     )
     rim = lax.ppermute(rim, "col", swap)
     near_body, near_span, near_middle = (0, pad), (span - wide, 0), (span + pad - wide, 0)
     near_segments = (
         (None, 0, 0, half, rows, (0, 0), near_body, wide),
-        (above_in[0], 1, 0, 0, half, near_span, near_body, wide),
-        (above_in[1], 2, 0, 0, half, near_span, near_body, wide),
-        (above_in[2], 4, 0, 0, half, near_middle, near_body, wide),
-        (below_in[0], 1, 0, half + rows, half, near_span, near_body, wide),
-        (below_in[1], 2, 0, half + rows, half, near_span, near_body, wide),
-        (below_in[2], 4, 0, half + rows, half, near_middle, near_body, wide),
+        (None, 1, 0, one_at, half, near_span, near_body, wide),
+        (apart, 2, 0, two_at, half, near_span, near_body, wide),
+        (at_middle, 4, 0, two_at, half, near_middle, near_body, wide),
         (None, 3, 0, 0, 2 * rows, (0, 0), (wide, 0), pad),
     )
     near1, near_n = first_layer(
@@ -513,16 +502,11 @@
     middle_side = ((pad, span - mid), (side_pads, 0))
     mid_segments = (
         (None, 0, 0, half, rows, (0, 0), (0, 0), mid + side_pads),
-        (odd, 1, 0, 0, half, *far_side, side_pads),
-        (even, 2, 0, 0, half, *far_side, side_pads),
-        (even, 1, 0, half + rows, half, *far_side, side_pads),
-        (odd, 2, 0, half + rows, half, *far_side, side_pads),
-        (above_in[0], 3, 0, 0, half, *rest_side, mid),
-        (above_in[1], 4, 0, 0, half, *rest_side, mid),
-        (above_in[2], 5, 0, 0, half, *middle_side, mid),
-        (below_in[0], 3, 0, half + rows, half, *rest_side, mid),
-        (below_in[1], 4, 0, half + rows, half, *rest_side, mid),
-        (below_in[2], 5, 0, half + rows, half, *middle_side, mid),
+        (None, 1, 0, one_at, half, *far_side, side_pads),
+        (None, 2, 0, two_at, half, *far_side, side_pads),
+        (None, 3, 0, one_at, half, *rest_side, mid),
+        (apart, 4, 0, two_at, half, *rest_side, mid),
+        (at_middle, 5, 0, two_at, half, *middle_side, mid),
     )
     mid1, mid_n = first_layer(
         flags,

time: 74.5 us -> 73.1 us (0.981)
  starting transfers between devices: 29.8 us -> 38.4 us
  waiting for transfers between devices: 19 us -> 10.5 us
  local copies, waits for them, and re-layouts: 4.68 us -> 3.31 us
    ppermute x1, waiting for transfers between devices: 11.4 us -> 0.01 us  [by_halves(): cross_far = lax.ppermute(far_n, 'row', partner)]
    ppermute x1, starting transfers between devices: 3.82 us -> 14.2 us  [by_halves(): near_side = lax.ppermute(near_rim, 'col', swap)]
    ppermute x1, waiting for transfers between devices: 4.2 us -> 7.23 us  [by_halves(): one = lax.ppermute(one, 'row', first_pairs)]
    ppermute x1, starting transfers between devices: 4.36 us -> 2.87 us  [by_halves(): cross_rim = lax.ppermute(near_rim, 'row', partner)]
    unnamed x8, local copies, waits for them, and re-layouts: 4.59 us -> 3.23 us
where the time goes in v9:
time: 73.1 us; the launch traced here: 72.8 us
  starting transfers between devices  38.4 us (53%)
  Pallas kernels  20.3 us (28%)
  waiting for transfers between devices  10.5 us (14%)
  local copies, waits for them, and re-layouts  3.31 us (5%)
    ppermute x1, starting transfers between devices, by_halves(): near_side = lax.ppermute(near_rim, 'col', swap)  14.2 us
    pallas_call x3, Pallas kernels, first_layer(): kernel_call(functools.partial(first_layer_kernel, segments, out_at, rows,...  8.99 us
    ppermute x1, waiting for transfers between devices, by_halves(): one = lax.ppermute(one, 'row', first_pairs)  7.23 us
    pallas_call x4, Pallas kernels, plain(): kernel_call(body, out, [smem_spec()] + [vmem_spec()] * (len(operands) + 2...  6.53 us
    ppermute x1, starting transfers between devices, by_halves(): one = lax.ppermute(one, 'row', first_pairs)  3.78 us
    unnamed x8, local copies, waits for them, and re-layouts  3.23 us
    ppermute x1, starting transfers between devices, by_halves(): cross_far = lax.ppermute(far_n, 'row', partner)  3.04 us
    ppermute x1, starting transfers between devices, by_halves(): cross_rim = lax.ppermute(near_rim, 'row', partner)  2.87 us
  transfers between devices with their start and end apart: 13, of which 4 were waited for; matrix products, arithmetic and copies ran while one was open for 0% of the time, Pallas kernels for 24%

profile of v9, /device:TPU:1, one launch (start us, length us, event | category | flops | bytes accessed | tf_op | source)
XLA Modules:
  0.0 72.8 jit_solution(1455938062604728018)
XLA Ops:
  0.0 0.1 stack.39.flag_ref
  0.1 0.0 copy-start.1
  0.1 1.2 %copy-done.1 = bf16[8,256,256]{2,1,0:T(8,128)(2,1)S(1)} copy-done((bf16[8,256,256]{2,1,0:T(8,128)(2,1)S(1)}, bf16[8,256,256]{2,1,0:T(8,128)(2,1)}, u32[]{:S(2)}) %copy-start.1) | copy-done | bytes 1048600
  1.3 0.0 copy-start.2
  1.3 0.0 copy-start.3
  1.3 0.8 %shard_map.47 = (bf16[8,112,256]{2,1,0:T(8,128)(2,1)S(1)}, bf16[8,112,256]{2,1,0:T(8,128)(2,1)S(1)}, bf16[8,96,256]{2,1,0:T(8,128)(2,1)S(1)}, bf16[4,112,256]{2,...) custom-call(s32[6]{0:T(128)S(1)} %stack.39.flag_ref, ...), custom_call_target="tpu_custom_call" | custom-call | flops 1 | bytes 1 | tf_op jit(solution)/shard_map/pallas_call | solution.py:156
  2.1 2.1 %collective-permute-start.7 = (bf16[4,112,256]{2,1,0:T(8,128)(2,1)S(1)}, bf16[4,112,256]{2,1,0:T(8,128)(2,1)S(1)}, u32[]{:S(2)}, u32[]{:S(2)}) collective-permute-start(bf16[4,112,256]{2,1,0:T(8,128)(2,1)S(1)} %get-tuple-element.58), channel_id=1, source_target_pairs={{0,2},{2,0},{4,6},{6,4},{8,10},{10,8},{12,14},{14,12},{1,3},{3,1},... | collective-permute-start | bytes 688136 | tf_op jit(solution)/shard_map/ppermute | solution.py:435
  4.2 0.7 collective-permute-start.8
  4.9 0.0 copy-start
  4.9 2.0 %copy-done = bf16[3,3,3,256,256]{4,3,2,1,0:T(8,128)(2,1)S(1)} copy-done((bf16[3,3,3,256,256]{4,3,2,1,0:T(8,128)(2,1)S(1)}, bf16[3,3,3,256,256]{4,3,2,1,0:T(8,128)(2,1)}, u32[]{:S(2)}) %copy-start) | copy-done | bytes 3538968
  6.9 0.7 shard_map.46
  7.6 0.7 collective-permute-start.2
  8.3 3.8 %collective-permute-start = (bf16[4,144,256]{2,1,0:T(8,128)(2,1)S(1)}, bf16[4,144,256]{2,1,0:T(8,128)(2,1)S(1)}, u32[]{:S(2)}, u32[]{:S(2)}) collective-permute-start(bf16[4,144,256]{2,1,0:T(8,128)(2,1)S(1)} %get-tuple-element.51), channel_id=1, source_target_pairs={{0,2},{2,0},{4,6},{6,4},{8,10},{10,8},{12,14},{14,12},{1,3},{3,1},... | collective-permute-start | bytes 884744 | tf_op jit(solution)/shard_map/ppermute | solution.py:450
  12.1 0.7 collective-permute-start.1
  12.8 0.0 copy-done.2
  12.8 0.0 copy-done.3
  12.8 0.5 collective-permute-done.7.rest_1_
  13.3 0.0 collective-permute-done.8.rest_2_
  13.3 2.5 %shard_map.52 = (bf16[8,96,256]{2,1,0:T(8,128)(2,1)S(1)}, bf16[8,96,256]{2,1,0:T(8,128)(2,1)S(1)}) custom-call(s32[6]{0:T(128)S(1)} %stack.39.flag_ref, f32[6,256]{1,0:T(8,128)S(1)} %pad_maximum_fusion.scale_ref, bf16[3,3,256,256]{3,2,1,0:T(8,128)(2,1)S(1)} %get-tuple-element.49.w_ref, bf16[8,112,256]{2,1,0:T(8,128)(2,1)S(1)} %get-tuple-element.61.rest_0_, ...), custom_call_target="tpu_custom_call" | custom-call | flops 1 | bytes 1 | tf_op jit(solution)/shard_map/pallas_call | solution.py:219
  15.8 3.0 %collective-permute-start.9 = (bf16[8,96,256]{2,1,0:T(8,128)(2,1)S(1)}, bf16[8,96,256]{2,1,0:T(8,128)(2,1)S(1)}, u32[]{:S(2)}, u32[]{:S(2)}) collective-permute-start(bf16[8,96,256]{2,1,0:T(8,128)(2,1)S(1)} %get-tuple-element.62.far_ref), channel_id=1, source_target_pairs={{0,8},{2,10},{4,12},{6,14},{8,0},{10,2},{12,4},{14,6},{1,9},{3,11}... | collective-permute-start | bytes 1179656 | tf_op jit(solution)/shard_map/ppermute | solution.py:465
  18.8 7.2 %collective-permute-done.refs_1_.rest_1_.rest_3_ = bf16[4,144,256]{2,1,0:T(8,128)(2,1)S(1)} collective-permute-done((bf16[4,144,256]{2,1,0:T(8,128)(2,1)S(1)}, bf16[4,144,256]{2,1,0:T(8,128)(2,1)S(1)}, u32[]{:S(2)}, u32[]{:S(2)}) %collective-permute-start) | collective-permute-done | bytes 294944 | tf_op jit(solution)/shard_map/ppermute | solution.py:450
  26.1 0.0 collective-permute-done.1.refs_2_.rest_2_.rest_4_
  26.1 0.0 collective-permute-done.2.refs_3_.rest_4_.rest_5_
  26.1 0.6 shard_map.48
  26.7 2.8 %collective-permute-start.3 = (bf16[16,16,256]{2,1,0:T(8,128)(2,1)S(1)}, bf16[16,16,256]{2,1,0:T(8,128)(2,1)S(1)}, u32[]{:S(2)}, u32[]{:S(2)}) collective-permute-start(bf16[16,16,256]{2,1,0:T(8,128)(2,1)S(1)} %shard_map.48), channel_id=1, source_target_pairs={{0,1},{1,0},{2,3},{3,2},{4,5},{5,4},{6,7},{7,6},{8,9},{9,8},{10,11... | collective-permute-start | bytes 393224 | tf_op jit(solution)/shard_map/ppermute | solution.py:478
  29.5 1.0 %collective-permute-done.3.rest_3_ = bf16[16,16,256]{2,1,0:T(8,128)(2,1)S(1)} collective-permute-done((bf16[16,16,256]{2,1,0:T(8,128)(2,1)S(1)}, bf16[16,16,256]{2,1,0:T(8,128)(2,1)S(1)}, u32[]{:S(2)}, u32[]{:S(2)}) %collective-permute-start.3) | collective-permute-done | bytes 131104 | tf_op jit(solution)/shard_map/ppermute | solution.py:478
  30.4 3.3 %shard_map.49 = (bf16[8,96,256]{2,1,0:T(8,128)(2,1)S(1)}, bf16[8,96,256]{2,1,0:T(8,128)(2,1)S(1)}) custom-call(s32[6]{0:T(128)S(1)} %stack.39.flag_ref, f32[6,256]{1,0:T(8,128)S(1)} %pad_maximum_fusion.scale_ref, bf16[3,3,256,256]{3,2,1,0:T(8,128)(2,1)S(1)} %get-tuple-element.49.w_ref, bf16[8,112,256]{2,1,0:T(8,128)(2,1)S(1)} %get-tuple-element.50.refs_0_.rest_0_, ...), custom_call_target="tpu_custom_call" | custom-call | flops 1 | bytes 1 | tf_op jit(solution)/shard_map/pallas_call | solution.py:219
  33.8 0.6 shard_map.50
  34.4 2.9 %collective-permute-start.5 = (bf16[8,32,256]{2,1,0:T(8,128)(2,1)S(1)}, bf16[8,32,256]{2,1,0:T(8,128)(2,1)S(1)}, u32[]{:S(2)}, u32[]{:S(2)}) collective-permute-start(bf16[8,32,256]{2,1,0:T(8,128)(2,1)S(1)} %get-tuple-element.64), channel_id=1, source_target_pairs={{0,8},{2,10},{4,12},{6,14},{8,0},{10,2},{12,4},{14,6},{1,9},{3,11}... | collective-permute-start | bytes 393224 | tf_op jit(solution)/shard_map/ppermute | solution.py:498
  37.3 0.1 collective-permute-start.4
  37.3 3.1 %shard_map.51 = (bf16[8,64,256]{2,1,0:T(8,128)(2,1)S(1)}, bf16[8,64,256]{2,1,0:T(8,128)(2,1)S(1)}) custom-call(s32[6]{0:T(128)S(1)} %stack.39.flag_ref, f32[6,256]{1,0:T(8,128)S(1)} %pad_maximum_fusion.scale_ref, bf16[3,3,256,256]{3,2,1,0:T(8,128)(2,1)S(1)} %get-tuple-element.49.w_ref, bf16[8,96,256]{2,1,0:T(8,128)(2,1)S(1)} %get-tuple-element.57.rest_0_, ...), custom_call_target="tpu_custom_call" | custom-call | flops 1 | bytes 1 | tf_op jit(solution)/shard_map/pallas_call | solution.py:219
  40.5 2.3 %collective-permute-start.11 = (bf16[8,64,256]{2,1,0:T(8,128)(2,1)S(1)}, bf16[8,64,256]{2,1,0:T(8,128)(2,1)S(1)}, u32[]{:S(2)}, u32[]{:S(2)}) collective-permute-start(bf16[8,64,256]{2,1,0:T(8,128)(2,1)S(1)} %get-tuple-element.60.mid_ref), channel_id=1, source_target_pairs={{0,8},{2,10},{4,12},{6,14},{8,0},{10,2},{12,4},{14,6},{1,9},{3,11}... | collective-permute-start | bytes 786440 | tf_op jit(solution)/shard_map/ppermute | solution.py:521
  42.8 0.0 collective-permute-done.9.cfar_ref
  42.8 14.2 %collective-permute-start.10 = (bf16[8,32,256]{2,1,0:T(8,128)(2,1)S(1)}, bf16[8,32,256]{2,1,0:T(8,128)(2,1)S(1)}, u32[]{:S(2)}, u32[]{:S(2)}) collective-permute-start(bf16[8,32,256]{2,1,0:T(8,128)(2,1)S(1)} %get-tuple-element.64), channel_id=1, source_target_pairs={{0,1},{1,0},{2,3},{3,2},{4,5},{5,4},{6,7},{7,6},{8,9},{9,8},{10,11... | collective-permute-start | bytes 393224 | tf_op jit(solution)/shard_map/ppermute | solution.py:524
  57.0 0.0 collective-permute-done.5.rim_ref
  57.0 2.8 %collective-permute-start.6 = (bf16[8,32,256]{2,1,0:T(8,128)(2,1)S(1)}, bf16[8,32,256]{2,1,0:T(8,128)(2,1)S(1)}, u32[]{:S(2)}, u32[]{:S(2)}) collective-permute-start(bf16[8,32,256]{2,1,0:T(8,128)(2,1)S(1)} %collective-permute-done.5.rim_ref), channel_id=1, source_target_pairs={{0,1},{1,0},{2,3},{3,2},{4,5},{5,4},{6,7},{7,6},{8,9},{9,8},{10,11... | collective-permute-start | bytes 393224 | tf_op jit(solution)/shard_map/ppermute | solution.py:548
  59.8 0.0 collective-permute-done.10.side_ref
  59.8 2.9 %shard_map.53 = (f32[8,256,256]{2,1,0:T(8,128)S(1)}, bf16[8,256,256]{2,1,0:T(8,128)(2,1)S(1)}, bf16[8,64,256]{2,1,0:T(8,128)(2,1)S(1)}, bf16[8,64,256]{2,1,0:T(8,128)(2,1)S(1)}) custom-call(s32[6]{0:T(128)S(1)} %stack.39.flag_ref, f32[6,256]{1,0:T(8,128)S(1)} %pad_maximum_fusion.scale_ref, bf16[2,3,256,256]{3,2,1,0:T(8,128)(2,1)S(1)} %get-tuple-element.44.w_ref, ...), custom_call_target="tpu_custom_call" | custom-call | flops 1 | bytes 1 | tf_op jit(solution)/shard_map/pallas_call | solution.py:526
  62.7 0.0 collective-permute-done.6.side_ref
  62.7 0.0 collective-permute-done.4.cnear_ref
  62.7 1.1 %shard_map.54 = (bf16[8,64,256]{2,1,0:T(8,128)(2,1)S(1)}, bf16[8,64,256]{2,1,0:T(8,128)(2,1)S(1)}) custom-call(s32[6]{0:T(128)S(1)} %stack.39.flag_ref, f32[6,256]{1,0:T(8,128)S(1)} %pad_maximum_fusion.scale_ref, bf16[2,3,256,256]{3,2,1,0:T(8,128)(2,1)S(1)} %get-tuple-element.44.w_ref, bf16[8,64,256]{2,1,0:T(8,128)(2,1)S(1)} %collective-permute-done.4.cnear_ref, ...), custom_call_target="tpu_custom_call" | custom-call | flops 1 | bytes 1 | tf_op jit(solution)/shard_map/pallas_call | solution.py:526
  63.9 1.0 %shard_map.55 = (f32[8,256,256]{2,1,0:T(8,128)S(1)}, bf16[2,8,64,256]{3,2,1,0:T(8,128)(2,1)S(1)}) custom-call(s32[6]{0:T(128)S(1)} %stack.39.flag_ref, f32[6,256]{1,0:T(8,128)S(1)} %pad_maximum_fusion.scale_ref, bf16[3,256,256]{2,1,0:T(8,128)(2,1)S(1)} %get-tuple-element.43.w_ref, bf16[8,64,256]{2,1,0:T(8,128)(2,1)S(1)} %get-tuple-element.70.near2_ref, ...), custom_call_target="tpu_custom_call" | custom-call | flops 1 | bytes 1 | tf_op jit(solution)/shard_map/pallas_call | solution.py:526
  64.9 1.8 %collective-permute-done.11.cmid_ref = bf16[8,64,256]{2,1,0:T(8,128)(2,1)S(1)} collective-permute-done((bf16[8,64,256]{2,1,0:T(8,128)(2,1)S(1)}, bf16[8,64,256]{2,1,0:T(8,128)(2,1)S(1)}, u32[]{:S(2)}, u32[]{:S(2)}) %collective-permute-start.11) | collective-permute-done | bytes 262176 | tf_op jit(solution)/shard_map/ppermute | solution.py:521
  66.7 2.4 %collective-permute-start.12 = (bf16[8,64,256]{2,1,0:T(8,128)(2,1)S(1)}, bf16[8,64,256]{2,1,0:T(8,128)(2,1)S(1)}, u32[]{:S(2)}, u32[]{:S(2)}) collective-permute-start(bf16[8,64,256]{2,1,0:T(8,128)(2,1)S(1)} %get-tuple-element.79.near_ref), channel_id=1, source_target_pairs={{0,1},{1,0},{2,3},{3,2},{4,5},{5,4},{6,7},{7,6},{8,9},{9,8},{10,11... | collective-permute-start | bytes 786440 | tf_op jit(solution)/shard_map/ppermute | solution.py:568
  69.1 1.5 %shard_map.56 = (bf16[8,128,256]{2,1,0:T(8,128)(2,1)S(1)}, bf16[8,128,256]{2,1,0:T(8,128)(2,1)S(1)}) custom-call(s32[6]{0:T(128)S(1)} %stack.39.flag_ref, f32[6,256]{1,0:T(8,128)S(1)} %pad_maximum_fusion.scale_ref, bf16[2,3,256,256]{3,2,1,0:T(8,128)(2,1)S(1)} %get-tuple-element.44.w_ref, bf16[8,64,256]{2,1,0:T(8,128)(2,1)S(1)} %collective-permute-done.11.cmid_ref, ...), custom_call_target="tpu_custom_call" | custom-call | flops 1 | bytes 1 | tf_op jit(solution)/shard_map/pallas_call | solution.py:526
  70.6 0.0 collective-permute-done.12.side_ref
  70.6 2.1 %shard_map.57 = bf16[8,256,256]{2,1,0:T(8,128)(2,1)} custom-call(s32[6]{0:T(128)S(1)} %stack.39.flag_ref, f32[6,256]{1,0:T(8,128)S(1)} %pad_maximum_fusion.scale_ref, bf16[3,256,256]{2,1,0:T(8,128)(2,1)S(1)} %get-tuple-element.43.w_ref, bf16[2,8,64,256]{3,2,1,0:T(8,128)(2,1)S(1)} %get-tuple-element.74.ends_ref, ...), custom_call_target="tpu_custom_call" | custom-call | flops 1 | bytes 1 | tf_op jit(solution)/shard_map/pallas_call | solution.py:576
  (1 shorter events, 0.0 us)
Async XLA Ops:
  0.1 1.2 %copy-start.1 = (bf16[8,256,256]{2,1,0:T(8,128)(2,1)S(1)}, bf16[8,256,256]{2,1,0:T(8,128)(2,1)}, u32[]{:S(2)}) copy-start(bf16[8,256,256]{2,1,0:T(8,128)(2,1)} %refs_0_.1) | copy-start | bytes 3145732
  1.3 11.4 %copy-start.2 = (f32[3,256]{1,0:T(4,128)S(1)}, f32[3,256]{1,0:T(4,128)}, u32[]{:S(2)}) copy-start(f32[3,256]{1,0:T(4,128)} %param.6) | copy-start | bytes 9220
  1.3 11.4 %copy-start.3 = (f32[3,256]{1,0:T(4,128)S(1)}, f32[3,256]{1,0:T(4,128)}, u32[]{:S(2)}) copy-start(f32[3,256]{1,0:T(4,128)} %param.5) | copy-start | bytes 9220
  2.1 11.2 %collective-permute-start.7 = (bf16[4,112,256]{2,1,0:T(8,128)(2,1)S(1)}, bf16[4,112,256]{2,1,0:T(8,128)(2,1)S(1)}, u32[]{:S(2)}, u32[]{:S(2)}) collective-permute-start(bf16[4,112,256]{2,1,0:T(8,128)(2,1)S(1)} %get-tuple-element.58), channel_id=1, source_target_pairs={{0,2},{2,0},{4,6},{6,4},{8,10},{10,8},{12,14},{14,12},{1,3},{3,1},... | collective-permute-start | bytes 688136 | tf_op jit(solution)/shard_map/ppermute | solution.py:435
  4.2 9.0 %collective-permute-start.8 = (bf16[4,112,256]{2,1,0:T(8,128)(2,1)S(1)}, bf16[4,112,256]{2,1,0:T(8,128)(2,1)S(1)}, u32[]{:S(2)}, u32[]{:S(2)}) collective-permute-start(bf16[4,112,256]{2,1,0:T(8,128)(2,1)S(1)} %get-tuple-element.59), channel_id=1, source_target_pairs={{2,4},{4,2},{6,8},{8,6},{10,12},{12,10},{3,5},{5,3},{7,9},{9,7},{1... | collective-permute-start | bytes 688136 | tf_op jit(solution)/shard_map/ppermute | solution.py:436
  4.9 2.0 %copy-start = (bf16[3,3,3,256,256]{4,3,2,1,0:T(8,128)(2,1)S(1)}, bf16[3,3,3,256,256]{4,3,2,1,0:T(8,128)(2,1)}, u32[]{:S(2)}) copy-start(bf16[3,3,3,256,256]{4,3,2,1,0:T(8,128)(2,1)} %w_ref.1) | copy-start | bytes 10616836
  7.6 18.5 %collective-permute-start.2 = (bf16[4,160,256]{2,1,0:T(8,128)(2,1)S(1)}, bf16[4,160,256]{2,1,0:T(8,128)(2,1)S(1)}, u32[]{:S(2)}, u32[]{:S(2)}) collective-permute-start(bf16[4,160,256]{2,1,0:T(8,128)(2,1)S(1)} %get-tuple-element.53), channel_id=1, source_target_pairs={{6,8},{8,6},{7,9},{9,7},{22,24},{24,22},{23,25},{25,23}} | collective-permute-start | bytes 983048 | tf_op jit(solution)/shard_map/ppermute | solution.py:452
  8.3 17.8 %collective-permute-start = (bf16[4,144,256]{2,1,0:T(8,128)(2,1)S(1)}, bf16[4,144,256]{2,1,0:T(8,128)(2,1)S(1)}, u32[]{:S(2)}, u32[]{:S(2)}) collective-permute-start(bf16[4,144,256]{2,1,0:T(8,128)(2,1)S(1)} %get-tuple-element.51), channel_id=1, source_target_pairs={{0,2},{2,0},{4,6},{6,4},{8,10},{10,8},{12,14},{14,12},{1,3},{3,1},... | collective-permute-start | bytes 884744 | tf_op jit(solution)/shard_map/ppermute | solution.py:450
  12.1 14.0 %collective-permute-start.1 = (bf16[4,144,256]{2,1,0:T(8,128)(2,1)S(1)}, bf16[4,144,256]{2,1,0:T(8,128)(2,1)S(1)}, u32[]{:S(2)}, u32[]{:S(2)}) collective-permute-start(bf16[4,144,256]{2,1,0:T(8,128)(2,1)S(1)} %get-tuple-element.52), channel_id=1, source_target_pairs={{2,4},{4,2},{10,12},{12,10},{3,5},{5,3},{11,13},{13,11},{18,20},{2... | collective-permute-start | bytes 884744 | tf_op jit(solution)/shard_map/ppermute | solution.py:451
  15.8 27.0 %collective-permute-start.9 = (bf16[8,96,256]{2,1,0:T(8,128)(2,1)S(1)}, bf16[8,96,256]{2,1,0:T(8,128)(2,1)S(1)}, u32[]{:S(2)}, u32[]{:S(2)}) collective-permute-start(bf16[8,96,256]{2,1,0:T(8,128)(2,1)S(1)} %get-tuple-element.62.far_ref), channel_id=1, source_target_pairs={{0,8},{2,10},{4,12},{6,14},{8,0},{10,2},{12,4},{14,6},{1,9},{3,11}... | collective-permute-start | bytes 1179656 | tf_op jit(solution)/shard_map/ppermute | solution.py:465
  26.7 3.8 %collective-permute-start.3 = (bf16[16,16,256]{2,1,0:T(8,128)(2,1)S(1)}, bf16[16,16,256]{2,1,0:T(8,128)(2,1)S(1)}, u32[]{:S(2)}, u32[]{:S(2)}) collective-permute-start(bf16[16,16,256]{2,1,0:T(8,128)(2,1)S(1)} %shard_map.48), channel_id=1, source_target_pairs={{0,1},{1,0},{2,3},{3,2},{4,5},{5,4},{6,7},{7,6},{8,9},{9,8},{10,11... | collective-permute-start | bytes 393224 | tf_op jit(solution)/shard_map/ppermute | solution.py:478
  34.4 22.6 %collective-permute-start.5 = (bf16[8,32,256]{2,1,0:T(8,128)(2,1)S(1)}, bf16[8,32,256]{2,1,0:T(8,128)(2,1)S(1)}, u32[]{:S(2)}, u32[]{:S(2)}) collective-permute-start(bf16[8,32,256]{2,1,0:T(8,128)(2,1)S(1)} %get-tuple-element.64), channel_id=1, source_target_pairs={{0,8},{2,10},{4,12},{6,14},{8,0},{10,2},{12,4},{14,6},{1,9},{3,11}... | collective-permute-start | bytes 393224 | tf_op jit(solution)/shard_map/ppermute | solution.py:498
  37.3 25.4 %collective-permute-start.4 = (bf16[8,64,256]{2,1,0:T(8,128)(2,1)S(1)}, bf16[8,64,256]{2,1,0:T(8,128)(2,1)S(1)}, u32[]{:S(2)}, u32[]{:S(2)}) collective-permute-start(bf16[8,64,256]{2,1,0:T(8,128)(2,1)S(1)} %get-tuple-element.55), channel_id=1, source_target_pairs={{0,8},{2,10},{4,12},{6,14},{8,0},{10,2},{12,4},{14,6},{1,9},{3,11}... | collective-permute-start | bytes 786440 | tf_op jit(solution)/shard_map/ppermute | solution.py:499
  40.5 26.2 %collective-permute-start.11 = (bf16[8,64,256]{2,1,0:T(8,128)(2,1)S(1)}, bf16[8,64,256]{2,1,0:T(8,128)(2,1)S(1)}, u32[]{:S(2)}, u32[]{:S(2)}) collective-permute-start(bf16[8,64,256]{2,1,0:T(8,128)(2,1)S(1)} %get-tuple-element.60.mid_ref), channel_id=1, source_target_pairs={{0,8},{2,10},{4,12},{6,14},{8,0},{10,2},{12,4},{14,6},{1,9},{3,11}... | collective-permute-start | bytes 786440 | tf_op jit(solution)/shard_map/ppermute | solution.py:521
  42.8 17.0 %collective-permute-start.10 = (bf16[8,32,256]{2,1,0:T(8,128)(2,1)S(1)}, bf16[8,32,256]{2,1,0:T(8,128)(2,1)S(1)}, u32[]{:S(2)}, u32[]{:S(2)}) collective-permute-start(bf16[8,32,256]{2,1,0:T(8,128)(2,1)S(1)} %get-tuple-element.64), channel_id=1, source_target_pairs={{0,1},{1,0},{2,3},{3,2},{4,5},{5,4},{6,7},{7,6},{8,9},{9,8},{10,11... | collective-permute-start | bytes 393224 | tf_op jit(solution)/shard_map/ppermute | solution.py:524
  57.0 5.7 %collective-permute-start.6 = (bf16[8,32,256]{2,1,0:T(8,128)(2,1)S(1)}, bf16[8,32,256]{2,1,0:T(8,128)(2,1)S(1)}, u32[]{:S(2)}, u32[]{:S(2)}) collective-permute-start(bf16[8,32,256]{2,1,0:T(8,128)(2,1)S(1)} %collective-permute-done.5.rim_ref), channel_id=1, source_target_pairs={{0,1},{1,0},{2,3},{3,2},{4,5},{5,4},{6,7},{7,6},{8,9},{9,8},{10,11... | collective-permute-start | bytes 393224 | tf_op jit(solution)/shard_map/ppermute | solution.py:548
  66.7 3.9 %collective-permute-start.12 = (bf16[8,64,256]{2,1,0:T(8,128)(2,1)S(1)}, bf16[8,64,256]{2,1,0:T(8,128)(2,1)S(1)}, u32[]{:S(2)}, u32[]{:S(2)}) collective-permute-start(bf16[8,64,256]{2,1,0:T(8,128)(2,1)S(1)} %get-tuple-element.79.near_ref), channel_id=1, source_target_pairs={{0,1},{1,0},{2,3},{3,2},{4,5},{5,4},{6,7},{7,6},{8,9},{9,8},{10,11... | collective-permute-start | bytes 786440 | tf_op jit(solution)/shard_map/ppermute | solution.py:568

commit v10 on v9

--- a/solution.py
+++ b/solution.py
@@ -119,7 +119,7 @@
 
 
 def row_of(flag_ref, row):
-    return row if isinstance(row, int) else jnp.where(flag_ref[4] == 0, *row)
+    return row if isinstance(row, int) else jnp.where(flag_ref[2] == 0, *row)
 
 
 def guarded(flag_ref, condition, action):
@@ -164,7 +164,7 @@
 def hold_kernel(flag_ref, w_ref, first_ref, second_ref, last_ref):
     first_ref[...] = w_ref[0]
     second_ref[0] = w_ref[1, 1]
-    second_ref[1] = w_ref[1, flag_ref[3]]
+    second_ref[1] = w_ref[1, flag_ref[1]]
     last_ref[...] = w_ref[2, 1]
 
 
@@ -398,22 +398,16 @@
     wide = strip + pad
     core, row = lax.axis_index("col"), lax.axis_index("row")
     upper_half = row < group
-    beside = (row == group) | (row == group - 1)
-    flags = jnp.stack(
-        [core, row == group - 1, row == group, jnp.where(upper_half, 2, 0), row % 2, beside]
-    ).astype(jnp.int32)
-    even, odd, apart, at_middle = (4, 0), (4, 1), (5, 0), (5, 1)
+    flags = jnp.stack([core, jnp.where(upper_half, 2, 0), row % 2]).astype(jnp.int32)
+    even, odd = (2, 0), (2, 1)
     one_at, two_at = (half + rows, 0), (0, half + rows)
     swap = [(0, 1), (1, 0)]
     partner = [(i, (i + group) % size) for i in range(size)]
     first_pairs = [(i, i ^ 1) for i in range(size)]
     second_pairs = [(i, ((i + 1) ^ 1) - 1) for i in range(1, size - 1)]
-    across = [(group - 1, group), (group, group - 1)]
-    second_within = [pair for pair in second_pairs if pair not in across]
 
     far_wide_at, near_wide_at = (0, cols - wide), (cols - wide, 0)
     span, span_at = cols - wide, (wide, 0)
-    middle_at = (wide - pad, 0)
     parts = (
         (None, 0, 0, rows, far_wide_at, wide, 0, 0),
         (None, 0, 0, rows, near_wide_at, wide, 1, 0),
@@ -426,11 +420,9 @@
         (odd, 0, 0, half, span_at, span, 5, 0),
         (even, 0, 0, half, span_at, span, 6, 0),
         (odd, 0, half, half, span_at, span, 6, 0),
-        ((1, 1), 0, half, half, middle_at, span + pad, 7, 0),
-        ((1, 0), 0, 0, half, middle_at, span + pad, 7, 0),
     )
     (
-        far_x, near_x, mid_x, far_one, far_two, one, two, middle
+        far_x, near_x, mid_x, far_one, far_two, one, two
     ) = copies(flags, (context_map,), parts)
     far_one = lax.ppermute(far_one, "row", first_pairs)
     far_two = lax.ppermute(far_two, "row", second_pairs)
@@ -446,10 +438,9 @@
         [smem_spec(), vmem_spec()],
         [],
     )(flags, conv_weights)
-    one, two, middle, first_w = lax.optimization_barrier((one, two, middle, first_w))
+    one, two, first_w = lax.optimization_barrier((one, two, first_w))
     one = lax.ppermute(one, "row", first_pairs)
-    two = lax.ppermute(two, "row", second_within)
-    middle = lax.ppermute(middle, "row", across)
+    two = lax.ppermute(two, "row", second_pairs)
 
     params = (scales, first_w)
     far_body, far_edge = (pad, 0), (0, wide)
@@ -464,28 +455,26 @@
     )
     cross_far = lax.ppermute(far_n, "row", partner)
 
-    near_end, span_end, middle_end = (wide - pad, 0), (span - pad, 0), (span, 0)
+    near_end, span_end = (wide - pad, 0), (span - pad, 0)
     (rim,) = copies(
         flags,
-        (near_x, one, two, middle),
+        (near_x, one, two),
         (
             (None, 1, 0, half, span_end, pad, 0, one_at),
-            (apart, 2, 0, half, span_end, pad, 0, two_at),
-            (at_middle, 3, 0, half, middle_end, pad, 0, two_at),
+            (None, 2, 0, half, span_end, pad, 0, two_at),
             (None, 0, 0, rows, near_end, pad, 0, half),
         ),
     )
     rim = lax.ppermute(rim, "col", swap)
-    near_body, near_span, near_middle = (0, pad), (span - wide, 0), (span + pad - wide, 0)
+    near_body, near_span = (0, pad), (span - wide, 0)
     near_segments = (
         (None, 0, 0, half, rows, (0, 0), near_body, wide),
         (None, 1, 0, one_at, half, near_span, near_body, wide),
-        (apart, 2, 0, two_at, half, near_span, near_body, wide),
-        (at_middle, 4, 0, two_at, half, near_middle, near_body, wide),
+        (None, 2, 0, two_at, half, near_span, near_body, wide),
         (None, 3, 0, 0, 2 * rows, (0, 0), (wide, 0), pad),
     )
     near1, near_n = first_layer(
-        flags, params, (near_x, one, two, rim, middle), near_segments, (pad, 0), strip
+        flags, params, (near_x, one, two, rim), near_segments, (pad, 0), strip
     )
     near_rim, near_rest = copies(
         flags,
@@ -499,20 +488,18 @@
     cross_near = lax.ppermute(near_rest, "row", partner)
     side_pads = 2 * pad
     far_side, rest_side = ((wide - side_pads, 0), (0, mid)), ((0, span - mid), (side_pads, 0))
-    middle_side = ((pad, span - mid), (side_pads, 0))
     mid_segments = (
         (None, 0, 0, half, rows, (0, 0), (0, 0), mid + side_pads),
         (None, 1, 0, one_at, half, *far_side, side_pads),
         (None, 2, 0, two_at, half, *far_side, side_pads),
         (None, 3, 0, one_at, half, *rest_side, mid),
-        (apart, 4, 0, two_at, half, *rest_side, mid),
-        (at_middle, 5, 0, two_at, half, *middle_side, mid),
+        (None, 4, 0, two_at, half, *rest_side, mid),
     )
     mid1, mid_n = first_layer(
         flags,
         params,
         (
-            mid_x, far_one, far_two, one, two, middle
+            mid_x, far_one, far_two, one, two
         ),
         mid_segments,
         (pad, pad),

time: 73.1 us -> 72.3 us (0.989)
  waiting for transfers between devices: 10.5 us -> 22.9 us
  starting transfers between devices: 38.4 us -> 27.1 us
  Pallas kernels: 20.3 us -> 18.7 us
    ppermute x1, waiting for transfers between devices: 0.01 us -> 10.5 us  [by_halves(): cross_far = lax.ppermute(far_n, 'row', partner)]
    ppermute x1, starting transfers between devices: 14.2 us -> 3.82 us  [by_halves(): near_side = lax.ppermute(near_rim, 'col', swap)]
    ppermute x1, starting transfers between devices: 2.87 us -> 4.61 us  [by_halves(): cross_rim = lax.ppermute(near_rim, 'row', partner)]
    pallas_call x3, Pallas kernels: 8.99 us -> 7.48 us  [first_layer(): kernel_call(functools.partial(first_layer_kernel, segments, out_at, rows,...]
    ppermute x1, starting transfers between devices: 2.81 us -> 1.61 us  [by_halves(): rim = lax.ppermute(rim, 'col', swap)]
  transfers between devices with their start and end apart: 13 -> 12, of which waited for: 4 -> 5; matrix products, arithmetic and copies ran while one was open for 0% -> 0% of each run, Pallas kernels for 24% -> 22%
where the time goes in v10:
time: 72.3 us; the launch traced here: 72.1 us
  starting transfers between devices  27.1 us (37%)
  waiting for transfers between devices  22.9 us (32%)
  Pallas kernels  18.7 us (26%)
  local copies, waits for them, and re-layouts  3.23 us (4%)
    ppermute x1, waiting for transfers between devices, by_halves(): cross_far = lax.ppermute(far_n, 'row', partner)  10.5 us
    ppermute x1, waiting for transfers between devices, by_halves(): one = lax.ppermute(one, 'row', first_pairs)  7.81 us
    pallas_call x3, Pallas kernels, first_layer(): kernel_call(functools.partial(first_layer_kernel, segments, out_at, rows,...  7.48 us
    pallas_call x4, Pallas kernels, plain(): kernel_call(body, out, [smem_spec()] + [vmem_spec()] * (len(operands) + 2...  6.53 us
    ppermute x1, starting transfers between devices, by_halves(): cross_rim = lax.ppermute(near_rim, 'row', partner)  4.61 us
    ppermute x1, starting transfers between devices, by_halves(): near_side = lax.ppermute(near_rim, 'col', swap)  3.82 us
    ppermute x1, starting transfers between devices, by_halves(): one = lax.ppermute(one, 'row', first_pairs)  3.78 us
    unnamed x8, local copies, waits for them, and re-layouts  3.23 us
  transfers between devices with their start and end apart: 12, of which 5 were waited for; matrix products, arithmetic and copies ran while one was open for 0% of the time, Pallas kernels for 22%

profile of v10, /device:TPU:1, one launch (start us, length us, event | category | flops | bytes accessed | tf_op | source)
XLA Modules:
  0.0 72.1 jit_solution(15937732622486642816)
XLA Ops:
  0.0 0.1 pad_add_fusion.flag_ref
  0.1 0.0 copy-start.1
  0.1 1.2 %copy-done.1 = bf16[8,256,256]{2,1,0:T(8,128)(2,1)S(1)} copy-done((bf16[8,256,256]{2,1,0:T(8,128)(2,1)S(1)}, bf16[8,256,256]{2,1,0:T(8,128)(2,1)}, u32[]{:S(2)}) %copy-start.1) | copy-done | bytes 1048600
  1.3 0.0 copy-start.2
  1.3 0.0 copy-start.3
  1.3 0.8 %shard_map.47 = (bf16[8,112,256]{2,1,0:T(8,128)(2,1)S(1)}, bf16[8,112,256]{2,1,0:T(8,128)(2,1)S(1)}, bf16[8,96,256]{2,1,0:T(8,128)(2,1)S(1)}, bf16[4,112,256]{2,...) custom-call(s32[3]{0:T(128)S(1)} %pad_add_fusion.flag_ref, ...), custom_call_target="tpu_custom_call" | custom-call | flops 1 | bytes 1 | tf_op jit(solution)/shard_map/pallas_call | solution.py:156
  2.1 2.1 %collective-permute-start.6 = (bf16[4,112,256]{2,1,0:T(8,128)(2,1)S(1)}, bf16[4,112,256]{2,1,0:T(8,128)(2,1)S(1)}, u32[]{:S(2)}, u32[]{:S(2)}) collective-permute-start(bf16[4,112,256]{2,1,0:T(8,128)(2,1)S(1)} %get-tuple-element.54), channel_id=1, source_target_pairs={{0,2},{2,0},{4,6},{6,4},{8,10},{10,8},{12,14},{14,12},{1,3},{3,1},... | collective-permute-start | bytes 688136 | tf_op jit(solution)/shard_map/ppermute | solution.py:427
  4.2 0.7 collective-permute-start.7
  4.9 0.0 copy-start
  4.9 2.0 %copy-done = bf16[3,3,3,256,256]{4,3,2,1,0:T(8,128)(2,1)S(1)} copy-done((bf16[3,3,3,256,256]{4,3,2,1,0:T(8,128)(2,1)S(1)}, bf16[3,3,3,256,256]{4,3,2,1,0:T(8,128)(2,1)}, u32[]{:S(2)}) %copy-start) | copy-done | bytes 3538968
  6.9 0.7 shard_map.46
  7.6 3.8 %collective-permute-start = (bf16[4,144,256]{2,1,0:T(8,128)(2,1)S(1)}, bf16[4,144,256]{2,1,0:T(8,128)(2,1)S(1)}, u32[]{:S(2)}, u32[]{:S(2)}) collective-permute-start(bf16[4,144,256]{2,1,0:T(8,128)(2,1)S(1)} %get-tuple-element.48), channel_id=1, source_target_pairs={{0,2},{2,0},{4,6},{6,4},{8,10},{10,8},{12,14},{14,12},{1,3},{3,1},... | collective-permute-start | bytes 884744 | tf_op jit(solution)/shard_map/ppermute | solution.py:442
  11.3 0.7 collective-permute-start.1
  12.0 0.0 copy-done.2
  12.0 0.0 copy-done.3
  12.0 1.2 %collective-permute-done.6.rest_1_ = bf16[4,112,256]{2,1,0:T(8,128)(2,1)S(1)} collective-permute-done((bf16[4,112,256]{2,1,0:T(8,128)(2,1)S(1)}, bf16[4,112,256]{2,1,0:T(8,128)(2,1)S(1)}, u32[]{:S(2)}, u32[]{:S(2)}) %collective-permute-start.6) | collective-permute-done | bytes 229408 | tf_op jit(solution)/shard_map/ppermute | solution.py:427
  13.2 0.0 collective-permute-done.7.rest_2_
  13.2 2.5 %shard_map.52 = (bf16[8,96,256]{2,1,0:T(8,128)(2,1)S(1)}, bf16[8,96,256]{2,1,0:T(8,128)(2,1)S(1)}) custom-call(s32[3]{0:T(128)S(1)} %pad_add_fusion.flag_ref, f32[6,256]{1,0:T(8,128)S(1)} %pad_maximum_fusion.scale_ref, bf16[3,3,256,256]{3,2,1,0:T(8,128)(2,1)S(1)} %get-tuple-element.46.w_ref, bf16[8,112,256]{2,1,0:T(8,128)(2,1)S(1)} %get-tuple-element.57.rest_0_, ...), custom_call_target="tpu_custom_call" | custom-call | flops 1 | bytes 1 | tf_op jit(solution)/shard_map/pallas_call | solution.py:219
  15.7 2.5 %collective-permute-start.8 = (bf16[8,96,256]{2,1,0:T(8,128)(2,1)S(1)}, bf16[8,96,256]{2,1,0:T(8,128)(2,1)S(1)}, u32[]{:S(2)}, u32[]{:S(2)}) collective-permute-start(bf16[8,96,256]{2,1,0:T(8,128)(2,1)S(1)} %get-tuple-element.58.far_ref), channel_id=1, source_target_pairs={{0,8},{2,10},{4,12},{6,14},{8,0},{10,2},{12,4},{14,6},{1,9},{3,11}... | collective-permute-start | bytes 1179656 | tf_op jit(solution)/shard_map/ppermute | solution.py:456
  18.2 7.8 %collective-permute-done.refs_1_.rest_1_.rest_3_ = bf16[4,144,256]{2,1,0:T(8,128)(2,1)S(1)} collective-permute-done((bf16[4,144,256]{2,1,0:T(8,128)(2,1)S(1)}, bf16[4,144,256]{2,1,0:T(8,128)(2,1)S(1)}, u32[]{:S(2)}, u32[]{:S(2)}) %collective-permute-start) | collective-permute-done | bytes 294944 | tf_op jit(solution)/shard_map/ppermute | solution.py:442
  26.0 0.0 collective-permute-done.1.refs_2_.rest_2_.rest_4_
  26.0 0.6 shard_map.48
  26.6 1.6 %collective-permute-start.2 = (bf16[16,16,256]{2,1,0:T(8,128)(2,1)S(1)}, bf16[16,16,256]{2,1,0:T(8,128)(2,1)S(1)}, u32[]{:S(2)}, u32[]{:S(2)}) collective-permute-start(bf16[16,16,256]{2,1,0:T(8,128)(2,1)S(1)} %shard_map.48), channel_id=1, source_target_pairs={{0,1},{1,0},{2,3},{3,2},{4,5},{5,4},{6,7},{7,6},{8,9},{9,8},{10,11... | collective-permute-start | bytes 393224 | tf_op jit(solution)/shard_map/ppermute | solution.py:468
  28.2 1.0 %collective-permute-done.2.rest_3_ = bf16[16,16,256]{2,1,0:T(8,128)(2,1)S(1)} collective-permute-done((bf16[16,16,256]{2,1,0:T(8,128)(2,1)S(1)}, bf16[16,16,256]{2,1,0:T(8,128)(2,1)S(1)}, u32[]{:S(2)}, u32[]{:S(2)}) %collective-permute-start.2) | collective-permute-done | bytes 131104 | tf_op jit(solution)/shard_map/ppermute | solution.py:468
  29.2 2.7 %shard_map.49 = (bf16[8,96,256]{2,1,0:T(8,128)(2,1)S(1)}, bf16[8,96,256]{2,1,0:T(8,128)(2,1)S(1)}) custom-call(s32[3]{0:T(128)S(1)} %pad_add_fusion.flag_ref, f32[6,256]{1,0:T(8,128)S(1)} %pad_maximum_fusion.scale_ref, bf16[3,3,256,256]{3,2,1,0:T(8,128)(2,1)S(1)} %get-tuple-element.46.w_ref, bf16[8,112,256]{2,1,0:T(8,128)(2,1)S(1)} %get-tuple-element.47.refs_0_.rest_0_, ...), custom_call_target="tpu_custom_call" | custom-call | flops 1 | bytes 1 | tf_op jit(solution)/shard_map/pallas_call | solution.py:219
  31.9 0.6 shard_map.50
  32.5 4.6 %collective-permute-start.4 = (bf16[8,32,256]{2,1,0:T(8,128)(2,1)S(1)}, bf16[8,32,256]{2,1,0:T(8,128)(2,1)S(1)}, u32[]{:S(2)}, u32[]{:S(2)}) collective-permute-start(bf16[8,32,256]{2,1,0:T(8,128)(2,1)S(1)} %get-tuple-element.60), channel_id=1, source_target_pairs={{0,8},{2,10},{4,12},{6,14},{8,0},{10,2},{12,4},{14,6},{1,9},{3,11}... | collective-permute-start | bytes 393224 | tf_op jit(solution)/shard_map/ppermute | solution.py:487
  37.1 0.1 collective-permute-start.3
  37.2 2.3 %shard_map.51 = (bf16[8,64,256]{2,1,0:T(8,128)(2,1)S(1)}, bf16[8,64,256]{2,1,0:T(8,128)(2,1)S(1)}) custom-call(s32[3]{0:T(128)S(1)} %pad_add_fusion.flag_ref, f32[6,256]{1,0:T(8,128)S(1)} %pad_maximum_fusion.scale_ref, bf16[3,3,256,256]{3,2,1,0:T(8,128)(2,1)S(1)} %get-tuple-element.46.w_ref, bf16[8,96,256]{2,1,0:T(8,128)(2,1)S(1)} %get-tuple-element.53.rest_0_, ...), custom_call_target="tpu_custom_call" | custom-call | flops 1 | bytes 1 | tf_op jit(solution)/shard_map/pallas_call | solution.py:219
  39.4 2.4 %collective-permute-start.10 = (bf16[8,64,256]{2,1,0:T(8,128)(2,1)S(1)}, bf16[8,64,256]{2,1,0:T(8,128)(2,1)S(1)}, u32[]{:S(2)}, u32[]{:S(2)}) collective-permute-start(bf16[8,64,256]{2,1,0:T(8,128)(2,1)S(1)} %get-tuple-element.56.mid_ref), channel_id=1, source_target_pairs={{0,8},{2,10},{4,12},{6,14},{8,0},{10,2},{12,4},{14,6},{1,9},{3,11}... | collective-permute-start | bytes 786440 | tf_op jit(solution)/shard_map/ppermute | solution.py:508
  41.8 10.5 %collective-permute-done.8.cfar_ref = bf16[8,96,256]{2,1,0:T(8,128)(2,1)S(1)} collective-permute-done((bf16[8,96,256]{2,1,0:T(8,128)(2,1)S(1)}, bf16[8,96,256]{2,1,0:T(8,128)(2,1)S(1)}, u32[]{:S(2)}, u32[]{:S(2)}) %collective-permute-start.8) | collective-permute-done | bytes 393248 | tf_op jit(solution)/shard_map/ppermute | solution.py:456
  52.3 3.8 %collective-permute-start.9 = (bf16[8,32,256]{2,1,0:T(8,128)(2,1)S(1)}, bf16[8,32,256]{2,1,0:T(8,128)(2,1)S(1)}, u32[]{:S(2)}, u32[]{:S(2)}) collective-permute-start(bf16[8,32,256]{2,1,0:T(8,128)(2,1)S(1)} %get-tuple-element.60), channel_id=1, source_target_pairs={{0,1},{1,0},{2,3},{3,2},{4,5},{5,4},{6,7},{7,6},{8,9},{9,8},{10,11... | collective-permute-start | bytes 393224 | tf_op jit(solution)/shard_map/ppermute | solution.py:511
  56.2 0.0 collective-permute-done.4.rim_ref
  56.2 2.8 %collective-permute-start.5 = (bf16[8,32,256]{2,1,0:T(8,128)(2,1)S(1)}, bf16[8,32,256]{2,1,0:T(8,128)(2,1)S(1)}, u32[]{:S(2)}, u32[]{:S(2)}) collective-permute-start(bf16[8,32,256]{2,1,0:T(8,128)(2,1)S(1)} %collective-permute-done.4.rim_ref), channel_id=1, source_target_pairs={{0,1},{1,0},{2,3},{3,2},{4,5},{5,4},{6,7},{7,6},{8,9},{9,8},{10,11... | collective-permute-start | bytes 393224 | tf_op jit(solution)/shard_map/ppermute | solution.py:535
  59.0 0.0 collective-permute-done.9.side_ref
  59.0 2.9 %shard_map.53 = (f32[8,256,256]{2,1,0:T(8,128)S(1)}, bf16[8,256,256]{2,1,0:T(8,128)(2,1)S(1)}, bf16[8,64,256]{2,1,0:T(8,128)(2,1)S(1)}, bf16[8,64,256]{2,1,0:T(8,128)(2,1)S(1)}) custom-call(s32[3]{0:T(128)S(1)} %pad_add_fusion.flag_ref, f32[6,256]{1,0:T(8,128)S(1)} %pad_maximum_fusion.scale_ref, bf16[2,3,256,256]{3,2,1,0:T(8,128)(2,1)S(1)} %get-tuple-element.42.w_ref, ...), custom_call_target="tpu_custom_call" | custom-call | flops 1 | bytes 1 | tf_op jit(solution)/shard_map/pallas_call | solution.py:513
  61.8 0.0 collective-permute-done.5.side_ref
  61.8 0.0 collective-permute-done.3.cnear_ref
  61.8 1.1 %shard_map.54 = (bf16[8,64,256]{2,1,0:T(8,128)(2,1)S(1)}, bf16[8,64,256]{2,1,0:T(8,128)(2,1)S(1)}) custom-call(s32[3]{0:T(128)S(1)} %pad_add_fusion.flag_ref, f32[6,256]{1,0:T(8,128)S(1)} %pad_maximum_fusion.scale_ref, bf16[2,3,256,256]{3,2,1,0:T(8,128)(2,1)S(1)} %get-tuple-element.42.w_ref, bf16[8,64,256]{2,1,0:T(8,128)(2,1)S(1)} %collective-permute-done.3.cnear_ref, ...), custom_call_target="tpu_custom_call" | custom-call | flops 1 | bytes 1 | tf_op jit(solution)/shard_map/pallas_call | solution.py:513
  63.0 1.0 %shard_map.55 = (f32[8,256,256]{2,1,0:T(8,128)S(1)}, bf16[2,8,64,256]{3,2,1,0:T(8,128)(2,1)S(1)}) custom-call(s32[3]{0:T(128)S(1)} %pad_add_fusion.flag_ref, f32[6,256]{1,0:T(8,128)S(1)} %pad_maximum_fusion.scale_ref, bf16[3,256,256]{2,1,0:T(8,128)(2,1)S(1)} %get-tuple-element.41.w_ref, bf16[8,64,256]{2,1,0:T(8,128)(2,1)S(1)} %get-tuple-element.66.near2_ref, ...), custom_call_target="tpu_custom_call" | custom-call | flops 1 | bytes 1 | tf_op jit(solution)/shard_map/pallas_call | solution.py:513
  64.0 2.3 %collective-permute-done.10.cmid_ref = bf16[8,64,256]{2,1,0:T(8,128)(2,1)S(1)} collective-permute-done((bf16[8,64,256]{2,1,0:T(8,128)(2,1)S(1)}, bf16[8,64,256]{2,1,0:T(8,128)(2,1)S(1)}, u32[]{:S(2)}, u32[]{:S(2)}) %collective-permute-start.10) | collective-permute-done | bytes 262176 | tf_op jit(solution)/shard_map/ppermute | solution.py:508
  66.4 2.1 %collective-permute-start.11 = (bf16[8,64,256]{2,1,0:T(8,128)(2,1)S(1)}, bf16[8,64,256]{2,1,0:T(8,128)(2,1)S(1)}, u32[]{:S(2)}, u32[]{:S(2)}) collective-permute-start(bf16[8,64,256]{2,1,0:T(8,128)(2,1)S(1)} %get-tuple-element.75.near_ref), channel_id=1, source_target_pairs={{0,1},{1,0},{2,3},{3,2},{4,5},{5,4},{6,7},{7,6},{8,9},{9,8},{10,11... | collective-permute-start | bytes 786440 | tf_op jit(solution)/shard_map/ppermute | solution.py:555
  68.5 1.5 %shard_map.56 = (bf16[8,128,256]{2,1,0:T(8,128)(2,1)S(1)}, bf16[8,128,256]{2,1,0:T(8,128)(2,1)S(1)}) custom-call(s32[3]{0:T(128)S(1)} %pad_add_fusion.flag_ref, f32[6,256]{1,0:T(8,128)S(1)} %pad_maximum_fusion.scale_ref, bf16[2,3,256,256]{3,2,1,0:T(8,128)(2,1)S(1)} %get-tuple-element.42.w_ref, bf16[8,64,256]{2,1,0:T(8,128)(2,1)S(1)} %collective-permute-done.10.cmid_ref, ...), custom_call_target="tpu_custom_call" | custom-call | flops 1 | bytes 1 | tf_op jit(solution)/shard_map/pallas_call | solution.py:513
  70.0 0.0 collective-permute-done.11.side_ref
  70.0 2.1 %shard_map.57 = bf16[8,256,256]{2,1,0:T(8,128)(2,1)} custom-call(s32[3]{0:T(128)S(1)} %pad_add_fusion.flag_ref, f32[6,256]{1,0:T(8,128)S(1)} %pad_maximum_fusion.scale_ref, bf16[3,256,256]{2,1,0:T(8,128)(2,1)S(1)} %get-tuple-element.41.w_ref, bf16[2,8,64,256]{3,2,1,0:T(8,128)(2,1)S(1)} %get-tuple-element.70.ends_ref, ...), custom_call_target="tpu_custom_call" | custom-call | flops 1 | bytes 1 | tf_op jit(solution)/shard_map/pallas_call | solution.py:563
  (1 shorter events, 0.0 us)
Async XLA Ops:
  0.1 1.2 %copy-start.1 = (bf16[8,256,256]{2,1,0:T(8,128)(2,1)S(1)}, bf16[8,256,256]{2,1,0:T(8,128)(2,1)}, u32[]{:S(2)}) copy-start(bf16[8,256,256]{2,1,0:T(8,128)(2,1)} %refs_0_.1) | copy-start | bytes 3145732
  1.3 10.7 %copy-start.2 = (f32[3,256]{1,0:T(4,128)S(1)}, f32[3,256]{1,0:T(4,128)}, u32[]{:S(2)}) copy-start(f32[3,256]{1,0:T(4,128)} %param.6) | copy-start | bytes 9220
  1.3 10.7 %copy-start.3 = (f32[3,256]{1,0:T(4,128)S(1)}, f32[3,256]{1,0:T(4,128)}, u32[]{:S(2)}) copy-start(f32[3,256]{1,0:T(4,128)} %param.5) | copy-start | bytes 9220
  2.1 11.2 %collective-permute-start.6 = (bf16[4,112,256]{2,1,0:T(8,128)(2,1)S(1)}, bf16[4,112,256]{2,1,0:T(8,128)(2,1)S(1)}, u32[]{:S(2)}, u32[]{:S(2)}) collective-permute-start(bf16[4,112,256]{2,1,0:T(8,128)(2,1)S(1)} %get-tuple-element.54), channel_id=1, source_target_pairs={{0,2},{2,0},{4,6},{6,4},{8,10},{10,8},{12,14},{14,12},{1,3},{3,1},... | collective-permute-start | bytes 688136 | tf_op jit(solution)/shard_map/ppermute | solution.py:427
  4.2 9.0 %collective-permute-start.7 = (bf16[4,112,256]{2,1,0:T(8,128)(2,1)S(1)}, bf16[4,112,256]{2,1,0:T(8,128)(2,1)S(1)}, u32[]{:S(2)}, u32[]{:S(2)}) collective-permute-start(bf16[4,112,256]{2,1,0:T(8,128)(2,1)S(1)} %get-tuple-element.55), channel_id=1, source_target_pairs={{2,4},{4,2},{6,8},{8,6},{10,12},{12,10},{3,5},{5,3},{7,9},{9,7},{1... | collective-permute-start | bytes 688136 | tf_op jit(solution)/shard_map/ppermute | solution.py:428
  4.9 2.0 %copy-start = (bf16[3,3,3,256,256]{4,3,2,1,0:T(8,128)(2,1)S(1)}, bf16[3,3,3,256,256]{4,3,2,1,0:T(8,128)(2,1)}, u32[]{:S(2)}) copy-start(bf16[3,3,3,256,256]{4,3,2,1,0:T(8,128)(2,1)} %w_ref.1) | copy-start | bytes 10616836
  7.6 18.5 %collective-permute-start = (bf16[4,144,256]{2,1,0:T(8,128)(2,1)S(1)}, bf16[4,144,256]{2,1,0:T(8,128)(2,1)S(1)}, u32[]{:S(2)}, u32[]{:S(2)}) collective-permute-start(bf16[4,144,256]{2,1,0:T(8,128)(2,1)S(1)} %get-tuple-element.48), channel_id=1, source_target_pairs={{0,2},{2,0},{4,6},{6,4},{8,10},{10,8},{12,14},{14,12},{1,3},{3,1},... | collective-permute-start | bytes 884744 | tf_op jit(solution)/shard_map/ppermute | solution.py:442
  11.3 14.7 %collective-permute-start.1 = (bf16[4,144,256]{2,1,0:T(8,128)(2,1)S(1)}, bf16[4,144,256]{2,1,0:T(8,128)(2,1)S(1)}, u32[]{:S(2)}, u32[]{:S(2)}) collective-permute-start(bf16[4,144,256]{2,1,0:T(8,128)(2,1)S(1)} %get-tuple-element.49), channel_id=1, source_target_pairs={{2,4},{4,2},{6,8},{8,6},{10,12},{12,10},{3,5},{5,3},{7,9},{9,7},{1... | collective-permute-start | bytes 884744 | tf_op jit(solution)/shard_map/ppermute | solution.py:443
  15.7 36.6 %collective-permute-start.8 = (bf16[8,96,256]{2,1,0:T(8,128)(2,1)S(1)}, bf16[8,96,256]{2,1,0:T(8,128)(2,1)S(1)}, u32[]{:S(2)}, u32[]{:S(2)}) collective-permute-start(bf16[8,96,256]{2,1,0:T(8,128)(2,1)S(1)} %get-tuple-element.58.far_ref), channel_id=1, source_target_pairs={{0,8},{2,10},{4,12},{6,14},{8,0},{10,2},{12,4},{14,6},{1,9},{3,11}... | collective-permute-start | bytes 1179656 | tf_op jit(solution)/shard_map/ppermute | solution.py:456
  26.6 2.6 %collective-permute-start.2 = (bf16[16,16,256]{2,1,0:T(8,128)(2,1)S(1)}, bf16[16,16,256]{2,1,0:T(8,128)(2,1)S(1)}, u32[]{:S(2)}, u32[]{:S(2)}) collective-permute-start(bf16[16,16,256]{2,1,0:T(8,128)(2,1)S(1)} %shard_map.48), channel_id=1, source_target_pairs={{0,1},{1,0},{2,3},{3,2},{4,5},{5,4},{6,7},{7,6},{8,9},{9,8},{10,11... | collective-permute-start | bytes 393224 | tf_op jit(solution)/shard_map/ppermute | solution.py:468
  32.5 23.7 %collective-permute-start.4 = (bf16[8,32,256]{2,1,0:T(8,128)(2,1)S(1)}, bf16[8,32,256]{2,1,0:T(8,128)(2,1)S(1)}, u32[]{:S(2)}, u32[]{:S(2)}) collective-permute-start(bf16[8,32,256]{2,1,0:T(8,128)(2,1)S(1)} %get-tuple-element.60), channel_id=1, source_target_pairs={{0,8},{2,10},{4,12},{6,14},{8,0},{10,2},{12,4},{14,6},{1,9},{3,11}... | collective-permute-start | bytes 393224 | tf_op jit(solution)/shard_map/ppermute | solution.py:487
  37.1 24.8 %collective-permute-start.3 = (bf16[8,64,256]{2,1,0:T(8,128)(2,1)S(1)}, bf16[8,64,256]{2,1,0:T(8,128)(2,1)S(1)}, u32[]{:S(2)}, u32[]{:S(2)}) collective-permute-start(bf16[8,64,256]{2,1,0:T(8,128)(2,1)S(1)} %get-tuple-element.51), channel_id=1, source_target_pairs={{0,8},{2,10},{4,12},{6,14},{8,0},{10,2},{12,4},{14,6},{1,9},{3,11}... | collective-permute-start | bytes 786440 | tf_op jit(solution)/shard_map/ppermute | solution.py:488
  39.4 26.9 %collective-permute-start.10 = (bf16[8,64,256]{2,1,0:T(8,128)(2,1)S(1)}, bf16[8,64,256]{2,1,0:T(8,128)(2,1)S(1)}, u32[]{:S(2)}, u32[]{:S(2)}) collective-permute-start(bf16[8,64,256]{2,1,0:T(8,128)(2,1)S(1)} %get-tuple-element.56.mid_ref), channel_id=1, source_target_pairs={{0,8},{2,10},{4,12},{6,14},{8,0},{10,2},{12,4},{14,6},{1,9},{3,11}... | collective-permute-start | bytes 786440 | tf_op jit(solution)/shard_map/ppermute | solution.py:508
  52.3 6.6 %collective-permute-start.9 = (bf16[8,32,256]{2,1,0:T(8,128)(2,1)S(1)}, bf16[8,32,256]{2,1,0:T(8,128)(2,1)S(1)}, u32[]{:S(2)}, u32[]{:S(2)}) collective-permute-start(bf16[8,32,256]{2,1,0:T(8,128)(2,1)S(1)} %get-tuple-element.60), channel_id=1, source_target_pairs={{0,1},{1,0},{2,3},{3,2},{4,5},{5,4},{6,7},{7,6},{8,9},{9,8},{10,11... | collective-permute-start | bytes 393224 | tf_op jit(solution)/shard_map/ppermute | solution.py:511
  56.2 5.7 %collective-permute-start.5 = (bf16[8,32,256]{2,1,0:T(8,128)(2,1)S(1)}, bf16[8,32,256]{2,1,0:T(8,128)(2,1)S(1)}, u32[]{:S(2)}, u32[]{:S(2)}) collective-permute-start(bf16[8,32,256]{2,1,0:T(8,128)(2,1)S(1)} %collective-permute-done.4.rim_ref), channel_id=1, source_target_pairs={{0,1},{1,0},{2,3},{3,2},{4,5},{5,4},{6,7},{7,6},{8,9},{9,8},{10,11... | collective-permute-start | bytes 393224 | tf_op jit(solution)/shard_map/ppermute | solution.py:535
  66.4 3.6 %collective-permute-start.11 = (bf16[8,64,256]{2,1,0:T(8,128)(2,1)S(1)}, bf16[8,64,256]{2,1,0:T(8,128)(2,1)S(1)}, u32[]{:S(2)}, u32[]{:S(2)}) collective-permute-start(bf16[8,64,256]{2,1,0:T(8,128)(2,1)S(1)} %get-tuple-element.75.near_ref), channel_id=1, source_target_pairs={{0,1},{1,0},{2,3},{3,2},{4,5},{5,4},{6,7},{7,6},{8,9},{9,8},{10,11... | collective-permute-start | bytes 786440 | tf_op jit(solution)/shard_map/ppermute | solution.py:555

commit v11 on v10

--- a/solution.py
+++ b/solution.py
@@ -168,8 +168,11 @@
     last_ref[...] = w_ref[2, 1]
 
 
-def first_layer_kernel(segments, out_at, rows, width, flag_ref, scale_ref, w_ref, *rest):
-    parts, (next_ref, normed_ref, window, taps) = rest[:-4], rest[-4:]
+def first_layer_kernel(
+    segments, out_at, cuts, rows, width, count, flag_ref, scale_ref, w_ref, *rest
+):
+    parts, (next_ref, normed_ref), (window, taps) = rest[:count], rest[count : count + 2], rest[-2:]
+    cut_refs = rest[count + 2 : -2]
     core = flag_ref[0]
     half = rows // 2
     channels = window.shape[2]
@@ -210,15 +213,19 @@
     result = update(current, response, scale_ref[3:4, :])
     next_ref[...] = result.reshape(rows, width, channels)
     normed_ref[...] = normalize(result, scale_ref[1:2, :]).reshape(rows, width, channels)
-
-
-def first_layer(flags, params, parts, segments, out_at, width):
+    for cut_ref, (at, columns) in zip(cut_refs, cuts):
+        cut_ref[...] = normed_ref[:, pl.ds(place(core, *at), columns), :]
+
+
+def first_layer(flags, params, parts, segments, out_at, width, cuts=()):
     rows, _, channels = parts[0].shape
     kind = parts[0].dtype
-    out = jax.ShapeDtypeStruct((rows, width, channels), kind)
     return kernel_call(
-        functools.partial(first_layer_kernel, segments, out_at, rows, width),
-        (out, out),
+        functools.partial(first_layer_kernel, segments, out_at, cuts, rows, width, len(parts)),
+        tuple(
+            jax.ShapeDtypeStruct((rows, columns, channels), kind)
+            for columns in (width, width) + tuple(columns for _, columns in cuts)
+        ),
         [smem_spec()] + [vmem_spec()] * (2 + len(parts)),
         [
             pltpu.VMEM((2 * rows, width + 2 * lane_pad, channels), kind),
@@ -473,16 +480,14 @@
         (None, 2, 0, two_at, half, near_span, near_body, wide),
         (None, 3, 0, 0, 2 * rows, (0, 0), (wide, 0), pad),
     )
-    near1, near_n = first_layer(
-        flags, params, (near_x, one, two, rim), near_segments, (pad, 0), strip
-    )
-    near_rim, near_rest = copies(
+    near1, near_n, near_rim, near_rest = first_layer(
         flags,
-        (near_n,),
-        (
-            (None, 0, 0, rows, (strip - step, 0), step, 0, 0),
-            (None, 0, 0, rows, (0, step), strip - step, 1, 0),
-        ),
+        params,
+        (near_x, one, two, rim),
+        near_segments,
+        (pad, 0),
+        strip,
+        (((strip - step, 0), step), ((0, step), strip - step)),
     )
     cross_rim = lax.ppermute(near_rim, "row", partner)
     cross_near = lax.ppermute(near_rest, "row", partner)

time: 72.3 us -> 72.3 us (level)
    pallas_call x3 -> x2, Pallas kernels: 1.89 us -> 1.32 us  [copies(): kernel_call(functools.partial(copy_kernel, moves, len(arrays)), out, [sme...]
  transfers between devices with their start and end apart: 12 -> 12, of which waited for: 5 -> 5; matrix products, arithmetic and copies ran while one was open for 0% -> 0% of each run, Pallas kernels for 22% -> 21%
where the time goes in v11:
time: 72.3 us; the launch traced here: 72.1 us
  starting transfers between devices  27.1 us (37%)
  waiting for transfers between devices  23.4 us (32%)
  Pallas kernels  18.2 us (25%)
  local copies, waits for them, and re-layouts  3.23 us (4%)
    ppermute x1, waiting for transfers between devices, by_halves(): cross_far = lax.ppermute(far_n, 'row', partner)  11.1 us
    ppermute x1, waiting for transfers between devices, by_halves(): one = lax.ppermute(one, 'row', first_pairs)  7.82 us
    pallas_call x3, Pallas kernels, first_layer(): kernel_call(functools.partial(first_layer_kernel, segments, out_at, cuts,...  7.55 us
    pallas_call x4, Pallas kernels, plain(): kernel_call(body, out, [smem_spec()] + [vmem_spec()] * (len(operands) + 2...  6.54 us
    ppermute x1, starting transfers between devices, by_halves(): cross_rim = lax.ppermute(near_rim, 'row', partner)  4.6 us
    ppermute x1, starting transfers between devices, by_halves(): near_side = lax.ppermute(near_rim, 'col', swap)  3.82 us
    ppermute x1, starting transfers between devices, by_halves(): one = lax.ppermute(one, 'row', first_pairs)  3.78 us
    unnamed x8, local copies, waits for them, and re-layouts  3.23 us
  transfers between devices with their start and end apart: 12, of which 5 were waited for; matrix products, arithmetic and copies ran while one was open for 0% of the time, Pallas kernels for 21%

profile of v11, /device:TPU:1, one launch (start us, length us, event | category | flops | bytes accessed | tf_op | source)
XLA Modules:
  0.0 72.1 jit_solution(14522305901317557605)
XLA Ops:
  0.0 0.1 pad_add_fusion.flag_ref
  0.1 0.0 copy-start.1
  0.1 1.2 %copy-done.1 = bf16[8,256,256]{2,1,0:T(8,128)(2,1)S(1)} copy-done((bf16[8,256,256]{2,1,0:T(8,128)(2,1)S(1)}, bf16[8,256,256]{2,1,0:T(8,128)(2,1)}, u32[]{:S(2)}) %copy-start.1) | copy-done | bytes 1048600
  1.3 0.0 copy-start.2
  1.3 0.0 copy-start.3
  1.3 0.8 %shard_map.47 = (bf16[8,112,256]{2,1,0:T(8,128)(2,1)S(1)}, bf16[8,112,256]{2,1,0:T(8,128)(2,1)S(1)}, bf16[8,96,256]{2,1,0:T(8,128)(2,1)S(1)}, bf16[4,112,256]{2,...) custom-call(s32[3]{0:T(128)S(1)} %pad_add_fusion.flag_ref, ...), custom_call_target="tpu_custom_call" | custom-call | flops 1 | bytes 1 | tf_op jit(solution)/shard_map/pallas_call | solution.py:156
  2.1 2.1 %collective-permute-start.6 = (bf16[4,112,256]{2,1,0:T(8,128)(2,1)S(1)}, bf16[4,112,256]{2,1,0:T(8,128)(2,1)S(1)}, u32[]{:S(2)}, u32[]{:S(2)}) collective-permute-start(bf16[4,112,256]{2,1,0:T(8,128)(2,1)S(1)} %get-tuple-element.54), channel_id=1, source_target_pairs={{0,2},{2,0},{4,6},{6,4},{8,10},{10,8},{12,14},{14,12},{1,3},{3,1},... | collective-permute-start | bytes 688136 | tf_op jit(solution)/shard_map/ppermute | solution.py:434
  4.2 0.7 collective-permute-start.7
  4.9 0.0 copy-start
  4.9 2.0 %copy-done = bf16[3,3,3,256,256]{4,3,2,1,0:T(8,128)(2,1)S(1)} copy-done((bf16[3,3,3,256,256]{4,3,2,1,0:T(8,128)(2,1)S(1)}, bf16[3,3,3,256,256]{4,3,2,1,0:T(8,128)(2,1)}, u32[]{:S(2)}) %copy-start) | copy-done | bytes 3538968
  6.9 0.7 shard_map.46
  7.6 3.8 %collective-permute-start = (bf16[4,144,256]{2,1,0:T(8,128)(2,1)S(1)}, bf16[4,144,256]{2,1,0:T(8,128)(2,1)S(1)}, u32[]{:S(2)}, u32[]{:S(2)}) collective-permute-start(bf16[4,144,256]{2,1,0:T(8,128)(2,1)S(1)} %get-tuple-element.48), channel_id=1, source_target_pairs={{0,2},{2,0},{4,6},{6,4},{8,10},{10,8},{12,14},{14,12},{1,3},{3,1},... | collective-permute-start | bytes 884744 | tf_op jit(solution)/shard_map/ppermute | solution.py:449
  11.3 0.7 collective-permute-start.1
  12.0 0.0 copy-done.2
  12.0 0.0 copy-done.3
  12.0 1.2 %collective-permute-done.6.rest_1_ = bf16[4,112,256]{2,1,0:T(8,128)(2,1)S(1)} collective-permute-done((bf16[4,112,256]{2,1,0:T(8,128)(2,1)S(1)}, bf16[4,112,256]{2,1,0:T(8,128)(2,1)S(1)}, u32[]{:S(2)}, u32[]{:S(2)}) %collective-permute-start.6) | collective-permute-done | bytes 229408 | tf_op jit(solution)/shard_map/ppermute | solution.py:434
  13.2 0.0 collective-permute-done.7.rest_2_
  13.2 2.5 %shard_map.51 = (bf16[8,96,256]{2,1,0:T(8,128)(2,1)S(1)}, bf16[8,96,256]{2,1,0:T(8,128)(2,1)S(1)}) custom-call(s32[3]{0:T(128)S(1)} %pad_add_fusion.flag_ref, f32[6,256]{1,0:T(8,128)S(1)} %pad_maximum_fusion.scale_ref, bf16[3,3,256,256]{3,2,1,0:T(8,128)(2,1)S(1)} %get-tuple-element.46.w_ref, bf16[8,112,256]{2,1,0:T(8,128)(2,1)S(1)} %get-tuple-element.57.rest_0_, ...), custom_call_target="tpu_custom_call" | custom-call | flops 1 | bytes 1 | tf_op jit(solution)/shard_map/pallas_call | solution.py:223
  15.7 2.5 %collective-permute-start.8 = (bf16[8,96,256]{2,1,0:T(8,128)(2,1)S(1)}, bf16[8,96,256]{2,1,0:T(8,128)(2,1)S(1)}, u32[]{:S(2)}, u32[]{:S(2)}) collective-permute-start(bf16[8,96,256]{2,1,0:T(8,128)(2,1)S(1)} %get-tuple-element.58.far_ref), channel_id=1, source_target_pairs={{0,8},{2,10},{4,12},{6,14},{8,0},{10,2},{12,4},{14,6},{1,9},{3,11}... | collective-permute-start | bytes 1179656 | tf_op jit(solution)/shard_map/ppermute | solution.py:463
  18.2 7.8 %collective-permute-done.refs_1_.rest_1_.rest_3_ = bf16[4,144,256]{2,1,0:T(8,128)(2,1)S(1)} collective-permute-done((bf16[4,144,256]{2,1,0:T(8,128)(2,1)S(1)}, bf16[4,144,256]{2,1,0:T(8,128)(2,1)S(1)}, u32[]{:S(2)}, u32[]{:S(2)}) %collective-permute-start) | collective-permute-done | bytes 294944 | tf_op jit(solution)/shard_map/ppermute | solution.py:449
  26.0 0.0 collective-permute-done.1.refs_2_.rest_2_.rest_4_
  26.0 0.6 shard_map.48
  26.6 1.6 %collective-permute-start.2 = (bf16[16,16,256]{2,1,0:T(8,128)(2,1)S(1)}, bf16[16,16,256]{2,1,0:T(8,128)(2,1)S(1)}, u32[]{:S(2)}, u32[]{:S(2)}) collective-permute-start(bf16[16,16,256]{2,1,0:T(8,128)(2,1)S(1)} %shard_map.48), channel_id=1, source_target_pairs={{0,1},{1,0},{2,3},{3,2},{4,5},{5,4},{6,7},{7,6},{8,9},{9,8},{10,11... | collective-permute-start | bytes 393224 | tf_op jit(solution)/shard_map/ppermute | solution.py:475
  28.2 1.0 %collective-permute-done.2.rest_3_ = bf16[16,16,256]{2,1,0:T(8,128)(2,1)S(1)} collective-permute-done((bf16[16,16,256]{2,1,0:T(8,128)(2,1)S(1)}, bf16[16,16,256]{2,1,0:T(8,128)(2,1)S(1)}, u32[]{:S(2)}, u32[]{:S(2)}) %collective-permute-start.2) | collective-permute-done | bytes 131104 | tf_op jit(solution)/shard_map/ppermute | solution.py:475
  29.2 2.8 %shard_map.49 = (bf16[8,96,256]{2,1,0:T(8,128)(2,1)S(1)}, bf16[8,96,256]{2,1,0:T(8,128)(2,1)S(1)}, bf16[8,32,256]{2,1,0:T(8,128)(2,1)S(1)}, bf16[8,64,256]{2,1,0:T(8,128)(2,1)S(1)}) custom-call(s32[3]{0:T(128)S(1)} %pad_add_fusion.flag_ref, f32[6,256]{1,0:T(8,128)S(1)} %pad_maximum_fusion.scale_ref, bf16[3,3,256,256]{3,2,1,0:T(8,128)(2,1)S(1)} %get-tuple-element.46.w_ref, ...), custom_call_target="tpu_custom_call" | custom-call | flops 1 | bytes 1 | tf_op jit(solution)/shard_map/pallas_call | solution.py:223
  31.9 4.6 %collective-permute-start.4 = (bf16[8,32,256]{2,1,0:T(8,128)(2,1)S(1)}, bf16[8,32,256]{2,1,0:T(8,128)(2,1)S(1)}, u32[]{:S(2)}, u32[]{:S(2)}) collective-permute-start(bf16[8,32,256]{2,1,0:T(8,128)(2,1)S(1)} %get-tuple-element.60), channel_id=1, source_target_pairs={{0,8},{2,10},{4,12},{6,14},{8,0},{10,2},{12,4},{14,6},{1,9},{3,11}... | collective-permute-start | bytes 393224 | tf_op jit(solution)/shard_map/ppermute | solution.py:492
  36.5 0.1 collective-permute-start.3
  36.6 2.3 %shard_map.50 = (bf16[8,64,256]{2,1,0:T(8,128)(2,1)S(1)}, bf16[8,64,256]{2,1,0:T(8,128)(2,1)S(1)}) custom-call(s32[3]{0:T(128)S(1)} %pad_add_fusion.flag_ref, f32[6,256]{1,0:T(8,128)S(1)} %pad_maximum_fusion.scale_ref, bf16[3,3,256,256]{3,2,1,0:T(8,128)(2,1)S(1)} %get-tuple-element.46.w_ref, bf16[8,96,256]{2,1,0:T(8,128)(2,1)S(1)} %get-tuple-element.53.rest_0_, ...), custom_call_target="tpu_custom_call" | custom-call | flops 1 | bytes 1 | tf_op jit(solution)/shard_map/pallas_call | solution.py:223
  38.9 2.4 %collective-permute-start.10 = (bf16[8,64,256]{2,1,0:T(8,128)(2,1)S(1)}, bf16[8,64,256]{2,1,0:T(8,128)(2,1)S(1)}, u32[]{:S(2)}, u32[]{:S(2)}) collective-permute-start(bf16[8,64,256]{2,1,0:T(8,128)(2,1)S(1)} %get-tuple-element.56.mid_ref), channel_id=1, source_target_pairs={{0,8},{2,10},{4,12},{6,14},{8,0},{10,2},{12,4},{14,6},{1,9},{3,11}... | collective-permute-start | bytes 786440 | tf_op jit(solution)/shard_map/ppermute | solution.py:513
  41.3 11.1 %collective-permute-done.8.cfar_ref = bf16[8,96,256]{2,1,0:T(8,128)(2,1)S(1)} collective-permute-done((bf16[8,96,256]{2,1,0:T(8,128)(2,1)S(1)}, bf16[8,96,256]{2,1,0:T(8,128)(2,1)S(1)}, u32[]{:S(2)}, u32[]{:S(2)}) %collective-permute-start.8) | collective-permute-done | bytes 393248 | tf_op jit(solution)/shard_map/ppermute | solution.py:463
  52.3 3.8 %collective-permute-start.9 = (bf16[8,32,256]{2,1,0:T(8,128)(2,1)S(1)}, bf16[8,32,256]{2,1,0:T(8,128)(2,1)S(1)}, u32[]{:S(2)}, u32[]{:S(2)}) collective-permute-start(bf16[8,32,256]{2,1,0:T(8,128)(2,1)S(1)} %get-tuple-element.60), channel_id=1, source_target_pairs={{0,1},{1,0},{2,3},{3,2},{4,5},{5,4},{6,7},{7,6},{8,9},{9,8},{10,11... | collective-permute-start | bytes 393224 | tf_op jit(solution)/shard_map/ppermute | solution.py:516
  56.2 0.0 collective-permute-done.4.rim_ref
  56.2 2.8 %collective-permute-start.5 = (bf16[8,32,256]{2,1,0:T(8,128)(2,1)S(1)}, bf16[8,32,256]{2,1,0:T(8,128)(2,1)S(1)}, u32[]{:S(2)}, u32[]{:S(2)}) collective-permute-start(bf16[8,32,256]{2,1,0:T(8,128)(2,1)S(1)} %collective-permute-done.4.rim_ref), channel_id=1, source_target_pairs={{0,1},{1,0},{2,3},{3,2},{4,5},{5,4},{6,7},{7,6},{8,9},{9,8},{10,11... | collective-permute-start | bytes 393224 | tf_op jit(solution)/shard_map/ppermute | solution.py:540
  59.0 0.0 collective-permute-done.9.side_ref
  59.0 2.9 %shard_map.52 = (f32[8,256,256]{2,1,0:T(8,128)S(1)}, bf16[8,256,256]{2,1,0:T(8,128)(2,1)S(1)}, bf16[8,64,256]{2,1,0:T(8,128)(2,1)S(1)}, bf16[8,64,256]{2,1,0:T(8,128)(2,1)S(1)}) custom-call(s32[3]{0:T(128)S(1)} %pad_add_fusion.flag_ref, f32[6,256]{1,0:T(8,128)S(1)} %pad_maximum_fusion.scale_ref, bf16[2,3,256,256]{3,2,1,0:T(8,128)(2,1)S(1)} %get-tuple-element.42.w_ref, ...), custom_call_target="tpu_custom_call" | custom-call | flops 1 | bytes 1 | tf_op jit(solution)/shard_map/pallas_call | solution.py:518
  61.8 0.0 collective-permute-done.5.side_ref
  61.8 0.0 collective-permute-done.3.cnear_ref
  61.8 1.1 %shard_map.53 = (bf16[8,64,256]{2,1,0:T(8,128)(2,1)S(1)}, bf16[8,64,256]{2,1,0:T(8,128)(2,1)S(1)}) custom-call(s32[3]{0:T(128)S(1)} %pad_add_fusion.flag_ref, f32[6,256]{1,0:T(8,128)S(1)} %pad_maximum_fusion.scale_ref, bf16[2,3,256,256]{3,2,1,0:T(8,128)(2,1)S(1)} %get-tuple-element.42.w_ref, bf16[8,64,256]{2,1,0:T(8,128)(2,1)S(1)} %collective-permute-done.3.cnear_ref, ...), custom_call_target="tpu_custom_call" | custom-call | flops 1 | bytes 1 | tf_op jit(solution)/shard_map/pallas_call | solution.py:518
  63.0 1.0 %shard_map.54 = (f32[8,256,256]{2,1,0:T(8,128)S(1)}, bf16[2,8,64,256]{3,2,1,0:T(8,128)(2,1)S(1)}) custom-call(s32[3]{0:T(128)S(1)} %pad_add_fusion.flag_ref, f32[6,256]{1,0:T(8,128)S(1)} %pad_maximum_fusion.scale_ref, bf16[3,256,256]{2,1,0:T(8,128)(2,1)S(1)} %get-tuple-element.41.w_ref, bf16[8,64,256]{2,1,0:T(8,128)(2,1)S(1)} %get-tuple-element.66.near2_ref, ...), custom_call_target="tpu_custom_call" | custom-call | flops 1 | bytes 1 | tf_op jit(solution)/shard_map/pallas_call | solution.py:518
  64.0 2.3 %collective-permute-done.10.cmid_ref = bf16[8,64,256]{2,1,0:T(8,128)(2,1)S(1)} collective-permute-done((bf16[8,64,256]{2,1,0:T(8,128)(2,1)S(1)}, bf16[8,64,256]{2,1,0:T(8,128)(2,1)S(1)}, u32[]{:S(2)}, u32[]{:S(2)}) %collective-permute-start.10) | collective-permute-done | bytes 262176 | tf_op jit(solution)/shard_map/ppermute | solution.py:513
  66.4 2.1 %collective-permute-start.11 = (bf16[8,64,256]{2,1,0:T(8,128)(2,1)S(1)}, bf16[8,64,256]{2,1,0:T(8,128)(2,1)S(1)}, u32[]{:S(2)}, u32[]{:S(2)}) collective-permute-start(bf16[8,64,256]{2,1,0:T(8,128)(2,1)S(1)} %get-tuple-element.75.near_ref), channel_id=1, source_target_pairs={{0,1},{1,0},{2,3},{3,2},{4,5},{5,4},{6,7},{7,6},{8,9},{9,8},{10,11... | collective-permute-start | bytes 786440 | tf_op jit(solution)/shard_map/ppermute | solution.py:560
  68.5 1.5 %shard_map.55 = (bf16[8,128,256]{2,1,0:T(8,128)(2,1)S(1)}, bf16[8,128,256]{2,1,0:T(8,128)(2,1)S(1)}) custom-call(s32[3]{0:T(128)S(1)} %pad_add_fusion.flag_ref, f32[6,256]{1,0:T(8,128)S(1)} %pad_maximum_fusion.scale_ref, bf16[2,3,256,256]{3,2,1,0:T(8,128)(2,1)S(1)} %get-tuple-element.42.w_ref, bf16[8,64,256]{2,1,0:T(8,128)(2,1)S(1)} %collective-permute-done.10.cmid_ref, ...), custom_call_target="tpu_custom_call" | custom-call | flops 1 | bytes 1 | tf_op jit(solution)/shard_map/pallas_call | solution.py:518
  70.0 0.0 collective-permute-done.11.side_ref
  70.0 2.1 %shard_map.56 = bf16[8,256,256]{2,1,0:T(8,128)(2,1)} custom-call(s32[3]{0:T(128)S(1)} %pad_add_fusion.flag_ref, f32[6,256]{1,0:T(8,128)S(1)} %pad_maximum_fusion.scale_ref, bf16[3,256,256]{2,1,0:T(8,128)(2,1)S(1)} %get-tuple-element.41.w_ref, bf16[2,8,64,256]{3,2,1,0:T(8,128)(2,1)S(1)} %get-tuple-element.70.ends_ref, ...), custom_call_target="tpu_custom_call" | custom-call | flops 1 | bytes 1 | tf_op jit(solution)/shard_map/pallas_call | solution.py:568
  (1 shorter events, 0.0 us)
Async XLA Ops:
  0.1 1.2 %copy-start.1 = (bf16[8,256,256]{2,1,0:T(8,128)(2,1)S(1)}, bf16[8,256,256]{2,1,0:T(8,128)(2,1)}, u32[]{:S(2)}) copy-start(bf16[8,256,256]{2,1,0:T(8,128)(2,1)} %refs_0_.1) | copy-start | bytes 3145732
  1.3 10.7 %copy-start.2 = (f32[3,256]{1,0:T(4,128)S(1)}, f32[3,256]{1,0:T(4,128)}, u32[]{:S(2)}) copy-start(f32[3,256]{1,0:T(4,128)} %param.6) | copy-start | bytes 9220
  1.3 10.7 %copy-start.3 = (f32[3,256]{1,0:T(4,128)S(1)}, f32[3,256]{1,0:T(4,128)}, u32[]{:S(2)}) copy-start(f32[3,256]{1,0:T(4,128)} %param.5) | copy-start | bytes 9220
  2.1 11.2 %collective-permute-start.6 = (bf16[4,112,256]{2,1,0:T(8,128)(2,1)S(1)}, bf16[4,112,256]{2,1,0:T(8,128)(2,1)S(1)}, u32[]{:S(2)}, u32[]{:S(2)}) collective-permute-start(bf16[4,112,256]{2,1,0:T(8,128)(2,1)S(1)} %get-tuple-element.54), channel_id=1, source_target_pairs={{0,2},{2,0},{4,6},{6,4},{8,10},{10,8},{12,14},{14,12},{1,3},{3,1},... | collective-permute-start | bytes 688136 | tf_op jit(solution)/shard_map/ppermute | solution.py:434
  4.2 9.0 %collective-permute-start.7 = (bf16[4,112,256]{2,1,0:T(8,128)(2,1)S(1)}, bf16[4,112,256]{2,1,0:T(8,128)(2,1)S(1)}, u32[]{:S(2)}, u32[]{:S(2)}) collective-permute-start(bf16[4,112,256]{2,1,0:T(8,128)(2,1)S(1)} %get-tuple-element.55), channel_id=1, source_target_pairs={{2,4},{4,2},{6,8},{8,6},{10,12},{12,10},{3,5},{5,3},{7,9},{9,7},{1... | collective-permute-start | bytes 688136 | tf_op jit(solution)/shard_map/ppermute | solution.py:435
  4.9 2.0 %copy-start = (bf16[3,3,3,256,256]{4,3,2,1,0:T(8,128)(2,1)S(1)}, bf16[3,3,3,256,256]{4,3,2,1,0:T(8,128)(2,1)}, u32[]{:S(2)}) copy-start(bf16[3,3,3,256,256]{4,3,2,1,0:T(8,128)(2,1)} %w_ref.1) | copy-start | bytes 10616836
  7.6 18.5 %collective-permute-start = (bf16[4,144,256]{2,1,0:T(8,128)(2,1)S(1)}, bf16[4,144,256]{2,1,0:T(8,128)(2,1)S(1)}, u32[]{:S(2)}, u32[]{:S(2)}) collective-permute-start(bf16[4,144,256]{2,1,0:T(8,128)(2,1)S(1)} %get-tuple-element.48), channel_id=1, source_target_pairs={{0,2},{2,0},{4,6},{6,4},{8,10},{10,8},{12,14},{14,12},{1,3},{3,1},... | collective-permute-start | bytes 884744 | tf_op jit(solution)/shard_map/ppermute | solution.py:449
  11.3 14.7 %collective-permute-start.1 = (bf16[4,144,256]{2,1,0:T(8,128)(2,1)S(1)}, bf16[4,144,256]{2,1,0:T(8,128)(2,1)S(1)}, u32[]{:S(2)}, u32[]{:S(2)}) collective-permute-start(bf16[4,144,256]{2,1,0:T(8,128)(2,1)S(1)} %get-tuple-element.49), channel_id=1, source_target_pairs={{2,4},{4,2},{6,8},{8,6},{10,12},{12,10},{3,5},{5,3},{7,9},{9,7},{1... | collective-permute-start | bytes 884744 | tf_op jit(solution)/shard_map/ppermute | solution.py:450
  15.7 36.6 %collective-permute-start.8 = (bf16[8,96,256]{2,1,0:T(8,128)(2,1)S(1)}, bf16[8,96,256]{2,1,0:T(8,128)(2,1)S(1)}, u32[]{:S(2)}, u32[]{:S(2)}) collective-permute-start(bf16[8,96,256]{2,1,0:T(8,128)(2,1)S(1)} %get-tuple-element.58.far_ref), channel_id=1, source_target_pairs={{0,8},{2,10},{4,12},{6,14},{8,0},{10,2},{12,4},{14,6},{1,9},{3,11}... | collective-permute-start | bytes 1179656 | tf_op jit(solution)/shard_map/ppermute | solution.py:463
  26.6 2.6 %collective-permute-start.2 = (bf16[16,16,256]{2,1,0:T(8,128)(2,1)S(1)}, bf16[16,16,256]{2,1,0:T(8,128)(2,1)S(1)}, u32[]{:S(2)}, u32[]{:S(2)}) collective-permute-start(bf16[16,16,256]{2,1,0:T(8,128)(2,1)S(1)} %shard_map.48), channel_id=1, source_target_pairs={{0,1},{1,0},{2,3},{3,2},{4,5},{5,4},{6,7},{7,6},{8,9},{9,8},{10,11... | collective-permute-start | bytes 393224 | tf_op jit(solution)/shard_map/ppermute | solution.py:475
  31.9 24.2 %collective-permute-start.4 = (bf16[8,32,256]{2,1,0:T(8,128)(2,1)S(1)}, bf16[8,32,256]{2,1,0:T(8,128)(2,1)S(1)}, u32[]{:S(2)}, u32[]{:S(2)}) collective-permute-start(bf16[8,32,256]{2,1,0:T(8,128)(2,1)S(1)} %get-tuple-element.60), channel_id=1, source_target_pairs={{0,8},{2,10},{4,12},{6,14},{8,0},{10,2},{12,4},{14,6},{1,9},{3,11}... | collective-permute-start | bytes 393224 | tf_op jit(solution)/shard_map/ppermute | solution.py:492
  36.5 25.3 %collective-permute-start.3 = (bf16[8,64,256]{2,1,0:T(8,128)(2,1)S(1)}, bf16[8,64,256]{2,1,0:T(8,128)(2,1)S(1)}, u32[]{:S(2)}, u32[]{:S(2)}) collective-permute-start(bf16[8,64,256]{2,1,0:T(8,128)(2,1)S(1)} %get-tuple-element.50), channel_id=1, source_target_pairs={{0,8},{2,10},{4,12},{6,14},{8,0},{10,2},{12,4},{14,6},{1,9},{3,11}... | collective-permute-start | bytes 786440 | tf_op jit(solution)/shard_map/ppermute | solution.py:493
  38.9 27.5 %collective-permute-start.10 = (bf16[8,64,256]{2,1,0:T(8,128)(2,1)S(1)}, bf16[8,64,256]{2,1,0:T(8,128)(2,1)S(1)}, u32[]{:S(2)}, u32[]{:S(2)}) collective-permute-start(bf16[8,64,256]{2,1,0:T(8,128)(2,1)S(1)} %get-tuple-element.56.mid_ref), channel_id=1, source_target_pairs={{0,8},{2,10},{4,12},{6,14},{8,0},{10,2},{12,4},{14,6},{1,9},{3,11}... | collective-permute-start | bytes 786440 | tf_op jit(solution)/shard_map/ppermute | solution.py:513
  52.3 6.6 %collective-permute-start.9 = (bf16[8,32,256]{2,1,0:T(8,128)(2,1)S(1)}, bf16[8,32,256]{2,1,0:T(8,128)(2,1)S(1)}, u32[]{:S(2)}, u32[]{:S(2)}) collective-permute-start(bf16[8,32,256]{2,1,0:T(8,128)(2,1)S(1)} %get-tuple-element.60), channel_id=1, source_target_pairs={{0,1},{1,0},{2,3},{3,2},{4,5},{5,4},{6,7},{7,6},{8,9},{9,8},{10,11... | collective-permute-start | bytes 393224 | tf_op jit(solution)/shard_map/ppermute | solution.py:516
  56.2 5.7 %collective-permute-start.5 = (bf16[8,32,256]{2,1,0:T(8,128)(2,1)S(1)}, bf16[8,32,256]{2,1,0:T(8,128)(2,1)S(1)}, u32[]{:S(2)}, u32[]{:S(2)}) collective-permute-start(bf16[8,32,256]{2,1,0:T(8,128)(2,1)S(1)} %collective-permute-done.4.rim_ref), channel_id=1, source_target_pairs={{0,1},{1,0},{2,3},{3,2},{4,5},{5,4},{6,7},{7,6},{8,9},{9,8},{10,11... | collective-permute-start | bytes 393224 | tf_op jit(solution)/shard_map/ppermute | solution.py:540
  66.4 3.6 %collective-permute-start.11 = (bf16[8,64,256]{2,1,0:T(8,128)(2,1)S(1)}, bf16[8,64,256]{2,1,0:T(8,128)(2,1)S(1)}, u32[]{:S(2)}, u32[]{:S(2)}) collective-permute-start(bf16[8,64,256]{2,1,0:T(8,128)(2,1)S(1)} %get-tuple-element.75.near_ref), channel_id=1, source_target_pairs={{0,1},{1,0},{2,3},{3,2},{4,5},{5,4},{6,7},{7,6},{8,9},{9,8},{10,11... | collective-permute-start | bytes 786440 | tf_op jit(solution)/shard_map/ppermute | solution.py:560
